TPU v7x, 32 devices: a whole 2x2x4 slice. The times are simulated.
32 devices in a mesh: grp: 2 (over y), res: 8 (over z, x), seq: 2 (over core).
Axes of the slice: x: 2, y: 2, z: 4, core: 2. Of those that a mesh axis runs over, the one named last changes fastest.
Arguments:
- homolog_matrix: bfloat16 [128, 32, 256], P(('grp', 'seq'), 'res'), parts along dimension 0, may hold values from -600 to 600
- standardizer_scaling: float32 [256], replicated, may hold values from 0.4 to 1.6
- standardizer_offset: float32 [256], replicated, may hold values from -3 to 3
- left_projection_matrix: bfloat16 [256, 32], replicated, may hold values from -0.375 to 0.375
- left_offset_vector: float32 [32], replicated, may hold values from -3 to 3
- right_projection_matrix: bfloat16 [256, 32], replicated, may hold values from -0.375 to 0.375
- right_offset_vector: float32 [32], replicated, may hold values from -3 to 3
- coupling_matrix: bfloat16 [1024, 128], replicated, may hold values from -0.75 to 0.75
- coupling_offset: float32 [128], replicated, may hold values from -3 to 3
- coupling_cotangent: bfloat16 [64, 32, 128], P(('grp', 'res'), 'seq'), parts along dimension 0, may hold values from -6 to 6
Outputs:
- pair_delta: bfloat16 [64, 32, 128], P(('grp', 'res'), 'seq'), parts along dimension 0
- alignment_gradient: bfloat16 [128, 32, 256], P(('grp', 'seq'), 'res'), parts along dimension 0
There are 2 independent parts, one for each index of `grp`. A program takes and returns all parts, laid end to end along the dimension named above; an argument that names none is the same for every part. Nothing has to cross between parts.
All inputs are finite; a program needn't handle non-finite values.
Results may differ from a plain program's by a relative error of at most 0.0063.
Values may be sent and summed in bfloat16 or wider, within the bound.
No kernel may reach another device: no remote copies, remote signals or barrier semaphores. Data moves between devices by JAX's collectives and lax.ppermute only.
A program may use at most 128 MiB of HBM per device.

v0:
```python
import jax
import jax.numpy as jnp
from jax import lax
from jax.sharding import PartitionSpec as P


def standardize_features(homolog_matrix, scaling_multiplier, additive_offset):
    incoming_tensor = homolog_matrix.astype(jnp.float32)
    row_mean = jnp.mean(incoming_tensor, axis=-1, keepdims=True)
    centred = incoming_tensor - row_mean
    reciprocal_spread = lax.rsqrt(jnp.mean(centred * centred, axis=-1, keepdims=True) + 1e-05)
    standardized_lines = centred * reciprocal_spread
    standardized_result = (standardized_lines * scaling_multiplier + additive_offset).astype(
        jnp.bfloat16
    )
    return (standardized_lines, reciprocal_spread, standardized_result)


def project_flat(flat_rows, weight, additive_offset):
    return (
        jnp.dot(flat_rows, weight, preferred_element_type=jnp.float32) + additive_offset
    ).astype(jnp.bfloat16)


def cot_outer(cot_block, coupling_matrix, seq_count, depth_p):
    first, second, pair_width = cot_block.shape
    result = (
        jnp.dot(
            cot_block.reshape(-1, pair_width), coupling_matrix.T, preferred_element_type=jnp.float32
        )
        / seq_count
    )
    return result.astype(jnp.bfloat16).reshape(first, second, depth_p, depth_p)


def body(
    homolog_matrix,
    standardizer_scaling,
    standardizer_offset,
    left_projection_matrix,
    left_offset_vector,
    right_projection_matrix,
    right_offset_vector,
    coupling_matrix,
    coupling_offset,
    coupling_cotangent,
):
    homolog_mesh_split, amino_mesh_split, feature_total = homolog_matrix.shape
    depth_p = left_projection_matrix.shape[1]
    pair_width = coupling_matrix.shape[1]
    seq_count = homolog_mesh_split * lax.axis_size("seq")
    res_count = amino_mesh_split * lax.axis_size("res")
    standardized_lines, reciprocal_spread, standardized_result = standardize_features(
        homolog_matrix, standardizer_scaling, standardizer_offset
    )
    flat_rows = standardized_result.reshape(homolog_mesh_split * amino_mesh_split, feature_total)
    left_proj = project_flat(flat_rows, left_projection_matrix, left_offset_vector).reshape(
        homolog_mesh_split, amino_mesh_split * depth_p
    )
    right_proj = project_flat(flat_rows, right_projection_matrix, right_offset_vector).reshape(
        homolog_mesh_split, amino_mesh_split * depth_p
    )
    left_all, right_all = (
        lax.all_gather(left_proj, "res", axis=1, tiled=True),
        lax.all_gather(right_proj, "res", axis=1, tiled=True),
    )
    left_own = left_proj.reshape(homolog_mesh_split, amino_mesh_split, depth_p)
    left_rows = left_all.reshape(homolog_mesh_split, res_count, depth_p)
    right_rows = right_all.reshape(homolog_mesh_split, res_count, depth_p)
    wide_weight = coupling_matrix.astype(jnp.float32)
    outer_sum = (
        jnp.einsum("sic,sjd->ijcd", left_own, right_rows, preferred_element_type=jnp.float32)
        / seq_count
    )
    pair_term = jnp.dot(
        outer_sum.reshape(-1, depth_p * depth_p), wide_weight, precision=lax.Precision.HIGHEST
    )
    pair_term = pair_term.reshape(amino_mesh_split, res_count, pair_width)
    summed = lax.psum_scatter(pair_term, "seq", scatter_dimension=1, tiled=True)
    pair_delta = (summed + coupling_offset).astype(jnp.bfloat16)
    cot_rows = lax.all_gather(coupling_cotangent, "seq", axis=1, tiled=True)
    cot_cols = lax.all_to_all(cot_rows, "res", split_axis=1, concat_axis=0, tiled=True)
    outer_rows = cot_outer(cot_rows, coupling_matrix, seq_count, depth_p)
    outer_cols = cot_outer(cot_cols, coupling_matrix, seq_count, depth_p)
    left_cot = jnp.einsum(
        "ijcd,sjd->sic", outer_rows, right_rows, preferred_element_type=jnp.float32
    )
    right_cot = jnp.einsum(
        "ijcd,sic->sjd", outer_cols, left_rows, preferred_element_type=jnp.float32
    )
    ln_cot = jnp.dot(
        left_cot.reshape(-1, depth_p),
        left_projection_matrix.astype(jnp.float32).T,
        precision=lax.Precision.HIGHEST,
    )
    ln_cot = ln_cot + jnp.dot(
        right_cot.reshape(-1, depth_p),
        right_projection_matrix.astype(jnp.float32).T,
        precision=lax.Precision.HIGHEST,
    )
    ln_cot = ln_cot.reshape(homolog_mesh_split, amino_mesh_split, feature_total)
    gain_gradient = ln_cot * standardizer_scaling
    alignment_gradient = reciprocal_spread * (
        gain_gradient
        - jnp.mean(gain_gradient, axis=-1, keepdims=True)
        - standardized_lines * jnp.mean(gain_gradient * standardized_lines, axis=-1, keepdims=True)
    )
    return (pair_delta, alignment_gradient.astype(jnp.bfloat16))


def solution(mesh):
    return jax.shard_map(
        body,
        mesh=mesh,
        in_specs=(
            P(("grp", "seq"), "res", None),
            P(),
            P(),
            P(),
            P(),
            P(),
            P(),
            P(),
            P(),
            P(("grp", "res"), "seq", None),
        ),
        out_specs=(P(("grp", "res"), "seq", None), P(("grp", "seq"), "res", None)),
        check_vma=False,
    )
```

profile of v0, /device:TPU:0, one launch (start us, length us, event | category | flops | bytes accessed | tf_op | source)
XLA Modules:
  0.0 94.7 jit_solution(9384315481444654136)
XLA Ops:
  7.2 2.5 %all_gather.10 = bf16[4,32,128]{2,1,0:T(8,128)(2,1)S(1)} all-gather(bf16[4,16,128]{2,1,0:T(8,128)(2,1)} %param.19), channel_id=1, replica_groups=mesh['grp'=2,'res'=8,'seq'=2] {'seq'}, dimensions={1}, use_global_device_ids=true | all-gather | bytes 49152 | tf_op jit(solution)/shard_map/all_gather | solution.py:81
  9.7 0.6 copy.50
  10.3 7.1 %all-to-all-start = ((bf16[4,32,128]{2,0,1:T(4,128)(2,1)}), bf16[4,32,128]{2,0,1:T(4,128)(2,1)S(1)}, u32[]{:S(2)}, u32[]{:S(2)}) async-start(bf16[4,32,128]{2,0,1:T(4,128)(2,1)} %copy.50), calls=%async_computation.1 | async-start | bytes 65536 | tf_op jit(solution)/shard_map/all_to_all | solution.py:82
  17.5 0.9 convert_reduce_fusion
  18.5 1.0 %fusion.19 = f32[32,4]{1,0:T(8,128)S(1)} fusion(bf16[32,4,256]{2,1,0:T(4,128)(2,1)} %param.10, f32[32,4]{1,0:T(8,128)S(1)} %broadcast_multiply_fusion.1), kind=kLoop, calls=%fused_computation.29 | loop fusion | flops 130944 | bytes 66560 | tf_op jit(solution)/shard_map/reduce_sum | solution.py:11
  19.5 1.0 %fusion.14 = bf16[32,4,256]{2,1,0:T(4,128)(2,1)S(1)} fusion(bf16[32,4,256]{2,1,0:T(4,128)(2,1)} %param.10, f32[256]{0:T(256)} %param.12, f32[256]{0:T(256)} %param.11, f32[32,4]{1,0:T(8,128)S(1)} %add_rsqrt_fusion, f32[32,4]{1,0:T(8,128)S(1)} %broadcast_multiply_fusion.1), kind=kLoop, calls=%fused_computation.24 | loop fusion | flops 196608 | bytes 134144 | tf_op jit(solution)/shard_map/convert_element_type | solution.py:13
  20.6 0.8 fusion.3
  21.5 0.8 fusion.2
  22.6 26.5 %all_gather.9 = bf16[32,1024]{1,0:T(8,128)(2,1)S(1)} all-gather(bf16[32,128]{1,0:T(8,128)(2,1)S(1)} %reshape.77), channel_id=1, replica_groups=mesh['grp'=2,'res'=8,'seq'=2] {'res'}, dimensions={1}, use_global_device_ids=true | all-gather | bytes 73728 | tf_op jit(solution)/shard_map/all_gather | solution.py:65
  49.3 1.8 %multiply_bitcast_fusion = f32[4,32,32,32]{2,3,0,1:T(8,128)} fusion(bf16[32,32,32,1]{0,2,3,1:T(8,128)(2,1)S(1)} %bitcast.54, bf16[32,4,32]{2,1,0:T(4,128)(2,1)S(1)} %bitcast.56), kind=kOutput, calls=%fused_computation | convolution fusion | flops 8519680 | bytes 598016 | tf_op jit(solution)/shard_map/sic,sjd->ijcd/dot_general | solution.py:72
  51.1 1.9 %copy.46 = f32[4,32,32,32]{3,2,1,0:T(8,128)S(1)} copy(f32[4,32,32,32]{2,3,0,1:T(8,128)} %multiply_bitcast_fusion) | data formatting | bytes 1048576 | tf_op jit(solution)/shard_map/div | solution.py:72
  53.0 1.0 %dot_general.35 = f32[4,32,1024]{2,1,0:T(8,128)S(1)} reshape(f32[4,32,32,32]{3,2,1,0:T(8,128)S(1)} %copy.46) | data formatting | bytes 1048576 | tf_op jit(solution)/shard_map/dot_general | solution.py:75
  54.0 1.0 %fusion.5 = f32[4,32,128]{2,1,0:T(8,128)} fusion(f32[4,32,1024]{2,1,0:T(8,128)S(1)} %dot_general.35, bf16[1024,128]{1,0:T(8,128)(2,1)S(1)} %copy-done), kind=kOutput, calls=%fused_computation.13 | convolution fusion | flops 201326592 | bytes 851968 | tf_op jit(solution)/shard_map/dot_general | solution.py:75
  55.0 0.2 fusion
  55.2 0.8 reshape.80
  56.0 0.9 convolution_bitcast_fusion.1
  57.3 26.0 %all_gather.11 = bf16[32,1024]{1,0:T(8,128)(2,1)S(1)} all-gather(bf16[32,128]{1,0:T(8,128)(2,1)S(1)} %reshape.82), channel_id=1, replica_groups=mesh['grp'=2,'res'=8,'seq'=2] {'res'}, dimensions={1}, use_global_device_ids=true | all-gather | bytes 73728 | tf_op jit(solution)/shard_map/all_gather | solution.py:64
  83.5 0.2 fusion.1
  83.8 0.8 reshape.85
  84.5 0.4 convolution_bitcast_fusion
  85.0 0.3 multiply_reduce_fusion
  85.4 0.2 fusion.15
  85.7 0.8 fusion.18
  86.5 1.4 %add_convert_fusion = bf16[4,16,128]{2,1,0:T(8,128)(2,1)} fusion(f32[4,16,128]{2,1,0:T(8,128)} %reduce-scatter.2.cloned.1.call-done, f32[128]{0:T(128)S(1)} %copy-done.5), kind=kLoop, calls=%fused_computation.33 | loop fusion | flops 16384 | bytes 49664 | tf_op jit(solution)/shard_map/convert_element_type | solution.py:80
  (33 shorter events, 1.5 us)
Async XLA Ops:
  7.2 46.8 %copy-start = (bf16[1024,128]{1,0:T(8,128)(2,1)S(1)}, bf16[1024,128]{1,0:T(8,128)(2,1)}, u32[]{:S(2)}) copy-start(bf16[1024,128]{1,0:T(8,128)(2,1)} %param.17) | copy-start | bytes 786436
  10.3 73.2 %all-to-all-start = ((bf16[4,32,128]{2,0,1:T(4,128)(2,1)}), bf16[4,32,128]{2,0,1:T(4,128)(2,1)S(1)}, u32[]{:S(2)}, u32[]{:S(2)}) async-start(bf16[4,32,128]{2,0,1:T(4,128)(2,1)} %copy.50), calls=%async_computation.1 | async-start | bytes 65536 | tf_op jit(solution)/shard_map/all_to_all | solution.py:82
  17.5 69.0 %reduce-scatter.2.cloned.1.call-start = ((), (), s32[]{:S(2)}) async-start(), calls=%async_computation.2 | async-start | bytes 98304 | tf_op jit(solution)/shard_map/reduce_scatter | solution.py:79
  54.0 3.1 %copy-start.3 = (bf16[256,32]{0,1:T(8,128)(2,1)S(1)}, bf16[256,32]{0,1:T(8,128)(2,1)}, u32[]{:S(2)}) copy-start(bf16[256,32]{0,1:T(8,128)(2,1)} %param.13) | copy-start | bytes 49156
  57.0 28.0 %copy-start.2 = (f32[256]{0:T(256)S(1)}, f32[256]{0:T(256)}, u32[]{:S(2)}) copy-start(f32[256]{0:T(256)} %param.11) | copy-start | bytes 3076
  57.0 28.0 %copy-start.4 = (bf16[256,32]{0,1:T(8,128)(2,1)S(1)}, bf16[256,32]{0,1:T(8,128)(2,1)}, u32[]{:S(2)}) copy-start(bf16[256,32]{0,1:T(8,128)(2,1)} %param.15) | copy-start | bytes 49156
  83.5 1.9 %copy-start.1 = (bf16[32,4,256]{2,1,0:T(4,128)(2,1)S(1)}, bf16[32,4,256]{2,1,0:T(4,128)(2,1)}, u32[]{:S(2)}) copy-start(bf16[32,4,256]{2,1,0:T(4,128)(2,1)} %param.10) | copy-start | bytes 196612
  83.8 2.7 %copy-start.5 = (f32[128]{0:T(128)S(1)}, f32[128]{0:T(128)}, u32[]{:S(2)}) copy-start(f32[128]{0:T(128)} %param.18) | copy-start | bytes 1540
Sparse Core Ops, SparseCore 0:
  55.1 6.7 reduce-scatter.1
where the time goes:
time: 95.3 us; the launch traced here: 94.7 us
  blocking collectives  55 us (58%)
  between operations  14.3 us (15%)
  starting transfers between devices  7.17 us (8%)
  matrix products  6.59 us (7%)
  local copies, waits for them, and re-layouts  6.27 us (7%)
  other arithmetic  5.4 us (6%)
    all_gather x1, blocking collectives, body(): lax.all_gather(right_proj, 'res', axis=1, tiled=True)  26.5 us
    all_gather x1, blocking collectives, body(): lax.all_gather(left_proj, 'res', axis=1, tiled=True)  26 us
    all_to_all x1, starting transfers between devices, body(): lax.all_to_all(cot_rows, 'res', split_axis=1, concat_axis=0, tiled=True)  7.14 us
    all_gather x1, blocking collectives, body(): cot_rows = lax.all_gather(coupling_cotangent, 'seq', axis=1, tiled=True)  2.52 us
    div x1, local copies, waits for them, and re-layouts, body(): jnp.einsum('sic,sjd->ijcd', left_own, right_rows, preferred_element_type=...  1.93 us
  transfers between devices with their start and end apart: 2, of which 0 were waited for; matrix products, arithmetic and copies ran while one was open for 17% of the time, Pallas kernels for 0%

commit v1 on v0

--- a/solution.py
+++ b/solution.py
@@ -60,10 +60,31 @@
     right_proj = project_flat(flat_rows, right_projection_matrix, right_offset_vector).reshape(
         homolog_mesh_split, amino_mesh_split * depth_p
     )
-    left_all, right_all = (
-        lax.all_gather(left_proj, "res", axis=1, tiled=True),
-        lax.all_gather(right_proj, "res", axis=1, tiled=True),
+    seq_index = lax.axis_index("seq")
+    swap = [(0, 1), (1, 0)]
+    other_cot = lax.ppermute(coupling_cotangent, "seq", swap)
+    cot_rows = jnp.where(
+        seq_index == 0,
+        jnp.concatenate([coupling_cotangent, other_cot], axis=1),
+        jnp.concatenate([other_cot, coupling_cotangent], axis=1),
     )
+    ranks = lax.axis_size("res")
+    proj_both = jnp.concatenate([left_proj, right_proj], axis=0)
+    cot_parts = cot_rows.reshape(amino_mesh_split, ranks, amino_mesh_split, pair_width)
+    cot_parts = cot_parts.transpose(1, 0, 2, 3).reshape(
+        ranks, amino_mesh_split * amino_mesh_split, pair_width
+    )
+    packed = jnp.concatenate(
+        [jnp.broadcast_to(proj_both[None], (ranks,) + proj_both.shape), cot_parts], axis=1
+    )
+    packed = lax.all_to_all(packed, "res", split_axis=0, concat_axis=0, tiled=True)
+    left_all = packed[:, :homolog_mesh_split].transpose(1, 0, 2).reshape(homolog_mesh_split, -1)
+    right_all = (
+        packed[:, homolog_mesh_split : 2 * homolog_mesh_split]
+        .transpose(1, 0, 2)
+        .reshape(homolog_mesh_split, -1)
+    )
+    cot_cols = packed[:, 2 * homolog_mesh_split :].reshape(res_count, amino_mesh_split, pair_width)
     left_own = left_proj.reshape(homolog_mesh_split, amino_mesh_split, depth_p)
     left_rows = left_all.reshape(homolog_mesh_split, res_count, depth_p)
     right_rows = right_all.reshape(homolog_mesh_split, res_count, depth_p)
@@ -76,10 +97,11 @@
         outer_sum.reshape(-1, depth_p * depth_p), wide_weight, precision=lax.Precision.HIGHEST
     )
     pair_term = pair_term.reshape(amino_mesh_split, res_count, pair_width)
-    summed = lax.psum_scatter(pair_term, "seq", scatter_dimension=1, tiled=True)
+    half = res_count // 2
+    own_half = lax.dynamic_slice_in_dim(pair_term, seq_index * half, half, axis=1)
+    other_half = lax.dynamic_slice_in_dim(pair_term, (1 - seq_index) * half, half, axis=1)
+    summed = own_half + lax.ppermute(other_half, "seq", swap)
     pair_delta = (summed + coupling_offset).astype(jnp.bfloat16)
-    cot_rows = lax.all_gather(coupling_cotangent, "seq", axis=1, tiled=True)
-    cot_cols = lax.all_to_all(cot_rows, "res", split_axis=1, concat_axis=0, tiled=True)
     outer_rows = cot_outer(cot_rows, coupling_matrix, seq_count, depth_p)
     outer_cols = cot_outer(cot_cols, coupling_matrix, seq_count, depth_p)
     left_cot = jnp.einsum(

time: 95.3 us -> 34.2 us (0.36)
  blocking collectives: 55 us -> 0 us
  between operations: 14.3 us -> 0.96 us
  waiting for transfers between devices: 0.02 us -> 7.46 us
    all_gather x3 -> x0, blocking collectives: 55 us -> none  [the longest x1 26.5 us: body(): lax.all_gather(right_proj, 'res', axis=1, tiled=True)]
    all_to_all x1, waiting for transfers between devices: 0.01 us -> 7.1 us  [body(): lax.all_to_all(packed, 'res', split_axis=0, concat_axis=0, tiled=True)]
  transfers between devices with their start and end apart: 2 -> 3, of which waited for: 0 -> 2; matrix products, arithmetic and copies ran while one was open for 17% -> 21% of each run, Pallas kernels for 0% -> 0%
where the time goes in v1:
time: 34.2 us; the launch traced here: 33.6 us
  waiting for transfers between devices  7.46 us (22%)
  starting transfers between devices  7.41 us (22%)
  other arithmetic  6.13 us (18%)
  matrix products  5.96 us (17%)
  local copies, waits for them, and re-layouts  5.69 us (17%)
  between operations  0.96 us (3%)
    all_to_all x1, waiting for transfers between devices, body(): lax.all_to_all(packed, 'res', split_axis=0, concat_axis=0, tiled=True)  7.1 us
    all_to_all x1, starting transfers between devices, body(): lax.all_to_all(packed, 'res', split_axis=0, concat_axis=0, tiled=True)  6.82 us
    div x1, local copies, waits for them, and re-layouts, body(): jnp.einsum('sic,sjd->ijcd', left_own, right_rows, preferred_element_type=...  1.93 us
    dot_general x1, matrix products, body(): jnp.einsum('sic,sjd->ijcd', left_own, right_rows, preferred_element_type=...  1.76 us
    dot_general x2, matrix products, project_flat(): jnp.dot(flat_rows, weight, preferred_element_type=jnp.float32)  1.63 us
    reshape x2, local copies, waits for them, and re-layouts, cot_outer(): return result.astype(jnp.bfloat16).reshape(first, second, depth_p, depth_p)  1.54 us
    reduce_sum x1, other arithmetic, standardize_features(): jnp.mean(centred * centred, axis=-1, keepdims=True) + 1e-05  1.02 us
    convert_element_type x1, other arithmetic, standardize_features(): (standardized_lines * scaling_multiplier + additive_offset).astype(jnp.bf...  1 us
  transfers between devices with their start and end apart: 3, of which 2 were waited for; matrix products, arithmetic and copies ran while one was open for 21% of the time, Pallas kernels for 0%

profile of v1, /device:TPU:0, one launch (start us, length us, event | category | flops | bytes accessed | tf_op | source)
XLA Modules:
  0.0 33.6 jit_solution(7420771927318330732)
XLA Ops:
  0.6 0.5 %collective-permute-start = (bf16[4,16,128]{2,1,0:T(8,128)(2,1)}, bf16[4,16,128]{2,1,0:T(8,128)(2,1)S(1)}, u32[]{:S(2)}, u32[]{:S(2)}) collective-permute-start(bf16[4,16,128]{2,1,0:T(8,128)(2,1)} %param.19), channel_id=1, source_target_pairs={{0,1},{1,0},{2,3},{3,2},{4,5},{5,4},{6,7},{7,6},{8,9},{9,8},{10,11... | collective-permute-start | bytes 49160 | tf_op jit(solution)/shard_map/ppermute | solution.py:65
  1.2 0.9 %convert_reduce_fusion = f32[32,4]{1,0:T(8,128)S(1)} fusion(bf16[32,4,256]{2,1,0:T(4,128)(2,1)} %param.10), kind=kLoop, calls=%fused_computation.17 | loop fusion | flops 65408 | bytes 66048 | tf_op jit(solution)/shard_map/reduce_sum | solution.py:9
  2.1 1.0 %fusion.19 = f32[32,4]{1,0:T(8,128)S(1)} fusion(bf16[32,4,256]{2,1,0:T(4,128)(2,1)} %param.10, f32[32,4]{1,0:T(8,128)S(1)} %broadcast_multiply_fusion.1), kind=kLoop, calls=%fused_computation.30 | loop fusion | flops 130944 | bytes 66560 | tf_op jit(solution)/shard_map/reduce_sum | solution.py:11
  3.2 1.0 %fusion.14 = bf16[32,4,256]{2,1,0:T(4,128)(2,1)S(1)} fusion(bf16[32,4,256]{2,1,0:T(4,128)(2,1)} %param.10, f32[256]{0:T(256)} %param.12, f32[256]{0:T(256)} %param.11, f32[32,4]{1,0:T(8,128)S(1)} %add_rsqrt_fusion, f32[32,4]{1,0:T(8,128)S(1)} %broadcast_multiply_fusion.1), kind=kLoop, calls=%fused_computation.25 | loop fusion | flops 196608 | bytes 134144 | tf_op jit(solution)/shard_map/convert_element_type | solution.py:13
  4.2 0.8 %fusion.2 = bf16[128,32]{0,1:T(8,128)(2,1)S(1)} fusion(bf16[128,256]{1,0:T(8,128)(2,1)S(1)} %reshape.77, bf16[256,32]{0,1:T(8,128)(2,1)} %param.13, f32[32]{0:T(128)} %param.14), kind=kOutput, calls=%fused_computation.10 | convolution fusion | flops 2105344 | bytes 90240 | tf_op jit(solution)/shard_map/dot_general | solution.py:21
  5.3 0.8 %fusion.3 = bf16[128,32]{0,1:T(8,128)(2,1)S(1)} fusion(bf16[128,256]{1,0:T(8,128)(2,1)S(1)} %reshape.77, bf16[256,32]{0,1:T(8,128)(2,1)} %param.15, f32[32]{0:T(128)} %param.16), kind=kOutput, calls=%fused_computation.11 | convolution fusion | flops 2105344 | bytes 90240 | tf_op jit(solution)/shard_map/dot_general | solution.py:21
  6.4 0.8 %maximum_select_fusion = bf16[4,32,128]{2,1,0:T(8,128)(2,1)S(1)} fusion(bf16[4,16,128]{2,1,0:T(8,128)(2,1)S(1)} %collective-permute-done, bf16[4,16,128]{2,1,0:T(8,128)(2,1)} %param.19, pred[]{:T(512)S(6)} %eq.3), kind=kLoop, calls=%fused_computation.34 | loop fusion | flops 147456 | bytes 65537 | tf_op jit(solution)/shard_map/jit(_where)/select_n | solution.py:66
  7.3 0.7 %pad_maximum_fusion = bf16[8,80,128]{2,1,0:T(8,128)(2,1)} fusion(bf16[8,16,128]{2,1,0:T(8,128)(2,1)S(1)} %copy.34, bf16[8,64,128]{2,1,0:T(8,128)(2,1)S(1)} %broadcast_in_dim.2), kind=kLoop, calls=%fused_computation.18 | loop fusion | flops 327680 | bytes 327680 | tf_op jit(solution)/shard_map/concatenate | solution.py:77
  8.0 6.8 %all-to-all-start = ((bf16[8,80,128]{2,1,0:T(8,128)(2,1)}), bf16[8,80,128]{2,1,0:T(8,128)(2,1)S(1)}, u32[]{:S(2)}, u32[]{:S(2)}) async-start(bf16[8,80,128]{2,1,0:T(8,128)(2,1)} %pad_maximum_fusion), calls=%async_computation | async-start | bytes 327680 | tf_op jit(solution)/shard_map/all_to_all | solution.py:80
  14.8 0.2 fusion
  15.0 0.8 %reshape.81 = bf16[4,32,32,32]{3,2,1,0:T(8,128)(2,1)S(1)} reshape(bf16[128,1024]{1,0:T(8,128)(2,1)S(1)} %fusion) | data formatting | bytes 524288 | tf_op jit(solution)/shard_map/reshape | solution.py:33
  15.8 7.1 %all-to-all-done = bf16[8,80,128]{2,1,0:T(8,128)(2,1)S(1)} async-done(((bf16[8,80,128]{2,1,0:T(8,128)(2,1)}), bf16[8,80,128]{2,1,0:T(8,128)(2,1)S(1)}, u32[]{:S(2)}, u32[]{:S(2)}) %all-to-all-start) | async-done | bytes 163872 | tf_op jit(solution)/shard_map/all_to_all | solution.py:80
  23.1 0.2 fusion.1
  23.4 0.8 %reshape.83 = bf16[32,4,32,32]{3,2,1,0:T(8,128)(2,1)S(1)} reshape(bf16[128,1024]{1,0:T(8,128)(2,1)S(1)} %fusion.1) | data formatting | bytes 524288 | tf_op jit(solution)/shard_map/reshape | solution.py:33
  24.2 0.4 %convolution_bitcast_fusion = f32[32,4,32]{2,0,1:T(8,128)S(1)} fusion(bf16[32,4,32,32]{3,2,1,0:T(8,128)(2,1)S(1)} %reshape.83, bf16[32,32,32]{2,1,0:T(8,128)(2,1)S(1)} %reshape_reshape.14), kind=kOutput, calls=%fused_computation.6 | convolution fusion | flops 8388608 | bytes 344064 | tf_op jit(solution)/shard_map/ijcd,sic->sjd/dot_general | solution.py:110
  24.8 0.9 %convolution_bitcast_fusion.1 = f32[32,4,32]{2,0,1:T(8,128)S(1)} fusion(bf16[32,32,32,1]{0,2,1,3:T(8,128)(2,1)S(1)} %bitcast.59, bf16[4,32,32,32]{3,2,1,0:T(8,128)(2,1)S(1)} %reshape.81), kind=kOutput, calls=%fused_computation.7 | convolution fusion | flops 8388608 | bytes 344064 | tf_op jit(solution)/shard_map/ijcd,sjd->sic/dot_general | solution.py:107
  26.0 0.3 multiply_reduce_fusion
  26.7 1.8 %multiply_bitcast_fusion = f32[4,32,32,32]{2,3,0,1:T(8,128)} fusion(bf16[32,32,32,1]{0,2,3,1:T(8,128)(2,1)S(1)} %bitcast.60, bf16[32,4,32]{2,1,0:T(4,128)(2,1)S(1)} %bitcast.61), kind=kOutput, calls=%fused_computation | convolution fusion | flops 8519680 | bytes 598016 | tf_op jit(solution)/shard_map/sic,sjd->ijcd/dot_general | solution.py:93
  28.4 1.9 %copy.38 = f32[4,32,32,32]{3,2,1,0:T(8,128)S(1)} copy(f32[4,32,32,32]{2,3,0,1:T(8,128)} %multiply_bitcast_fusion) | data formatting | bytes 1048576 | tf_op jit(solution)/shard_map/div | solution.py:93
  30.4 1.0 %dot_general.35 = f32[4,32,1024]{2,1,0:T(8,128)S(1)} reshape(f32[4,32,32,32]{3,2,1,0:T(8,128)S(1)} %copy.38) | data formatting | bytes 1048576 | tf_op jit(solution)/shard_map/dot_general | solution.py:96
  31.3 0.4 %fusion.5 = f32[4,32,128]{2,1,0:T(8,128)S(1)} fusion(f32[4,32,1024]{2,1,0:T(8,128)S(1)} %dot_general.35, bf16[1024,128]{1,0:T(8,128)(2,1)S(1)} %copy-done), kind=kOutput, calls=%fused_computation.13 | convolution fusion | flops 201326592 | bytes 851968 | tf_op jit(solution)/shard_map/dot_general | solution.py:96
  31.8 0.8 %fusion.18 = bf16[32,4,256]{2,1,0:T(4,128)(2,1)} fusion(bf16[32,4,256]{2,1,0:T(4,128)(2,1)S(1)} %copy-done.1, f32[32,4,256]{2,1,0:T(4,128)S(1)} %reshape.85, f32[32,4]{1,0:T(8,128)S(1)} %broadcast_multiply_fusion, f32[32,4]{1,0:T(8,128)S(1)} %div.36, f32[256]{0:T(256)S(1)} %copy-done.2, f32[32,4]{1,0:T(8,128)S(1)} %add_rsqrt_fusion, ...), kind=kLoop, calls=%fused_computation.29 | loop fusion | flops 294912 | bytes 265216 | tf_op jit(solution)/shard_map/convert_element_type | solution.py:130
  32.6 0.4 %collective-permute-done.1 = f32[4,16,128]{2,1,0:T(8,128)S(1)} collective-permute-done((f32[4,16,128]{2,1,0:T(8,128)S(1)}, f32[4,16,128]{2,1,0:T(8,128)S(1)}, u32[]{:S(2)}, u32[]{:S(2)}) %collective-permute-start.1) | collective-permute-done | bytes 32800 | tf_op jit(solution)/shard_map/ppermute | solution.py:103
  33.0 0.6 %add_convert_fusion = bf16[4,16,128]{2,1,0:T(8,128)(2,1)} fusion(f32[4,16,128]{2,1,0:T(8,128)S(1)} %collective-permute-done.1, f32[4,32,128]{2,1,0:T(8,128)S(1)} %fusion.5, s32[]{:T(128)S(6)} %select_n.25, f32[128]{0:T(128)S(1)} %copy-done.5), kind=kLoop, calls=%fused_computation.37 | loop fusion | flops 24576 | bytes 82436 | tf_op jit(solution)/shard_map/convert_element_type | solution.py:104
  (39 shorter events, 1.8 us)
Async XLA Ops:
  0.6 14.1 %copy-start = (bf16[1024,128]{1,0:T(8,128)(2,1)S(1)}, bf16[1024,128]{1,0:T(8,128)(2,1)}, u32[]{:S(2)}) copy-start(bf16[1024,128]{1,0:T(8,128)(2,1)} %param.17) | copy-start | bytes 786436
  0.6 5.8 %collective-permute-start = (bf16[4,16,128]{2,1,0:T(8,128)(2,1)}, bf16[4,16,128]{2,1,0:T(8,128)(2,1)S(1)}, u32[]{:S(2)}, u32[]{:S(2)}) collective-permute-start(bf16[4,16,128]{2,1,0:T(8,128)(2,1)} %param.19), channel_id=1, source_target_pairs={{0,1},{1,0},{2,3},{3,2},{4,5},{5,4},{6,7},{7,6},{8,9},{9,8},{10,11... | collective-permute-start | bytes 49160 | tf_op jit(solution)/shard_map/ppermute | solution.py:65
  8.0 14.9 %all-to-all-start = ((bf16[8,80,128]{2,1,0:T(8,128)(2,1)}), bf16[8,80,128]{2,1,0:T(8,128)(2,1)S(1)}, u32[]{:S(2)}, u32[]{:S(2)}) async-start(bf16[8,80,128]{2,1,0:T(8,128)(2,1)} %pad_maximum_fusion), calls=%async_computation | async-start | bytes 327680 | tf_op jit(solution)/shard_map/all_to_all | solution.py:80
  23.4 2.4 %copy-start.3 = (bf16[256,32]{0,1:T(8,128)(2,1)S(1)}, bf16[256,32]{0,1:T(8,128)(2,1)}, u32[]{:S(2)}) copy-start(bf16[256,32]{0,1:T(8,128)(2,1)} %param.13) | copy-start | bytes 49156
  24.1 1.8 %copy-start.2 = (f32[256]{0:T(256)S(1)}, f32[256]{0:T(256)}, u32[]{:S(2)}) copy-start(f32[256]{0:T(256)} %param.11) | copy-start | bytes 3076
  24.2 1.8 %copy-start.4 = (bf16[256,32]{0,1:T(8,128)(2,1)S(1)}, bf16[256,32]{0,1:T(8,128)(2,1)}, u32[]{:S(2)}) copy-start(bf16[256,32]{0,1:T(8,128)(2,1)} %param.15) | copy-start | bytes 49156
  24.2 2.1 %copy-start.1 = (bf16[32,4,256]{2,1,0:T(4,128)(2,1)S(1)}, bf16[32,4,256]{2,1,0:T(4,128)(2,1)}, u32[]{:S(2)}) copy-start(bf16[32,4,256]{2,1,0:T(4,128)(2,1)} %param.10) | copy-start | bytes 196612
  30.4 2.6 %copy-start.5 = (f32[128]{0:T(128)S(1)}, f32[128]{0:T(128)}, u32[]{:S(2)}) copy-start(f32[128]{0:T(128)} %param.18) | copy-start | bytes 1540
  31.7 1.3 %collective-permute-start.1 = (f32[4,16,128]{2,1,0:T(8,128)S(1)}, f32[4,16,128]{2,1,0:T(8,128)S(1)}, u32[]{:S(2)}, u32[]{:S(2)}) collective-permute-start(f32[4,16,128]{2,1,0:T(8,128)S(1)} %constant_dynamic-slice_fusion), channel_id=1, source_target_pairs={{0,1},{1,0},{2,3},{3,2},{4,5},{5,4},{6,7},{7,6},{8,9},{9,8},{10,11... | collective-permute-start | bytes 98312 | tf_op jit(solution)/shard_map/ppermute | solution.py:103

commit v2 on v1

--- a/solution.py
+++ b/solution.py
@@ -31,6 +31,19 @@
         / seq_count
     )
     return result.astype(jnp.bfloat16).reshape(first, second, depth_p, depth_p)
+
+
+def exchange(packed, ranks):
+    if ranks > 16:
+        return lax.all_to_all(packed, "res", split_axis=0, concat_axis=0, tiled=True)
+    rank = lax.axis_index("res")
+    arrived = [lax.dynamic_index_in_dim(packed, rank, 0)]
+    for shift in range(1, ranks):
+        leaving = lax.dynamic_index_in_dim(packed, (rank - shift) % ranks, 0)
+        pairs = [(source, (source - shift) % ranks) for source in range(ranks)]
+        arrived.append(lax.ppermute(leaving, "res", pairs))
+    twice = jnp.concatenate(arrived + arrived, axis=0)
+    return lax.dynamic_slice_in_dim(twice, ranks - rank, ranks, axis=0)
 
 
 def body(
@@ -77,7 +90,7 @@
     packed = jnp.concatenate(
         [jnp.broadcast_to(proj_both[None], (ranks,) + proj_both.shape), cot_parts], axis=1
     )
-    packed = lax.all_to_all(packed, "res", split_axis=0, concat_axis=0, tiled=True)
+    packed = exchange(packed, ranks)
     left_all = packed[:, :homolog_mesh_split].transpose(1, 0, 2).reshape(homolog_mesh_split, -1)
     right_all = (
         packed[:, homolog_mesh_split : 2 * homolog_mesh_split]

time: 34.2 us -> 37.4 us (1.094)
  starting transfers between devices: 7.41 us -> 12.7 us
  waiting for transfers between devices: 7.46 us -> 5.65 us
  other arithmetic: 6.13 us -> 5.5 us
    ppermute x0 -> x7, starting transfers between devices: none -> 12.1 us  [exchange(): arrived.append(lax.ppermute(leaving, 'res', pairs))]
    all_to_all x1 -> x0, waiting for transfers between devices: 7.1 us -> none  [body(): lax.all_to_all(packed, 'res', split_axis=0, concat_axis=0, tiled=True)]
    all_to_all x1 -> x0, starting transfers between devices: 6.82 us -> none  [body(): lax.all_to_all(packed, 'res', split_axis=0, concat_axis=0, tiled=True)]
    ppermute x0 -> x7, waiting for transfers between devices: none -> 5.29 us  [exchange(): arrived.append(lax.ppermute(leaving, 'res', pairs))]
    concatenate x1 -> x2, other arithmetic: 0.67 us -> 0.03 us  [body(): jnp.concatenate([jnp.broadcast_to(proj_both[None], (ranks,) + proj_both.s...]
  transfers between devices with their start and end apart: 3 -> 9, of which waited for: 2 -> 4; matrix products, arithmetic and copies ran while one was open for 21% -> 19% of each run, Pallas kernels for 0% -> 0%
where the time goes in v2:
time: 37.4 us; the launch traced here: 36.8 us
  starting transfers between devices  12.7 us (34%)
  matrix products  5.96 us (16%)
  local copies, waits for them, and re-layouts  5.85 us (16%)
  waiting for transfers between devices  5.65 us (15%)
  other arithmetic  5.5 us (15%)
  between operations  1.19 us (3%)
    ppermute x7, starting transfers between devices, exchange(): arrived.append(lax.ppermute(leaving, 'res', pairs))  12.1 us
    ppermute x7, waiting for transfers between devices, exchange(): arrived.append(lax.ppermute(leaving, 'res', pairs))  5.29 us
    div x1, local copies, waits for them, and re-layouts, body(): jnp.einsum('sic,sjd->ijcd', left_own, right_rows, preferred_element_type=...  1.93 us
    dot_general x1, matrix products, body(): jnp.einsum('sic,sjd->ijcd', left_own, right_rows, preferred_element_type=...  1.76 us
    dot_general x2, matrix products, project_flat(): jnp.dot(flat_rows, weight, preferred_element_type=jnp.float32)  1.63 us
    reshape x2, local copies, waits for them, and re-layouts, cot_outer(): return result.astype(jnp.bfloat16).reshape(first, second, depth_p, depth_p)  1.54 us
    reduce_sum x1, other arithmetic, standardize_features(): jnp.mean(centred * centred, axis=-1, keepdims=True) + 1e-05  1.02 us
    convert_element_type x1, other arithmetic, standardize_features(): (standardized_lines * scaling_multiplier + additive_offset).astype(jnp.bf...  1 us
  transfers between devices with their start and end apart: 9, of which 4 were waited for; matrix products, arithmetic and copies ran while one was open for 19% of the time, Pallas kernels for 0%

profile of v2, /device:TPU:0, one launch (start us, length us, event | category | flops | bytes accessed | tf_op | source)
XLA Modules:
  0.0 36.8 jit_solution(11208411711131424369)
XLA Ops:
  0.6 0.5 %collective-permute-start = (bf16[4,16,128]{2,1,0:T(8,128)(2,1)}, bf16[4,16,128]{2,1,0:T(8,128)(2,1)S(1)}, u32[]{:S(2)}, u32[]{:S(2)}) collective-permute-start(bf16[4,16,128]{2,1,0:T(8,128)(2,1)} %param.19), channel_id=1, source_target_pairs={{0,1},{1,0},{2,3},{3,2},{4,5},{5,4},{6,7},{7,6},{8,9},{9,8},{10,11... | collective-permute-start | bytes 49160 | tf_op jit(solution)/shard_map/ppermute | solution.py:78
  1.2 0.9 %convert_reduce_fusion = f32[32,4]{1,0:T(8,128)S(1)} fusion(bf16[32,4,256]{2,1,0:T(4,128)(2,1)} %param.10), kind=kLoop, calls=%fused_computation.33 | loop fusion | flops 65408 | bytes 66048 | tf_op jit(solution)/shard_map/reduce_sum | solution.py:9
  2.1 1.0 %fusion.19 = f32[32,4]{1,0:T(8,128)S(1)} fusion(bf16[32,4,256]{2,1,0:T(4,128)(2,1)} %param.10, f32[32,4]{1,0:T(8,128)S(1)} %broadcast_multiply_fusion.1), kind=kLoop, calls=%fused_computation.45 | loop fusion | flops 130944 | bytes 66560 | tf_op jit(solution)/shard_map/reduce_sum | solution.py:11
  3.2 1.0 %fusion.14 = bf16[32,4,256]{2,1,0:T(4,128)(2,1)S(1)} fusion(bf16[32,4,256]{2,1,0:T(4,128)(2,1)} %param.10, f32[256]{0:T(256)} %param.12, f32[256]{0:T(256)} %param.11, f32[32,4]{1,0:T(8,128)S(1)} %add_rsqrt_fusion, f32[32,4]{1,0:T(8,128)S(1)} %broadcast_multiply_fusion.1), kind=kLoop, calls=%fused_computation.40 | loop fusion | flops 196608 | bytes 134144 | tf_op jit(solution)/shard_map/convert_element_type | solution.py:13
  4.2 0.8 %fusion.2 = bf16[128,32]{0,1:T(8,128)(2,1)S(1)} fusion(bf16[128,256]{1,0:T(8,128)(2,1)S(1)} %reshape.77, bf16[256,32]{0,1:T(8,128)(2,1)} %param.13, f32[32]{0:T(128)} %param.14), kind=kOutput, calls=%fused_computation.10 | convolution fusion | flops 2105344 | bytes 90240 | tf_op jit(solution)/shard_map/dot_general | solution.py:21
  5.3 0.8 %fusion.3 = bf16[128,32]{0,1:T(8,128)(2,1)S(1)} fusion(bf16[128,256]{1,0:T(8,128)(2,1)S(1)} %reshape.77, bf16[256,32]{0,1:T(8,128)(2,1)} %param.15, f32[32]{0:T(128)} %param.16), kind=kOutput, calls=%fused_computation.11 | convolution fusion | flops 2105344 | bytes 90240 | tf_op jit(solution)/shard_map/dot_general | solution.py:21
  6.6 0.8 %maximum_select_fusion = bf16[4,32,128]{2,1,0:T(8,128)(2,1)S(1)} fusion(bf16[4,16,128]{2,1,0:T(8,128)(2,1)S(1)} %collective-permute-done, bf16[4,16,128]{2,1,0:T(8,128)(2,1)} %param.19, pred[]{:T(512)S(6)} %eq.11), kind=kLoop, calls=%fused_computation.65 | loop fusion | flops 147456 | bytes 65537 | tf_op jit(solution)/shard_map/jit(_where)/select_n | solution.py:79
  7.5 5.6 %collective-permute-start.1 = (bf16[1,80,128]{2,1,0:T(8,128)(2,1)S(1)}, bf16[1,80,128]{2,1,0:T(8,128)(2,1)S(1)}, u32[]{:S(2)}, u32[]{:S(2)}) collective-permute-start(bf16[1,80,128]{2,1,0:T(8,128)(2,1)S(1)} %get-tuple-element.6), channel_id=1, source_target_pairs={{0,14},{2,0},{4,2},{6,4},{8,6},{10,8},{12,10},{14,12},{1,15},{3,1}... | collective-permute-start | bytes 61448 | tf_op jit(solution)/shard_map/ppermute | solution.py:44
  13.1 0.4 %collective-permute-start.2 = (bf16[1,80,128]{2,1,0:T(8,128)(2,1)S(1)}, bf16[1,80,128]{2,1,0:T(8,128)(2,1)S(1)}, u32[]{:S(2)}, u32[]{:S(2)}) collective-permute-start(bf16[1,80,128]{2,1,0:T(8,128)(2,1)S(1)} %get-tuple-element.7), channel_id=1, source_target_pairs={{0,12},{2,14},{4,0},{6,2},{8,4},{10,6},{12,8},{14,10},{1,13},{3,15... | collective-permute-start | bytes 61448 | tf_op jit(solution)/shard_map/ppermute | solution.py:44
  13.5 3.0 %collective-permute-start.4 = (bf16[1,80,128]{2,1,0:T(8,128)(2,1)S(1)}, bf16[1,80,128]{2,1,0:T(8,128)(2,1)S(1)}, u32[]{:S(2)}, u32[]{:S(2)}) collective-permute-start(bf16[1,80,128]{2,1,0:T(8,128)(2,1)S(1)} %get-tuple-element.9), channel_id=1, source_target_pairs={{0,8},{2,10},{4,12},{6,14},{8,0},{10,2},{12,4},{14,6},{1,9},{3,11}... | collective-permute-start | bytes 61448 | tf_op jit(solution)/shard_map/ppermute | solution.py:44
  16.8 0.8 %reshape.81 = bf16[4,32,32,32]{3,2,1,0:T(8,128)(2,1)S(1)} reshape(bf16[128,1024]{1,0:T(8,128)(2,1)S(1)} %fusion) | data formatting | bytes 524288 | tf_op jit(solution)/shard_map/reshape | solution.py:33
  17.6 1.9 %collective-permute-start.6 = (bf16[1,80,128]{2,1,0:T(8,128)(2,1)S(1)}, bf16[1,80,128]{2,1,0:T(8,128)(2,1)S(1)}, u32[]{:S(2)}, u32[]{:S(2)}) collective-permute-start(bf16[1,80,128]{2,1,0:T(8,128)(2,1)S(1)} %get-tuple-element.10), channel_id=1, source_target_pairs={{0,4},{2,6},{4,8},{6,10},{8,12},{10,14},{12,0},{14,2},{1,5},{3,7},... | collective-permute-start | bytes 61448 | tf_op jit(solution)/shard_map/ppermute | solution.py:44
  19.5 1.2 %collective-permute-start.7 = (bf16[1,80,128]{2,1,0:T(8,128)(2,1)S(1)}, bf16[1,80,128]{2,1,0:T(8,128)(2,1)S(1)}, u32[]{:S(2)}, u32[]{:S(2)}) collective-permute-start(bf16[1,80,128]{2,1,0:T(8,128)(2,1)S(1)} %get-tuple-element.4), channel_id=1, source_target_pairs={{0,2},{2,4},{4,6},{6,8},{8,10},{10,12},{12,14},{14,0},{1,3},{3,5},... | collective-permute-start | bytes 61448 | tf_op jit(solution)/shard_map/ppermute | solution.py:44
  20.7 1.4 %collective-permute-done.5 = bf16[1,80,128]{2,1,0:T(8,128)(2,1)S(1)} collective-permute-done((bf16[1,80,128]{2,1,0:T(8,128)(2,1)S(1)}, bf16[1,80,128]{2,1,0:T(8,128)(2,1)S(1)}, u32[]{:S(2)}, u32[]{:S(2)}) %collective-permute-start.5) | collective-permute-done | bytes 20512 | tf_op jit(solution)/shard_map/ppermute | solution.py:44
  22.1 2.0 %collective-permute-done.6 = bf16[1,80,128]{2,1,0:T(8,128)(2,1)S(1)} collective-permute-done((bf16[1,80,128]{2,1,0:T(8,128)(2,1)S(1)}, bf16[1,80,128]{2,1,0:T(8,128)(2,1)S(1)}, u32[]{:S(2)}, u32[]{:S(2)}) %collective-permute-start.6) | collective-permute-done | bytes 20512 | tf_op jit(solution)/shard_map/ppermute | solution.py:44
  24.1 1.9 %collective-permute-done.7 = bf16[1,80,128]{2,1,0:T(8,128)(2,1)S(1)} collective-permute-done((bf16[1,80,128]{2,1,0:T(8,128)(2,1)S(1)}, bf16[1,80,128]{2,1,0:T(8,128)(2,1)S(1)}, u32[]{:S(2)}, u32[]{:S(2)}) %collective-permute-start.7) | collective-permute-done | bytes 20512 | tf_op jit(solution)/shard_map/ppermute | solution.py:44
  26.4 0.8 %reshape.83 = bf16[32,4,32,32]{3,2,1,0:T(8,128)(2,1)S(1)} reshape(bf16[128,1024]{1,0:T(8,128)(2,1)S(1)} %fusion.1) | data formatting | bytes 524288 | tf_op jit(solution)/shard_map/reshape | solution.py:33
  28.0 0.9 %convolution_bitcast_fusion.1 = f32[32,4,32]{2,0,1:T(8,128)S(1)} fusion(bf16[32,32,32,1]{0,2,1,3:T(8,128)(2,1)S(1)} %bitcast.59, bf16[4,32,32,32]{3,2,1,0:T(8,128)(2,1)S(1)} %reshape.81), kind=kOutput, calls=%fused_computation.7 | convolution fusion | flops 8388608 | bytes 344064 | tf_op jit(solution)/shard_map/ijcd,sjd->sic/dot_general | solution.py:120
  29.9 1.8 %multiply_bitcast_fusion = f32[4,32,32,32]{2,3,0,1:T(8,128)} fusion(bf16[32,32,32,1]{0,2,3,1:T(8,128)(2,1)S(1)} %bitcast.60, bf16[32,4,32]{2,1,0:T(4,128)(2,1)S(1)} %bitcast.61), kind=kOutput, calls=%fused_computation | convolution fusion | flops 8519680 | bytes 598016 | tf_op jit(solution)/shard_map/sic,sjd->ijcd/dot_general | solution.py:106
  31.7 1.9 %copy.38 = f32[4,32,32,32]{3,2,1,0:T(8,128)S(1)} copy(f32[4,32,32,32]{2,3,0,1:T(8,128)} %multiply_bitcast_fusion) | data formatting | bytes 1048576 | tf_op jit(solution)/shard_map/div | solution.py:106
  33.6 1.0 %dot_general.35 = f32[4,32,1024]{2,1,0:T(8,128)S(1)} reshape(f32[4,32,32,32]{3,2,1,0:T(8,128)S(1)} %copy.38) | data formatting | bytes 1048576 | tf_op jit(solution)/shard_map/dot_general | solution.py:109
  34.6 0.4 %fusion.5 = f32[4,32,128]{2,1,0:T(8,128)S(1)} fusion(f32[4,32,1024]{2,1,0:T(8,128)S(1)} %dot_general.35, bf16[1024,128]{1,0:T(8,128)(2,1)S(1)} %copy-done), kind=kOutput, calls=%fused_computation.29 | convolution fusion | flops 201326592 | bytes 851968 | tf_op jit(solution)/shard_map/dot_general | solution.py:109
  35.0 0.8 %fusion.18 = bf16[32,4,256]{2,1,0:T(4,128)(2,1)} fusion(bf16[32,4,256]{2,1,0:T(4,128)(2,1)S(1)} %copy-done.1, f32[32,4,256]{2,1,0:T(4,128)S(1)} %reshape.85, f32[32,4]{1,0:T(8,128)S(1)} %broadcast_multiply_fusion, f32[32,4]{1,0:T(8,128)S(1)} %div.36, f32[256]{0:T(256)S(1)} %copy-done.2, f32[32,4]{1,0:T(8,128)S(1)} %add_rsqrt_fusion, ...), kind=kLoop, calls=%fused_computation.44 | loop fusion | flops 294912 | bytes 265216 | tf_op jit(solution)/shard_map/convert_element_type | solution.py:143
  36.2 0.6 %add_convert_fusion = bf16[4,16,128]{2,1,0:T(8,128)(2,1)} fusion(f32[4,16,128]{2,1,0:T(8,128)S(1)} %collective-permute-done.8, f32[4,32,128]{2,1,0:T(8,128)S(1)} %fusion.5, s32[]{:T(128)S(6)} %select_n.100, f32[128]{0:T(128)S(1)} %copy-done.5), kind=kLoop, calls=%fused_computation.68 | loop fusion | flops 24576 | bytes 82436 | tf_op jit(solution)/shard_map/convert_element_type | solution.py:117
  (67 shorter events, 3.4 us)
Async XLA Ops:
  0.6 15.9 %copy-start = (bf16[1024,128]{1,0:T(8,128)(2,1)S(1)}, bf16[1024,128]{1,0:T(8,128)(2,1)}, u32[]{:S(2)}) copy-start(bf16[1024,128]{1,0:T(8,128)(2,1)} %param.17) | copy-start | bytes 786436
  0.6 5.9 %collective-permute-start = (bf16[4,16,128]{2,1,0:T(8,128)(2,1)}, bf16[4,16,128]{2,1,0:T(8,128)(2,1)S(1)}, u32[]{:S(2)}, u32[]{:S(2)}) collective-permute-start(bf16[4,16,128]{2,1,0:T(8,128)(2,1)} %param.19), channel_id=1, source_target_pairs={{0,1},{1,0},{2,3},{3,2},{4,5},{5,4},{6,7},{7,6},{8,9},{9,8},{10,11... | collective-permute-start | bytes 49160 | tf_op jit(solution)/shard_map/ppermute | solution.py:78
  7.5 10.1 %collective-permute-start.1 = (bf16[1,80,128]{2,1,0:T(8,128)(2,1)S(1)}, bf16[1,80,128]{2,1,0:T(8,128)(2,1)S(1)}, u32[]{:S(2)}, u32[]{:S(2)}) collective-permute-start(bf16[1,80,128]{2,1,0:T(8,128)(2,1)S(1)} %get-tuple-element.6), channel_id=1, source_target_pairs={{0,14},{2,0},{4,2},{6,4},{8,6},{10,8},{12,10},{14,12},{1,15},{3,1}... | collective-permute-start | bytes 61448 | tf_op jit(solution)/shard_map/ppermute | solution.py:44
  13.1 6.4 %collective-permute-start.2 = (bf16[1,80,128]{2,1,0:T(8,128)(2,1)S(1)}, bf16[1,80,128]{2,1,0:T(8,128)(2,1)S(1)}, u32[]{:S(2)}, u32[]{:S(2)}) collective-permute-start(bf16[1,80,128]{2,1,0:T(8,128)(2,1)S(1)} %get-tuple-element.7), channel_id=1, source_target_pairs={{0,12},{2,14},{4,0},{6,2},{8,4},{10,6},{12,8},{14,10},{1,13},{3,15... | collective-permute-start | bytes 61448 | tf_op jit(solution)/shard_map/ppermute | solution.py:44
  13.5 7.1 %collective-permute-start.3 = (bf16[1,80,128]{2,1,0:T(8,128)(2,1)S(1)}, bf16[1,80,128]{2,1,0:T(8,128)(2,1)S(1)}, u32[]{:S(2)}, u32[]{:S(2)}) collective-permute-start(bf16[1,80,128]{2,1,0:T(8,128)(2,1)S(1)} %get-tuple-element.8), channel_id=1, source_target_pairs={{0,10},{2,12},{4,14},{6,0},{8,2},{10,4},{12,6},{14,8},{1,11},{3,13... | collective-permute-start | bytes 61448 | tf_op jit(solution)/shard_map/ppermute | solution.py:44
  13.5 7.1 %collective-permute-start.4 = (bf16[1,80,128]{2,1,0:T(8,128)(2,1)S(1)}, bf16[1,80,128]{2,1,0:T(8,128)(2,1)S(1)}, u32[]{:S(2)}, u32[]{:S(2)}) collective-permute-start(bf16[1,80,128]{2,1,0:T(8,128)(2,1)S(1)} %get-tuple-element.9), channel_id=1, source_target_pairs={{0,8},{2,10},{4,12},{6,14},{8,0},{10,2},{12,4},{14,6},{1,9},{3,11}... | collective-permute-start | bytes 61448 | tf_op jit(solution)/shard_map/ppermute | solution.py:44
  16.5 5.6 %collective-permute-start.5 = (bf16[1,80,128]{2,1,0:T(8,128)(2,1)S(1)}, bf16[1,80,128]{2,1,0:T(8,128)(2,1)S(1)}, u32[]{:S(2)}, u32[]{:S(2)}) collective-permute-start(bf16[1,80,128]{2,1,0:T(8,128)(2,1)S(1)} %get-tuple-element.11), channel_id=1, source_target_pairs={{0,6},{2,8},{4,10},{6,12},{8,14},{10,0},{12,2},{14,4},{1,7},{3,9},... | collective-permute-start | bytes 61448 | tf_op jit(solution)/shard_map/ppermute | solution.py:44
  17.6 6.6 %collective-permute-start.6 = (bf16[1,80,128]{2,1,0:T(8,128)(2,1)S(1)}, bf16[1,80,128]{2,1,0:T(8,128)(2,1)S(1)}, u32[]{:S(2)}, u32[]{:S(2)}) collective-permute-start(bf16[1,80,128]{2,1,0:T(8,128)(2,1)S(1)} %get-tuple-element.10), channel_id=1, source_target_pairs={{0,4},{2,6},{4,8},{6,10},{8,12},{10,14},{12,0},{14,2},{1,5},{3,7},... | collective-permute-start | bytes 61448 | tf_op jit(solution)/shard_map/ppermute | solution.py:44
  19.5 6.5 %collective-permute-start.7 = (bf16[1,80,128]{2,1,0:T(8,128)(2,1)S(1)}, bf16[1,80,128]{2,1,0:T(8,128)(2,1)S(1)}, u32[]{:S(2)}, u32[]{:S(2)}) collective-permute-start(bf16[1,80,128]{2,1,0:T(8,128)(2,1)S(1)} %get-tuple-element.4), channel_id=1, source_target_pairs={{0,2},{2,4},{4,6},{6,8},{8,10},{10,12},{12,14},{14,0},{1,3},{3,5},... | collective-permute-start | bytes 61448 | tf_op jit(solution)/shard_map/ppermute | solution.py:44
  27.1 1.9 %copy-start.3 = (bf16[256,32]{0,1:T(8,128)(2,1)S(1)}, bf16[256,32]{0,1:T(8,128)(2,1)}, u32[]{:S(2)}) copy-start(bf16[256,32]{0,1:T(8,128)(2,1)} %param.13) | copy-start | bytes 49156
  27.2 2.0 %copy-start.2 = (f32[256]{0:T(256)S(1)}, f32[256]{0:T(256)}, u32[]{:S(2)}) copy-start(f32[256]{0:T(256)} %param.11) | copy-start | bytes 3076
  27.2 2.0 %copy-start.4 = (bf16[256,32]{0,1:T(8,128)(2,1)S(1)}, bf16[256,32]{0,1:T(8,128)(2,1)}, u32[]{:S(2)}) copy-start(bf16[256,32]{0,1:T(8,128)(2,1)} %param.15) | copy-start | bytes 49156
  27.4 2.1 %copy-start.1 = (bf16[32,4,256]{2,1,0:T(4,128)(2,1)S(1)}, bf16[32,4,256]{2,1,0:T(4,128)(2,1)}, u32[]{:S(2)}) copy-start(bf16[32,4,256]{2,1,0:T(4,128)(2,1)} %param.10) | copy-start | bytes 196612
  33.6 2.6 %copy-start.5 = (f32[128]{0:T(128)S(1)}, f32[128]{0:T(128)}, u32[]{:S(2)}) copy-start(f32[128]{0:T(128)} %param.18) | copy-start | bytes 1540
  35.0 1.3 %collective-permute-start.8 = (f32[4,16,128]{2,1,0:T(8,128)S(1)}, f32[4,16,128]{2,1,0:T(8,128)S(1)}, u32[]{:S(2)}, u32[]{:S(2)}) collective-permute-start(f32[4,16,128]{2,1,0:T(8,128)S(1)} %constant_dynamic-slice_fusion), channel_id=1, source_target_pairs={{0,1},{1,0},{2,3},{3,2},{4,5},{5,4},{6,7},{7,6},{8,9},{9,8},{10,11... | collective-permute-start | bytes 98312 | tf_op jit(solution)/shard_map/ppermute | solution.py:116

commit v3 on v0

v3 whole, which is shorter than its diff:
```python
import functools

import jax
import jax.numpy as jnp
from jax import lax
from jax.experimental import pallas as pl
from jax.experimental.pallas import tpu as pltpu
from jax.sharding import PartitionSpec as P

LANES = 128
BF16 = jnp.bfloat16
F32 = jnp.float32
NT = (((1,), (1,)), ((), ()))
TN = (((0,), (0,)), ((), ()))


def lane_block(shape, width):
    return lax.broadcasted_iota(jnp.int32, shape, 1) // width


def pick(blocks, pieces):
    result = pieces[0]
    for place in range(1, len(pieces)):
        result = jnp.where(blocks == place, pieces[place], result)
    return result


def split_three(value):
    top = value.astype(BF16)
    rest = value - top.astype(F32)
    middle = rest.astype(BF16)
    low = (rest - middle.astype(F32)).astype(BF16)
    return top, middle, low


def normalise(rows):
    centred = rows - jnp.mean(rows, axis=-1, keepdims=True)
    inv_std = lax.rsqrt(jnp.mean(centred * centred, axis=-1, keepdims=True) + 1e-05)
    return centred * inv_std, inv_std


def residue_rows(x_ref):
    return jnp.concatenate(
        [x_ref[:, place, :].astype(F32) for place in range(x_ref.shape[1])], axis=0
    )


def project_kernel(
    x_ref, gain_ref, offset_ref, left_w_ref, left_b_ref, right_w_ref, right_b_ref, w_ref,
    left_ref, right_ref, sorted_w_ref, wide_ref,
):
    seqs, residues, _ = x_ref.shape
    depth = left_w_ref.shape[0]
    normed, _ = normalise(residue_rows(x_ref))
    ln_out = (normed * gain_ref[...] + offset_ref[...]).astype(BF16)
    blocks = lane_block((seqs, LANES), depth)
    for weight_ref, bias_ref, out_ref in (
        (left_w_ref, left_b_ref, left_ref),
        (right_w_ref, right_b_ref, right_ref),
    ):
        weight = jnp.concatenate([weight_ref[...]] * residues, axis=0)
        bias = jnp.concatenate([bias_ref[...]] * residues, axis=1)
        wide = lax.dot_general(ln_out, weight, NT, preferred_element_type=F32)
        own = pick(blocks, [wide[p * seqs : (p + 1) * seqs] for p in range(residues)])
        out_ref[...] = (own + bias).astype(BF16)
    wide_ref[...] = w_ref[...].astype(F32)
    for d in range(depth):
        sorted_w_ref[d * depth : (d + 1) * depth, :] = wide_ref[
            pl.ds(d, depth, stride=depth), :
        ].astype(BF16)


def cot_kernel(scale, own_ref, other_ref, sorted_w_ref, left_ref, right_ref,
               send_ref, outer_ref, turn_ref):
    residues, columns, _ = own_ref.shape
    depth = sorted_w_ref.shape[0] // (LANES // residues)
    depth = LANES // residues
    first = lax.axis_index("seq") == 0
    own = own_ref[...].reshape(residues * columns, LANES)
    other = other_ref[...].reshape(residues * columns, LANES)
    low = jnp.where(first, own, other)
    high = jnp.where(first, other, own)
    both = jnp.concatenate([low, high], axis=0)
    flat = lax.dot_general(both, sorted_w_ref[...], NT, preferred_element_type=F32) * scale
    blocks = lane_block((columns, LANES), depth)
    for half in range(2):
        for tile in range(depth * depth // LANES):
            block = flat[
                half * residues * columns : (half + 1) * residues * columns,
                tile * LANES : (tile + 1) * LANES,
            ]
            turned = [block] + [pltpu.roll(block, depth * t, 1) for t in range(1, residues)]
            for e in range(residues):
                piece = pick(
                    blocks,
                    [
                        turned[(i - e) % residues][i * columns : (i + 1) * columns]
                        for i in range(residues)
                    ],
                )
                turn_ref[pl.ds(half * columns * depth + tile * residues + e, columns, stride=depth), :] = piece
    outer = turn_ref[...].astype(BF16)
    half_rows = columns * depth
    partial = lax.dot_general(left_ref[...], outer, NT, preferred_element_type=F32).astype(BF16)
    seqs = left_ref.shape[0]
    ranks = columns // residues
    for half in range(2):
        outer_ref[half] = outer[half * half_rows : (half + 1) * half_rows]
        for rank in range(ranks):
            at = (half * ranks + rank) * LANES
            send_ref[half, rank, 0:seqs, :] = right_ref[...]
            send_ref[half, rank, seqs : 2 * seqs, :] = partial[:, at : at + LANES]


def grad_kernel(steps, got_ref, outer_ref, x_ref, gain_ref, left_w_ref, right_w_ref,
                grad_ref, left_cot_ref, right_cot_ref):
    step = pl.program_id(0)
    _, ranks, twice, _ = got_ref.shape
    seqs = twice // 2
    residues = x_ref.shape[1]
    depth = LANES // residues

    @pl.when(step == 0)
    def _():
        left_cot_ref[...] = jnp.zeros_like(left_cot_ref)
        right_cot_ref[...] = jnp.zeros_like(right_cot_ref)

    places = [(half, rank) for half in range(2) for rank in range(ranks)]
    right_all = jnp.concatenate([got_ref[h, r, 0:seqs, :] for h, r in places], axis=1)
    outer = jnp.concatenate([outer_ref[0], outer_ref[1]], axis=0)
    left_cot_ref[...] += jnp.dot(right_all, outer, preferred_element_type=F32)
    total = got_ref[0, 0, seqs:twice, :].astype(F32)
    for h, r in places[1:]:
        total = total + got_ref[h, r, seqs:twice, :].astype(F32)
    right_cot_ref[...] += total

    @pl.when(step == steps - 1)
    def _():
        blocks = lane_block((seqs, LANES), depth)
        left_cot, right_cot = left_cot_ref[...], right_cot_ref[...]
        spread = jnp.concatenate(
            [
                jnp.concatenate(
                    [
                        jnp.where(blocks == place, left_cot, 0.0),
                        jnp.where(blocks == place, right_cot, 0.0),
                    ],
                    axis=1,
                )
                for place in range(residues)
            ],
            axis=0,
        )
        weight = jnp.concatenate(
            [left_w_ref[...]] * residues + [right_w_ref[...]] * residues, axis=0
        )
        rows = residues * seqs
        parts = jnp.concatenate(split_three(spread), axis=0)
        ln_cot = jnp.dot(parts, weight, preferred_element_type=F32)
        ln_cot = ln_cot[0:rows] + (ln_cot[rows : 2 * rows] + ln_cot[2 * rows : 3 * rows])
        gained = ln_cot * gain_ref[...]
        normed, inv_std = normalise(residue_rows(x_ref))
        grad = inv_std * (
            gained
            - jnp.mean(gained, axis=-1, keepdims=True)
            - normed * jnp.mean(gained * normed, axis=-1, keepdims=True)
        )
        for place in range(residues):
            grad_ref[:, place, :] = grad[place * seqs : (place + 1) * seqs].astype(BF16)


def pair_kernel(scale, got_ref, far_ref, left_ref, far_left_ref, sorted_w_ref, offset_ref,
                pair_ref, turn_ref):
    residues, columns, _ = pair_ref.shape
    depth = LANES // residues
    ranks = columns // residues
    mine = lax.axis_index("seq")
    near = jnp.concatenate([got_ref[mine, r] for r in range(ranks)], axis=1)
    far = jnp.concatenate([far_ref[r] for r in range(ranks)], axis=1)
    right = jnp.concatenate([near, far], axis=0)
    left = jnp.concatenate([left_ref[...], far_left_ref[...]], axis=0)
    turn_ref[...] = lax.dot_general(right, left, TN, preferred_element_type=F32) * scale
    blocks = lane_block((columns, LANES), depth)
    tiles = []
    for tile in range(depth * depth // LANES):
        pieces = [
            turn_ref[pl.ds(tile * residues + e, columns, stride=depth), :]
            for e in range(residues)
        ]
        rows = jnp.concatenate(pieces, axis=0)
        turned = [rows] + [pltpu.roll(rows, depth * t, 1) for t in range(1, residues)]
        tiles.append(
            jnp.concatenate(
                [
                    pick(
                        blocks,
                        [
                            turned[(e - i) % residues][e * columns : (e + 1) * columns]
                            for e in range(residues)
                        ],
                    )
                    for i in range(residues)
                ],
                axis=0,
            )
        )
    flat = jnp.concatenate(tiles, axis=1)
    rows = residues * columns
    parts = jnp.concatenate(split_three(flat), axis=0)
    pair = jnp.dot(parts, sorted_w_ref[...], preferred_element_type=F32)
    pair = pair[0:rows] + (pair[rows : 2 * rows] + pair[2 * rows : 3 * rows])
    pair_ref[...] = (pair + offset_ref[...]).astype(BF16).reshape(pair_ref.shape)


def body(
    homolog_matrix,
    standardizer_scaling,
    standardizer_offset,
    left_projection_matrix,
    left_offset_vector,
    right_projection_matrix,
    right_offset_vector,
    coupling_matrix,
    coupling_offset,
    coupling_cotangent,
):
    seqs, residues, features = homolog_matrix.shape
    depth = left_projection_matrix.shape[1]
    ranks = lax.axis_size("res")
    scale = 1.0 / (seqs * lax.axis_size("seq"))
    half_ranks = ranks // 2
    half_columns = half_ranks * residues
    step_ranks = 4
    columns = step_ranks * residues
    steps = half_ranks // step_ranks
    mine = lax.axis_index("seq")
    swap = [(0, 1), (1, 0)]

    other_cot = lax.ppermute(coupling_cotangent, "seq", swap)
    gain = standardizer_scaling.reshape(1, -1)
    left_w = left_projection_matrix.T
    right_w = right_projection_matrix.T

    left, right, sorted_w = pl.pallas_call(
        project_kernel,
        out_shape=(
            jax.ShapeDtypeStruct((seqs, LANES), BF16),
            jax.ShapeDtypeStruct((seqs, LANES), BF16),
            jax.ShapeDtypeStruct(coupling_matrix.shape, BF16),
        ),
        scratch_shapes=[pltpu.VMEM(coupling_matrix.shape, F32)],
        name="project",
    )(
        homolog_matrix,
        gain,
        standardizer_offset.reshape(1, -1),
        left_w,
        left_offset_vector.reshape(1, -1),
        right_w,
        right_offset_vector.reshape(1, -1),
        coupling_matrix,
    )

    whole = lambda shape: pl.BlockSpec(shape, lambda g: (0,) * len(shape))
    cot_block = pl.BlockSpec((residues, columns, LANES), lambda g: (0, g, 0))
    outer_block = pl.BlockSpec((2, columns * depth, LANES), lambda g: (0, g, 0))
    send_block = pl.BlockSpec((2, step_ranks, 2 * seqs, LANES), lambda g: (0, g, 0, 0))
    send, outer = pl.pallas_call(
        functools.partial(cot_kernel, scale),
        grid=(steps,),
        in_specs=[
            cot_block,
            cot_block,
            whole(sorted_w.shape),
            whole(left.shape),
            whole(right.shape),
        ],
        out_specs=(send_block, outer_block),
        out_shape=(
            jax.ShapeDtypeStruct((2, half_ranks, 2 * seqs, LANES), BF16),
            jax.ShapeDtypeStruct((2, half_columns * depth, LANES), BF16),
        ),
        scratch_shapes=[pltpu.VMEM((2 * columns * depth, LANES), F32)],
        name="cotangent",
    )(coupling_cotangent, other_cot, sorted_w, left, right)

    got = lax.all_to_all(
        send.reshape(ranks, 2 * seqs, LANES), "res", split_axis=0, concat_axis=0, tiled=True
    ).reshape(send.shape)

    leaving = lax.dynamic_index_in_dim(got, 1 - mine, 0, keepdims=False)[:, 0:seqs, :]
    far = lax.ppermute(jnp.concatenate([leaving, left[None]], axis=0), "seq", swap)

    gradient = pl.pallas_call(
        functools.partial(grad_kernel, steps),
        grid=(steps,),
        in_specs=[
            send_block,
            outer_block,
            whole(homolog_matrix.shape),
            whole(gain.shape),
            whole(left_w.shape),
            whole(right_w.shape),
        ],
        out_specs=whole(homolog_matrix.shape),
        out_shape=jax.ShapeDtypeStruct(homolog_matrix.shape, BF16),
        scratch_shapes=[pltpu.VMEM((seqs, LANES), F32)] * 2,
        name="gradient",
    )(got, outer, homolog_matrix, gain, left_w, right_w)

    pair_delta = pl.pallas_call(
        functools.partial(pair_kernel, scale),
        grid=(steps,),
        in_specs=[
            pl.BlockSpec((2, step_ranks, seqs, LANES), lambda g: (0, g, 0, 0)),
            pl.BlockSpec((step_ranks, seqs, LANES), lambda g: (g, 0, 0)),
            whole(left.shape),
            pl.BlockSpec((None, seqs, LANES), lambda g: (half_ranks, 0, 0)),
            whole(sorted_w.shape),
            whole((1, LANES)),
        ],
        out_specs=cot_block,
        out_shape=jax.ShapeDtypeStruct(coupling_cotangent.shape, BF16),
        scratch_shapes=[pltpu.VMEM((columns * depth, LANES), F32)],
        name="pair",
    )(got, far, left, far, sorted_w, coupling_offset.reshape(1, -1))
    return (pair_delta, gradient)


def solution(mesh):
    return jax.shard_map(
        body,
        mesh=mesh,
        in_specs=(
            P(("grp", "seq"), "res", None),
            P(),
            P(),
            P(),
            P(),
            P(),
            P(),
            P(),
            P(),
            P(("grp", "res"), "seq", None),
        ),
        out_specs=(P(("grp", "res"), "seq", None), P(("grp", "seq"), "res", None)),
        check_vma=False,
    )
```

time: 95.3 us -> 27.7 us (0.29)
  blocking collectives: 55 us -> 0 us
  between operations: 14.3 us -> 0.67 us
  Pallas kernels: 0 us -> 9.65 us
  waiting for transfers between devices: 0.02 us -> 7.65 us
  matrix products: 6.59 us -> 0 us
  other arithmetic: 5.4 us -> 0.01 us
  local copies, waits for them, and re-layouts: 6.27 us -> 1.93 us
    all_gather x3 -> x0, blocking collectives: 55 us -> none  [the longest x1 26.5 us: body(): lax.all_gather(right_proj, 'res', axis=1, tiled=True)]
    pallas_call x0 -> x4, Pallas kernels: none -> 9.65 us  [the longest x1 2.75 us: body(): pl.pallas_call(functools.partial(cot_kernel, scale), grid=(steps,), in_sp...]
    all_to_all x1, waiting for transfers between devices: 0.01 us -> 7.64 us  [body(): lax.all_to_all(send.reshape(ranks, 2 * seqs, LANES), 'res', split_axis=0,...]
    dot_general x10 -> x0, matrix products: 6.59 us -> none  [the longest x1 1.77 us: body(): jnp.einsum('sic,sjd->ijcd', left_own, right_rows, preferred_element_type=...]
    convert_element_type x3 -> x0, other arithmetic: 3.2 us -> none  [the longest x1 1.37 us: body(): pair_delta = (summed + coupling_offset).astype(jnp.bfloat16)]
    reduce_sum x3 -> x0, other arithmetic: 2.18 us -> none  [the longest x1 1.02 us: standardize_features(): jnp.mean(centred * centred, axis=-1, keepdims=True) + 1e-05]
    div x2 -> x0, local copies, waits for them, and re-layouts: 2.03 us -> none  [the longest x1 1.93 us: body(): jnp.einsum('sic,sjd->ijcd', left_own, right_rows, preferred_element_type=...]
    reshape x7 -> x0, local copies, waits for them, and re-layouts: 1.98 us -> none  [the longest x2 1.54 us: cot_outer(): return result.astype(jnp.bfloat16).reshape(first, second, depth_p, depth_p)]
  transfers between devices with their start and end apart: 2 -> 3, of which waited for: 0 -> 1; matrix products, arithmetic and copies ran while one was open for 17% -> 0% of each run, Pallas kernels for 0% -> 17%
where the time goes in v3:
time: 27.7 us; the launch traced here: 27.3 us
  Pallas kernels  9.65 us (35%)
  waiting for transfers between devices  7.65 us (28%)
  starting transfers between devices  7.4 us (27%)
  local copies, waits for them, and re-layouts  1.93 us (7%)
  between operations  0.67 us (2%)
    all_to_all x1, waiting for transfers between devices, body(): lax.all_to_all(send.reshape(ranks, 2 * seqs, LANES), 'res', split_axis=0,...  7.64 us
    all_to_all x1, starting transfers between devices, body(): lax.all_to_all(send.reshape(ranks, 2 * seqs, LANES), 'res', split_axis=0,...  6.82 us
    pallas_call x1, Pallas kernels, body(): pl.pallas_call(functools.partial(cot_kernel, scale), grid=(steps,), in_sp...  2.75 us
    pallas_call x1, Pallas kernels, body(): pl.pallas_call(project_kernel, out_shape=(jax.ShapeDtypeStruct((seqs, LAN...  2.39 us
    pallas_call x1, Pallas kernels, body(): pl.pallas_call(functools.partial(pair_kernel, scale), grid=(steps,), in_s...  2.36 us
    pallas_call x1, Pallas kernels, body(): pl.pallas_call(functools.partial(grad_kernel, steps), grid=(steps,), in_s...  2.16 us
    unnamed x8, local copies, waits for them, and re-layouts  1.92 us
  transfers between devices with their start and end apart: 3, of which 1 were waited for; matrix products, arithmetic and copies ran while one was open for 0% of the time, Pallas kernels for 17%

profile of v3, /device:TPU:0, one launch (start us, length us, event | category | flops | bytes accessed | tf_op | source)
XLA Modules:
  0.0 27.3 jit_solution(5414822130572192854)
XLA Ops:
  0.6 0.5 %collective-permute-start = (bf16[4,16,128]{2,1,0:T(8,128)(2,1)}, bf16[4,16,128]{2,1,0:T(8,128)(2,1)S(1)}, u32[]{:S(2)}, u32[]{:S(2)}) collective-permute-start(bf16[4,16,128]{2,1,0:T(8,128)(2,1)} %own_ref.1), channel_id=1, source_target_pairs={{0,1},{1,0},{2,3},{3,2},{4,5},{5,4},{6,7},{7,6},{8,9},{9,8},{10,11... | collective-permute-start | bytes 49160 | tf_op jit(solution)/shard_map/ppermute | solution.py:239
  1.1 2.4 %project.1 = (bf16[32,128]{1,0:T(8,128)(2,1)}, bf16[32,128]{1,0:T(8,128)(2,1)}, bf16[1024,128]{1,0:T(8,128)(2,1)}) custom-call(bf16[32,4,256]{2,1,0:T(4,128)(2,1)} %x_ref.3, f32[1,256]{1,0:T(1,128)} %bitcast.21, f32[1,256]{1,0:T(1,128)} %bitcast.23, bf16[32,256]{1,0:T(8,128)(2,1)} %bitcast.17, f32[1,32]{1,0:T(1,128)} %bitcast.24, bf16[32,256]{1,0:T(8,128)(2,1)} %bitcast.19, ...), custom_call_target="tpu_custom_call" | custom-call | tf_op jit(solution)/shard_map/project/pallas_call | solution.py:244
  3.5 0.0 collective-permute-done.other_ref
  3.5 0.0 copy-start.3
  3.5 0.6 %copy-done.3 = bf16[4,16,128]{2,1,0:T(8,128)(2,1)} copy-done((bf16[4,16,128]{2,1,0:T(8,128)(2,1)}, bf16[4,16,128]{2,1,0:T(8,128)(2,1)S(1)}, u32[]{:S(2)}) %copy-start.3) | copy-done | bytes 16408
  4.1 2.7 %cotangent.1 = (bf16[2,4,64,128]{3,2,1,0:T(8,128)(2,1)}, bf16[2,512,128]{2,1,0:T(8,128)(2,1)}) custom-call(bf16[4,16,128]{2,1,0:T(8,128)(2,1)} %own_ref.1, bf16[4,16,128]{2,1,0:T(8,128)(2,1)} %copy-done.3, bf16[1024,128]{1,0:T(8,128)(2,1)} %get-tuple-element.7.sorted_w_ref, bf16[32,128]{1,0:T(8,128)(2,1)} %get-tuple-element.8.left_ref, ...), custom_call_target="tpu_custom_call" | custom-call | tf_op jit(solution)/shard_map/cotangent/pallas_call | solution.py:268
  6.9 6.8 %all-to-all-start = ((bf16[8,64,128]{2,1,0:T(8,128)(2,1)}), bf16[8,64,128]{2,1,0:T(8,128)(2,1)S(1)}, u32[]{:S(2)}, u32[]{:S(2)}) async-start(bf16[8,64,128]{2,1,0:T(8,128)(2,1)} %bitcast.15), calls=%async_computation | async-start | bytes 262144 | tf_op jit(solution)/shard_map/all_to_all | solution.py:287
  13.7 7.6 %all-to-all-done = bf16[8,64,128]{2,1,0:T(8,128)(2,1)S(1)} async-done(((bf16[8,64,128]{2,1,0:T(8,128)(2,1)}), bf16[8,64,128]{2,1,0:T(8,128)(2,1)S(1)}, u32[]{:S(2)}, u32[]{:S(2)}) %all-to-all-start) | async-done | bytes 131104 | tf_op jit(solution)/shard_map/all_to_all | solution.py:287
  21.4 0.0 copy-start
  21.4 0.0 copy-start.2
  21.4 0.7 %copy-done.2 = bf16[32,128]{1,0:T(8,128)(2,1)S(1)} copy-done((bf16[32,128]{1,0:T(8,128)(2,1)S(1)}, bf16[32,128]{1,0:T(8,128)(2,1)}, u32[]{:S(2)}) %copy-start.2) | copy-done | bytes 8216
  22.1 0.0 copy-done
  22.1 0.1 collective-permute-start.1
  22.2 2.2 %gradient.1 = bf16[32,4,256]{2,1,0:T(4,128)(2,1)} custom-call(bf16[2,4,64,128]{3,2,1,0:T(8,128)(2,1)} %bitcast.13, bf16[2,512,128]{2,1,0:T(8,128)(2,1)} %get-tuple-element.11.outer_ref, bf16[32,4,256]{2,1,0:T(4,128)(2,1)} %x_ref.3, f32[1,256]{1,0:T(1,128)} %bitcast.22, bf16[32,256]{1,0:T(8,128)(2,1)} %bitcast.18, bf16[32,256]{1,0:T(8,128)(2,1)} %bitcast.20), custom_call_target="tpu_custom_call" | custom-call | tf_op jit(solution)/shard_map/gradient/pallas_call | solution.py:294
  24.3 0.0 collective-permute-done.1.far_ref.far_left_ref
  24.3 0.0 copy-start.1
  24.3 0.6 %copy-done.1 = bf16[5,32,128]{2,1,0:T(8,128)(2,1)} copy-done((bf16[5,32,128]{2,1,0:T(8,128)(2,1)}, bf16[5,32,128]{2,1,0:T(8,128)(2,1)S(1)}, u32[]{:S(2)}) %copy-start.1) | copy-done | bytes 40984
  25.0 2.4 %pair.1 = bf16[4,16,128]{2,1,0:T(8,128)(2,1)} custom-call(bf16[2,4,64,128]{3,2,1,0:T(8,128)(2,1)} %bitcast.14, bf16[5,32,128]{2,1,0:T(8,128)(2,1)} %copy-done.1, bf16[32,128]{1,0:T(8,128)(2,1)} %get-tuple-element.8.left_ref, bf16[5,32,128]{2,1,0:T(8,128)(2,1)} %copy-done.1, bf16[1024,128]{1,0:T(8,128)(2,1)} %get-tuple-element.7.sorted_w_ref, f32[1,128]{1,0:T(1,128)} %bitcast.26), custom_call_target="tpu_custom_call" | custom-call | tf_op jit(solution)/shard_map/pair/pallas_call | solution.py:311
  (3 shorter events, 0.0 us)
Async XLA Ops:
  0.6 2.9 %collective-permute-start = (bf16[4,16,128]{2,1,0:T(8,128)(2,1)}, bf16[4,16,128]{2,1,0:T(8,128)(2,1)S(1)}, u32[]{:S(2)}, u32[]{:S(2)}) collective-permute-start(bf16[4,16,128]{2,1,0:T(8,128)(2,1)} %own_ref.1), channel_id=1, source_target_pairs={{0,1},{1,0},{2,3},{3,2},{4,5},{5,4},{6,7},{7,6},{8,9},{9,8},{10,11... | collective-permute-start | bytes 49160 | tf_op jit(solution)/shard_map/ppermute | solution.py:239
  3.5 0.6 %copy-start.3 = (bf16[4,16,128]{2,1,0:T(8,128)(2,1)}, bf16[4,16,128]{2,1,0:T(8,128)(2,1)S(1)}, u32[]{:S(2)}) copy-start(bf16[4,16,128]{2,1,0:T(8,128)(2,1)S(1)} %collective-permute-done.other_ref) | copy-start | bytes 49156
  6.9 14.5 %all-to-all-start = ((bf16[8,64,128]{2,1,0:T(8,128)(2,1)}), bf16[8,64,128]{2,1,0:T(8,128)(2,1)S(1)}, u32[]{:S(2)}, u32[]{:S(2)}) async-start(bf16[8,64,128]{2,1,0:T(8,128)(2,1)} %bitcast.15), calls=%async_computation | async-start | bytes 262144 | tf_op jit(solution)/shard_map/all_to_all | solution.py:287
  21.4 0.7 %copy-start = (bf16[8,64,128]{2,1,0:T(8,128)(2,1)}, bf16[8,64,128]{2,1,0:T(8,128)(2,1)S(1)}, u32[]{:S(2)}) copy-start(bf16[8,64,128]{2,1,0:T(8,128)(2,1)S(1)} %all-to-all-done) | copy-start | bytes 393220
  21.4 0.7 %copy-start.2 = (bf16[32,128]{1,0:T(8,128)(2,1)S(1)}, bf16[32,128]{1,0:T(8,128)(2,1)}, u32[]{:S(2)}) copy-start(bf16[32,128]{1,0:T(8,128)(2,1)} %get-tuple-element.8.left_ref) | copy-start | bytes 24580
  22.1 2.2 %collective-permute-start.1 = (bf16[5,32,128]{2,1,0:T(8,128)(2,1)S(1)}, bf16[5,32,128]{2,1,0:T(8,128)(2,1)S(1)}, u32[]{:S(2)}, u32[]{:S(2)}) collective-permute-start(bf16[5,32,128]{2,1,0:T(8,128)(2,1)S(1)} %pad_maximum_fusion), channel_id=1, source_target_pairs={{0,1},{1,0},{2,3},{3,2},{4,5},{5,4},{6,7},{7,6},{8,9},{9,8},{10,11... | collective-permute-start | bytes 122888 | tf_op jit(solution)/shard_map/ppermute | solution.py:292
  24.3 0.6 %copy-start.1 = (bf16[5,32,128]{2,1,0:T(8,128)(2,1)}, bf16[5,32,128]{2,1,0:T(8,128)(2,1)S(1)}, u32[]{:S(2)}) copy-start(bf16[5,32,128]{2,1,0:T(8,128)(2,1)S(1)} %collective-permute-done.1.far_ref.far_left_ref) | copy-start | bytes 122884

commit v4 on v3

--- a/solution.py
+++ b/solution.py
@@ -212,7 +212,7 @@
     pair_ref[...] = (pair + offset_ref[...]).astype(BF16).reshape(pair_ref.shape)
 
 
-def body(
+def wide_slice(
     homolog_matrix,
     standardizer_scaling,
     standardizer_offset,
@@ -327,6 +327,304 @@
     return (pair_delta, gradient)
 
 
+STEP_MASKS = (2, 4, 1)
+
+
+def cube_place(mask):
+    first, second, third = STEP_MASKS
+    bit = lambda step: lax.shift_right_logical(mask, step.bit_length() - 1) & 1
+    return bit(second) * 4 + bit(third) * 2 + bit(first)
+
+
+def fetch(source, target, semaphore):
+    copy = pltpu.make_async_copy(source, target, semaphore)
+    copy.start()
+    return copy
+
+
+def cube_project_kernel(
+    x_ref, gain_ref, offset_ref, left_w_ref, left_b_ref, right_w_ref, right_b_ref, w_hbm, pair_offset_ref,
+    left_ref, right_ref, sorted_w_ref, normed_ref, inv_std_ref, spread_w_ref, gain_out_ref,
+    pair_offset_out_ref, raw_ref, wide_ref, semaphore,
+):
+    copy = fetch(w_hbm, raw_ref, semaphore)
+    seqs, residues, _ = x_ref.shape
+    depth = left_w_ref.shape[0]
+    normed, inv_std = normalise(residue_rows(x_ref))
+    normed_ref[...] = normed
+    inv_std_ref[...] = jnp.broadcast_to(inv_std, inv_std_ref.shape)
+    ln_out = (normed * gain_ref[...] + offset_ref[...]).astype(BF16)
+    blocks = lane_block((seqs, LANES), depth)
+    spread = []
+    for weight_ref, bias_ref, out_ref in (
+        (left_w_ref, left_b_ref, left_ref),
+        (right_w_ref, right_b_ref, right_ref),
+    ):
+        weight = jnp.concatenate([weight_ref[...]] * residues, axis=0)
+        spread.append(weight)
+        bias = jnp.concatenate([bias_ref[...]] * residues, axis=1)
+        wide = lax.dot_general(ln_out, weight, NT, preferred_element_type=F32)
+        own = pick(blocks, [wide[p * seqs : (p + 1) * seqs] for p in range(residues)])
+        out_ref[...] = (own + bias).astype(BF16)
+    spread_w_ref[...] = jnp.concatenate(spread, axis=0)
+    gain_out_ref[...] = gain_ref[...]
+    pair_offset_out_ref[...] = pair_offset_ref[...]
+    copy.wait()
+    wide_ref[...] = raw_ref[...].astype(F32)
+    for d in range(depth):
+        sorted_w_ref[d * depth : (d + 1) * depth, :] = wide_ref[
+            pl.ds(d, depth, stride=depth), :
+        ].astype(BF16)
+
+
+def cube_cot_kernel(scale, own_ref, other_ref, sorted_w_ref, left_ref, right_ref,
+                    send_ref, keep_ref, outer_ref, turn_ref):
+    residues, columns, _ = own_ref.shape
+    depth = LANES // residues
+    first = lax.axis_index("seq") == 0
+    own = own_ref[...].reshape(residues * columns, LANES)
+    other = other_ref[...].reshape(residues * columns, LANES)
+    both = jnp.concatenate([jnp.where(first, own, other), jnp.where(first, other, own)], axis=0)
+    flat = lax.dot_general(both, sorted_w_ref[...], NT, preferred_element_type=F32) * scale
+    blocks = lane_block((columns, LANES), depth)
+    for half in range(2):
+        for tile in range(depth * depth // LANES):
+            block = flat[
+                half * residues * columns : (half + 1) * residues * columns,
+                tile * LANES : (tile + 1) * LANES,
+            ]
+            turned = [block] + [pltpu.roll(block, depth * t, 1) for t in range(1, residues)]
+            for e in range(residues):
+                start = half * columns * depth + tile * residues + e
+                turn_ref[pl.ds(start, columns, stride=depth), :] = pick(
+                    blocks,
+                    [
+                        turned[(i - e) % residues][i * columns : (i + 1) * columns]
+                        for i in range(residues)
+                    ],
+                )
+    outer = turn_ref[...].astype(BF16)
+    outer_ref[...] = outer
+    partial = lax.dot_general(left_ref[...], outer, NT, preferred_element_type=F32)
+    rank = lax.axis_index("res")
+    send_ref[0] = right_ref[...]
+    for place in range(2 * columns // residues):
+        distance = lax.bitwise_xor(rank, place)
+        spot = cube_spot(distance)
+        piece = partial[:, place * LANES : (place + 1) * LANES]
+
+        @pl.when(spot >= 4)
+        def _():
+            send_ref[spot - 3] = piece.astype(BF16)
+
+        @pl.when(spot < 4)
+        def _():
+            keep_ref[spot] = piece
+
+
+def cube_spot(mask):
+    first, second, third = STEP_MASKS
+    bit = lambda step: lax.shift_right_logical(mask, step.bit_length() - 1) & 1
+    return bit(first) * 4 + bit(second) * 2 + bit(third)
+
+
+def cube_grad_kernel(right_ref, outer_ref, keep_ref, one_ref, two_ref, three_ref, normed_ref,
+                     inv_std_ref, gain_ref, spread_w_ref, grad_ref):
+    ranks, seqs, _ = right_ref.shape
+    residues = grad_ref.shape[1]
+    depth = LANES // residues
+    rank = lax.axis_index("res")
+    right_all = jnp.concatenate(
+        [right_ref[cube_place(lax.bitwise_xor(rank, place))] for place in range(ranks)], axis=1
+    )
+    left_cot = jnp.dot(right_all, outer_ref[...], preferred_element_type=F32)
+    right_cot = (
+        keep_ref[0] + one_ref[1].astype(F32) + two_ref[2].astype(F32) + three_ref[4].astype(F32)
+    )
+    blocks = lane_block((seqs, LANES), depth)
+    spread = jnp.concatenate(
+        [
+            jnp.concatenate(
+                [jnp.where(blocks == place, cot, 0.0) for cot in (left_cot, right_cot)], axis=1
+            )
+            for place in range(residues)
+        ],
+        axis=0,
+    )
+    rows = residues * seqs
+    parts = jnp.concatenate(split_three(spread), axis=0)
+    ln_cot = jnp.dot(parts, spread_w_ref[...], preferred_element_type=F32)
+    ln_cot = ln_cot[0:rows] + (ln_cot[rows : 2 * rows] + ln_cot[2 * rows : 3 * rows])
+    gained = ln_cot * gain_ref[...]
+    normed = normed_ref[...]
+    grad = inv_std_ref[:, 0:1] * (
+        gained
+        - jnp.mean(gained, axis=-1, keepdims=True)
+        - normed * jnp.mean(gained * normed, axis=-1, keepdims=True)
+    )
+    for place in range(residues):
+        grad_ref[:, place, :] = grad[place * seqs : (place + 1) * seqs].astype(BF16)
+
+
+def cube_pair_kernel(scale, right_ref, far_ref, left_ref, sorted_w_ref, offset_ref,
+                     pair_ref, turn_ref):
+    residues, columns, _ = pair_ref.shape
+    depth = LANES // residues
+    ranks = columns // residues
+    rank = lax.axis_index("res")
+    base = lax.axis_index("seq") * ranks
+    near, far = [], []
+    for place in range(ranks):
+        spot = cube_place(lax.bitwise_xor(rank, base + place))
+        near.append(right_ref[spot])
+        far.append(far_ref[spot & (ranks - 1)])
+    right = jnp.concatenate(
+        [jnp.concatenate(near, axis=1), jnp.concatenate(far, axis=1)], axis=0
+    )
+    left = jnp.concatenate([left_ref[...], far_ref[ranks]], axis=0)
+    turn_ref[...] = lax.dot_general(right, left, TN, preferred_element_type=F32) * scale
+    blocks = lane_block((columns, LANES), depth)
+    tiles = []
+    for tile in range(depth * depth // LANES):
+        pieces = [
+            turn_ref[pl.ds(tile * residues + e, columns, stride=depth), :]
+            for e in range(residues)
+        ]
+        rows = jnp.concatenate(pieces, axis=0)
+        turned = [rows] + [pltpu.roll(rows, depth * t, 1) for t in range(1, residues)]
+        tiles.append(
+            jnp.concatenate(
+                [
+                    pick(
+                        blocks,
+                        [
+                            turned[(e - i) % residues][e * columns : (e + 1) * columns]
+                            for e in range(residues)
+                        ],
+                    )
+                    for i in range(residues)
+                ],
+                axis=0,
+            )
+        )
+    flat = jnp.concatenate(tiles, axis=1)
+    rows = residues * columns
+    parts = jnp.concatenate(split_three(flat), axis=0)
+    pair = jnp.dot(parts, sorted_w_ref[...], preferred_element_type=F32)
+    pair = pair[0:rows] + (pair[rows : 2 * rows] + pair[2 * rows : 3 * rows])
+    pair_ref[...] = (pair + offset_ref[...]).astype(BF16).reshape(pair_ref.shape)
+
+
+def cube_slice(
+    homolog_matrix,
+    standardizer_scaling,
+    standardizer_offset,
+    left_projection_matrix,
+    left_offset_vector,
+    right_projection_matrix,
+    right_offset_vector,
+    coupling_matrix,
+    coupling_offset,
+    coupling_cotangent,
+):
+    seqs, residues, features = homolog_matrix.shape
+    ranks = lax.axis_size("res")
+    rows = seqs * residues
+    scale = 1.0 / (seqs * lax.axis_size("seq"))
+    rank = lax.axis_index("res")
+    mine = lax.axis_index("seq")
+    swap = [(0, 1), (1, 0)]
+    vmem = pl.BlockSpec(memory_space=pltpu.VMEM)
+    like = jax.ShapeDtypeStruct
+
+    other_cot = lax.ppermute(coupling_cotangent, "seq", swap)
+    left, right, sorted_w, normed, inv_std, spread_w, gain, pair_offset = pl.pallas_call(
+        cube_project_kernel,
+        in_specs=[vmem] * 7 + [pl.BlockSpec(memory_space=pl.ANY), vmem],
+        out_specs=[vmem] * 8,
+        out_shape=(
+            like((seqs, LANES), BF16),
+            like((seqs, LANES), BF16),
+            like(coupling_matrix.shape, BF16),
+            like((rows, features), F32),
+            like((rows, LANES), F32),
+            like((2 * LANES, features), BF16),
+            like((1, features), F32),
+            like((1, LANES), F32),
+        ),
+        scratch_shapes=[
+            pltpu.VMEM(coupling_matrix.shape, BF16),
+            pltpu.VMEM(coupling_matrix.shape, F32),
+            pltpu.SemaphoreType.DMA,
+        ],
+        name="project",
+    )(
+        homolog_matrix,
+        standardizer_scaling.reshape(1, -1),
+        standardizer_offset.reshape(1, -1),
+        left_projection_matrix.T,
+        left_offset_vector.reshape(1, -1),
+        right_projection_matrix.T,
+        right_offset_vector.reshape(1, -1),
+        coupling_matrix,
+        coupling_offset.reshape(1, -1),
+    )
+
+    send, keep, outer = pl.pallas_call(
+        functools.partial(cube_cot_kernel, scale),
+        in_specs=[vmem] * 5,
+        out_specs=[vmem] * 3,
+        out_shape=(
+            like((1 + ranks // 2, seqs, LANES), BF16),
+            like((ranks // 2, seqs, LANES), F32),
+            like((ranks * LANES, LANES), BF16),
+        ),
+        scratch_shapes=[pltpu.VMEM((ranks * LANES, LANES), F32)],
+        name="cotangent",
+    )(coupling_cotangent, other_cot, sorted_w, left, right)
+
+    def swap_over(mask, value):
+        return lax.ppermute(value, "res", [(source, source ^ mask) for source in range(ranks)])
+
+    own = right[None]
+    one = swap_over(STEP_MASKS[0], send)
+    send = jnp.concatenate([own, one[0:1], (keep[2:4] + one[3:5].astype(F32)).astype(BF16)])
+    two = swap_over(STEP_MASKS[1], send)
+    summed = keep[1:2] + one[2:3].astype(F32) + two[3:4].astype(F32)
+    send = jnp.concatenate([own, one[0:1], two[0:2], summed.astype(BF16)])
+    three = swap_over(STEP_MASKS[2], send)
+    gathered = jnp.concatenate([own, one[0:1], three[0:2], two[0:2], three[2:4]])
+
+    half = gathered.reshape(2, ranks // 2, seqs, LANES)
+    beyond = 1 - lax.bitwise_xor(lax.shift_right_logical(rank, 2), mine)
+    leaving = lax.dynamic_index_in_dim(half, beyond, 0, keepdims=False)
+    far = lax.ppermute(jnp.concatenate([leaving, left[None]]), "seq", swap)
+
+    gradient = pl.pallas_call(
+        cube_grad_kernel,
+        in_specs=[vmem] * 10,
+        out_specs=vmem,
+        out_shape=like(homolog_matrix.shape, BF16),
+        name="gradient",
+    )(gathered, outer, keep, one, two, three, normed, inv_std, gain, spread_w)
+
+    pair_delta = pl.pallas_call(
+        functools.partial(cube_pair_kernel, scale),
+        in_specs=[vmem] * 5,
+        out_specs=vmem,
+        out_shape=like(coupling_cotangent.shape, BF16),
+        scratch_shapes=[pltpu.VMEM((ranks // 2 * LANES, LANES), F32)],
+        name="pair",
+    )(gathered, far, left, sorted_w, pair_offset)
+    return (pair_delta, gradient)
+
+
+def body(*arrays):
+    if lax.axis_size("res") == 8:
+        return cube_slice(*arrays)
+    return wide_slice(*arrays)
+
+
 def solution(mesh):
     return jax.shard_map(
         body,

time: 27.7 us -> 30.3 us (1.094)
  other arithmetic: 0.01 us -> 1.54 us
  waiting for transfers between devices: 7.65 us -> 6.73 us
  Pallas kernels: 9.65 us -> 10.5 us
  local copies, waits for them, and re-layouts: 1.93 us -> 2.53 us
  starting transfers between devices: 7.4 us -> 7.81 us
    all_to_all x1 -> x0, waiting for transfers between devices: 7.64 us -> none  [body(): lax.all_to_all(send.reshape(ranks, 2 * seqs, LANES), 'res', split_axis=0,...]
    ppermute x2 -> x5, starting transfers between devices: 0.59 us -> 7.81 us  [the longest x3 7.22 us: swap_over(): lax.ppermute(value, 'res', [(source, source ^ mask) for source in range(r...]
    all_to_all x1 -> x0, starting transfers between devices: 6.82 us -> none  [body(): lax.all_to_all(send.reshape(ranks, 2 * seqs, LANES), 'res', split_axis=0,...]
    ppermute x2 -> x5, waiting for transfers between devices: 0.01 us -> 6.73 us  [the longest x3 6.73 us: swap_over(): lax.ppermute(value, 'res', [(source, source ^ mask) for source in range(r...]
    convert_element_type x0 -> x2, other arithmetic: none -> 1.52 us  [the longest x1 0.78 us: cube_slice(): (keep[2:4] + one[3:5].astype(F32)).astype(BF16)]
    pallas_call x4, Pallas kernels: 9.65 us -> 10.5 us  [the longest x1 2.93 us: cube_slice(): pl.pallas_call(cube_project_kernel, in_specs=[vmem] * 7 + [pl.BlockSpec(m...]
    unnamed x8 -> x19, local copies, waits for them, and re-layouts: 1.92 us -> 2.5 us
  transfers between devices with their start and end apart: 3 -> 5, of which waited for: 1 -> 3; matrix products, arithmetic and copies ran while one was open for 0% -> 0% of each run, Pallas kernels for 17% -> 18%
where the time goes in v4:
time: 30.3 us; the launch traced here: 29.8 us
  Pallas kernels  10.5 us (35%)
  starting transfers between devices  7.81 us (26%)
  waiting for transfers between devices  6.73 us (22%)
  local copies, waits for them, and re-layouts  2.53 us (8%)
  other arithmetic  1.54 us (5%)
  between operations  0.7 us (2%)
    ppermute x3, starting transfers between devices, swap_over(): lax.ppermute(value, 'res', [(source, source ^ mask) for source in range(r...  7.22 us
    ppermute x3, waiting for transfers between devices, swap_over(): lax.ppermute(value, 'res', [(source, source ^ mask) for source in range(r...  6.73 us
    pallas_call x1, Pallas kernels, cube_slice(): pl.pallas_call(cube_project_kernel, in_specs=[vmem] * 7 + [pl.BlockSpec(m...  2.93 us
    pallas_call x1, Pallas kernels, cube_slice(): pl.pallas_call(functools.partial(cube_cot_kernel, scale), in_specs=[vmem]...  2.92 us
    unnamed x19, local copies, waits for them, and re-layouts  2.5 us
    pallas_call x1, Pallas kernels, cube_slice(): pl.pallas_call(cube_grad_kernel, in_specs=[vmem] * 10, out_specs=vmem, ou...  2.34 us
    pallas_call x1, Pallas kernels, cube_slice(): pl.pallas_call(functools.partial(cube_pair_kernel, scale), in_specs=[vmem...  2.29 us
    convert_element_type x1, other arithmetic, cube_slice(): (keep[2:4] + one[3:5].astype(F32)).astype(BF16)  0.78 us
  transfers between devices with their start and end apart: 5, of which 3 were waited for; matrix products, arithmetic and copies ran while one was open for 0% of the time, Pallas kernels for 18%

profile of v4, /device:TPU:0, one launch (start us, length us, event | category | flops | bytes accessed | tf_op | source)
XLA Modules:
  0.0 29.8 jit_solution(13867510837534588083)
XLA Ops:
  0.6 0.5 %collective-permute-start = (bf16[4,16,128]{2,1,0:T(8,128)(2,1)}, bf16[4,16,128]{2,1,0:T(8,128)(2,1)S(1)}, u32[]{:S(2)}, u32[]{:S(2)}) collective-permute-start(bf16[4,16,128]{2,1,0:T(8,128)(2,1)} %own_ref.1), channel_id=1, source_target_pairs={{0,1},{1,0},{2,3},{3,2},{4,5},{5,4},{6,7},{7,6},{8,9},{9,8},{10,11... | collective-permute-start | bytes 49160 | tf_op jit(solution)/shard_map/ppermute | solution.py:540
  1.2 2.9 %project.1 = (bf16[32,128]{1,0:T(8,128)(2,1)}, bf16[32,128]{1,0:T(8,128)(2,1)}, bf16[1024,128]{1,0:T(8,128)(2,1)}, f32[128,256]{1,0:T(8,128)}, f32[128,128]{1,0:...) custom-call(bf16[32,4,256]{2,1,0:T(4,128)(2,1)} %x_ref.1, f32[1,256]{1,0:T(1,128)} %bitcast.19, ...), custom_call_target="tpu_custom_call" | custom-call | tf_op jit(solution)/shard_map/project/pallas_call | solution.py:541
  4.1 0.0 collective-permute-done.other_ref
  4.1 0.0 copy-start.7
  4.1 0.6 %copy-done.7 = bf16[4,16,128]{2,1,0:T(8,128)(2,1)} copy-done((bf16[4,16,128]{2,1,0:T(8,128)(2,1)}, bf16[4,16,128]{2,1,0:T(8,128)(2,1)S(1)}, u32[]{:S(2)}) %copy-start.7) | copy-done | bytes 16408
  4.7 2.9 %cotangent.1 = (bf16[5,32,128]{2,1,0:T(8,128)(2,1)}, f32[4,32,128]{2,1,0:T(8,128)}, bf16[1024,128]{1,0:T(8,128)(2,1)}) custom-call(bf16[4,16,128]{2,1,0:T(8,128)(2,1)} %own_ref.1, bf16[4,16,128]{2,1,0:T(8,128)(2,1)} %copy-done.7, bf16[1024,128]{1,0:T(8,128)(2,1)} %get-tuple-element.14.sorted_w_ref, bf16[32,128]{1,0:T(8,128)(2,1)} %get-tuple-element.15.left_ref, ...), custom_call_target="tpu_custom_call" | custom-call | tf_op jit(solution)/shard_map/cotangent/pallas_call | solution.py:573
  7.6 2.6 %collective-permute-start.1 = (bf16[5,32,128]{2,1,0:T(8,128)(2,1)}, bf16[5,32,128]{2,1,0:T(8,128)(2,1)S(1)}, u32[]{:S(2)}, u32[]{:S(2)}) collective-permute-start(bf16[5,32,128]{2,1,0:T(8,128)(2,1)} %get-tuple-element.16), channel_id=1, source_target_pairs={{0,4},{2,6},{4,0},{6,2},{8,12},{10,14},{12,8},{14,10},{1,5},{3,7},... | collective-permute-start | bytes 122888 | tf_op jit(solution)/shard_map/ppermute | solution.py:587
  10.2 0.0 copy-done.4
  10.2 2.4 %collective-permute-done.1.one_ref = bf16[5,32,128]{2,1,0:T(8,128)(2,1)S(1)} collective-permute-done((bf16[5,32,128]{2,1,0:T(8,128)(2,1)}, bf16[5,32,128]{2,1,0:T(8,128)(2,1)S(1)}, u32[]{:S(2)}, u32[]{:S(2)}) %collective-permute-start.1) | collective-permute-done | bytes 40992 | tf_op jit(solution)/shard_map/ppermute | solution.py:587
  12.6 0.8 %add_convert_fusion = bf16[2,32,128]{2,1,0:T(8,128)(2,1)S(1)} fusion(f32[4,32,128]{2,1,0:T(8,128)} %get-tuple-element.17.keep_ref, bf16[5,32,128]{2,1,0:T(8,128)(2,1)S(1)} %collective-permute-done.1.one_ref), kind=kLoop, calls=%fused_computation.4 | loop fusion | flops 24576 | bytes 65536 | tf_op jit(solution)/shard_map/convert_element_type | solution.py:591
  13.4 2.9 %collective-permute-start.2 = (bf16[4,32,128]{2,1,0:T(8,128)(2,1)S(1)}, bf16[4,32,128]{2,1,0:T(8,128)(2,1)S(1)}, u32[]{:S(2)}, u32[]{:S(2)}) collective-permute-start(bf16[4,32,128]{2,1,0:T(8,128)(2,1)S(1)} %pad_maximum_fusion.2), channel_id=1, source_target_pairs={{0,8},{2,10},{4,12},{6,14},{8,0},{10,2},{12,4},{14,6},{1,9},{3,11}... | collective-permute-start | bytes 98312 | tf_op jit(solution)/shard_map/ppermute | solution.py:587
  16.3 2.0 %collective-permute-done.2.two_ref = bf16[4,32,128]{2,1,0:T(8,128)(2,1)S(1)} collective-permute-done((bf16[4,32,128]{2,1,0:T(8,128)(2,1)S(1)}, bf16[4,32,128]{2,1,0:T(8,128)(2,1)S(1)}, u32[]{:S(2)}, u32[]{:S(2)}) %collective-permute-start.2) | collective-permute-done | bytes 32800 | tf_op jit(solution)/shard_map/ppermute | solution.py:587
  18.3 0.7 %add_convert_fusion.1 = bf16[1,32,128]{2,1,0:T(8,128)(2,1)S(1)} fusion(f32[4,32,128]{2,1,0:T(8,128)} %get-tuple-element.17.keep_ref, bf16[4,32,128]{2,1,0:T(8,128)(2,1)S(1)} %collective-permute-done.2.two_ref, bf16[5,32,128]{2,1,0:T(8,128)(2,1)S(1)} %collective-permute-done.1.one_ref), kind=kLoop, calls=%fused_computation.7 | loop fusion | flops 20480 | bytes 40960 | tf_op jit(solution)/shard_map/convert_element_type | solution.py:594
  19.1 1.8 %collective-permute-start.3 = (bf16[5,32,128]{2,1,0:T(8,128)(2,1)S(1)}, bf16[5,32,128]{2,1,0:T(8,128)(2,1)S(1)}, u32[]{:S(2)}, u32[]{:S(2)}) collective-permute-start(bf16[5,32,128]{2,1,0:T(8,128)(2,1)S(1)} %pad_maximum_fusion), channel_id=1, source_target_pairs={{0,2},{2,0},{4,6},{6,4},{8,10},{10,8},{12,14},{14,12},{1,3},{3,1},... | collective-permute-start | bytes 122888 | tf_op jit(solution)/shard_map/ppermute | solution.py:587
  20.8 2.3 %collective-permute-done.3.three_ref = bf16[5,32,128]{2,1,0:T(8,128)(2,1)S(1)} collective-permute-done((bf16[5,32,128]{2,1,0:T(8,128)(2,1)S(1)}, bf16[5,32,128]{2,1,0:T(8,128)(2,1)S(1)}, u32[]{:S(2)}, u32[]{:S(2)}) %collective-permute-start.3) | collective-permute-done | bytes 40992 | tf_op jit(solution)/shard_map/ppermute | solution.py:587
  23.2 0.0 copy-done.1
  23.2 0.6 %copy-done.3 = bf16[5,32,128]{2,1,0:T(8,128)(2,1)} copy-done((bf16[5,32,128]{2,1,0:T(8,128)(2,1)}, bf16[5,32,128]{2,1,0:T(8,128)(2,1)S(1)}, u32[]{:S(2)}) %copy-start.3) | copy-done | bytes 40984
  23.8 0.7 %copy-done.5 = bf16[32,128]{1,0:T(8,128)(2,1)S(1)} copy-done((bf16[32,128]{1,0:T(8,128)(2,1)S(1)}, bf16[32,128]{1,0:T(8,128)(2,1)}, u32[]{:S(2)}) %copy-start.5) | copy-done | bytes 8216
  24.5 0.0 copy-done
  24.5 0.1 collective-permute-start.4
  24.5 2.3 %gradient.1 = bf16[32,4,256]{2,1,0:T(4,128)(2,1)} custom-call(bf16[8,32,128]{2,1,0:T(8,128)(2,1)} %copy-done, bf16[1024,128]{1,0:T(8,128)(2,1)} %get-tuple-element.19.outer_ref, f32[4,32,128]{2,1,0:T(8,128)} %get-tuple-element.17.keep_ref, bf16[5,32,128]{2,1,0:T(8,128)(2,1)} %copy-done.2, bf16[4,32,128]{2,1,0:T(8,128)(2,1)} %copy-done.1, ...), custom_call_target="tpu_custom_call" | custom-call | tf_op jit(solution)/shard_map/gradient/pallas_call | solution.py:603
  26.9 0.0 collective-permute-done.4.far_ref
  26.9 0.6 %copy-done.6 = bf16[5,32,128]{2,1,0:T(8,128)(2,1)} copy-done((bf16[5,32,128]{2,1,0:T(8,128)(2,1)}, bf16[5,32,128]{2,1,0:T(8,128)(2,1)S(1)}, u32[]{:S(2)}) %copy-start.6) | copy-done | bytes 40984
  27.5 2.3 %pair.1 = bf16[4,16,128]{2,1,0:T(8,128)(2,1)} custom-call(bf16[8,32,128]{2,1,0:T(8,128)(2,1)} %copy-done, bf16[5,32,128]{2,1,0:T(8,128)(2,1)} %copy-done.6, bf16[32,128]{1,0:T(8,128)(2,1)} %get-tuple-element.15.left_ref, bf16[1024,128]{1,0:T(8,128)(2,1)} %get-tuple-element.14.sorted_w_ref, f32[1,128]{1,0:T(1,128)} %get-tuple-element.18.offset_ref), custom_call_target="tpu_custom_call" | custom-call | tf_op jit(solution)/shard_map/pair/pallas_call | solution.py:611
  (18 shorter events, 0.1 us)
Async XLA Ops:
  0.6 3.5 %collective-permute-start = (bf16[4,16,128]{2,1,0:T(8,128)(2,1)}, bf16[4,16,128]{2,1,0:T(8,128)(2,1)S(1)}, u32[]{:S(2)}, u32[]{:S(2)}) collective-permute-start(bf16[4,16,128]{2,1,0:T(8,128)(2,1)} %own_ref.1), channel_id=1, source_target_pairs={{0,1},{1,0},{2,3},{3,2},{4,5},{5,4},{6,7},{7,6},{8,9},{9,8},{10,11... | collective-permute-start | bytes 49160 | tf_op jit(solution)/shard_map/ppermute | solution.py:540
  4.1 0.6 %copy-start.7 = (bf16[4,16,128]{2,1,0:T(8,128)(2,1)}, bf16[4,16,128]{2,1,0:T(8,128)(2,1)S(1)}, u32[]{:S(2)}) copy-start(bf16[4,16,128]{2,1,0:T(8,128)(2,1)S(1)} %collective-permute-done.other_ref) | copy-start | bytes 49156
  4.7 5.5 %copy-start.4 = (bf16[32,128]{1,0:T(8,128)(2,1)S(1)}, bf16[32,128]{1,0:T(8,128)(2,1)}, u32[]{:S(2)}) copy-start(bf16[32,128]{1,0:T(8,128)(2,1)} %get-tuple-element.13.right_ref) | copy-start | bytes 24580
  7.6 5.0 %collective-permute-start.1 = (bf16[5,32,128]{2,1,0:T(8,128)(2,1)}, bf16[5,32,128]{2,1,0:T(8,128)(2,1)S(1)}, u32[]{:S(2)}, u32[]{:S(2)}) collective-permute-start(bf16[5,32,128]{2,1,0:T(8,128)(2,1)} %get-tuple-element.16), channel_id=1, source_target_pairs={{0,4},{2,6},{4,0},{6,2},{8,12},{10,14},{12,8},{14,10},{1,5},{3,7},... | collective-permute-start | bytes 122888 | tf_op jit(solution)/shard_map/ppermute | solution.py:587
  12.6 5.7 %copy-start.2 = (bf16[5,32,128]{2,1,0:T(8,128)(2,1)}, bf16[5,32,128]{2,1,0:T(8,128)(2,1)S(1)}, u32[]{:S(2)}) copy-start(bf16[5,32,128]{2,1,0:T(8,128)(2,1)S(1)} %collective-permute-done.1.one_ref) | copy-start | bytes 122884
  13.4 4.9 %collective-permute-start.2 = (bf16[4,32,128]{2,1,0:T(8,128)(2,1)S(1)}, bf16[4,32,128]{2,1,0:T(8,128)(2,1)S(1)}, u32[]{:S(2)}, u32[]{:S(2)}) collective-permute-start(bf16[4,32,128]{2,1,0:T(8,128)(2,1)S(1)} %pad_maximum_fusion.2), channel_id=1, source_target_pairs={{0,8},{2,10},{4,12},{6,14},{8,0},{10,2},{12,4},{14,6},{1,9},{3,11}... | collective-permute-start | bytes 98312 | tf_op jit(solution)/shard_map/ppermute | solution.py:587
  18.3 4.8 %copy-start.1 = (bf16[4,32,128]{2,1,0:T(8,128)(2,1)}, bf16[4,32,128]{2,1,0:T(8,128)(2,1)S(1)}, u32[]{:S(2)}) copy-start(bf16[4,32,128]{2,1,0:T(8,128)(2,1)S(1)} %collective-permute-done.2.two_ref) | copy-start | bytes 98308
  19.1 4.1 %collective-permute-start.3 = (bf16[5,32,128]{2,1,0:T(8,128)(2,1)S(1)}, bf16[5,32,128]{2,1,0:T(8,128)(2,1)S(1)}, u32[]{:S(2)}, u32[]{:S(2)}) collective-permute-start(bf16[5,32,128]{2,1,0:T(8,128)(2,1)S(1)} %pad_maximum_fusion), channel_id=1, source_target_pairs={{0,2},{2,0},{4,6},{6,4},{8,10},{10,8},{12,14},{14,12},{1,3},{3,1},... | collective-permute-start | bytes 122888 | tf_op jit(solution)/shard_map/ppermute | solution.py:587
  23.1 0.6 %copy-start.3 = (bf16[5,32,128]{2,1,0:T(8,128)(2,1)}, bf16[5,32,128]{2,1,0:T(8,128)(2,1)S(1)}, u32[]{:S(2)}) copy-start(bf16[5,32,128]{2,1,0:T(8,128)(2,1)S(1)} %collective-permute-done.3.three_ref) | copy-start | bytes 122884
  23.8 0.7 %copy-start = (bf16[8,32,128]{2,1,0:T(8,128)(2,1)}, bf16[8,32,128]{2,1,0:T(8,128)(2,1)S(1)}, u32[]{:S(2)}) copy-start(bf16[8,32,128]{2,1,0:T(8,128)(2,1)S(1)} %slice_dynamic-update-slice_fusion.right_ref) | copy-start | bytes 196612
  23.8 0.7 %copy-start.5 = (bf16[32,128]{1,0:T(8,128)(2,1)S(1)}, bf16[32,128]{1,0:T(8,128)(2,1)}, u32[]{:S(2)}) copy-start(bf16[32,128]{1,0:T(8,128)(2,1)} %get-tuple-element.15.left_ref) | copy-start | bytes 24580
  24.5 2.4 %collective-permute-start.4 = (bf16[5,32,128]{2,1,0:T(8,128)(2,1)S(1)}, bf16[5,32,128]{2,1,0:T(8,128)(2,1)S(1)}, u32[]{:S(2)}, u32[]{:S(2)}) collective-permute-start(bf16[5,32,128]{2,1,0:T(8,128)(2,1)S(1)} %pad_maximum_fusion.1), channel_id=1, source_target_pairs={{0,1},{1,0},{2,3},{3,2},{4,5},{5,4},{6,7},{7,6},{8,9},{9,8},{10,11... | collective-permute-start | bytes 122888 | tf_op jit(solution)/shard_map/ppermute | solution.py:601
  26.9 0.6 %copy-start.6 = (bf16[5,32,128]{2,1,0:T(8,128)(2,1)}, bf16[5,32,128]{2,1,0:T(8,128)(2,1)S(1)}, u32[]{:S(2)}) copy-start(bf16[5,32,128]{2,1,0:T(8,128)(2,1)S(1)} %collective-permute-done.4.far_ref) | copy-start | bytes 122884

commit v5 on v4

--- a/solution.py
+++ b/solution.py
@@ -327,33 +327,45 @@
     return (pair_delta, gradient)
 
 
-STEP_MASKS = (2, 4, 1)
-
-
-def cube_place(mask):
-    first, second, third = STEP_MASKS
-    bit = lambda step: lax.shift_right_logical(mask, step.bit_length() - 1) & 1
-    return bit(second) * 4 + bit(third) * 2 + bit(first)
-
-
 def fetch(source, target, semaphore):
     copy = pltpu.make_async_copy(source, target, semaphore)
     copy.start()
     return copy
 
 
-def cube_project_kernel(
-    x_ref, gain_ref, offset_ref, left_w_ref, left_b_ref, right_w_ref, right_b_ref, w_hbm, pair_offset_ref,
+def small_project_kernel(
+    x_hbm, gain_hbm, offset_hbm, left_w_hbm, left_b_hbm, right_w_hbm, right_b_hbm, w_hbm, pair_offset_hbm,
     left_ref, right_ref, sorted_w_ref, normed_ref, inv_std_ref, spread_w_ref, gain_out_ref,
-    pair_offset_out_ref, raw_ref, wide_ref, semaphore,
+    pair_offset_out_ref,
+    x_ref, offset_ref, left_w_ref, left_b_ref, right_w_ref, right_b_ref, raw_ref, wide_ref, semaphores,
 ):
-    copy = fetch(w_hbm, raw_ref, semaphore)
+    copies = [
+        pltpu.make_async_copy(source, target, semaphores.at[place])
+        for place, (source, target) in enumerate(
+            (
+                (x_hbm, x_ref),
+                (gain_hbm, gain_out_ref),
+                (offset_hbm, offset_ref),
+                (left_w_hbm, left_w_ref),
+                (left_b_hbm, left_b_ref),
+                (right_w_hbm, right_w_ref),
+                (right_b_hbm, right_b_ref),
+                (w_hbm, raw_ref),
+                (pair_offset_hbm, pair_offset_out_ref),
+            )
+        )
+    ]
+    for copy in copies:
+        copy.start()
     seqs, residues, _ = x_ref.shape
     depth = left_w_ref.shape[0]
+    copies[0].wait()
     normed, inv_std = normalise(residue_rows(x_ref))
     normed_ref[...] = normed
     inv_std_ref[...] = jnp.broadcast_to(inv_std, inv_std_ref.shape)
-    ln_out = (normed * gain_ref[...] + offset_ref[...]).astype(BF16)
+    for copy in copies[1:7]:
+        copy.wait()
+    ln_out = (normed * gain_out_ref[...] + offset_ref[...]).astype(BF16)
     blocks = lane_block((seqs, LANES), depth)
     spread = []
     for weight_ref, bias_ref, out_ref in (
@@ -367,9 +379,8 @@
         own = pick(blocks, [wide[p * seqs : (p + 1) * seqs] for p in range(residues)])
         out_ref[...] = (own + bias).astype(BF16)
     spread_w_ref[...] = jnp.concatenate(spread, axis=0)
-    gain_out_ref[...] = gain_ref[...]
-    pair_offset_out_ref[...] = pair_offset_ref[...]
-    copy.wait()
+    for copy in copies[7:]:
+        copy.wait()
     wide_ref[...] = raw_ref[...].astype(F32)
     for d in range(depth):
         sorted_w_ref[d * depth : (d + 1) * depth, :] = wide_ref[
@@ -377,7 +388,7 @@
         ].astype(BF16)
 
 
-def cube_cot_kernel(scale, own_ref, other_ref, sorted_w_ref, left_ref, right_ref,
+def small_cot_kernel(scale, own_ref, other_ref, sorted_w_ref, left_ref, right_ref,
                     send_ref, keep_ref, outer_ref, turn_ref):
     residues, columns, _ = own_ref.shape
     depth = LANES // residues
@@ -409,38 +420,32 @@
     rank = lax.axis_index("res")
     send_ref[0] = right_ref[...]
     for place in range(2 * columns // residues):
+        piece = partial[:, place * LANES : (place + 1) * LANES]
         distance = lax.bitwise_xor(rank, place)
-        spot = cube_spot(distance)
-        piece = partial[:, place * LANES : (place + 1) * LANES]
-
-        @pl.when(spot >= 4)
+        spot = lax.shift_right_logical(distance, 1)
+
+        @pl.when(distance & 1 == 1)
         def _():
-            send_ref[spot - 3] = piece.astype(BF16)
-
-        @pl.when(spot < 4)
+            send_ref[spot + 1] = piece.astype(BF16)
+
+        @pl.when(distance & 1 == 0)
         def _():
             keep_ref[spot] = piece
 
 
-def cube_spot(mask):
-    first, second, third = STEP_MASKS
-    bit = lambda step: lax.shift_right_logical(mask, step.bit_length() - 1) & 1
-    return bit(first) * 4 + bit(second) * 2 + bit(third)
-
-
-def cube_grad_kernel(right_ref, outer_ref, keep_ref, one_ref, two_ref, three_ref, normed_ref,
-                     inv_std_ref, gain_ref, spread_w_ref, grad_ref):
+def small_grad_kernel(right_ref, outer_ref, keep_ref, beside_ref, far_refs, normed_ref, inv_std_ref,
+                      gain_ref, spread_w_ref, grad_ref):
     ranks, seqs, _ = right_ref.shape
     residues = grad_ref.shape[1]
     depth = LANES // residues
     rank = lax.axis_index("res")
     right_all = jnp.concatenate(
-        [right_ref[cube_place(lax.bitwise_xor(rank, place))] for place in range(ranks)], axis=1
+        [right_ref[lax.bitwise_xor(rank, place)] for place in range(ranks)], axis=1
     )
     left_cot = jnp.dot(right_all, outer_ref[...], preferred_element_type=F32)
-    right_cot = (
-        keep_ref[0] + one_ref[1].astype(F32) + two_ref[2].astype(F32) + three_ref[4].astype(F32)
-    )
+    right_cot = keep_ref[0] + beside_ref[1].astype(F32)
+    for far_ref in far_refs:
+        right_cot = right_cot + far_ref[2].astype(F32)
     blocks = lane_block((seqs, LANES), depth)
     spread = jnp.concatenate(
         [
@@ -466,7 +471,7 @@
         grad_ref[:, place, :] = grad[place * seqs : (place + 1) * seqs].astype(BF16)
 
 
-def cube_pair_kernel(scale, right_ref, far_ref, left_ref, sorted_w_ref, offset_ref,
+def small_pair_kernel(scale, right_ref, far_ref, left_ref, sorted_w_ref, offset_ref,
                      pair_ref, turn_ref):
     residues, columns, _ = pair_ref.shape
     depth = LANES // residues
@@ -475,9 +480,9 @@
     base = lax.axis_index("seq") * ranks
     near, far = [], []
     for place in range(ranks):
-        spot = cube_place(lax.bitwise_xor(rank, base + place))
-        near.append(right_ref[spot])
-        far.append(far_ref[spot & (ranks - 1)])
+        distance = lax.bitwise_xor(rank, base + place)
+        near.append(right_ref[distance])
+        far.append(far_ref[distance & (ranks - 1)])
     right = jnp.concatenate(
         [jnp.concatenate(near, axis=1), jnp.concatenate(far, axis=1)], axis=0
     )
@@ -515,7 +520,7 @@
     pair_ref[...] = (pair + offset_ref[...]).astype(BF16).reshape(pair_ref.shape)
 
 
-def cube_slice(
+def small_slice(
     homolog_matrix,
     standardizer_scaling,
     standardizer_offset,
@@ -528,19 +533,21 @@
     coupling_cotangent,
 ):
     seqs, residues, features = homolog_matrix.shape
+    depth = left_projection_matrix.shape[1]
     ranks = lax.axis_size("res")
     rows = seqs * residues
     scale = 1.0 / (seqs * lax.axis_size("seq"))
     rank = lax.axis_index("res")
     mine = lax.axis_index("seq")
     swap = [(0, 1), (1, 0)]
+    limit = pltpu.CompilerParams(vmem_limit_bytes=8 * 1024 * 1024)
     vmem = pl.BlockSpec(memory_space=pltpu.VMEM)
     like = jax.ShapeDtypeStruct
 
     other_cot = lax.ppermute(coupling_cotangent, "seq", swap)
     left, right, sorted_w, normed, inv_std, spread_w, gain, pair_offset = pl.pallas_call(
-        cube_project_kernel,
-        in_specs=[vmem] * 7 + [pl.BlockSpec(memory_space=pl.ANY), vmem],
+        small_project_kernel,
+        in_specs=[pl.BlockSpec(memory_space=pltpu.HBM)] * 9,
         out_specs=[vmem] * 8,
         out_shape=(
             like((seqs, LANES), BF16),
@@ -553,10 +560,17 @@
             like((1, LANES), F32),
         ),
         scratch_shapes=[
+            pltpu.VMEM(homolog_matrix.shape, BF16),
+            pltpu.VMEM((1, features), F32),
+            pltpu.VMEM((depth, features), BF16),
+            pltpu.VMEM((1, depth), F32),
+            pltpu.VMEM((depth, features), BF16),
+            pltpu.VMEM((1, depth), F32),
             pltpu.VMEM(coupling_matrix.shape, BF16),
             pltpu.VMEM(coupling_matrix.shape, F32),
-            pltpu.SemaphoreType.DMA,
+            pltpu.SemaphoreType.DMA((9,)),
         ],
+        compiler_params=limit,
         name="project",
     )(
         homolog_matrix,
@@ -571,7 +585,7 @@
     )
 
     send, keep, outer = pl.pallas_call(
-        functools.partial(cube_cot_kernel, scale),
+        functools.partial(small_cot_kernel, scale),
         in_specs=[vmem] * 5,
         out_specs=[vmem] * 3,
         out_shape=(
@@ -580,6 +594,7 @@
             like((ranks * LANES, LANES), BF16),
         ),
         scratch_shapes=[pltpu.VMEM((ranks * LANES, LANES), F32)],
+        compiler_params=limit,
         name="cotangent",
     )(coupling_cotangent, other_cot, sorted_w, left, right)
 
@@ -587,13 +602,15 @@
         return lax.ppermute(value, "res", [(source, source ^ mask) for source in range(ranks)])
 
     own = right[None]
-    one = swap_over(STEP_MASKS[0], send)
-    send = jnp.concatenate([own, one[0:1], (keep[2:4] + one[3:5].astype(F32)).astype(BF16)])
-    two = swap_over(STEP_MASKS[1], send)
-    summed = keep[1:2] + one[2:3].astype(F32) + two[3:4].astype(F32)
-    send = jnp.concatenate([own, one[0:1], two[0:2], summed.astype(BF16)])
-    three = swap_over(STEP_MASKS[2], send)
-    gathered = jnp.concatenate([own, one[0:1], three[0:2], two[0:2], three[2:4]])
+    beside = swap_over(1, send)
+    both = jnp.concatenate([own, beside[0:1]])
+    far_parts = {}
+    for mask in (6, 4, 2):
+        spot = mask // 2
+        summed = (keep[spot] + beside[1 + spot].astype(F32)).astype(BF16)
+        far_parts[mask] = swap_over(mask, jnp.concatenate([both, summed[None]]))
+    far_parts = [far_parts[mask] for mask in (2, 4, 6)]
+    gathered = jnp.concatenate([both] + [part[0:2] for part in far_parts])
 
     half = gathered.reshape(2, ranks // 2, seqs, LANES)
     beyond = 1 - lax.bitwise_xor(lax.shift_right_logical(rank, 2), mine)
@@ -601,19 +618,21 @@
     far = lax.ppermute(jnp.concatenate([leaving, left[None]]), "seq", swap)
 
     gradient = pl.pallas_call(
-        cube_grad_kernel,
-        in_specs=[vmem] * 10,
+        small_grad_kernel,
+        in_specs=[vmem] * 4 + [[vmem] * 3] + [vmem] * 4,
         out_specs=vmem,
         out_shape=like(homolog_matrix.shape, BF16),
+        compiler_params=limit,
         name="gradient",
-    )(gathered, outer, keep, one, two, three, normed, inv_std, gain, spread_w)
+    )(gathered, outer, keep, beside, far_parts, normed, inv_std, gain, spread_w)
 
     pair_delta = pl.pallas_call(
-        functools.partial(cube_pair_kernel, scale),
+        functools.partial(small_pair_kernel, scale),
         in_specs=[vmem] * 5,
         out_specs=vmem,
         out_shape=like(coupling_cotangent.shape, BF16),
         scratch_shapes=[pltpu.VMEM((ranks // 2 * LANES, LANES), F32)],
+        compiler_params=limit,
         name="pair",
     )(gathered, far, left, sorted_w, pair_offset)
     return (pair_delta, gradient)
@@ -621,7 +640,7 @@
 
 def body(*arrays):
     if lax.axis_size("res") == 8:
-        return cube_slice(*arrays)
+        return small_slice(*arrays)
     return wide_slice(*arrays)
 
 

time: 30.3 us -> 25.2 us (0.83)
  Pallas kernels: 10.5 us -> 4.58 us
  other arithmetic: 1.54 us -> 0.03 us
  local copies, waits for them, and re-layouts: 2.53 us -> 3.98 us
  waiting for transfers between devices: 6.73 us -> 7.88 us
    pallas_call x4, Pallas kernels: 10.5 us -> 4.58 us  [the longest x1 1.31 us: small_slice(): pl.pallas_call(functools.partial(small_pair_kernel, scale), in_specs=[vme...]
    convert_element_type x2 -> x1, other arithmetic: 1.52 us -> 0.01 us  [small_slice(): summed = (keep[spot] + beside[1 + spot].astype(F32)).astype(BF16)]
    unnamed x19 -> x23, local copies, waits for them, and re-layouts: 2.5 us -> 3.96 us
    ppermute x3 -> x4, waiting for transfers between devices: 6.73 us -> 7.83 us  [swap_over(): lax.ppermute(value, 'res', [(source, source ^ mask) for source in range(r...]
    ppermute x3 -> x4, starting transfers between devices: 7.22 us -> 7.08 us  [swap_over(): lax.ppermute(value, 'res', [(source, source ^ mask) for source in range(r...]
  transfers between devices with their start and end apart: 5 -> 6, of which waited for: 3 -> 4; matrix products, arithmetic and copies ran while one was open for 0% -> 0% of each run, Pallas kernels for 18% -> 9%
where the time goes in v5:
time: 25.2 us; the launch traced here: 24.9 us
  waiting for transfers between devices  7.88 us (31%)
  starting transfers between devices  7.67 us (30%)
  Pallas kernels  4.58 us (18%)
  local copies, waits for them, and re-layouts  3.98 us (16%)
  between operations  0.72 us (3%)
    ppermute x4, waiting for transfers between devices, swap_over(): lax.ppermute(value, 'res', [(source, source ^ mask) for source in range(r...  7.83 us
    ppermute x4, starting transfers between devices, swap_over(): lax.ppermute(value, 'res', [(source, source ^ mask) for source in range(r...  7.08 us
    unnamed x23, local copies, waits for them, and re-layouts  3.96 us
    pallas_call x1, Pallas kernels, small_slice(): pl.pallas_call(functools.partial(small_pair_kernel, scale), in_specs=[vme...  1.31 us
    pallas_call x1, Pallas kernels, small_slice(): pl.pallas_call(small_grad_kernel, in_specs=[vmem] * 4 + [[vmem] * 3] + [v...  1.15 us
    pallas_call x1, Pallas kernels, small_slice(): pl.pallas_call(functools.partial(small_cot_kernel, scale), in_specs=[vmem...  1.15 us
    pallas_call x1, Pallas kernels, small_slice(): pl.pallas_call(small_project_kernel, in_specs=[pl.BlockSpec(memory_space=...  0.97 us
    ppermute x1, starting transfers between devices, small_slice(): other_cot = lax.ppermute(coupling_cotangent, 'seq', swap)  0.52 us
  transfers between devices with their start and end apart: 6, of which 4 were waited for; matrix products, arithmetic and copies ran while one was open for 0% of the time, Pallas kernels for 9%

profile of v5, /device:TPU:0, one launch (start us, length us, event | category | flops | bytes accessed | tf_op | source)
XLA Modules:
  0.0 24.9 jit_solution(10417074354084265159)
XLA Ops:
  0.6 0.5 %collective-permute-start = (bf16[4,16,128]{2,1,0:T(8,128)(2,1)}, bf16[4,16,128]{2,1,0:T(8,128)(2,1)S(1)}, u32[]{:S(2)}, u32[]{:S(2)}) collective-permute-start(bf16[4,16,128]{2,1,0:T(8,128)(2,1)} %own_ref.1), channel_id=1, source_target_pairs={{0,1},{1,0},{2,3},{3,2},{4,5},{5,4},{6,7},{7,6},{8,9},{9,8},{10,11... | collective-permute-start | bytes 49160 | tf_op jit(solution)/shard_map/ppermute | solution.py:547
  1.2 0.7 %copy-done.6 = f32[256]{0:T(256)S(1)} copy-done((f32[256]{0:T(256)S(1)}, f32[256]{0:T(256)}, u32[]{:S(2)}) %copy-start.6) | copy-done | bytes 1048
  1.8 0.0 copy-done.9
  1.8 0.0 copy-done.5
  1.9 0.0 copy-done.7
  1.9 0.9 %copy-done = bf16[1024,128]{1,0:T(8,128)(2,1)S(1)} copy-done((bf16[1024,128]{1,0:T(8,128)(2,1)S(1)}, bf16[1024,128]{1,0:T(8,128)(2,1)}, u32[]{:S(2)}) %copy-start) | copy-done | bytes 262168
  2.8 0.8 %copy-done.1 = bf16[32,4,256]{2,1,0:T(4,128)(2,1)S(1)} copy-done((bf16[32,4,256]{2,1,0:T(4,128)(2,1)S(1)}, bf16[32,4,256]{2,1,0:T(4,128)(2,1)}, u32[]{:S(2)}) %copy-start.1) | copy-done | bytes 65560
  3.7 0.7 %copy-done.2 = bf16[256,32]{0,1:T(8,128)(2,1)S(1)} copy-done((bf16[256,32]{0,1:T(8,128)(2,1)S(1)}, bf16[256,32]{0,1:T(8,128)(2,1)}, u32[]{:S(2)}) %copy-start.2) | copy-done | bytes 16408
  4.4 0.7 %copy-done.3 = bf16[256,32]{0,1:T(8,128)(2,1)S(1)} copy-done((bf16[256,32]{0,1:T(8,128)(2,1)S(1)}, bf16[256,32]{0,1:T(8,128)(2,1)}, u32[]{:S(2)}) %copy-start.3) | copy-done | bytes 16408
  5.1 1.0 %project.1 = (bf16[32,128]{1,0:T(8,128)(2,1)S(1)}, bf16[32,128]{1,0:T(8,128)(2,1)S(1)}, bf16[1024,128]{1,0:T(8,128)(2,1)S(1)}, f32[128,256]{1,0:T(8,128)S(1)}, f...) custom-call(bf16[32,4,256]{2,1,0:T(4,128)(2,1)S(1)} %copy-done.1, ...), custom_call_target="tpu_custom_call" | custom-call | tf_op jit(solution)/shard_map/project/pallas_call | solution.py:548
  6.1 0.0 collective-permute-done.other_ref
  6.1 1.1 %cotangent.1 = (bf16[5,32,128]{2,1,0:T(8,128)(2,1)S(1)}, f32[4,32,128]{2,1,0:T(8,128)S(1)}, bf16[1024,128]{1,0:T(8,128)(2,1)S(1)}) custom-call(bf16[4,16,128]{2,1,0:T(8,128)(2,1)S(1)} %copy-done.4, bf16[4,16,128]{2,1,0:T(8,128)(2,1)S(1)} %collective-permute-done.other_ref, bf16[1024,128]{1,0:T(8,128)(2,1)S(1)} %get-tuple-element.14.sorted_w_ref, ...), custom_call_target="tpu_custom_call" | custom-call | tf_op jit(solution)/shard_map/cotangent/pallas_call | solution.py:587
  7.3 2.6 %collective-permute-start.1 = (bf16[5,32,128]{2,1,0:T(8,128)(2,1)S(1)}, bf16[5,32,128]{2,1,0:T(8,128)(2,1)S(1)}, u32[]{:S(2)}, u32[]{:S(2)}) collective-permute-start(bf16[5,32,128]{2,1,0:T(8,128)(2,1)S(1)} %get-tuple-element.16), channel_id=1, source_target_pairs={{0,2},{2,0},{4,6},{6,4},{8,10},{10,8},{12,14},{14,12},{1,3},{3,1},... | collective-permute-start | bytes 122888 | tf_op jit(solution)/shard_map/ppermute | solution.py:602
  9.8 2.2 %collective-permute-done.1.beside_ref = bf16[5,32,128]{2,1,0:T(8,128)(2,1)S(1)} collective-permute-done((bf16[5,32,128]{2,1,0:T(8,128)(2,1)S(1)}, bf16[5,32,128]{2,1,0:T(8,128)(2,1)S(1)}, u32[]{:S(2)}, u32[]{:S(2)}) %collective-permute-start.1) | collective-permute-done | bytes 40992 | tf_op jit(solution)/shard_map/ppermute | solution.py:602
  12.1 1.9 %collective-permute-start.2 = (bf16[3,32,128]{2,1,0:T(8,128)(2,1)S(1)}, bf16[3,32,128]{2,1,0:T(8,128)(2,1)S(1)}, u32[]{:S(2)}, u32[]{:S(2)}) collective-permute-start(bf16[3,32,128]{2,1,0:T(8,128)(2,1)S(1)} %get-tuple-element.31), channel_id=1, source_target_pairs={{0,4},{2,6},{4,0},{6,2},{8,12},{10,14},{12,8},{14,10},{1,5},{3,7},... | collective-permute-start | bytes 73736 | tf_op jit(solution)/shard_map/ppermute | solution.py:602
  14.0 2.6 %collective-permute-start.3 = (bf16[3,32,128]{2,1,0:T(8,128)(2,1)S(1)}, bf16[3,32,128]{2,1,0:T(8,128)(2,1)S(1)}, u32[]{:S(2)}, u32[]{:S(2)}) collective-permute-start(bf16[3,32,128]{2,1,0:T(8,128)(2,1)S(1)} %get-tuple-element.30), channel_id=1, source_target_pairs={{0,8},{2,10},{4,12},{6,14},{8,0},{10,2},{12,4},{14,6},{1,9},{3,11}... | collective-permute-start | bytes 73736 | tf_op jit(solution)/shard_map/ppermute | solution.py:602
  16.6 0.0 collective-permute-start.4
  16.6 0.0 collective-permute-done.2.far_refs_0_
  16.6 2.2 %collective-permute-done.3.far_refs_1_ = bf16[3,32,128]{2,1,0:T(8,128)(2,1)S(1)} collective-permute-done((bf16[3,32,128]{2,1,0:T(8,128)(2,1)S(1)}, bf16[3,32,128]{2,1,0:T(8,128)(2,1)S(1)}, u32[]{:S(2)}, u32[]{:S(2)}) %collective-permute-start.3) | collective-permute-done | bytes 24608 | tf_op jit(solution)/shard_map/ppermute | solution.py:602
  18.8 3.4 %collective-permute-done.4.far_refs_2_ = bf16[3,32,128]{2,1,0:T(8,128)(2,1)S(1)} collective-permute-done((bf16[3,32,128]{2,1,0:T(8,128)(2,1)S(1)}, bf16[3,32,128]{2,1,0:T(8,128)(2,1)S(1)}, u32[]{:S(2)}, u32[]{:S(2)}) %collective-permute-start.4) | collective-permute-done | bytes 24608 | tf_op jit(solution)/shard_map/ppermute | solution.py:602
  22.3 0.1 collective-permute-start.5
  22.3 1.2 %gradient.1 = bf16[32,4,256]{2,1,0:T(4,128)(2,1)} custom-call(bf16[8,32,128]{2,1,0:T(8,128)(2,1)S(1)} %slice_dynamic-update-slice_fusion.right_ref, bf16[1024,128]{1,0:T(8,128)(2,1)S(1)} %get-tuple-element.19.outer_ref, f32[4,32,128]{2,1,0:T(8,128)S(1)} %get-tuple-element.17.keep_ref, bf16[5,32,128]{2,1,0:T(8,128)(2,1)S(1)} %collective-permute-done.1.beside_ref, ...), custom_call_target="tpu_custom_call" | custom-call | tf_op jit(solution)/shard_map/gradient/pallas_call | solution.py:620
  23.5 0.1 collective-permute-done.5.far_ref
  23.6 1.3 %pair.1 = bf16[4,16,128]{2,1,0:T(8,128)(2,1)} custom-call(bf16[8,32,128]{2,1,0:T(8,128)(2,1)S(1)} %slice_dynamic-update-slice_fusion.right_ref, bf16[5,32,128]{2,1,0:T(8,128)(2,1)S(1)} %collective-permute-done.5.far_ref, bf16[32,128]{1,0:T(8,128)(2,1)S(1)} %get-tuple-element.15.left_ref, bf16[1024,128]{1,0:T(8,128)(2,1)S(1)} %get-tuple-element.14.sorted_w_ref, ...), custom_call_target="tpu_custom_call" | custom-call | tf_op jit(solution)/shard_map/pair/pallas_call | solution.py:629
  (21 shorter events, 0.1 us)
Async XLA Ops:
  0.6 5.5 %collective-permute-start = (bf16[4,16,128]{2,1,0:T(8,128)(2,1)}, bf16[4,16,128]{2,1,0:T(8,128)(2,1)S(1)}, u32[]{:S(2)}, u32[]{:S(2)}) collective-permute-start(bf16[4,16,128]{2,1,0:T(8,128)(2,1)} %own_ref.1), channel_id=1, source_target_pairs={{0,1},{1,0},{2,3},{3,2},{4,5},{5,4},{6,7},{7,6},{8,9},{9,8},{10,11... | collective-permute-start | bytes 49160 | tf_op jit(solution)/shard_map/ppermute | solution.py:547
  1.2 0.7 %copy-start.6 = (f32[256]{0:T(256)S(1)}, f32[256]{0:T(256)}, u32[]{:S(2)}) copy-start(f32[256]{0:T(256)} %param.12) | copy-start | bytes 3076
  1.2 0.7 %copy-start.8 = (f32[32]{0:T(128)S(1)}, f32[32]{0:T(128)}, u32[]{:S(2)}) copy-start(f32[32]{0:T(128)} %param.16) | copy-start | bytes 388
  1.2 0.7 %copy-start.9 = (f32[128]{0:T(128)S(1)}, f32[128]{0:T(128)}, u32[]{:S(2)}) copy-start(f32[128]{0:T(128)} %param.18) | copy-start | bytes 1540
  1.2 0.7 %copy-start.5 = (f32[256]{0:T(256)S(1)}, f32[256]{0:T(256)}, u32[]{:S(2)}) copy-start(f32[256]{0:T(256)} %param.11) | copy-start | bytes 3076
  1.2 0.7 %copy-start.7 = (f32[32]{0:T(128)S(1)}, f32[32]{0:T(128)}, u32[]{:S(2)}) copy-start(f32[32]{0:T(128)} %param.14) | copy-start | bytes 388
  1.9 1.0 %copy-start = (bf16[1024,128]{1,0:T(8,128)(2,1)S(1)}, bf16[1024,128]{1,0:T(8,128)(2,1)}, u32[]{:S(2)}) copy-start(bf16[1024,128]{1,0:T(8,128)(2,1)} %w_hbm.1) | copy-start | bytes 786436
  2.8 0.8 %copy-start.1 = (bf16[32,4,256]{2,1,0:T(4,128)(2,1)S(1)}, bf16[32,4,256]{2,1,0:T(4,128)(2,1)}, u32[]{:S(2)}) copy-start(bf16[32,4,256]{2,1,0:T(4,128)(2,1)} %x_hbm.1) | copy-start | bytes 196612
  3.7 0.7 %copy-start.2 = (bf16[256,32]{0,1:T(8,128)(2,1)S(1)}, bf16[256,32]{0,1:T(8,128)(2,1)}, u32[]{:S(2)}) copy-start(bf16[256,32]{0,1:T(8,128)(2,1)} %param.13) | copy-start | bytes 49156
  4.4 0.7 %copy-start.3 = (bf16[256,32]{0,1:T(8,128)(2,1)S(1)}, bf16[256,32]{0,1:T(8,128)(2,1)}, u32[]{:S(2)}) copy-start(bf16[256,32]{0,1:T(8,128)(2,1)} %param.15) | copy-start | bytes 49156
  5.1 1.0 %copy-start.4 = (bf16[4,16,128]{2,1,0:T(8,128)(2,1)S(1)}, bf16[4,16,128]{2,1,0:T(8,128)(2,1)}, u32[]{:S(2)}) copy-start(bf16[4,16,128]{2,1,0:T(8,128)(2,1)} %own_ref.1) | copy-start | bytes 49156
  7.3 4.8 %collective-permute-start.1 = (bf16[5,32,128]{2,1,0:T(8,128)(2,1)S(1)}, bf16[5,32,128]{2,1,0:T(8,128)(2,1)S(1)}, u32[]{:S(2)}, u32[]{:S(2)}) collective-permute-start(bf16[5,32,128]{2,1,0:T(8,128)(2,1)S(1)} %get-tuple-element.16), channel_id=1, source_target_pairs={{0,2},{2,0},{4,6},{6,4},{8,10},{10,8},{12,14},{14,12},{1,3},{3,1},... | collective-permute-start | bytes 122888 | tf_op jit(solution)/shard_map/ppermute | solution.py:602
  12.1 4.5 %collective-permute-start.2 = (bf16[3,32,128]{2,1,0:T(8,128)(2,1)S(1)}, bf16[3,32,128]{2,1,0:T(8,128)(2,1)S(1)}, u32[]{:S(2)}, u32[]{:S(2)}) collective-permute-start(bf16[3,32,128]{2,1,0:T(8,128)(2,1)S(1)} %get-tuple-element.31), channel_id=1, source_target_pairs={{0,4},{2,6},{4,0},{6,2},{8,12},{10,14},{12,8},{14,10},{1,5},{3,7},... | collective-permute-start | bytes 73736 | tf_op jit(solution)/shard_map/ppermute | solution.py:602
  14.0 4.8 %collective-permute-start.3 = (bf16[3,32,128]{2,1,0:T(8,128)(2,1)S(1)}, bf16[3,32,128]{2,1,0:T(8,128)(2,1)S(1)}, u32[]{:S(2)}, u32[]{:S(2)}) collective-permute-start(bf16[3,32,128]{2,1,0:T(8,128)(2,1)S(1)} %get-tuple-element.30), channel_id=1, source_target_pairs={{0,8},{2,10},{4,12},{6,14},{8,0},{10,2},{12,4},{14,6},{1,9},{3,11}... | collective-permute-start | bytes 73736 | tf_op jit(solution)/shard_map/ppermute | solution.py:602
  16.6 5.6 %collective-permute-start.4 = (bf16[3,32,128]{2,1,0:T(8,128)(2,1)S(1)}, bf16[3,32,128]{2,1,0:T(8,128)(2,1)S(1)}, u32[]{:S(2)}, u32[]{:S(2)}) collective-permute-start(bf16[3,32,128]{2,1,0:T(8,128)(2,1)S(1)} %get-tuple-element.29), channel_id=1, source_target_pairs={{0,12},{2,14},{4,8},{6,10},{8,4},{10,6},{12,0},{14,2},{1,13},{3,15... | collective-permute-start | bytes 73736 | tf_op jit(solution)/shard_map/ppermute | solution.py:602
  22.3 1.3 %collective-permute-start.5 = (bf16[5,32,128]{2,1,0:T(8,128)(2,1)S(1)}, bf16[5,32,128]{2,1,0:T(8,128)(2,1)S(1)}, u32[]{:S(2)}, u32[]{:S(2)}) collective-permute-start(bf16[5,32,128]{2,1,0:T(8,128)(2,1)S(1)} %pad_maximum_fusion), channel_id=1, source_target_pairs={{0,1},{1,0},{2,3},{3,2},{4,5},{5,4},{6,7},{7,6},{8,9},{9,8},{10,11... | collective-permute-start | bytes 122888 | tf_op jit(solution)/shard_map/ppermute | solution.py:618

commit v6 on v5

--- a/solution.py
+++ b/solution.py
@@ -422,18 +422,18 @@
     for place in range(2 * columns // residues):
         piece = partial[:, place * LANES : (place + 1) * LANES]
         distance = lax.bitwise_xor(rank, place)
-        spot = lax.shift_right_logical(distance, 1)
-
-        @pl.when(distance & 1 == 1)
+        spot = distance & 3
+
+        @pl.when(distance >= 4)
         def _():
             send_ref[spot + 1] = piece.astype(BF16)
 
-        @pl.when(distance & 1 == 0)
+        @pl.when(distance < 4)
         def _():
             keep_ref[spot] = piece
 
 
-def small_grad_kernel(right_ref, outer_ref, keep_ref, beside_ref, far_refs, normed_ref, inv_std_ref,
+def small_grad_kernel(right_ref, outer_ref, keep_ref, far_ref, near_refs, normed_ref, inv_std_ref,
                       gain_ref, spread_w_ref, grad_ref):
     ranks, seqs, _ = right_ref.shape
     residues = grad_ref.shape[1]
@@ -443,9 +443,9 @@
         [right_ref[lax.bitwise_xor(rank, place)] for place in range(ranks)], axis=1
     )
     left_cot = jnp.dot(right_all, outer_ref[...], preferred_element_type=F32)
-    right_cot = keep_ref[0] + beside_ref[1].astype(F32)
-    for far_ref in far_refs:
-        right_cot = right_cot + far_ref[2].astype(F32)
+    right_cot = keep_ref[0] + far_ref[1].astype(F32)
+    for near_ref in near_refs:
+        right_cot = right_cot + near_ref[2].astype(F32)
     blocks = lane_block((seqs, LANES), depth)
     spread = jnp.concatenate(
         [
@@ -573,15 +573,20 @@
         compiler_params=limit,
         name="project",
     )(
-        homolog_matrix,
-        standardizer_scaling.reshape(1, -1),
-        standardizer_offset.reshape(1, -1),
-        left_projection_matrix.T,
-        left_offset_vector.reshape(1, -1),
-        right_projection_matrix.T,
-        right_offset_vector.reshape(1, -1),
-        coupling_matrix,
-        coupling_offset.reshape(1, -1),
+        *[
+            pltpu.with_memory_space_constraint(array, pltpu.HBM)
+            for array in (
+                homolog_matrix,
+                standardizer_scaling.reshape(1, -1),
+                standardizer_offset.reshape(1, -1),
+                left_projection_matrix.T,
+                left_offset_vector.reshape(1, -1),
+                right_projection_matrix.T,
+                right_offset_vector.reshape(1, -1),
+                coupling_matrix,
+                coupling_offset.reshape(1, -1),
+            )
+        ]
     )
 
     send, keep, outer = pl.pallas_call(
@@ -602,15 +607,19 @@
         return lax.ppermute(value, "res", [(source, source ^ mask) for source in range(ranks)])
 
     own = right[None]
-    beside = swap_over(1, send)
-    both = jnp.concatenate([own, beside[0:1]])
-    far_parts = {}
-    for mask in (6, 4, 2):
-        spot = mask // 2
-        summed = (keep[spot] + beside[1 + spot].astype(F32)).astype(BF16)
-        far_parts[mask] = swap_over(mask, jnp.concatenate([both, summed[None]]))
-    far_parts = [far_parts[mask] for mask in (2, 4, 6)]
-    gathered = jnp.concatenate([both] + [part[0:2] for part in far_parts])
+    beyond_two = swap_over(4, send)
+    both = jnp.concatenate([own, beyond_two[0:1]])
+    near_parts = {}
+    gathered = jnp.concatenate(
+        [own, jnp.zeros((3, seqs, LANES), BF16), beyond_two[0:1], jnp.zeros((3, seqs, LANES), BF16)]
+    )
+    for mask in (3, 2, 1):
+        summed = (keep[mask] + beyond_two[1 + mask].astype(F32)).astype(BF16)
+        part = swap_over(mask, jnp.concatenate([both, summed[None]]))
+        near_parts[mask] = part
+        gathered = lax.dynamic_update_slice_in_dim(gathered, part[0:1], mask, 0)
+        gathered = lax.dynamic_update_slice_in_dim(gathered, part[1:2], 4 + mask, 0)
+    near_parts = [near_parts[mask] for mask in (1, 2, 3)]
 
     half = gathered.reshape(2, ranks // 2, seqs, LANES)
     beyond = 1 - lax.bitwise_xor(lax.shift_right_logical(rank, 2), mine)
@@ -624,7 +633,7 @@
         out_shape=like(homolog_matrix.shape, BF16),
         compiler_params=limit,
         name="gradient",
-    )(gathered, outer, keep, beside, far_parts, normed, inv_std, gain, spread_w)
+    )(gathered, outer, keep, beyond_two, near_parts, normed, inv_std, gain, spread_w)
 
     pair_delta = pl.pallas_call(
         functools.partial(small_pair_kernel, scale),

time: 25.2 us -> 19.7 us (0.78)
  local copies, waits for them, and re-layouts: 3.98 us -> 0.06 us
  waiting for transfers between devices: 7.88 us -> 5.63 us
  Pallas kernels: 4.58 us -> 5.28 us
    unnamed x23 -> x2, local copies, waits for them, and re-layouts: 3.96 us -> 0.01 us
    ppermute x4, waiting for transfers between devices: 7.83 us -> 5.57 us  [swap_over(): lax.ppermute(value, 'res', [(source, source ^ mask) for source in range(r...]
    pallas_call x1, Pallas kernels: 0.97 us -> 1.68 us  [small_slice(): pl.pallas_call(small_project_kernel, in_specs=[pl.BlockSpec(memory_space=...]
  transfers between devices with their start and end apart: 6 -> 6, of which waited for: 4 -> 5; matrix products, arithmetic and copies ran while one was open for 0% -> 0% of each run, Pallas kernels for 9% -> 14%
where the time goes in v6:
time: 19.7 us; the launch traced here: 19.6 us
  starting transfers between devices  7.88 us (40%)
  waiting for transfers between devices  5.63 us (29%)
  Pallas kernels  5.28 us (27%)
  between operations  0.7 us (4%)
    ppermute x4, starting transfers between devices, swap_over(): lax.ppermute(value, 'res', [(source, source ^ mask) for source in range(r...  7.29 us
    ppermute x4, waiting for transfers between devices, swap_over(): lax.ppermute(value, 'res', [(source, source ^ mask) for source in range(r...  5.57 us
    pallas_call x1, Pallas kernels, small_slice(): pl.pallas_call(small_project_kernel, in_specs=[pl.BlockSpec(memory_space=...  1.68 us
    pallas_call x1, Pallas kernels, small_slice(): pl.pallas_call(functools.partial(small_pair_kernel, scale), in_specs=[vme...  1.31 us
    pallas_call x1, Pallas kernels, small_slice(): pl.pallas_call(small_grad_kernel, in_specs=[vmem] * 4 + [[vmem] * 3] + [v...  1.15 us
    pallas_call x1, Pallas kernels, small_slice(): pl.pallas_call(functools.partial(small_cot_kernel, scale), in_specs=[vmem...  1.13 us
    ppermute x1, starting transfers between devices, small_slice(): other_cot = lax.ppermute(coupling_cotangent, 'seq', swap)  0.52 us
  transfers between devices with their start and end apart: 6, of which 5 were waited for; matrix products, arithmetic and copies ran while one was open for 0% of the time, Pallas kernels for 14%

profile of v6, /device:TPU:0, one launch (start us, length us, event | category | flops | bytes accessed | tf_op | source)
XLA Modules:
  0.0 19.6 jit_solution(6227162747320292278)
XLA Ops:
  0.6 0.5 %collective-permute-start = (bf16[4,16,128]{2,1,0:T(8,128)(2,1)}, bf16[4,16,128]{2,1,0:T(8,128)(2,1)S(1)}, u32[]{:S(2)}, u32[]{:S(2)}) collective-permute-start(bf16[4,16,128]{2,1,0:T(8,128)(2,1)} %own_ref.1), channel_id=1, source_target_pairs={{0,1},{1,0},{2,3},{3,2},{4,5},{5,4},{6,7},{7,6},{8,9},{9,8},{10,11... | collective-permute-start | bytes 49160 | tf_op jit(solution)/shard_map/ppermute | solution.py:547
  1.2 0.0 copy-start
  1.2 1.7 %project.1 = (bf16[32,128]{1,0:T(8,128)(2,1)S(1)}, bf16[32,128]{1,0:T(8,128)(2,1)S(1)}, bf16[1024,128]{1,0:T(8,128)(2,1)S(1)}, f32[128,256]{1,0:T(8,128)S(1)}, f...) custom-call(bf16[32,4,256]{2,1,0:T(4,128)(2,1)} %x_hbm.1, ...), custom_call_target="tpu_custom_call" | custom-call | tf_op jit(solution)/shard_map/project/pallas_call | solution.py:548
  2.8 0.0 collective-permute-done.other_ref
  2.9 0.0 copy-done
  2.9 1.1 %cotangent.1 = (bf16[5,32,128]{2,1,0:T(8,128)(2,1)S(1)}, f32[4,32,128]{2,1,0:T(8,128)S(1)}, bf16[1024,128]{1,0:T(8,128)(2,1)S(1)}) custom-call(bf16[4,16,128]{2,1,0:T(8,128)(2,1)S(1)} %copy-done, bf16[4,16,128]{2,1,0:T(8,128)(2,1)S(1)} %collective-permute-done.other_ref, bf16[1024,128]{1,0:T(8,128)(2,1)S(1)} %get-tuple-element.14.sorted_w_ref, ...), custom_call_target="tpu_custom_call" | custom-call | tf_op jit(solution)/shard_map/cotangent/pallas_call | solution.py:592
  4.0 3.7 %collective-permute-start.1 = (bf16[5,32,128]{2,1,0:T(8,128)(2,1)S(1)}, bf16[5,32,128]{2,1,0:T(8,128)(2,1)S(1)}, u32[]{:S(2)}, u32[]{:S(2)}) collective-permute-start(bf16[5,32,128]{2,1,0:T(8,128)(2,1)S(1)} %get-tuple-element.16), channel_id=1, source_target_pairs={{0,8},{2,10},{4,12},{6,14},{8,0},{10,2},{12,4},{14,6},{1,9},{3,11}... | collective-permute-start | bytes 122888 | tf_op jit(solution)/shard_map/ppermute | solution.py:607
  7.7 2.2 %collective-permute-done.1.far_ref = bf16[5,32,128]{2,1,0:T(8,128)(2,1)S(1)} collective-permute-done((bf16[5,32,128]{2,1,0:T(8,128)(2,1)S(1)}, bf16[5,32,128]{2,1,0:T(8,128)(2,1)S(1)}, u32[]{:S(2)}, u32[]{:S(2)}) %collective-permute-start.1) | collective-permute-done | bytes 40992 | tf_op jit(solution)/shard_map/ppermute | solution.py:607
  9.9 2.7 %collective-permute-start.2 = (bf16[3,32,128]{2,1,0:T(8,128)(2,1)S(1)}, bf16[3,32,128]{2,1,0:T(8,128)(2,1)S(1)}, u32[]{:S(2)}, u32[]{:S(2)}) collective-permute-start(bf16[3,32,128]{2,1,0:T(8,128)(2,1)S(1)} %get-tuple-element.29), channel_id=1, source_target_pairs={{0,6},{2,4},{4,2},{6,0},{8,14},{10,12},{12,10},{14,8},{1,7},{3,5},... | collective-permute-start | bytes 73736 | tf_op jit(solution)/shard_map/ppermute | solution.py:607
  12.6 0.5 %collective-permute-start.3 = (bf16[3,32,128]{2,1,0:T(8,128)(2,1)S(1)}, bf16[3,32,128]{2,1,0:T(8,128)(2,1)S(1)}, u32[]{:S(2)}, u32[]{:S(2)}) collective-permute-start(bf16[3,32,128]{2,1,0:T(8,128)(2,1)S(1)} %get-tuple-element.28), channel_id=1, source_target_pairs={{0,4},{2,6},{4,0},{6,2},{8,12},{10,14},{12,8},{14,10},{1,5},{3,7},... | collective-permute-start | bytes 73736 | tf_op jit(solution)/shard_map/ppermute | solution.py:607
  13.1 0.5 %collective-permute-start.4 = (bf16[3,32,128]{2,1,0:T(8,128)(2,1)S(1)}, bf16[3,32,128]{2,1,0:T(8,128)(2,1)S(1)}, u32[]{:S(2)}, u32[]{:S(2)}) collective-permute-start(bf16[3,32,128]{2,1,0:T(8,128)(2,1)S(1)} %get-tuple-element.27), channel_id=1, source_target_pairs={{0,2},{2,0},{4,6},{6,4},{8,10},{10,8},{12,14},{14,12},{1,3},{3,1},... | collective-permute-start | bytes 73736 | tf_op jit(solution)/shard_map/ppermute | solution.py:607
  13.6 1.2 %collective-permute-done.2.near_refs_2_ = bf16[3,32,128]{2,1,0:T(8,128)(2,1)S(1)} collective-permute-done((bf16[3,32,128]{2,1,0:T(8,128)(2,1)S(1)}, bf16[3,32,128]{2,1,0:T(8,128)(2,1)S(1)}, u32[]{:S(2)}, u32[]{:S(2)}) %collective-permute-start.2) | collective-permute-done | bytes 24608 | tf_op jit(solution)/shard_map/ppermute | solution.py:607
  14.7 1.8 %collective-permute-done.3.near_refs_1_ = bf16[3,32,128]{2,1,0:T(8,128)(2,1)S(1)} collective-permute-done((bf16[3,32,128]{2,1,0:T(8,128)(2,1)S(1)}, bf16[3,32,128]{2,1,0:T(8,128)(2,1)S(1)}, u32[]{:S(2)}, u32[]{:S(2)}) %collective-permute-start.3) | collective-permute-done | bytes 24608 | tf_op jit(solution)/shard_map/ppermute | solution.py:607
  16.5 0.4 %collective-permute-done.4.near_refs_0_ = bf16[3,32,128]{2,1,0:T(8,128)(2,1)S(1)} collective-permute-done((bf16[3,32,128]{2,1,0:T(8,128)(2,1)S(1)}, bf16[3,32,128]{2,1,0:T(8,128)(2,1)S(1)}, u32[]{:S(2)}, u32[]{:S(2)}) %collective-permute-start.4) | collective-permute-done | bytes 24608 | tf_op jit(solution)/shard_map/ppermute | solution.py:607
  17.0 0.1 collective-permute-start.5
  17.1 1.2 %gradient.1 = bf16[32,4,256]{2,1,0:T(4,128)(2,1)} custom-call(bf16[8,32,128]{2,1,0:T(8,128)(2,1)S(1)} %slice_dynamic-update-slice_fusion.right_ref, bf16[1024,128]{1,0:T(8,128)(2,1)S(1)} %get-tuple-element.19.outer_ref, f32[4,32,128]{2,1,0:T(8,128)S(1)} %get-tuple-element.17.keep_ref, bf16[5,32,128]{2,1,0:T(8,128)(2,1)S(1)} %collective-permute-done.1.far_ref, ...), custom_call_target="tpu_custom_call" | custom-call | tf_op jit(solution)/shard_map/gradient/pallas_call | solution.py:629
  18.2 0.1 collective-permute-done.5.far_ref
  18.3 1.3 %pair.1 = bf16[4,16,128]{2,1,0:T(8,128)(2,1)} custom-call(bf16[8,32,128]{2,1,0:T(8,128)(2,1)S(1)} %slice_dynamic-update-slice_fusion.right_ref, bf16[5,32,128]{2,1,0:T(8,128)(2,1)S(1)} %collective-permute-done.5.far_ref, bf16[32,128]{1,0:T(8,128)(2,1)S(1)} %get-tuple-element.15.left_ref, bf16[1024,128]{1,0:T(8,128)(2,1)S(1)} %get-tuple-element.14.sorted_w_ref, ...), custom_call_target="tpu_custom_call" | custom-call | tf_op jit(solution)/shard_map/pair/pallas_call | solution.py:638
  (13 shorter events, 0.1 us)
Async XLA Ops:
  0.6 2.2 %collective-permute-start = (bf16[4,16,128]{2,1,0:T(8,128)(2,1)}, bf16[4,16,128]{2,1,0:T(8,128)(2,1)S(1)}, u32[]{:S(2)}, u32[]{:S(2)}) collective-permute-start(bf16[4,16,128]{2,1,0:T(8,128)(2,1)} %own_ref.1), channel_id=1, source_target_pairs={{0,1},{1,0},{2,3},{3,2},{4,5},{5,4},{6,7},{7,6},{8,9},{9,8},{10,11... | collective-permute-start | bytes 49160 | tf_op jit(solution)/shard_map/ppermute | solution.py:547
  1.2 1.7 %copy-start = (bf16[4,16,128]{2,1,0:T(8,128)(2,1)S(1)}, bf16[4,16,128]{2,1,0:T(8,128)(2,1)}, u32[]{:S(2)}) copy-start(bf16[4,16,128]{2,1,0:T(8,128)(2,1)} %own_ref.1) | copy-start | bytes 49156
  4.0 5.9 %collective-permute-start.1 = (bf16[5,32,128]{2,1,0:T(8,128)(2,1)S(1)}, bf16[5,32,128]{2,1,0:T(8,128)(2,1)S(1)}, u32[]{:S(2)}, u32[]{:S(2)}) collective-permute-start(bf16[5,32,128]{2,1,0:T(8,128)(2,1)S(1)} %get-tuple-element.16), channel_id=1, source_target_pairs={{0,8},{2,10},{4,12},{6,14},{8,0},{10,2},{12,4},{14,6},{1,9},{3,11}... | collective-permute-start | bytes 122888 | tf_op jit(solution)/shard_map/ppermute | solution.py:607
  9.9 4.8 %collective-permute-start.2 = (bf16[3,32,128]{2,1,0:T(8,128)(2,1)S(1)}, bf16[3,32,128]{2,1,0:T(8,128)(2,1)S(1)}, u32[]{:S(2)}, u32[]{:S(2)}) collective-permute-start(bf16[3,32,128]{2,1,0:T(8,128)(2,1)S(1)} %get-tuple-element.29), channel_id=1, source_target_pairs={{0,6},{2,4},{4,2},{6,0},{8,14},{10,12},{12,10},{14,8},{1,7},{3,5},... | collective-permute-start | bytes 73736 | tf_op jit(solution)/shard_map/ppermute | solution.py:607
  12.6 3.9 %collective-permute-start.3 = (bf16[3,32,128]{2,1,0:T(8,128)(2,1)S(1)}, bf16[3,32,128]{2,1,0:T(8,128)(2,1)S(1)}, u32[]{:S(2)}, u32[]{:S(2)}) collective-permute-start(bf16[3,32,128]{2,1,0:T(8,128)(2,1)S(1)} %get-tuple-element.28), channel_id=1, source_target_pairs={{0,4},{2,6},{4,0},{6,2},{8,12},{10,14},{12,8},{14,10},{1,5},{3,7},... | collective-permute-start | bytes 73736 | tf_op jit(solution)/shard_map/ppermute | solution.py:607
  13.1 3.8 %collective-permute-start.4 = (bf16[3,32,128]{2,1,0:T(8,128)(2,1)S(1)}, bf16[3,32,128]{2,1,0:T(8,128)(2,1)S(1)}, u32[]{:S(2)}, u32[]{:S(2)}) collective-permute-start(bf16[3,32,128]{2,1,0:T(8,128)(2,1)S(1)} %get-tuple-element.27), channel_id=1, source_target_pairs={{0,2},{2,0},{4,6},{6,4},{8,10},{10,8},{12,14},{14,12},{1,3},{3,1},... | collective-permute-start | bytes 73736 | tf_op jit(solution)/shard_map/ppermute | solution.py:607
  17.0 1.3 %collective-permute-start.5 = (bf16[5,32,128]{2,1,0:T(8,128)(2,1)S(1)}, bf16[5,32,128]{2,1,0:T(8,128)(2,1)S(1)}, u32[]{:S(2)}, u32[]{:S(2)}) collective-permute-start(bf16[5,32,128]{2,1,0:T(8,128)(2,1)S(1)} %pad_maximum_fusion.1), channel_id=1, source_target_pairs={{0,1},{1,0},{2,3},{3,2},{4,5},{5,4},{6,7},{7,6},{8,9},{9,8},{10,11... | collective-permute-start | bytes 122888 | tf_op jit(solution)/shard_map/ppermute | solution.py:627

commit v7 on v6

--- a/solution.py
+++ b/solution.py
@@ -333,54 +333,53 @@
     return copy
 
 
-def small_project_kernel(
-    x_hbm, gain_hbm, offset_hbm, left_w_hbm, left_b_hbm, right_w_hbm, right_b_hbm, w_hbm, pair_offset_hbm,
-    left_ref, right_ref, sorted_w_ref, normed_ref, inv_std_ref, spread_w_ref, gain_out_ref,
-    pair_offset_out_ref,
-    x_ref, offset_ref, left_w_ref, left_b_ref, right_w_ref, right_b_ref, raw_ref, wide_ref, semaphores,
-):
+def start_copies(pairs, semaphores):
     copies = [
         pltpu.make_async_copy(source, target, semaphores.at[place])
-        for place, (source, target) in enumerate(
-            (
-                (x_hbm, x_ref),
-                (gain_hbm, gain_out_ref),
-                (offset_hbm, offset_ref),
-                (left_w_hbm, left_w_ref),
-                (left_b_hbm, left_b_ref),
-                (right_w_hbm, right_w_ref),
-                (right_b_hbm, right_b_ref),
-                (w_hbm, raw_ref),
-                (pair_offset_hbm, pair_offset_out_ref),
-            )
-        )
+        for place, (source, target) in enumerate(pairs)
     ]
     for copy in copies:
         copy.start()
+    return copies
+
+
+def small_project_kernel(
+    x_hbm, gain_hbm, offset_hbm, left_w_hbm, left_b_hbm, right_w_hbm, right_b_hbm, w_hbm,
+    left_ref, right_ref, sorted_w_ref,
+    x_ref, gain_ref, offset_ref, left_w_ref, left_b_ref, right_w_ref, right_b_ref, raw_ref, wide_ref,
+    semaphores,
+):
+    copies = start_copies(
+        (
+            (x_hbm, x_ref),
+            (gain_hbm, gain_ref),
+            (offset_hbm, offset_ref),
+            (left_w_hbm, left_w_ref),
+            (left_b_hbm, left_b_ref),
+            (right_w_hbm, right_w_ref),
+            (right_b_hbm, right_b_ref),
+            (w_hbm, raw_ref),
+        ),
+        semaphores,
+    )
     seqs, residues, _ = x_ref.shape
     depth = left_w_ref.shape[0]
     copies[0].wait()
-    normed, inv_std = normalise(residue_rows(x_ref))
-    normed_ref[...] = normed
-    inv_std_ref[...] = jnp.broadcast_to(inv_std, inv_std_ref.shape)
+    normed, _ = normalise(residue_rows(x_ref))
     for copy in copies[1:7]:
         copy.wait()
-    ln_out = (normed * gain_out_ref[...] + offset_ref[...]).astype(BF16)
+    ln_out = (normed * gain_ref[...] + offset_ref[...]).astype(BF16)
     blocks = lane_block((seqs, LANES), depth)
-    spread = []
     for weight_ref, bias_ref, out_ref in (
         (left_w_ref, left_b_ref, left_ref),
         (right_w_ref, right_b_ref, right_ref),
     ):
         weight = jnp.concatenate([weight_ref[...]] * residues, axis=0)
-        spread.append(weight)
         bias = jnp.concatenate([bias_ref[...]] * residues, axis=1)
         wide = lax.dot_general(ln_out, weight, NT, preferred_element_type=F32)
         own = pick(blocks, [wide[p * seqs : (p + 1) * seqs] for p in range(residues)])
         out_ref[...] = (own + bias).astype(BF16)
-    spread_w_ref[...] = jnp.concatenate(spread, axis=0)
-    for copy in copies[7:]:
-        copy.wait()
+    copies[7].wait()
     wide_ref[...] = raw_ref[...].astype(F32)
     for d in range(depth):
         sorted_w_ref[d * depth : (d + 1) * depth, :] = wide_ref[
@@ -388,61 +387,88 @@
         ].astype(BF16)
 
 
-def small_cot_kernel(scale, own_ref, other_ref, sorted_w_ref, left_ref, right_ref,
-                    send_ref, keep_ref, outer_ref, turn_ref):
+def half_pieces(scale, half, own_ref, other_ref, sorted_w_ref, left_ref, turn_ref):
     residues, columns, _ = own_ref.shape
     depth = LANES // residues
-    first = lax.axis_index("seq") == 0
     own = own_ref[...].reshape(residues * columns, LANES)
     other = other_ref[...].reshape(residues * columns, LANES)
-    both = jnp.concatenate([jnp.where(first, own, other), jnp.where(first, other, own)], axis=0)
-    flat = lax.dot_general(both, sorted_w_ref[...], NT, preferred_element_type=F32) * scale
+    cot = jnp.where(lax.axis_index("seq") == half, own, other)
+    flat = lax.dot_general(cot, sorted_w_ref[...], NT, preferred_element_type=F32) * scale
     blocks = lane_block((columns, LANES), depth)
-    for half in range(2):
-        for tile in range(depth * depth // LANES):
-            block = flat[
-                half * residues * columns : (half + 1) * residues * columns,
-                tile * LANES : (tile + 1) * LANES,
-            ]
-            turned = [block] + [pltpu.roll(block, depth * t, 1) for t in range(1, residues)]
-            for e in range(residues):
-                start = half * columns * depth + tile * residues + e
-                turn_ref[pl.ds(start, columns, stride=depth), :] = pick(
-                    blocks,
-                    [
-                        turned[(i - e) % residues][i * columns : (i + 1) * columns]
-                        for i in range(residues)
-                    ],
-                )
+    for tile in range(depth * depth // LANES):
+        block = flat[:, tile * LANES : (tile + 1) * LANES]
+        turned = [block] + [pltpu.roll(block, depth * t, 1) for t in range(1, residues)]
+        for e in range(residues):
+            turn_ref[pl.ds(tile * residues + e, columns, stride=depth), :] = pick(
+                blocks,
+                [
+                    turned[(i - e) % residues][i * columns : (i + 1) * columns]
+                    for i in range(residues)
+                ],
+            )
     outer = turn_ref[...].astype(BF16)
+    partial = lax.dot_general(left_ref[...], outer, NT, preferred_element_type=F32)
+    return outer, [
+        partial[:, place * LANES : (place + 1) * LANES] for place in range(columns // residues)
+    ]
+
+
+def small_far_kernel(scale, own_ref, other_ref, sorted_w_ref, left_ref, right_ref,
+                     send_ref, outer_ref, turn_ref):
+    rank = lax.axis_index("res")
+    half = 1 - lax.shift_right_logical(rank, 2)
+    outer, pieces = half_pieces(scale, half, own_ref, other_ref, sorted_w_ref, left_ref, turn_ref)
     outer_ref[...] = outer
-    partial = lax.dot_general(left_ref[...], outer, NT, preferred_element_type=F32)
+    send_ref[0] = right_ref[...]
+    for place, piece in enumerate(pieces):
+        send_ref[1 + lax.bitwise_xor(rank & 3, place)] = piece.astype(BF16)
+
+
+def small_near_kernel(
+    scale, x_hbm, gain_hbm, left_w_hbm, right_w_hbm, pair_offset_hbm,
+    own_ref, other_ref, sorted_w_ref, left_ref,
+    keep_ref, outer_ref, normed_ref, inv_std_ref, spread_w_ref, gain_ref, pair_offset_ref,
+    x_ref, left_w_ref, right_w_ref, turn_ref, semaphores,
+):
+    copies = start_copies(
+        (
+            (x_hbm, x_ref),
+            (gain_hbm, gain_ref),
+            (left_w_hbm, left_w_ref),
+            (right_w_hbm, right_w_ref),
+            (pair_offset_hbm, pair_offset_ref),
+        ),
+        semaphores,
+    )
+    residues = x_ref.shape[1]
     rank = lax.axis_index("res")
-    send_ref[0] = right_ref[...]
-    for place in range(2 * columns // residues):
-        piece = partial[:, place * LANES : (place + 1) * LANES]
-        distance = lax.bitwise_xor(rank, place)
-        spot = distance & 3
-
-        @pl.when(distance >= 4)
-        def _():
-            send_ref[spot + 1] = piece.astype(BF16)
-
-        @pl.when(distance < 4)
-        def _():
-            keep_ref[spot] = piece
-
-
-def small_grad_kernel(right_ref, outer_ref, keep_ref, far_ref, near_refs, normed_ref, inv_std_ref,
+    half = lax.shift_right_logical(rank, 2)
+    outer, pieces = half_pieces(scale, half, own_ref, other_ref, sorted_w_ref, left_ref, turn_ref)
+    outer_ref[...] = outer
+    for place, piece in enumerate(pieces):
+        keep_ref[lax.bitwise_xor(rank & 3, place)] = piece
+    for copy in copies:
+        copy.wait()
+    normed, inv_std = normalise(residue_rows(x_ref))
+    normed_ref[...] = normed
+    inv_std_ref[...] = jnp.broadcast_to(inv_std, inv_std_ref.shape)
+    spread_w_ref[...] = jnp.concatenate(
+        [left_w_ref[...]] * residues + [right_w_ref[...]] * residues, axis=0
+    )
+
+
+def small_grad_kernel(right_ref, outer_near_ref, outer_far_ref, keep_ref, far_ref, near_refs, normed_ref, inv_std_ref,
                       gain_ref, spread_w_ref, grad_ref):
     ranks, seqs, _ = right_ref.shape
     residues = grad_ref.shape[1]
     depth = LANES // residues
     rank = lax.axis_index("res")
+    places = [lax.bitwise_xor(rank & 3, place) for place in range(ranks // 2)]
     right_all = jnp.concatenate(
-        [right_ref[lax.bitwise_xor(rank, place)] for place in range(ranks)], axis=1
-    )
-    left_cot = jnp.dot(right_all, outer_ref[...], preferred_element_type=F32)
+        [right_ref[place] for place in places] + [right_ref[4 + place] for place in places], axis=1
+    )
+    outer = jnp.concatenate([outer_near_ref[...], outer_far_ref[...]], axis=0)
+    left_cot = jnp.dot(right_all, outer, preferred_element_type=F32)
     right_cot = keep_ref[0] + far_ref[1].astype(F32)
     for near_ref in near_refs:
         right_cot = right_cot + near_ref[2].astype(F32)
@@ -545,14 +571,67 @@
     like = jax.ShapeDtypeStruct
 
     other_cot = lax.ppermute(coupling_cotangent, "seq", swap)
-    left, right, sorted_w, normed, inv_std, spread_w, gain, pair_offset = pl.pallas_call(
+    hbm = pl.BlockSpec(memory_space=pltpu.HBM)
+    pin = lambda array: pltpu.with_memory_space_constraint(array, pltpu.HBM)
+    x = pin(homolog_matrix)
+    gain_row = pin(standardizer_scaling.reshape(1, -1))
+    left_w = pin(left_projection_matrix.T)
+    right_w = pin(right_projection_matrix.T)
+    left, right, sorted_w = pl.pallas_call(
         small_project_kernel,
-        in_specs=[pl.BlockSpec(memory_space=pltpu.HBM)] * 9,
-        out_specs=[vmem] * 8,
+        in_specs=[hbm] * 8,
+        out_specs=[vmem] * 3,
         out_shape=(
             like((seqs, LANES), BF16),
             like((seqs, LANES), BF16),
             like(coupling_matrix.shape, BF16),
+        ),
+        scratch_shapes=[
+            pltpu.VMEM(homolog_matrix.shape, BF16),
+            pltpu.VMEM((1, features), F32),
+            pltpu.VMEM((1, features), F32),
+            pltpu.VMEM((depth, features), BF16),
+            pltpu.VMEM((1, depth), F32),
+            pltpu.VMEM((depth, features), BF16),
+            pltpu.VMEM((1, depth), F32),
+            pltpu.VMEM(coupling_matrix.shape, BF16),
+            pltpu.VMEM(coupling_matrix.shape, F32),
+            pltpu.SemaphoreType.DMA((8,)),
+        ],
+        compiler_params=limit,
+        name="project",
+    )(
+        x,
+        gain_row,
+        pin(standardizer_offset.reshape(1, -1)),
+        left_w,
+        pin(left_offset_vector.reshape(1, -1)),
+        right_w,
+        pin(right_offset_vector.reshape(1, -1)),
+        pin(coupling_matrix),
+    )
+
+    half_rows = ranks // 2 * LANES
+    send, outer_far = pl.pallas_call(
+        functools.partial(small_far_kernel, scale),
+        in_specs=[vmem] * 5,
+        out_specs=[vmem] * 2,
+        out_shape=(
+            like((1 + ranks // 2, seqs, LANES), BF16),
+            like((half_rows, LANES), BF16),
+        ),
+        scratch_shapes=[pltpu.VMEM((half_rows, LANES), F32)],
+        compiler_params=limit,
+        name="far_pieces",
+    )(coupling_cotangent, other_cot, sorted_w, left, right)
+
+    keep, outer_near, normed, inv_std, spread_w, gain, pair_offset = pl.pallas_call(
+        functools.partial(small_near_kernel, scale),
+        in_specs=[hbm] * 5 + [vmem] * 4,
+        out_specs=[vmem] * 7,
+        out_shape=(
+            like((ranks // 2, seqs, LANES), F32),
+            like((half_rows, LANES), BF16),
             like((rows, features), F32),
             like((rows, LANES), F32),
             like((2 * LANES, features), BF16),
@@ -561,47 +640,24 @@
         ),
         scratch_shapes=[
             pltpu.VMEM(homolog_matrix.shape, BF16),
-            pltpu.VMEM((1, features), F32),
             pltpu.VMEM((depth, features), BF16),
-            pltpu.VMEM((1, depth), F32),
             pltpu.VMEM((depth, features), BF16),
-            pltpu.VMEM((1, depth), F32),
-            pltpu.VMEM(coupling_matrix.shape, BF16),
-            pltpu.VMEM(coupling_matrix.shape, F32),
-            pltpu.SemaphoreType.DMA((9,)),
+            pltpu.VMEM((half_rows, LANES), F32),
+            pltpu.SemaphoreType.DMA((5,)),
         ],
         compiler_params=limit,
-        name="project",
+        name="near_pieces",
     )(
-        *[
-            pltpu.with_memory_space_constraint(array, pltpu.HBM)
-            for array in (
-                homolog_matrix,
-                standardizer_scaling.reshape(1, -1),
-                standardizer_offset.reshape(1, -1),
-                left_projection_matrix.T,
-                left_offset_vector.reshape(1, -1),
-                right_projection_matrix.T,
-                right_offset_vector.reshape(1, -1),
-                coupling_matrix,
-                coupling_offset.reshape(1, -1),
-            )
-        ]
-    )
-
-    send, keep, outer = pl.pallas_call(
-        functools.partial(small_cot_kernel, scale),
-        in_specs=[vmem] * 5,
-        out_specs=[vmem] * 3,
-        out_shape=(
-            like((1 + ranks // 2, seqs, LANES), BF16),
-            like((ranks // 2, seqs, LANES), F32),
-            like((ranks * LANES, LANES), BF16),
-        ),
-        scratch_shapes=[pltpu.VMEM((ranks * LANES, LANES), F32)],
-        compiler_params=limit,
-        name="cotangent",
-    )(coupling_cotangent, other_cot, sorted_w, left, right)
+        x,
+        gain_row,
+        left_w,
+        right_w,
+        pin(coupling_offset.reshape(1, -1)),
+        coupling_cotangent,
+        other_cot,
+        sorted_w,
+        left,
+    )
 
     def swap_over(mask, value):
         return lax.ppermute(value, "res", [(source, source ^ mask) for source in range(ranks)])
@@ -628,12 +684,12 @@
 
     gradient = pl.pallas_call(
         small_grad_kernel,
-        in_specs=[vmem] * 4 + [[vmem] * 3] + [vmem] * 4,
+        in_specs=[vmem] * 5 + [[vmem] * 3] + [vmem] * 4,
         out_specs=vmem,
         out_shape=like(homolog_matrix.shape, BF16),
         compiler_params=limit,
         name="gradient",
-    )(gathered, outer, keep, beyond_two, near_parts, normed, inv_std, gain, spread_w)
+    )(gathered, outer_near, outer_far, keep, beyond_two, near_parts, normed, inv_std, gain, spread_w)
 
     pair_delta = pl.pallas_call(
         functools.partial(small_pair_kernel, scale),

time: 19.7 us -> 19.3 us (0.980)
  waiting for transfers between devices: 5.63 us -> 3.98 us
  Pallas kernels: 5.28 us -> 6.44 us
    ppermute x4, waiting for transfers between devices: 5.57 us -> 3.93 us  [swap_over(): lax.ppermute(value, 'res', [(source, source ^ mask) for source in range(r...]
    pallas_call x3 -> x4, Pallas kernels: 3.96 us -> 5.13 us  [the longest x1 1.67 us: small_slice(): pl.pallas_call(small_project_kernel, in_specs=[hbm] * 8, out_specs=[vmem]...]
  transfers between devices with their start and end apart: 6 -> 6, of which waited for: 5 -> 5; matrix products, arithmetic and copies ran while one was open for 0% -> 0% of each run, Pallas kernels for 14% -> 23%
where the time goes in v7:
time: 19.3 us; the launch traced here: 19.1 us
  starting transfers between devices  7.87 us (41%)
  Pallas kernels  6.44 us (33%)
  waiting for transfers between devices  3.98 us (21%)
  between operations  0.7 us (4%)
    ppermute x4, starting transfers between devices, swap_over(): lax.ppermute(value, 'res', [(source, source ^ mask) for source in range(r...  7.29 us
    ppermute x4, waiting for transfers between devices, swap_over(): lax.ppermute(value, 'res', [(source, source ^ mask) for source in range(r...  3.93 us
    pallas_call x1, Pallas kernels, small_slice(): pl.pallas_call(small_project_kernel, in_specs=[hbm] * 8, out_specs=[vmem]...  1.67 us
    pallas_call x1, Pallas kernels, small_slice(): pl.pallas_call(functools.partial(small_near_kernel, scale), in_specs=[hbm...  1.64 us
    pallas_call x1, Pallas kernels, small_slice(): pl.pallas_call(functools.partial(small_pair_kernel, scale), in_specs=[vme...  1.31 us
    pallas_call x1, Pallas kernels, small_slice(): pl.pallas_call(small_grad_kernel, in_specs=[vmem] * 5 + [[vmem] * 3] + [v...  1.15 us
    pallas_call x1, Pallas kernels, small_slice(): pl.pallas_call(functools.partial(small_far_kernel, scale), in_specs=[vmem...  0.67 us
    ppermute x1, starting transfers between devices, small_slice(): other_cot = lax.ppermute(coupling_cotangent, 'seq', swap)  0.52 us
  transfers between devices with their start and end apart: 6, of which 5 were waited for; matrix products, arithmetic and copies ran while one was open for 0% of the time, Pallas kernels for 23%

profile of v7, /device:TPU:0, one launch (start us, length us, event | category | flops | bytes accessed | tf_op | source)
XLA Modules:
  0.0 19.1 jit_solution(3965757792667892884)
XLA Ops:
  0.6 0.5 %collective-permute-start = (bf16[4,16,128]{2,1,0:T(8,128)(2,1)}, bf16[4,16,128]{2,1,0:T(8,128)(2,1)S(1)}, u32[]{:S(2)}, u32[]{:S(2)}) collective-permute-start(bf16[4,16,128]{2,1,0:T(8,128)(2,1)} %own_ref.3), channel_id=1, source_target_pairs={{0,1},{1,0},{2,3},{3,2},{4,5},{5,4},{6,7},{7,6},{8,9},{9,8},{10,11... | collective-permute-start | bytes 49160 | tf_op jit(solution)/shard_map/ppermute | solution.py:573
  1.1 0.0 copy-start
  1.2 1.7 %project.1 = (bf16[32,128]{1,0:T(8,128)(2,1)S(1)}, bf16[32,128]{1,0:T(8,128)(2,1)S(1)}, bf16[1024,128]{1,0:T(8,128)(2,1)S(1)}) custom-call(bf16[32,4,256]{2,1,0:T(4,128)(2,1)} %x_hbm.3, f32[1,256]{1,0:T(1,128)} %bitcast.20, f32[1,256]{1,0:T(1,128)} %bitcast.22, bf16[32,256]{1,0:T(8,128)(2,1)} %bitcast.16, f32[1,32]{1,0:T(1,128)} %bitcast.23, ...), custom_call_target="tpu_custom_call" | custom-call | tf_op jit(solution)/shard_map/project/pallas_call | solution.py:580
  2.8 0.0 collective-permute-done.other_ref
  2.8 0.0 copy-done
  2.8 0.7 %far_pieces.1 = (bf16[5,32,128]{2,1,0:T(8,128)(2,1)S(1)}, bf16[512,128]{1,0:T(8,128)(2,1)S(1)}) custom-call(bf16[4,16,128]{2,1,0:T(8,128)(2,1)S(1)} %copy-done, bf16[4,16,128]{2,1,0:T(8,128)(2,1)S(1)} %collective-permute-done.other_ref, bf16[1024,128]{1,0:T(8,128)(2,1)S(1)} %get-tuple-element.15.sorted_w_ref, ...), custom_call_target="tpu_custom_call" | custom-call | tf_op jit(solution)/shard_map/far_pieces/pallas_call | solution.py:615
  3.5 3.7 %collective-permute-start.1 = (bf16[5,32,128]{2,1,0:T(8,128)(2,1)S(1)}, bf16[5,32,128]{2,1,0:T(8,128)(2,1)S(1)}, u32[]{:S(2)}, u32[]{:S(2)}) collective-permute-start(bf16[5,32,128]{2,1,0:T(8,128)(2,1)S(1)} %get-tuple-element.17), channel_id=1, source_target_pairs={{0,8},{2,10},{4,12},{6,14},{8,0},{10,2},{12,4},{14,6},{1,9},{3,11}... | collective-permute-start | bytes 122888 | tf_op jit(solution)/shard_map/ppermute | solution.py:663
  7.2 1.6 %near_pieces.1 = (f32[4,32,128]{2,1,0:T(8,128)S(1)}, bf16[512,128]{1,0:T(8,128)(2,1)S(1)}, f32[128,256]{1,0:T(8,128)S(1)}, f32[128,128]{1,0:T(8,128)S(1)}, bf16[...) custom-call(bf16[32,4,256]{2,1,0:T(4,128)(2,1)} %x_hbm.3, f32[1,256]{1,0:T(1,128)} %bitcast.21, ...), custom_call_target="tpu_custom_call" | custom-call | tf_op jit(solution)/shard_map/near_pieces/pallas_call | solution.py:628
  8.8 0.6 %collective-permute-done.1.far_ref = bf16[5,32,128]{2,1,0:T(8,128)(2,1)S(1)} collective-permute-done((bf16[5,32,128]{2,1,0:T(8,128)(2,1)S(1)}, bf16[5,32,128]{2,1,0:T(8,128)(2,1)S(1)}, u32[]{:S(2)}, u32[]{:S(2)}) %collective-permute-start.1) | collective-permute-done | bytes 40992 | tf_op jit(solution)/shard_map/ppermute | solution.py:663
  9.4 2.7 %collective-permute-start.2 = (bf16[3,32,128]{2,1,0:T(8,128)(2,1)S(1)}, bf16[3,32,128]{2,1,0:T(8,128)(2,1)S(1)}, u32[]{:S(2)}, u32[]{:S(2)}) collective-permute-start(bf16[3,32,128]{2,1,0:T(8,128)(2,1)S(1)} %get-tuple-element.31), channel_id=1, source_target_pairs={{0,6},{2,4},{4,2},{6,0},{8,14},{10,12},{12,10},{14,8},{1,7},{3,5},... | collective-permute-start | bytes 73736 | tf_op jit(solution)/shard_map/ppermute | solution.py:663
  12.1 0.5 %collective-permute-start.3 = (bf16[3,32,128]{2,1,0:T(8,128)(2,1)S(1)}, bf16[3,32,128]{2,1,0:T(8,128)(2,1)S(1)}, u32[]{:S(2)}, u32[]{:S(2)}) collective-permute-start(bf16[3,32,128]{2,1,0:T(8,128)(2,1)S(1)} %get-tuple-element.30), channel_id=1, source_target_pairs={{0,4},{2,6},{4,0},{6,2},{8,12},{10,14},{12,8},{14,10},{1,5},{3,7},... | collective-permute-start | bytes 73736 | tf_op jit(solution)/shard_map/ppermute | solution.py:663
  12.6 0.4 %collective-permute-start.4 = (bf16[3,32,128]{2,1,0:T(8,128)(2,1)S(1)}, bf16[3,32,128]{2,1,0:T(8,128)(2,1)S(1)}, u32[]{:S(2)}, u32[]{:S(2)}) collective-permute-start(bf16[3,32,128]{2,1,0:T(8,128)(2,1)S(1)} %get-tuple-element.29), channel_id=1, source_target_pairs={{0,2},{2,0},{4,6},{6,4},{8,10},{10,8},{12,14},{14,12},{1,3},{3,1},... | collective-permute-start | bytes 73736 | tf_op jit(solution)/shard_map/ppermute | solution.py:663
  13.1 1.2 %collective-permute-done.2.near_refs_2_ = bf16[3,32,128]{2,1,0:T(8,128)(2,1)S(1)} collective-permute-done((bf16[3,32,128]{2,1,0:T(8,128)(2,1)S(1)}, bf16[3,32,128]{2,1,0:T(8,128)(2,1)S(1)}, u32[]{:S(2)}, u32[]{:S(2)}) %collective-permute-start.2) | collective-permute-done | bytes 24608 | tf_op jit(solution)/shard_map/ppermute | solution.py:663
  14.3 1.8 %collective-permute-done.3.near_refs_1_ = bf16[3,32,128]{2,1,0:T(8,128)(2,1)S(1)} collective-permute-done((bf16[3,32,128]{2,1,0:T(8,128)(2,1)S(1)}, bf16[3,32,128]{2,1,0:T(8,128)(2,1)S(1)}, u32[]{:S(2)}, u32[]{:S(2)}) %collective-permute-start.3) | collective-permute-done | bytes 24608 | tf_op jit(solution)/shard_map/ppermute | solution.py:663
  16.0 0.4 %collective-permute-done.4.near_refs_0_ = bf16[3,32,128]{2,1,0:T(8,128)(2,1)S(1)} collective-permute-done((bf16[3,32,128]{2,1,0:T(8,128)(2,1)S(1)}, bf16[3,32,128]{2,1,0:T(8,128)(2,1)S(1)}, u32[]{:S(2)}, u32[]{:S(2)}) %collective-permute-start.4) | collective-permute-done | bytes 24608 | tf_op jit(solution)/shard_map/ppermute | solution.py:663
  16.5 0.1 collective-permute-start.5
  16.6 1.2 %gradient.1 = bf16[32,4,256]{2,1,0:T(4,128)(2,1)} custom-call(bf16[8,32,128]{2,1,0:T(8,128)(2,1)S(1)} %slice_dynamic-update-slice_fusion.right_ref, bf16[512,128]{1,0:T(8,128)(2,1)S(1)} %get-tuple-element.20.outer_near_ref, bf16[512,128]{1,0:T(8,128)(2,1)S(1)} %get-tuple-element.21.outer_far_ref, f32[4,32,128]{2,1,0:T(8,128)S(1)} %get-tuple-element.18.keep_ref, ...), custom_call_target="tpu_custom_call" | custom-call | tf_op jit(solution)/shard_map/gradient/pallas_call | solution.py:685
  17.7 0.1 collective-permute-done.5.far_ref
  17.8 1.3 %pair.1 = bf16[4,16,128]{2,1,0:T(8,128)(2,1)} custom-call(bf16[8,32,128]{2,1,0:T(8,128)(2,1)S(1)} %slice_dynamic-update-slice_fusion.right_ref, bf16[5,32,128]{2,1,0:T(8,128)(2,1)S(1)} %collective-permute-done.5.far_ref, bf16[32,128]{1,0:T(8,128)(2,1)S(1)} %get-tuple-element.16.left_ref, bf16[1024,128]{1,0:T(8,128)(2,1)S(1)} %get-tuple-element.15.sorted_w_ref, ...), custom_call_target="tpu_custom_call" | custom-call | tf_op jit(solution)/shard_map/pair/pallas_call | solution.py:694
  (13 shorter events, 0.1 us)
Async XLA Ops:
  0.6 2.2 %collective-permute-start = (bf16[4,16,128]{2,1,0:T(8,128)(2,1)}, bf16[4,16,128]{2,1,0:T(8,128)(2,1)S(1)}, u32[]{:S(2)}, u32[]{:S(2)}) collective-permute-start(bf16[4,16,128]{2,1,0:T(8,128)(2,1)} %own_ref.3), channel_id=1, source_target_pairs={{0,1},{1,0},{2,3},{3,2},{4,5},{5,4},{6,7},{7,6},{8,9},{9,8},{10,11... | collective-permute-start | bytes 49160 | tf_op jit(solution)/shard_map/ppermute | solution.py:573
  1.1 1.7 %copy-start = (bf16[4,16,128]{2,1,0:T(8,128)(2,1)S(1)}, bf16[4,16,128]{2,1,0:T(8,128)(2,1)}, u32[]{:S(2)}) copy-start(bf16[4,16,128]{2,1,0:T(8,128)(2,1)} %own_ref.3) | copy-start | bytes 49156
  3.5 5.9 %collective-permute-start.1 = (bf16[5,32,128]{2,1,0:T(8,128)(2,1)S(1)}, bf16[5,32,128]{2,1,0:T(8,128)(2,1)S(1)}, u32[]{:S(2)}, u32[]{:S(2)}) collective-permute-start(bf16[5,32,128]{2,1,0:T(8,128)(2,1)S(1)} %get-tuple-element.17), channel_id=1, source_target_pairs={{0,8},{2,10},{4,12},{6,14},{8,0},{10,2},{12,4},{14,6},{1,9},{3,11}... | collective-permute-start | bytes 122888 | tf_op jit(solution)/shard_map/ppermute | solution.py:663
  9.4 4.8 %collective-permute-start.2 = (bf16[3,32,128]{2,1,0:T(8,128)(2,1)S(1)}, bf16[3,32,128]{2,1,0:T(8,128)(2,1)S(1)}, u32[]{:S(2)}, u32[]{:S(2)}) collective-permute-start(bf16[3,32,128]{2,1,0:T(8,128)(2,1)S(1)} %get-tuple-element.31), channel_id=1, source_target_pairs={{0,6},{2,4},{4,2},{6,0},{8,14},{10,12},{12,10},{14,8},{1,7},{3,5},... | collective-permute-start | bytes 73736 | tf_op jit(solution)/shard_map/ppermute | solution.py:663
  12.1 3.9 %collective-permute-start.3 = (bf16[3,32,128]{2,1,0:T(8,128)(2,1)S(1)}, bf16[3,32,128]{2,1,0:T(8,128)(2,1)S(1)}, u32[]{:S(2)}, u32[]{:S(2)}) collective-permute-start(bf16[3,32,128]{2,1,0:T(8,128)(2,1)S(1)} %get-tuple-element.30), channel_id=1, source_target_pairs={{0,4},{2,6},{4,0},{6,2},{8,12},{10,14},{12,8},{14,10},{1,5},{3,7},... | collective-permute-start | bytes 73736 | tf_op jit(solution)/shard_map/ppermute | solution.py:663
  12.6 3.8 %collective-permute-start.4 = (bf16[3,32,128]{2,1,0:T(8,128)(2,1)S(1)}, bf16[3,32,128]{2,1,0:T(8,128)(2,1)S(1)}, u32[]{:S(2)}, u32[]{:S(2)}) collective-permute-start(bf16[3,32,128]{2,1,0:T(8,128)(2,1)S(1)} %get-tuple-element.29), channel_id=1, source_target_pairs={{0,2},{2,0},{4,6},{6,4},{8,10},{10,8},{12,14},{14,12},{1,3},{3,1},... | collective-permute-start | bytes 73736 | tf_op jit(solution)/shard_map/ppermute | solution.py:663
  16.5 1.3 %collective-permute-start.5 = (bf16[5,32,128]{2,1,0:T(8,128)(2,1)S(1)}, bf16[5,32,128]{2,1,0:T(8,128)(2,1)S(1)}, u32[]{:S(2)}, u32[]{:S(2)}) collective-permute-start(bf16[5,32,128]{2,1,0:T(8,128)(2,1)S(1)} %pad_maximum_fusion.1), channel_id=1, source_target_pairs={{0,1},{1,0},{2,3},{3,2},{4,5},{5,4},{6,7},{7,6},{8,9},{9,8},{10,11... | collective-permute-start | bytes 122888 | tf_op jit(solution)/shard_map/ppermute | solution.py:683

commit v8 on v7

--- a/solution.py
+++ b/solution.py
@@ -457,7 +457,7 @@
     )
 
 
-def small_grad_kernel(right_ref, outer_near_ref, outer_far_ref, keep_ref, far_ref, near_refs, normed_ref, inv_std_ref,
+def small_grad_kernel(spots, right_ref, outer_near_ref, outer_far_ref, keep_ref, far_ref, near_refs, normed_ref, inv_std_ref,
                       gain_ref, spread_w_ref, grad_ref):
     ranks, seqs, _ = right_ref.shape
     residues = grad_ref.shape[1]
@@ -470,8 +470,8 @@
     outer = jnp.concatenate([outer_near_ref[...], outer_far_ref[...]], axis=0)
     left_cot = jnp.dot(right_all, outer, preferred_element_type=F32)
     right_cot = keep_ref[0] + far_ref[1].astype(F32)
-    for near_ref in near_refs:
-        right_cot = right_cot + near_ref[2].astype(F32)
+    for near_ref, spot in zip(near_refs, spots):
+        right_cot = right_cot + near_ref[spot].astype(F32)
     blocks = lane_block((seqs, LANES), depth)
     spread = jnp.concatenate(
         [
@@ -659,32 +659,40 @@
         left,
     )
 
-    def swap_over(mask, value):
-        return lax.ppermute(value, "res", [(source, source ^ mask) for source in range(ranks)])
+    def swap_over(mask, value, direction="both"):
+        pairs = [(source, source ^ mask) for source in range(ranks)]
+        if direction == "down":
+            pairs = [(source, target) for source, target in pairs if source > target]
+        if direction == "up":
+            pairs = [(source, target) for source, target in pairs if source < target]
+        return lax.ppermute(value, "res", pairs)
 
     own = right[None]
     beyond_two = swap_over(4, send)
     both = jnp.concatenate([own, beyond_two[0:1]])
-    near_parts = {}
     gathered = jnp.concatenate(
         [own, jnp.zeros((3, seqs, LANES), BF16), beyond_two[0:1], jnp.zeros((3, seqs, LANES), BF16)]
-    )
-    for mask in (3, 2, 1):
-        summed = (keep[mask] + beyond_two[1 + mask].astype(F32)).astype(BF16)
-        part = swap_over(mask, jnp.concatenate([both, summed[None]]))
-        near_parts[mask] = part
-        gathered = lax.dynamic_update_slice_in_dim(gathered, part[0:1], mask, 0)
-        gathered = lax.dynamic_update_slice_in_dim(gathered, part[1:2], 4 + mask, 0)
-    near_parts = [near_parts[mask] for mask in (1, 2, 3)]
-
-    half = gathered.reshape(2, ranks // 2, seqs, LANES)
+    ).reshape(2, ranks // 2, seqs, LANES)
+    near_parts = []
+    for mask, direction in ((3, "down"), (2, "both"), (3, "up"), (1, "both")):
+        summed = (keep[mask] + beyond_two[1 + mask].astype(F32)).astype(BF16)[None]
+        pieces = [summed, both] if direction == "up" else [both, summed]
+        part = swap_over(mask, jnp.concatenate(pieces), direction)
+        near_parts.append(part)
+        slot = (part[1:3] if direction == "up" else part[0:2])[:, None]
+        if direction == "up":
+            slot = slot + gathered[:, mask : mask + 1]
+        gathered = lax.dynamic_update_slice_in_dim(gathered, slot, mask, 1)
+
+    half = gathered
+    gathered = half.reshape(ranks, seqs, LANES)
     beyond = 1 - lax.bitwise_xor(lax.shift_right_logical(rank, 2), mine)
     leaving = lax.dynamic_index_in_dim(half, beyond, 0, keepdims=False)
     far = lax.ppermute(jnp.concatenate([leaving, left[None]]), "seq", swap)
 
     gradient = pl.pallas_call(
-        small_grad_kernel,
-        in_specs=[vmem] * 5 + [[vmem] * 3] + [vmem] * 4,
+        functools.partial(small_grad_kernel, (2, 2, 0, 2)),
+        in_specs=[vmem] * 5 + [[vmem] * 4] + [vmem] * 4,
         out_specs=vmem,
         out_shape=like(homolog_matrix.shape, BF16),
         compiler_params=limit,

time: 19.3 us -> 22.3 us (1.16)
  starting transfers between devices: 7.87 us -> 12.6 us
  waiting for transfers between devices: 3.98 us -> 2.08 us
    ppermute x4 -> x5, starting transfers between devices: 7.29 us -> 12 us  [swap_over(): return lax.ppermute(value, 'res', pairs)]
    ppermute x4 -> x5, waiting for transfers between devices: 3.93 us -> 2.04 us  [swap_over(): return lax.ppermute(value, 'res', pairs)]
  transfers between devices with their start and end apart: 6 -> 7, of which waited for: 5 -> 2; matrix products, arithmetic and copies ran while one was open for 0% -> 0% of each run, Pallas kernels for 23% -> 20%
where the time goes in v8:
time: 22.3 us; the launch traced here: 22.1 us
  starting transfers between devices  12.6 us (57%)
  Pallas kernels  6.44 us (29%)
  waiting for transfers between devices  2.08 us (9%)
  between operations  0.79 us (4%)
    ppermute x5, starting transfers between devices, swap_over(): return lax.ppermute(value, 'res', pairs)  12 us
    ppermute x5, waiting for transfers between devices, swap_over(): return lax.ppermute(value, 'res', pairs)  2.04 us
    pallas_call x1, Pallas kernels, small_slice(): pl.pallas_call(small_project_kernel, in_specs=[hbm] * 8, out_specs=[vmem]...  1.67 us
    pallas_call x1, Pallas kernels, small_slice(): pl.pallas_call(functools.partial(small_near_kernel, scale), in_specs=[hbm...  1.64 us
    pallas_call x1, Pallas kernels, small_slice(): pl.pallas_call(functools.partial(small_pair_kernel, scale), in_specs=[vme...  1.31 us
    pallas_call x1, Pallas kernels, small_slice(): pl.pallas_call(functools.partial(small_grad_kernel, (2, 2, 0, 2)), in_spe...  1.15 us
    pallas_call x1, Pallas kernels, small_slice(): pl.pallas_call(functools.partial(small_far_kernel, scale), in_specs=[vmem...  0.67 us
    ppermute x1, starting transfers between devices, small_slice(): other_cot = lax.ppermute(coupling_cotangent, 'seq', swap)  0.52 us
  transfers between devices with their start and end apart: 7, of which 2 were waited for; matrix products, arithmetic and copies ran while one was open for 0% of the time, Pallas kernels for 20%

profile of v8, /device:TPU:0, one launch (start us, length us, event | category | flops | bytes accessed | tf_op | source)
XLA Modules:
  0.0 22.1 jit_solution(6560655500861837897)
XLA Ops:
  0.6 0.5 %collective-permute-start = (bf16[4,16,128]{2,1,0:T(8,128)(2,1)}, bf16[4,16,128]{2,1,0:T(8,128)(2,1)S(1)}, u32[]{:S(2)}, u32[]{:S(2)}) collective-permute-start(bf16[4,16,128]{2,1,0:T(8,128)(2,1)} %own_ref.3), channel_id=1, source_target_pairs={{0,1},{1,0},{2,3},{3,2},{4,5},{5,4},{6,7},{7,6},{8,9},{9,8},{10,11... | collective-permute-start | bytes 49160 | tf_op jit(solution)/shard_map/ppermute | solution.py:573
  1.1 0.0 copy-start
  1.2 1.7 %project.1 = (bf16[32,128]{1,0:T(8,128)(2,1)S(1)}, bf16[32,128]{1,0:T(8,128)(2,1)S(1)}, bf16[1024,128]{1,0:T(8,128)(2,1)S(1)}) custom-call(bf16[32,4,256]{2,1,0:T(4,128)(2,1)} %x_hbm.3, f32[1,256]{1,0:T(1,128)} %bitcast.39, f32[1,256]{1,0:T(1,128)} %bitcast.41, bf16[32,256]{1,0:T(8,128)(2,1)} %bitcast.35, f32[1,32]{1,0:T(1,128)} %bitcast.42, ...), custom_call_target="tpu_custom_call" | custom-call | tf_op jit(solution)/shard_map/project/pallas_call | solution.py:580
  2.8 0.0 collective-permute-done.other_ref
  2.8 0.0 copy-done
  2.8 0.7 %far_pieces.1 = (bf16[5,32,128]{2,1,0:T(8,128)(2,1)S(1)}, bf16[512,128]{1,0:T(8,128)(2,1)S(1)}) custom-call(bf16[4,16,128]{2,1,0:T(8,128)(2,1)S(1)} %copy-done, bf16[4,16,128]{2,1,0:T(8,128)(2,1)S(1)} %collective-permute-done.other_ref, bf16[1024,128]{1,0:T(8,128)(2,1)S(1)} %get-tuple-element.15.sorted_w_ref, ...), custom_call_target="tpu_custom_call" | custom-call | tf_op jit(solution)/shard_map/far_pieces/pallas_call | solution.py:615
  3.5 3.7 %collective-permute-start.1 = (bf16[5,32,128]{2,1,0:T(8,128)(2,1)S(1)}, bf16[5,32,128]{2,1,0:T(8,128)(2,1)S(1)}, u32[]{:S(2)}, u32[]{:S(2)}) collective-permute-start(bf16[5,32,128]{2,1,0:T(8,128)(2,1)S(1)} %get-tuple-element.17), channel_id=1, source_target_pairs={{0,8},{2,10},{4,12},{6,14},{8,0},{10,2},{12,4},{14,6},{1,9},{3,11}... | collective-permute-start | bytes 122888 | tf_op jit(solution)/shard_map/ppermute | solution.py:668
  7.2 1.6 %near_pieces.1 = (f32[4,32,128]{2,1,0:T(8,128)S(1)}, bf16[512,128]{1,0:T(8,128)(2,1)S(1)}, f32[128,256]{1,0:T(8,128)S(1)}, f32[128,128]{1,0:T(8,128)S(1)}, bf16[...) custom-call(bf16[32,4,256]{2,1,0:T(4,128)(2,1)} %x_hbm.3, f32[1,256]{1,0:T(1,128)} %bitcast.40, ...), custom_call_target="tpu_custom_call" | custom-call | tf_op jit(solution)/shard_map/near_pieces/pallas_call | solution.py:628
  8.8 0.6 %collective-permute-done.1.far_ref = bf16[5,32,128]{2,1,0:T(8,128)(2,1)S(1)} collective-permute-done((bf16[5,32,128]{2,1,0:T(8,128)(2,1)S(1)}, bf16[5,32,128]{2,1,0:T(8,128)(2,1)S(1)}, u32[]{:S(2)}, u32[]{:S(2)}) %collective-permute-start.1) | collective-permute-done | bytes 40992 | tf_op jit(solution)/shard_map/ppermute | solution.py:668
  9.4 1.3 %collective-permute-start.2 = (bf16[3,32,128]{2,1,0:T(8,128)(2,1)S(1)}, bf16[3,32,128]{2,1,0:T(8,128)(2,1)S(1)}, u32[]{:S(2)}, u32[]{:S(2)}) collective-permute-start(bf16[3,32,128]{2,1,0:T(8,128)(2,1)S(1)} %get-tuple-element.33), channel_id=1, source_target_pairs={{4,2},{6,0},{12,10},{14,8},{5,3},{7,1},{13,11},{15,9},{20,18},{22,... | collective-permute-start | bytes 73736 | tf_op jit(solution)/shard_map/ppermute | solution.py:668
  10.8 1.6 %collective-permute-start.5 = (bf16[3,32,128]{2,1,0:T(8,128)(2,1)S(1)}, bf16[3,32,128]{2,1,0:T(8,128)(2,1)S(1)}, u32[]{:S(2)}, u32[]{:S(2)}) collective-permute-start(bf16[3,32,128]{2,1,0:T(8,128)(2,1)S(1)} %get-tuple-element.31), channel_id=1, source_target_pairs={{0,2},{2,0},{4,6},{6,4},{8,10},{10,8},{12,14},{14,12},{1,3},{3,1},... | collective-permute-start | bytes 73736 | tf_op jit(solution)/shard_map/ppermute | solution.py:668
  12.4 2.5 %collective-permute-start.3 = (bf16[3,32,128]{2,1,0:T(8,128)(2,1)S(1)}, bf16[3,32,128]{2,1,0:T(8,128)(2,1)S(1)}, u32[]{:S(2)}, u32[]{:S(2)}) collective-permute-start(bf16[3,32,128]{2,1,0:T(8,128)(2,1)S(1)} %get-tuple-element.32), channel_id=1, source_target_pairs={{0,4},{2,6},{4,0},{6,2},{8,12},{10,14},{12,8},{14,10},{1,5},{3,7},... | collective-permute-start | bytes 73736 | tf_op jit(solution)/shard_map/ppermute | solution.py:668
  15.0 2.9 %collective-permute-start.4 = (bf16[3,32,128]{2,1,0:T(8,128)(2,1)S(1)}, bf16[3,32,128]{2,1,0:T(8,128)(2,1)S(1)}, u32[]{:S(2)}, u32[]{:S(2)}) collective-permute-start(bf16[3,32,128]{2,1,0:T(8,128)(2,1)S(1)} %get-tuple-element.34), channel_id=1, source_target_pairs={{0,6},{2,4},{8,14},{10,12},{1,7},{3,5},{9,15},{11,13},{16,22},{18,... | collective-permute-start | bytes 73736 | tf_op jit(solution)/shard_map/ppermute | solution.py:668
  17.9 0.0 collective-permute-done.2.near_refs_0_
  17.9 0.0 collective-permute-done.3.near_refs_1_
  17.9 1.5 %collective-permute-done.4.near_refs_2_ = bf16[3,32,128]{2,1,0:T(8,128)(2,1)S(1)} collective-permute-done((bf16[3,32,128]{2,1,0:T(8,128)(2,1)S(1)}, bf16[3,32,128]{2,1,0:T(8,128)(2,1)S(1)}, u32[]{:S(2)}, u32[]{:S(2)}) %collective-permute-start.4) | collective-permute-done | bytes 24608 | tf_op jit(solution)/shard_map/ppermute | solution.py:668
  19.4 0.0 collective-permute-done.5.near_refs_3_
  19.5 0.1 collective-permute-start.6
  19.6 1.2 %gradient.1 = bf16[32,4,256]{2,1,0:T(4,128)(2,1)} custom-call(bf16[8,32,128]{2,1,0:T(8,128)(2,1)S(1)} %bitcast.29, bf16[512,128]{1,0:T(8,128)(2,1)S(1)} %get-tuple-element.20.outer_near_ref, bf16[512,128]{1,0:T(8,128)(2,1)S(1)} %get-tuple-element.21.outer_far_ref, f32[4,32,128]{2,1,0:T(8,128)S(1)} %get-tuple-element.18.keep_ref, ...), custom_call_target="tpu_custom_call" | custom-call | tf_op jit(solution)/shard_map/gradient/pallas_call | solution.py:693
  20.7 0.0 collective-permute-done.6.far_ref
  20.7 1.3 %pair.1 = bf16[4,16,128]{2,1,0:T(8,128)(2,1)} custom-call(bf16[8,32,128]{2,1,0:T(8,128)(2,1)S(1)} %bitcast.30, bf16[5,32,128]{2,1,0:T(8,128)(2,1)S(1)} %collective-permute-done.6.far_ref, bf16[32,128]{1,0:T(8,128)(2,1)S(1)} %get-tuple-element.16.left_ref, bf16[1024,128]{1,0:T(8,128)(2,1)S(1)} %get-tuple-element.15.sorted_w_ref, ...), custom_call_target="tpu_custom_call" | custom-call | tf_op jit(solution)/shard_map/pair/pallas_call | solution.py:702
  (13 shorter events, 0.1 us)
Async XLA Ops:
  0.6 2.2 %collective-permute-start = (bf16[4,16,128]{2,1,0:T(8,128)(2,1)}, bf16[4,16,128]{2,1,0:T(8,128)(2,1)S(1)}, u32[]{:S(2)}, u32[]{:S(2)}) collective-permute-start(bf16[4,16,128]{2,1,0:T(8,128)(2,1)} %own_ref.3), channel_id=1, source_target_pairs={{0,1},{1,0},{2,3},{3,2},{4,5},{5,4},{6,7},{7,6},{8,9},{9,8},{10,11... | collective-permute-start | bytes 49160 | tf_op jit(solution)/shard_map/ppermute | solution.py:573
  1.1 1.7 %copy-start = (bf16[4,16,128]{2,1,0:T(8,128)(2,1)S(1)}, bf16[4,16,128]{2,1,0:T(8,128)(2,1)}, u32[]{:S(2)}) copy-start(bf16[4,16,128]{2,1,0:T(8,128)(2,1)} %own_ref.3) | copy-start | bytes 49156
  3.5 5.9 %collective-permute-start.1 = (bf16[5,32,128]{2,1,0:T(8,128)(2,1)S(1)}, bf16[5,32,128]{2,1,0:T(8,128)(2,1)S(1)}, u32[]{:S(2)}, u32[]{:S(2)}) collective-permute-start(bf16[5,32,128]{2,1,0:T(8,128)(2,1)S(1)} %get-tuple-element.17), channel_id=1, source_target_pairs={{0,8},{2,10},{4,12},{6,14},{8,0},{10,2},{12,4},{14,6},{1,9},{3,11}... | collective-permute-start | bytes 122888 | tf_op jit(solution)/shard_map/ppermute | solution.py:668
  9.4 8.4 %collective-permute-start.2 = (bf16[3,32,128]{2,1,0:T(8,128)(2,1)S(1)}, bf16[3,32,128]{2,1,0:T(8,128)(2,1)S(1)}, u32[]{:S(2)}, u32[]{:S(2)}) collective-permute-start(bf16[3,32,128]{2,1,0:T(8,128)(2,1)S(1)} %get-tuple-element.33), channel_id=1, source_target_pairs={{4,2},{6,0},{12,10},{14,8},{5,3},{7,1},{13,11},{15,9},{20,18},{22,... | collective-permute-start | bytes 73736 | tf_op jit(solution)/shard_map/ppermute | solution.py:668
  10.8 8.6 %collective-permute-start.5 = (bf16[3,32,128]{2,1,0:T(8,128)(2,1)S(1)}, bf16[3,32,128]{2,1,0:T(8,128)(2,1)S(1)}, u32[]{:S(2)}, u32[]{:S(2)}) collective-permute-start(bf16[3,32,128]{2,1,0:T(8,128)(2,1)S(1)} %get-tuple-element.31), channel_id=1, source_target_pairs={{0,2},{2,0},{4,6},{6,4},{8,10},{10,8},{12,14},{14,12},{1,3},{3,1},... | collective-permute-start | bytes 73736 | tf_op jit(solution)/shard_map/ppermute | solution.py:668
  12.4 5.5 %collective-permute-start.3 = (bf16[3,32,128]{2,1,0:T(8,128)(2,1)S(1)}, bf16[3,32,128]{2,1,0:T(8,128)(2,1)S(1)}, u32[]{:S(2)}, u32[]{:S(2)}) collective-permute-start(bf16[3,32,128]{2,1,0:T(8,128)(2,1)S(1)} %get-tuple-element.32), channel_id=1, source_target_pairs={{0,4},{2,6},{4,0},{6,2},{8,12},{10,14},{12,8},{14,10},{1,5},{3,7},... | collective-permute-start | bytes 73736 | tf_op jit(solution)/shard_map/ppermute | solution.py:668
  15.0 4.4 %collective-permute-start.4 = (bf16[3,32,128]{2,1,0:T(8,128)(2,1)S(1)}, bf16[3,32,128]{2,1,0:T(8,128)(2,1)S(1)}, u32[]{:S(2)}, u32[]{:S(2)}) collective-permute-start(bf16[3,32,128]{2,1,0:T(8,128)(2,1)S(1)} %get-tuple-element.34), channel_id=1, source_target_pairs={{0,6},{2,4},{8,14},{10,12},{1,7},{3,5},{9,15},{11,13},{16,22},{18,... | collective-permute-start | bytes 73736 | tf_op jit(solution)/shard_map/ppermute | solution.py:668
  19.5 1.3 %collective-permute-start.6 = (bf16[5,32,128]{2,1,0:T(8,128)(2,1)S(1)}, bf16[5,32,128]{2,1,0:T(8,128)(2,1)S(1)}, u32[]{:S(2)}, u32[]{:S(2)}) collective-permute-start(bf16[5,32,128]{2,1,0:T(8,128)(2,1)S(1)} %pad_maximum_fusion.1), channel_id=1, source_target_pairs={{0,1},{1,0},{2,3},{3,2},{4,5},{5,4},{6,7},{7,6},{8,9},{9,8},{10,11... | collective-permute-start | bytes 122888 | tf_op jit(solution)/shard_map/ppermute | solution.py:691

commit v9 on v6

--- a/solution.py
+++ b/solution.py
@@ -333,117 +333,131 @@
     return copy
 
 
-def small_project_kernel(
-    x_hbm, gain_hbm, offset_hbm, left_w_hbm, left_b_hbm, right_w_hbm, right_b_hbm, w_hbm, pair_offset_hbm,
-    left_ref, right_ref, sorted_w_ref, normed_ref, inv_std_ref, spread_w_ref, gain_out_ref,
-    pair_offset_out_ref,
-    x_ref, offset_ref, left_w_ref, left_b_ref, right_w_ref, right_b_ref, raw_ref, wide_ref, semaphores,
-):
+def start_copies(pairs, semaphores):
     copies = [
         pltpu.make_async_copy(source, target, semaphores.at[place])
-        for place, (source, target) in enumerate(
-            (
-                (x_hbm, x_ref),
-                (gain_hbm, gain_out_ref),
-                (offset_hbm, offset_ref),
-                (left_w_hbm, left_w_ref),
-                (left_b_hbm, left_b_ref),
-                (right_w_hbm, right_w_ref),
-                (right_b_hbm, right_b_ref),
-                (w_hbm, raw_ref),
-                (pair_offset_hbm, pair_offset_out_ref),
-            )
-        )
+        for place, (source, target) in enumerate(pairs)
     ]
     for copy in copies:
         copy.start()
+    return copies
+
+
+def small_project_kernel(
+    x_hbm, gain_hbm, offset_hbm, left_w_hbm, left_b_hbm, right_w_hbm, right_b_hbm, pair_offset_hbm,
+    both_ref, normed_ref, inv_std_ref, spread_w_ref, gain_ref, pair_offset_ref,
+    x_ref, offset_ref, left_w_ref, left_b_ref, right_w_ref, right_b_ref, semaphores,
+):
+    copies = start_copies(
+        (
+            (x_hbm, x_ref),
+            (gain_hbm, gain_ref),
+            (offset_hbm, offset_ref),
+            (left_w_hbm, left_w_ref),
+            (left_b_hbm, left_b_ref),
+            (right_w_hbm, right_w_ref),
+            (right_b_hbm, right_b_ref),
+            (pair_offset_hbm, pair_offset_ref),
+        ),
+        semaphores,
+    )
     seqs, residues, _ = x_ref.shape
     depth = left_w_ref.shape[0]
     copies[0].wait()
     normed, inv_std = normalise(residue_rows(x_ref))
-    normed_ref[...] = normed
-    inv_std_ref[...] = jnp.broadcast_to(inv_std, inv_std_ref.shape)
-    for copy in copies[1:7]:
+    for copy in copies[1:]:
         copy.wait()
-    ln_out = (normed * gain_out_ref[...] + offset_ref[...]).astype(BF16)
+    ln_out = (normed * gain_ref[...] + offset_ref[...]).astype(BF16)
     blocks = lane_block((seqs, LANES), depth)
     spread = []
-    for weight_ref, bias_ref, out_ref in (
-        (left_w_ref, left_b_ref, left_ref),
-        (right_w_ref, right_b_ref, right_ref),
+    for place, (weight_ref, bias_ref) in enumerate(
+        ((left_w_ref, left_b_ref), (right_w_ref, right_b_ref))
     ):
         weight = jnp.concatenate([weight_ref[...]] * residues, axis=0)
         spread.append(weight)
         bias = jnp.concatenate([bias_ref[...]] * residues, axis=1)
         wide = lax.dot_general(ln_out, weight, NT, preferred_element_type=F32)
         own = pick(blocks, [wide[p * seqs : (p + 1) * seqs] for p in range(residues)])
-        out_ref[...] = (own + bias).astype(BF16)
+        both_ref[place] = (own + bias).astype(BF16)
+    normed_ref[...] = normed
+    inv_std_ref[...] = jnp.broadcast_to(inv_std, inv_std_ref.shape)
     spread_w_ref[...] = jnp.concatenate(spread, axis=0)
-    for copy in copies[7:]:
-        copy.wait()
-    wide_ref[...] = raw_ref[...].astype(F32)
+
+
+def outer_rows(scale, cot, residues, sorted_w_ref, turn_ref):
+    columns = cot.shape[0] // residues
+    depth = LANES // residues
+    flat = lax.dot_general(cot, sorted_w_ref[...], NT, preferred_element_type=F32) * scale
+    blocks = lane_block((columns, LANES), depth)
+    for tile in range(depth * depth // LANES):
+        block = flat[:, tile * LANES : (tile + 1) * LANES]
+        turned = [block] + [pltpu.roll(block, depth * t, 1) for t in range(1, residues)]
+        for e in range(residues):
+            turn_ref[pl.ds(tile * residues + e, columns, stride=depth), :] = pick(
+                blocks,
+                [
+                    turned[(i - e) % residues][i * columns : (i + 1) * columns]
+                    for i in range(residues)
+                ],
+            )
+    return turn_ref[...].astype(BF16)
+
+
+def small_own_kernel(scale, own_ref, other_ref, w_ref, both_ref,
+                     keep_ref, outer_near_ref, outer_far_ref, sorted_w_ref, turn_refs, wide_ref):
+    residues, columns, _ = own_ref.shape
+    depth = LANES // residues
+    wide_ref[...] = w_ref[...].astype(F32)
     for d in range(depth):
         sorted_w_ref[d * depth : (d + 1) * depth, :] = wide_ref[
             pl.ds(d, depth, stride=depth), :
         ].astype(BF16)
-
-
-def small_cot_kernel(scale, own_ref, other_ref, sorted_w_ref, left_ref, right_ref,
-                    send_ref, keep_ref, outer_ref, turn_ref):
-    residues, columns, _ = own_ref.shape
-    depth = LANES // residues
-    first = lax.axis_index("seq") == 0
+    rank = lax.axis_index("res")
+    own_is_near = lax.axis_index("seq") == lax.shift_right_logical(rank, 2)
     own = own_ref[...].reshape(residues * columns, LANES)
     other = other_ref[...].reshape(residues * columns, LANES)
-    both = jnp.concatenate([jnp.where(first, own, other), jnp.where(first, other, own)], axis=0)
-    flat = lax.dot_general(both, sorted_w_ref[...], NT, preferred_element_type=F32) * scale
-    blocks = lane_block((columns, LANES), depth)
-    for half in range(2):
-        for tile in range(depth * depth // LANES):
-            block = flat[
-                half * residues * columns : (half + 1) * residues * columns,
-                tile * LANES : (tile + 1) * LANES,
-            ]
-            turned = [block] + [pltpu.roll(block, depth * t, 1) for t in range(1, residues)]
-            for e in range(residues):
-                start = half * columns * depth + tile * residues + e
-                turn_ref[pl.ds(start, columns, stride=depth), :] = pick(
-                    blocks,
-                    [
-                        turned[(i - e) % residues][i * columns : (i + 1) * columns]
-                        for i in range(residues)
-                    ],
-                )
-    outer = turn_ref[...].astype(BF16)
-    outer_ref[...] = outer
-    partial = lax.dot_general(left_ref[...], outer, NT, preferred_element_type=F32)
+    near = outer_rows(
+        scale, jnp.where(own_is_near, own, other), residues, sorted_w_ref, turn_refs[0]
+    )
+    outer_near_ref[...] = near
+    partial = lax.dot_general(both_ref[0], near, NT, preferred_element_type=F32)
+    for place in range(columns // residues):
+        keep_ref[lax.bitwise_xor(rank & 3, place)] = partial[:, place * LANES : (place + 1) * LANES]
+    outer_far_ref[...] = outer_rows(
+        scale, jnp.where(own_is_near, other, own), residues, sorted_w_ref, turn_refs[1]
+    )
+
+
+def small_partner_kernel(scale, residues, got_ref, sorted_w_ref, keep_ref, both_ref,
+                         leaving_ref, keep_out_ref, turn_ref):
     rank = lax.axis_index("res")
-    send_ref[0] = right_ref[...]
-    for place in range(2 * columns // residues):
-        piece = partial[:, place * LANES : (place + 1) * LANES]
-        distance = lax.bitwise_xor(rank, place)
-        spot = distance & 3
-
-        @pl.when(distance >= 4)
-        def _():
-            send_ref[spot + 1] = piece.astype(BF16)
-
-        @pl.when(distance < 4)
-        def _():
-            keep_ref[spot] = piece
-
-
-def small_grad_kernel(right_ref, outer_ref, keep_ref, far_ref, near_refs, normed_ref, inv_std_ref,
+    seqs = got_ref.shape[1]
+    cot = got_ref[2:4].reshape(2 * seqs, LANES)
+    outer = outer_rows(scale, cot, residues, sorted_w_ref, turn_ref)
+    partial = lax.dot_general(got_ref[0], outer, NT, preferred_element_type=F32)
+    for place in range(leaving_ref.shape[0]):
+        leaving_ref[place, 0] = both_ref[1]
+        leaving_ref[place, 1] = got_ref[1]
+    for place in range(leaving_ref.shape[0]):
+        distance = lax.bitwise_xor(rank & 3, place)
+        total = keep_ref[distance] + partial[:, place * LANES : (place + 1) * LANES]
+        leaving_ref[distance, 2] = total.astype(BF16)
+        keep_out_ref[distance] = total
+
+
+def small_grad_kernel(right_ref, outer_near_ref, outer_far_ref, keep_ref, near_refs, normed_ref, inv_std_ref,
                       gain_ref, spread_w_ref, grad_ref):
     ranks, seqs, _ = right_ref.shape
     residues = grad_ref.shape[1]
     depth = LANES // residues
     rank = lax.axis_index("res")
+    places = [lax.bitwise_xor(rank & 3, place) for place in range(ranks // 2)]
     right_all = jnp.concatenate(
-        [right_ref[lax.bitwise_xor(rank, place)] for place in range(ranks)], axis=1
-    )
-    left_cot = jnp.dot(right_all, outer_ref[...], preferred_element_type=F32)
-    right_cot = keep_ref[0] + far_ref[1].astype(F32)
+        [right_ref[place] for place in places] + [right_ref[4 + place] for place in places], axis=1
+    )
+    outer = jnp.concatenate([outer_near_ref[...], outer_far_ref[...]], axis=0)
+    left_cot = jnp.dot(right_all, outer, preferred_element_type=F32)
+    right_cot = keep_ref[0]
     for near_ref in near_refs:
         right_cot = right_cot + near_ref[2].astype(F32)
     blocks = lane_block((seqs, LANES), depth)
@@ -545,14 +559,14 @@
     like = jax.ShapeDtypeStruct
 
     other_cot = lax.ppermute(coupling_cotangent, "seq", swap)
-    left, right, sorted_w, normed, inv_std, spread_w, gain, pair_offset = pl.pallas_call(
+    hbm = pl.BlockSpec(memory_space=pltpu.HBM)
+    pin = lambda array: pltpu.with_memory_space_constraint(array, pltpu.HBM)
+    both, normed, inv_std, spread_w, gain, pair_offset = pl.pallas_call(
         small_project_kernel,
-        in_specs=[pl.BlockSpec(memory_space=pltpu.HBM)] * 9,
-        out_specs=[vmem] * 8,
+        in_specs=[hbm] * 8,
+        out_specs=[vmem] * 6,
         out_shape=(
-            like((seqs, LANES), BF16),
-            like((seqs, LANES), BF16),
-            like(coupling_matrix.shape, BF16),
+            like((2, seqs, LANES), BF16),
             like((rows, features), F32),
             like((rows, LANES), F32),
             like((2 * LANES, features), BF16),
@@ -566,15 +580,13 @@
             pltpu.VMEM((1, depth), F32),
             pltpu.VMEM((depth, features), BF16),
             pltpu.VMEM((1, depth), F32),
-            pltpu.VMEM(coupling_matrix.shape, BF16),
-            pltpu.VMEM(coupling_matrix.shape, F32),
-            pltpu.SemaphoreType.DMA((9,)),
+            pltpu.SemaphoreType.DMA((8,)),
         ],
         compiler_params=limit,
         name="project",
     )(
         *[
-            pltpu.with_memory_space_constraint(array, pltpu.HBM)
+            pin(array)
             for array in (
                 homolog_matrix,
                 standardizer_scaling.reshape(1, -1),
@@ -583,43 +595,63 @@
                 left_offset_vector.reshape(1, -1),
                 right_projection_matrix.T,
                 right_offset_vector.reshape(1, -1),
-                coupling_matrix,
                 coupling_offset.reshape(1, -1),
             )
         ]
     )
 
-    send, keep, outer = pl.pallas_call(
-        functools.partial(small_cot_kernel, scale),
-        in_specs=[vmem] * 5,
-        out_specs=[vmem] * 3,
-        out_shape=(
-            like((1 + ranks // 2, seqs, LANES), BF16),
-            like((ranks // 2, seqs, LANES), F32),
-            like((ranks * LANES, LANES), BF16),
-        ),
-        scratch_shapes=[pltpu.VMEM((ranks * LANES, LANES), F32)],
-        compiler_params=limit,
-        name="cotangent",
-    )(coupling_cotangent, other_cot, sorted_w, left, right)
-
     def swap_over(mask, value):
         return lax.ppermute(value, "res", [(source, source ^ mask) for source in range(ranks)])
 
-    own = right[None]
-    beyond_two = swap_over(4, send)
-    both = jnp.concatenate([own, beyond_two[0:1]])
-    near_parts = {}
+    own_is_near = mine == lax.shift_right_logical(rank, 2)
+    far_cot = jnp.where(own_is_near, other_cot, coupling_cotangent).reshape(2, seqs, LANES)
+    beyond_two = swap_over(4, jnp.concatenate([both, far_cot]))
+
+    half_rows = ranks // 2 * LANES
+    turn = pltpu.VMEM((half_rows, LANES), F32)
+    keep, outer_near, outer_far, sorted_w = pl.pallas_call(
+        functools.partial(small_own_kernel, scale),
+        in_specs=[vmem] * 4,
+        out_specs=[vmem] * 4,
+        out_shape=(
+            like((ranks // 2, seqs, LANES), F32),
+            like((half_rows, LANES), BF16),
+            like((half_rows, LANES), BF16),
+            like(coupling_matrix.shape, BF16),
+        ),
+        scratch_shapes=[[turn, turn], pltpu.VMEM(coupling_matrix.shape, F32)],
+        compiler_params=limit,
+        name="own_pieces",
+    )(coupling_cotangent, other_cot, coupling_matrix, both)
+
+    leaving_parts, keep = pl.pallas_call(
+        functools.partial(small_partner_kernel, scale, residues),
+        in_specs=[vmem] * 4,
+        out_specs=[vmem] * 2,
+        out_shape=(
+            like((ranks // 2, 3, seqs, LANES), BF16),
+            like((ranks // 2, seqs, LANES), F32),
+        ),
+        scratch_shapes=[turn],
+        compiler_params=limit,
+        name="partner_pieces",
+    )(beyond_two, sorted_w, keep, both)
+
+    left = both[0]
     gathered = jnp.concatenate(
-        [own, jnp.zeros((3, seqs, LANES), BF16), beyond_two[0:1], jnp.zeros((3, seqs, LANES), BF16)]
-    )
+        [
+            both[1:2],
+            jnp.zeros((3, seqs, LANES), BF16),
+            beyond_two[1:2],
+            jnp.zeros((3, seqs, LANES), BF16),
+        ]
+    )
+    near_parts = []
     for mask in (3, 2, 1):
-        summed = (keep[mask] + beyond_two[1 + mask].astype(F32)).astype(BF16)
-        part = swap_over(mask, jnp.concatenate([both, summed[None]]))
-        near_parts[mask] = part
+        part = swap_over(mask, leaving_parts[mask])
+        near_parts.append(part)
         gathered = lax.dynamic_update_slice_in_dim(gathered, part[0:1], mask, 0)
         gathered = lax.dynamic_update_slice_in_dim(gathered, part[1:2], 4 + mask, 0)
-    near_parts = [near_parts[mask] for mask in (1, 2, 3)]
 
     half = gathered.reshape(2, ranks // 2, seqs, LANES)
     beyond = 1 - lax.bitwise_xor(lax.shift_right_logical(rank, 2), mine)
@@ -633,7 +665,7 @@
         out_shape=like(homolog_matrix.shape, BF16),
         compiler_params=limit,
         name="gradient",
-    )(gathered, outer, keep, beyond_two, near_parts, normed, inv_std, gain, spread_w)
+    )(gathered, outer_near, outer_far, keep, near_parts, normed, inv_std, gain, spread_w)
 
     pair_delta = pl.pallas_call(
         functools.partial(small_pair_kernel, scale),

time: 19.7 us -> 19.5 us (0.990)
  waiting for transfers between devices: 5.63 us -> 3.18 us
  local copies, waits for them, and re-layouts: 0.06 us -> 0.77 us
  Pallas kernels: 5.28 us -> 5.96 us
  starting transfers between devices: 7.88 us -> 8.52 us
    ppermute x4, waiting for transfers between devices: 5.57 us -> 3.12 us  [swap_over(): lax.ppermute(value, 'res', [(source, source ^ mask) for source in range(r...]
    slice x1 -> x2, local copies, waits for them, and re-layouts: 0.01 us -> 0.69 us  [small_slice(): beyond_two[1:2]]
    pallas_call x2 -> x3, Pallas kernels: 2.81 us -> 3.49 us  [the longest x1 1.49 us: small_slice(): pl.pallas_call(functools.partial(small_own_kernel, scale), in_specs=[vmem...]
    ppermute x4, starting transfers between devices: 7.29 us -> 7.93 us  [swap_over(): lax.ppermute(value, 'res', [(source, source ^ mask) for source in range(r...]
  transfers between devices with their start and end apart: 6 -> 6, of which waited for: 5 -> 5; matrix products, arithmetic and copies ran while one was open for 0% -> 0% of each run, Pallas kernels for 14% -> 21%
where the time goes in v9:
time: 19.5 us; the launch traced here: 19.2 us
  starting transfers between devices  8.52 us (44%)
  Pallas kernels  5.96 us (31%)
  waiting for transfers between devices  3.18 us (16%)
  local copies, waits for them, and re-layouts  0.77 us (4%)
  between operations  0.73 us (4%)
    ppermute x4, starting transfers between devices, swap_over(): lax.ppermute(value, 'res', [(source, source ^ mask) for source in range(r...  7.93 us
    ppermute x4, waiting for transfers between devices, swap_over(): lax.ppermute(value, 'res', [(source, source ^ mask) for source in range(r...  3.12 us
    pallas_call x1, Pallas kernels, small_slice(): pl.pallas_call(functools.partial(small_own_kernel, scale), in_specs=[vmem...  1.49 us
    pallas_call x1, Pallas kernels, small_slice(): pl.pallas_call(small_project_kernel, in_specs=[hbm] * 8, out_specs=[vmem]...  1.34 us
    pallas_call x1, Pallas kernels, small_slice(): pl.pallas_call(functools.partial(small_pair_kernel, scale), in_specs=[vme...  1.32 us
    pallas_call x1, Pallas kernels, small_slice(): pl.pallas_call(small_grad_kernel, in_specs=[vmem] * 4 + [[vmem] * 3] + [v...  1.15 us
    slice x2, local copies, waits for them, and re-layouts, small_slice(): beyond_two[1:2]  0.69 us
    pallas_call x1, Pallas kernels, small_slice(): pl.pallas_call(functools.partial(small_partner_kernel, scale, residues),...  0.66 us
  transfers between devices with their start and end apart: 6, of which 5 were waited for; matrix products, arithmetic and copies ran while one was open for 0% of the time, Pallas kernels for 21%

profile of v9, /device:TPU:0, one launch (start us, length us, event | category | flops | bytes accessed | tf_op | source)
XLA Modules:
  0.0 19.2 jit_solution(9706411400601085943)
XLA Ops:
  0.6 0.0 copy-start
  0.6 0.5 %collective-permute-start = (bf16[4,16,128]{2,1,0:T(8,128)(2,1)}, bf16[4,16,128]{2,1,0:T(8,128)(2,1)S(1)}, u32[]{:S(2)}, u32[]{:S(2)}) collective-permute-start(bf16[4,16,128]{2,1,0:T(8,128)(2,1)} %own_ref.1), channel_id=1, source_target_pairs={{0,1},{1,0},{2,3},{3,2},{4,5},{5,4},{6,7},{7,6},{8,9},{9,8},{10,11... | collective-permute-start | bytes 49160 | tf_op jit(solution)/shard_map/ppermute | solution.py:561
  1.2 1.3 %project.1 = (bf16[2,32,128]{2,1,0:T(8,128)(2,1)S(1)}, f32[128,256]{1,0:T(8,128)S(1)}, f32[128,128]{1,0:T(8,128)S(1)}, bf16[256,256]{1,0:T(8,128)(2,1)S(1)}, f32[1,256]{1,0:T(1,128)S(1)}, /*index=5*/f32[1,128]{1,0:T(1,128)S(1)}) custom-call(bf16[32,4,256]{2,1,0:T(4,128)(2,1)} %x_hbm.1, f32[1,256]{1,0:T(1,128)} %bitcast.23, f32[1,256]{1,0:T(1,128)} %bitcast.24, ...), custom_call_target="tpu_custom_call" | custom-call | tf_op jit(solution)/shard_map/project/pallas_call | solution.py:564
  2.5 0.0 collective-permute-done.other_ref
  2.6 0.0 copy-start.1
  2.6 4.4 %collective-permute-start.1 = (bf16[4,32,128]{2,1,0:T(8,128)(2,1)S(1)}, bf16[4,32,128]{2,1,0:T(8,128)(2,1)S(1)}, u32[]{:S(2)}, u32[]{:S(2)}) collective-permute-start(bf16[4,32,128]{2,1,0:T(8,128)(2,1)S(1)} %pad_maximum_fusion.2), channel_id=1, source_target_pairs={{0,8},{2,10},{4,12},{6,14},{8,0},{10,2},{12,4},{14,6},{1,9},{3,11}... | collective-permute-start | bytes 98312 | tf_op jit(solution)/shard_map/ppermute | solution.py:604
  7.0 0.0 copy-done
  7.0 0.0 copy-done.1
  7.0 1.5 %own_pieces.1 = (f32[4,32,128]{2,1,0:T(8,128)S(1)}, bf16[512,128]{1,0:T(8,128)(2,1)S(1)}, bf16[512,128]{1,0:T(8,128)(2,1)S(1)}, bf16[1024,128]{1,0:T(8,128)(2,1)S(1)}) custom-call(bf16[4,16,128]{2,1,0:T(8,128)(2,1)S(1)} %copy-done.1, bf16[4,16,128]{2,1,0:T(8,128)(2,1)S(1)} %collective-permute-done.other_ref, bf16[1024,128]{1,0:T(8,128)(2,1)S(1)} %copy-done, ...), custom_call_target="tpu_custom_call" | custom-call | tf_op jit(solution)/shard_map/own_pieces/pallas_call | solution.py:612
  8.5 0.4 %collective-permute-done.1.got_ref = bf16[4,32,128]{2,1,0:T(8,128)(2,1)S(1)} collective-permute-done((bf16[4,32,128]{2,1,0:T(8,128)(2,1)S(1)}, bf16[4,32,128]{2,1,0:T(8,128)(2,1)S(1)}, u32[]{:S(2)}, u32[]{:S(2)}) %collective-permute-start.1) | collective-permute-done | bytes 32800 | tf_op jit(solution)/shard_map/ppermute | solution.py:604
  8.8 0.0 copy-start.2
  8.8 0.7 %partner_pieces.1 = (bf16[4,3,32,128]{3,2,1,0:T(8,128)(2,1)S(1)}, f32[4,32,128]{2,1,0:T(8,128)S(1)}) custom-call(bf16[4,32,128]{2,1,0:T(8,128)(2,1)S(1)} %collective-permute-done.1.got_ref, bf16[1024,128]{1,0:T(8,128)(2,1)S(1)} %get-tuple-element.15.sorted_w_ref, f32[4,32,128]{2,1,0:T(8,128)S(1)} %get-tuple-element.16.keep_ref, ...), custom_call_target="tpu_custom_call" | custom-call | tf_op jit(solution)/shard_map/partner_pieces/pallas_call | solution.py:627
  9.5 2.8 %collective-permute-start.2 = (bf16[3,32,128]{2,1,0:T(8,128)(2,1)S(1)}, bf16[3,32,128]{2,1,0:T(8,128)(2,1)S(1)}, u32[]{:S(2)}, u32[]{:S(2)}) collective-permute-start(bf16[3,32,128]{2,1,0:T(8,128)(2,1)S(1)} %get-tuple-element.28), channel_id=1, source_target_pairs={{0,6},{2,4},{4,2},{6,0},{8,14},{10,12},{12,10},{14,8},{1,7},{3,5},... | collective-permute-start | bytes 73736 | tf_op jit(solution)/shard_map/ppermute | solution.py:604
  12.3 0.4 %collective-permute-start.3 = (bf16[3,32,128]{2,1,0:T(8,128)(2,1)S(1)}, bf16[3,32,128]{2,1,0:T(8,128)(2,1)S(1)}, u32[]{:S(2)}, u32[]{:S(2)}) collective-permute-start(bf16[3,32,128]{2,1,0:T(8,128)(2,1)S(1)} %get-tuple-element.27), channel_id=1, source_target_pairs={{0,4},{2,6},{4,0},{6,2},{8,12},{10,14},{12,8},{14,10},{1,5},{3,7},... | collective-permute-start | bytes 73736 | tf_op jit(solution)/shard_map/ppermute | solution.py:604
  12.7 0.3 %collective-permute-start.4 = (bf16[3,32,128]{2,1,0:T(8,128)(2,1)S(1)}, bf16[3,32,128]{2,1,0:T(8,128)(2,1)S(1)}, u32[]{:S(2)}, u32[]{:S(2)}) collective-permute-start(bf16[3,32,128]{2,1,0:T(8,128)(2,1)S(1)} %get-tuple-element.26), channel_id=1, source_target_pairs={{0,2},{2,0},{4,6},{6,4},{8,10},{10,8},{12,14},{14,12},{1,3},{3,1},... | collective-permute-start | bytes 73736 | tf_op jit(solution)/shard_map/ppermute | solution.py:604
  13.1 0.0 copy-done.2
  13.1 0.7 %slice-done = bf16[1,32,128]{2,1,0:T(8,128)(2,1)S(1)} async-done(((bf16[4,32,128]{2,1,0:T(8,128)(2,1)}), bf16[1,32,128]{2,1,0:T(8,128)(2,1)S(1)}, s32[]{:S(2)}) %slice-start) | async-done | bytes 8216 | tf_op jit(solution)/shard_map/slice | solution.py:645
  13.8 0.5 %collective-permute-done.2.near_refs_0_ = bf16[3,32,128]{2,1,0:T(8,128)(2,1)S(1)} collective-permute-done((bf16[3,32,128]{2,1,0:T(8,128)(2,1)S(1)}, bf16[3,32,128]{2,1,0:T(8,128)(2,1)S(1)}, u32[]{:S(2)}, u32[]{:S(2)}) %collective-permute-start.2) | collective-permute-done | bytes 24608 | tf_op jit(solution)/shard_map/ppermute | solution.py:604
  14.3 1.8 %collective-permute-done.3.near_refs_1_ = bf16[3,32,128]{2,1,0:T(8,128)(2,1)S(1)} collective-permute-done((bf16[3,32,128]{2,1,0:T(8,128)(2,1)S(1)}, bf16[3,32,128]{2,1,0:T(8,128)(2,1)S(1)}, u32[]{:S(2)}, u32[]{:S(2)}) %collective-permute-start.3) | collective-permute-done | bytes 24608 | tf_op jit(solution)/shard_map/ppermute | solution.py:604
  16.1 0.4 %collective-permute-done.4.near_refs_2_ = bf16[3,32,128]{2,1,0:T(8,128)(2,1)S(1)} collective-permute-done((bf16[3,32,128]{2,1,0:T(8,128)(2,1)S(1)}, bf16[3,32,128]{2,1,0:T(8,128)(2,1)S(1)}, u32[]{:S(2)}, u32[]{:S(2)}) %collective-permute-start.4) | collective-permute-done | bytes 24608 | tf_op jit(solution)/shard_map/ppermute | solution.py:604
  16.6 0.1 collective-permute-start.5
  16.7 1.2 %gradient.1 = bf16[32,4,256]{2,1,0:T(4,128)(2,1)} custom-call(bf16[8,32,128]{2,1,0:T(8,128)(2,1)S(1)} %slice_dynamic-update-slice_fusion.right_ref, bf16[512,128]{1,0:T(8,128)(2,1)S(1)} %get-tuple-element.19.outer_near_ref, bf16[512,128]{1,0:T(8,128)(2,1)S(1)} %get-tuple-element.20.outer_far_ref, f32[4,32,128]{2,1,0:T(8,128)S(1)} %get-tuple-element.21.keep_ref, ...), custom_call_target="tpu_custom_call" | custom-call | tf_op jit(solution)/shard_map/gradient/pallas_call | solution.py:661
  17.8 0.1 collective-permute-done.5.far_ref
  17.9 1.3 %pair.1 = bf16[4,16,128]{2,1,0:T(8,128)(2,1)} custom-call(bf16[8,32,128]{2,1,0:T(8,128)(2,1)S(1)} %slice_dynamic-update-slice_fusion.right_ref, bf16[5,32,128]{2,1,0:T(8,128)(2,1)S(1)} %collective-permute-done.5.far_ref, bf16[32,128]{1,0:T(8,128)(2,1)S(1)} %get-tuple-element.29.left_ref, bf16[1024,128]{1,0:T(8,128)(2,1)S(1)} %get-tuple-element.15.sorted_w_ref, ...), custom_call_target="tpu_custom_call" | custom-call | tf_op jit(solution)/shard_map/pair/pallas_call | solution.py:670
  (15 shorter events, 0.1 us)
Async XLA Ops:
  0.6 6.3 %copy-start = (bf16[1024,128]{1,0:T(8,128)(2,1)S(1)}, bf16[1024,128]{1,0:T(8,128)(2,1)}, u32[]{:S(2)}) copy-start(bf16[1024,128]{1,0:T(8,128)(2,1)} %w_ref.1) | copy-start | bytes 786436
  0.6 1.9 %collective-permute-start = (bf16[4,16,128]{2,1,0:T(8,128)(2,1)}, bf16[4,16,128]{2,1,0:T(8,128)(2,1)S(1)}, u32[]{:S(2)}, u32[]{:S(2)}) collective-permute-start(bf16[4,16,128]{2,1,0:T(8,128)(2,1)} %own_ref.1), channel_id=1, source_target_pairs={{0,1},{1,0},{2,3},{3,2},{4,5},{5,4},{6,7},{7,6},{8,9},{9,8},{10,11... | collective-permute-start | bytes 49160 | tf_op jit(solution)/shard_map/ppermute | solution.py:561
  2.6 4.4 %copy-start.1 = (bf16[4,16,128]{2,1,0:T(8,128)(2,1)S(1)}, bf16[4,16,128]{2,1,0:T(8,128)(2,1)}, u32[]{:S(2)}) copy-start(bf16[4,16,128]{2,1,0:T(8,128)(2,1)} %own_ref.1) | copy-start | bytes 49156
  2.6 6.3 %collective-permute-start.1 = (bf16[4,32,128]{2,1,0:T(8,128)(2,1)S(1)}, bf16[4,32,128]{2,1,0:T(8,128)(2,1)S(1)}, u32[]{:S(2)}, u32[]{:S(2)}) collective-permute-start(bf16[4,32,128]{2,1,0:T(8,128)(2,1)S(1)} %pad_maximum_fusion.2), channel_id=1, source_target_pairs={{0,8},{2,10},{4,12},{6,14},{8,0},{10,2},{12,4},{14,6},{1,9},{3,11}... | collective-permute-start | bytes 98312 | tf_op jit(solution)/shard_map/ppermute | solution.py:604
  8.8 4.2 %copy-start.2 = (bf16[4,32,128]{2,1,0:T(8,128)(2,1)}, bf16[4,32,128]{2,1,0:T(8,128)(2,1)S(1)}, u32[]{:S(2)}) copy-start(bf16[4,32,128]{2,1,0:T(8,128)(2,1)S(1)} %collective-permute-done.1.got_ref) | copy-start | bytes 98308
  9.5 4.8 %collective-permute-start.2 = (bf16[3,32,128]{2,1,0:T(8,128)(2,1)S(1)}, bf16[3,32,128]{2,1,0:T(8,128)(2,1)S(1)}, u32[]{:S(2)}, u32[]{:S(2)}) collective-permute-start(bf16[3,32,128]{2,1,0:T(8,128)(2,1)S(1)} %get-tuple-element.28), channel_id=1, source_target_pairs={{0,6},{2,4},{4,2},{6,0},{8,14},{10,12},{12,10},{14,8},{1,7},{3,5},... | collective-permute-start | bytes 73736 | tf_op jit(solution)/shard_map/ppermute | solution.py:604
  12.3 3.8 %collective-permute-start.3 = (bf16[3,32,128]{2,1,0:T(8,128)(2,1)S(1)}, bf16[3,32,128]{2,1,0:T(8,128)(2,1)S(1)}, u32[]{:S(2)}, u32[]{:S(2)}) collective-permute-start(bf16[3,32,128]{2,1,0:T(8,128)(2,1)S(1)} %get-tuple-element.27), channel_id=1, source_target_pairs={{0,4},{2,6},{4,0},{6,2},{8,12},{10,14},{12,8},{14,10},{1,5},{3,7},... | collective-permute-start | bytes 73736 | tf_op jit(solution)/shard_map/ppermute | solution.py:604
  12.7 3.8 %collective-permute-start.4 = (bf16[3,32,128]{2,1,0:T(8,128)(2,1)S(1)}, bf16[3,32,128]{2,1,0:T(8,128)(2,1)S(1)}, u32[]{:S(2)}, u32[]{:S(2)}) collective-permute-start(bf16[3,32,128]{2,1,0:T(8,128)(2,1)S(1)} %get-tuple-element.26), channel_id=1, source_target_pairs={{0,2},{2,0},{4,6},{6,4},{8,10},{10,8},{12,14},{14,12},{1,3},{3,1},... | collective-permute-start | bytes 73736 | tf_op jit(solution)/shard_map/ppermute | solution.py:604
  13.1 0.7 %slice-start = ((bf16[4,32,128]{2,1,0:T(8,128)(2,1)}), bf16[1,32,128]{2,1,0:T(8,128)(2,1)S(1)}, s32[]{:S(2)}) async-start(bf16[4,32,128]{2,1,0:T(8,128)(2,1)} %copy-done.2), calls=%async_computation | async-start | bytes 16384 | tf_op jit(solution)/shard_map/slice | solution.py:645
  16.6 1.3 %collective-permute-start.5 = (bf16[5,32,128]{2,1,0:T(8,128)(2,1)S(1)}, bf16[5,32,128]{2,1,0:T(8,128)(2,1)S(1)}, u32[]{:S(2)}, u32[]{:S(2)}) collective-permute-start(bf16[5,32,128]{2,1,0:T(8,128)(2,1)S(1)} %pad_maximum_fusion.1), channel_id=1, source_target_pairs={{0,1},{1,0},{2,3},{3,2},{4,5},{5,4},{6,7},{7,6},{8,9},{9,8},{10,11... | collective-permute-start | bytes 122888 | tf_op jit(solution)/shard_map/ppermute | solution.py:659

commit v10 on v9

--- a/solution.py
+++ b/solution.py
@@ -345,7 +345,7 @@
 
 def small_project_kernel(
     x_hbm, gain_hbm, offset_hbm, left_w_hbm, left_b_hbm, right_w_hbm, right_b_hbm, pair_offset_hbm,
-    both_ref, normed_ref, inv_std_ref, spread_w_ref, gain_ref, pair_offset_ref,
+    cot_hbm, both_ref, normed_ref, inv_std_ref, spread_w_ref, gain_ref, pair_offset_ref, cot_ref,
     x_ref, offset_ref, left_w_ref, left_b_ref, right_w_ref, right_b_ref, semaphores,
 ):
     copies = start_copies(
@@ -358,6 +358,7 @@
             (right_w_hbm, right_w_ref),
             (right_b_hbm, right_b_ref),
             (pair_offset_hbm, pair_offset_ref),
+            (cot_hbm, cot_ref),
         ),
         semaphores,
     )
@@ -429,12 +430,14 @@
 
 
 def small_partner_kernel(scale, residues, got_ref, sorted_w_ref, keep_ref, both_ref,
-                         leaving_ref, keep_out_ref, turn_ref):
+                         leaving_ref, keep_out_ref, right_ref, turn_ref):
     rank = lax.axis_index("res")
     seqs = got_ref.shape[1]
     cot = got_ref[2:4].reshape(2 * seqs, LANES)
     outer = outer_rows(scale, cot, residues, sorted_w_ref, turn_ref)
     partial = lax.dot_general(got_ref[0], outer, NT, preferred_element_type=F32)
+    right_ref[0] = both_ref[1]
+    right_ref[1] = got_ref[1]
     for place in range(leaving_ref.shape[0]):
         leaving_ref[place, 0] = both_ref[1]
         leaving_ref[place, 1] = got_ref[1]
@@ -561,10 +564,10 @@
     other_cot = lax.ppermute(coupling_cotangent, "seq", swap)
     hbm = pl.BlockSpec(memory_space=pltpu.HBM)
     pin = lambda array: pltpu.with_memory_space_constraint(array, pltpu.HBM)
-    both, normed, inv_std, spread_w, gain, pair_offset = pl.pallas_call(
+    both, normed, inv_std, spread_w, gain, pair_offset, own_cot = pl.pallas_call(
         small_project_kernel,
-        in_specs=[hbm] * 8,
-        out_specs=[vmem] * 6,
+        in_specs=[hbm] * 9,
+        out_specs=[vmem] * 7,
         out_shape=(
             like((2, seqs, LANES), BF16),
             like((rows, features), F32),
@@ -572,6 +575,7 @@
             like((2 * LANES, features), BF16),
             like((1, features), F32),
             like((1, LANES), F32),
+            like(coupling_cotangent.shape, BF16),
         ),
         scratch_shapes=[
             pltpu.VMEM(homolog_matrix.shape, BF16),
@@ -580,7 +584,7 @@
             pltpu.VMEM((1, depth), F32),
             pltpu.VMEM((depth, features), BF16),
             pltpu.VMEM((1, depth), F32),
-            pltpu.SemaphoreType.DMA((8,)),
+            pltpu.SemaphoreType.DMA((9,)),
         ],
         compiler_params=limit,
         name="project",
@@ -596,6 +600,7 @@
                 right_projection_matrix.T,
                 right_offset_vector.reshape(1, -1),
                 coupling_offset.reshape(1, -1),
+                coupling_cotangent,
             )
         ]
     )
@@ -604,7 +609,7 @@
         return lax.ppermute(value, "res", [(source, source ^ mask) for source in range(ranks)])
 
     own_is_near = mine == lax.shift_right_logical(rank, 2)
-    far_cot = jnp.where(own_is_near, other_cot, coupling_cotangent).reshape(2, seqs, LANES)
+    far_cot = jnp.where(own_is_near, other_cot, own_cot).reshape(2, seqs, LANES)
     beyond_two = swap_over(4, jnp.concatenate([both, far_cot]))
 
     half_rows = ranks // 2 * LANES
@@ -622,15 +627,16 @@
         scratch_shapes=[[turn, turn], pltpu.VMEM(coupling_matrix.shape, F32)],
         compiler_params=limit,
         name="own_pieces",
-    )(coupling_cotangent, other_cot, coupling_matrix, both)
-
-    leaving_parts, keep = pl.pallas_call(
+    )(own_cot, other_cot, coupling_matrix, both)
+
+    leaving_parts, keep, right = pl.pallas_call(
         functools.partial(small_partner_kernel, scale, residues),
         in_specs=[vmem] * 4,
-        out_specs=[vmem] * 2,
+        out_specs=[vmem] * 3,
         out_shape=(
             like((ranks // 2, 3, seqs, LANES), BF16),
             like((ranks // 2, seqs, LANES), F32),
+            like((2, seqs, LANES), BF16),
         ),
         scratch_shapes=[turn],
         compiler_params=limit,
@@ -640,9 +646,9 @@
     left = both[0]
     gathered = jnp.concatenate(
         [
-            both[1:2],
+            right[0:1],
             jnp.zeros((3, seqs, LANES), BF16),
-            beyond_two[1:2],
+            right[1:2],
             jnp.zeros((3, seqs, LANES), BF16),
         ]
     )

time: 19.5 us -> 18.8 us (0.964)
  waiting for transfers between devices: 3.18 us -> 4.02 us
  starting transfers between devices: 8.52 us -> 7.81 us
  local copies, waits for them, and re-layouts: 0.77 us -> 0.07 us
    ppermute x4, waiting for transfers between devices: 3.12 us -> 3.96 us  [swap_over(): lax.ppermute(value, 'res', [(source, source ^ mask) for source in range(r...]
    ppermute x4, starting transfers between devices: 7.93 us -> 7.23 us  [swap_over(): lax.ppermute(value, 'res', [(source, source ^ mask) for source in range(r...]
    slice x2 -> x1, local copies, waits for them, and re-layouts: 0.69 us -> 0.01 us  [small_slice(): right[0:1]]
where the time goes in v10:
time: 18.8 us; the launch traced here: 18.6 us
  starting transfers between devices  7.81 us (42%)
  Pallas kernels  5.97 us (32%)
  waiting for transfers between devices  4.02 us (21%)
  between operations  0.72 us (4%)
    ppermute x4, starting transfers between devices, swap_over(): lax.ppermute(value, 'res', [(source, source ^ mask) for source in range(r...  7.23 us
    ppermute x4, waiting for transfers between devices, swap_over(): lax.ppermute(value, 'res', [(source, source ^ mask) for source in range(r...  3.96 us
    pallas_call x1, Pallas kernels, small_slice(): pl.pallas_call(functools.partial(small_own_kernel, scale), in_specs=[vmem...  1.49 us
    pallas_call x1, Pallas kernels, small_slice(): pl.pallas_call(small_project_kernel, in_specs=[hbm] * 9, out_specs=[vmem]...  1.35 us
    pallas_call x1, Pallas kernels, small_slice(): pl.pallas_call(functools.partial(small_pair_kernel, scale), in_specs=[vme...  1.32 us
    pallas_call x1, Pallas kernels, small_slice(): pl.pallas_call(small_grad_kernel, in_specs=[vmem] * 4 + [[vmem] * 3] + [v...  1.15 us
    pallas_call x1, Pallas kernels, small_slice(): pl.pallas_call(functools.partial(small_partner_kernel, scale, residues),...  0.66 us
    ppermute x1, starting transfers between devices, small_slice(): other_cot = lax.ppermute(coupling_cotangent, 'seq', swap)  0.52 us
  transfers between devices with their start and end apart: 6, of which 5 were waited for; matrix products, arithmetic and copies ran while one was open for 0% of the time, Pallas kernels for 21%

profile of v10, /device:TPU:0, one launch (start us, length us, event | category | flops | bytes accessed | tf_op | source)
XLA Modules:
  0.0 18.6 jit_solution(9039644414986803597)
XLA Ops:
  0.6 0.0 copy-start
  0.6 0.5 %collective-permute-start = (bf16[4,16,128]{2,1,0:T(8,128)(2,1)}, bf16[4,16,128]{2,1,0:T(8,128)(2,1)S(1)}, u32[]{:S(2)}, u32[]{:S(2)}) collective-permute-start(bf16[4,16,128]{2,1,0:T(8,128)(2,1)} %cot_hbm.1), channel_id=1, source_target_pairs={{0,1},{1,0},{2,3},{3,2},{4,5},{5,4},{6,7},{7,6},{8,9},{9,8},{10,11... | collective-permute-start | bytes 49160 | tf_op jit(solution)/shard_map/ppermute | solution.py:564
  1.2 1.4 %project.1 = (bf16[2,32,128]{2,1,0:T(8,128)(2,1)S(1)}, f32[128,256]{1,0:T(8,128)S(1)}, f32[128,128]{1,0:T(8,128)S(1)}, bf16[256,256]{1,0:T(8,128)(2,1)S(1)}, f32...) custom-call(bf16[32,4,256]{2,1,0:T(4,128)(2,1)} %x_hbm.1, f32[1,256]{1,0:T(1,128)} %bitcast.23, ...), custom_call_target="tpu_custom_call" | custom-call | tf_op jit(solution)/shard_map/project/pallas_call | solution.py:567
  2.5 0.0 collective-permute-done.other_ref
  2.6 3.7 %collective-permute-start.1 = (bf16[4,32,128]{2,1,0:T(8,128)(2,1)S(1)}, bf16[4,32,128]{2,1,0:T(8,128)(2,1)S(1)}, u32[]{:S(2)}, u32[]{:S(2)}) collective-permute-start(bf16[4,32,128]{2,1,0:T(8,128)(2,1)S(1)} %pad_maximum_fusion.2), channel_id=1, source_target_pairs={{0,8},{2,10},{4,12},{6,14},{8,0},{10,2},{12,4},{14,6},{1,9},{3,11}... | collective-permute-start | bytes 98312 | tf_op jit(solution)/shard_map/ppermute | solution.py:609
  6.2 0.0 copy-done
  6.2 1.5 %own_pieces.1 = (f32[4,32,128]{2,1,0:T(8,128)S(1)}, bf16[512,128]{1,0:T(8,128)(2,1)S(1)}, bf16[512,128]{1,0:T(8,128)(2,1)S(1)}, bf16[1024,128]{1,0:T(8,128)(2,1)S(1)}) custom-call(bf16[4,16,128]{2,1,0:T(8,128)(2,1)S(1)} %get-tuple-element.17.own_ref, bf16[4,16,128]{2,1,0:T(8,128)(2,1)S(1)} %collective-permute-done.other_ref, bf16[1024,128]{1,0:T(8,128)(2,1)S(1)} %copy-done, ...), custom_call_target="tpu_custom_call" | custom-call | tf_op jit(solution)/shard_map/own_pieces/pallas_call | solution.py:617
  7.7 0.5 %collective-permute-done.1.got_ref = bf16[4,32,128]{2,1,0:T(8,128)(2,1)S(1)} collective-permute-done((bf16[4,32,128]{2,1,0:T(8,128)(2,1)S(1)}, bf16[4,32,128]{2,1,0:T(8,128)(2,1)S(1)}, u32[]{:S(2)}, u32[]{:S(2)}) %collective-permute-start.1) | collective-permute-done | bytes 32800 | tf_op jit(solution)/shard_map/ppermute | solution.py:609
  8.3 0.7 %partner_pieces.1 = (bf16[4,3,32,128]{3,2,1,0:T(8,128)(2,1)S(1)}, f32[4,32,128]{2,1,0:T(8,128)S(1)}, bf16[2,32,128]{2,1,0:T(8,128)(2,1)S(1)}) custom-call(bf16[4,32,128]{2,1,0:T(8,128)(2,1)S(1)} %collective-permute-done.1.got_ref, bf16[1024,128]{1,0:T(8,128)(2,1)S(1)} %get-tuple-element.18.sorted_w_ref, f32[4,32,128]{2,1,0:T(8,128)S(1)} %get-tuple-element.19.keep_ref, ...), custom_call_target="tpu_custom_call" | custom-call | tf_op jit(solution)/shard_map/partner_pieces/pallas_call | solution.py:632
  9.0 2.8 %collective-permute-start.2 = (bf16[3,32,128]{2,1,0:T(8,128)(2,1)S(1)}, bf16[3,32,128]{2,1,0:T(8,128)(2,1)S(1)}, u32[]{:S(2)}, u32[]{:S(2)}) collective-permute-start(bf16[3,32,128]{2,1,0:T(8,128)(2,1)S(1)} %get-tuple-element.32), channel_id=1, source_target_pairs={{0,6},{2,4},{4,2},{6,0},{8,14},{10,12},{12,10},{14,8},{1,7},{3,5},... | collective-permute-start | bytes 73736 | tf_op jit(solution)/shard_map/ppermute | solution.py:609
  11.7 0.4 %collective-permute-start.3 = (bf16[3,32,128]{2,1,0:T(8,128)(2,1)S(1)}, bf16[3,32,128]{2,1,0:T(8,128)(2,1)S(1)}, u32[]{:S(2)}, u32[]{:S(2)}) collective-permute-start(bf16[3,32,128]{2,1,0:T(8,128)(2,1)S(1)} %get-tuple-element.31), channel_id=1, source_target_pairs={{0,4},{2,6},{4,0},{6,2},{8,12},{10,14},{12,8},{14,10},{1,5},{3,7},... | collective-permute-start | bytes 73736 | tf_op jit(solution)/shard_map/ppermute | solution.py:609
  12.2 0.4 %collective-permute-start.4 = (bf16[3,32,128]{2,1,0:T(8,128)(2,1)S(1)}, bf16[3,32,128]{2,1,0:T(8,128)(2,1)S(1)}, u32[]{:S(2)}, u32[]{:S(2)}) collective-permute-start(bf16[3,32,128]{2,1,0:T(8,128)(2,1)S(1)} %get-tuple-element.30), channel_id=1, source_target_pairs={{0,2},{2,0},{4,6},{6,4},{8,10},{10,8},{12,14},{14,12},{1,3},{3,1},... | collective-permute-start | bytes 73736 | tf_op jit(solution)/shard_map/ppermute | solution.py:609
  12.5 1.5 %collective-permute-done.2.near_refs_0_ = bf16[3,32,128]{2,1,0:T(8,128)(2,1)S(1)} collective-permute-done((bf16[3,32,128]{2,1,0:T(8,128)(2,1)S(1)}, bf16[3,32,128]{2,1,0:T(8,128)(2,1)S(1)}, u32[]{:S(2)}, u32[]{:S(2)}) %collective-permute-start.2) | collective-permute-done | bytes 24608 | tf_op jit(solution)/shard_map/ppermute | solution.py:609
  14.0 1.5 %collective-permute-done.3.near_refs_1_ = bf16[3,32,128]{2,1,0:T(8,128)(2,1)S(1)} collective-permute-done((bf16[3,32,128]{2,1,0:T(8,128)(2,1)S(1)}, bf16[3,32,128]{2,1,0:T(8,128)(2,1)S(1)}, u32[]{:S(2)}, u32[]{:S(2)}) %collective-permute-start.3) | collective-permute-done | bytes 24608 | tf_op jit(solution)/shard_map/ppermute | solution.py:609
  15.6 0.4 %collective-permute-done.4.near_refs_2_ = bf16[3,32,128]{2,1,0:T(8,128)(2,1)S(1)} collective-permute-done((bf16[3,32,128]{2,1,0:T(8,128)(2,1)S(1)}, bf16[3,32,128]{2,1,0:T(8,128)(2,1)S(1)}, u32[]{:S(2)}, u32[]{:S(2)}) %collective-permute-start.4) | collective-permute-done | bytes 24608 | tf_op jit(solution)/shard_map/ppermute | solution.py:609
  16.0 0.1 collective-permute-start.5
  16.1 1.2 %gradient.1 = bf16[32,4,256]{2,1,0:T(4,128)(2,1)} custom-call(bf16[8,32,128]{2,1,0:T(8,128)(2,1)S(1)} %slice_dynamic-update-slice_fusion.right_ref, bf16[512,128]{1,0:T(8,128)(2,1)S(1)} %get-tuple-element.23.outer_near_ref, bf16[512,128]{1,0:T(8,128)(2,1)S(1)} %get-tuple-element.24.outer_far_ref, f32[4,32,128]{2,1,0:T(8,128)S(1)} %get-tuple-element.25.keep_ref, ...), custom_call_target="tpu_custom_call" | custom-call | tf_op jit(solution)/shard_map/gradient/pallas_call | solution.py:667
  17.3 0.1 collective-permute-done.5.far_ref
  17.3 1.3 %pair.1 = bf16[4,16,128]{2,1,0:T(8,128)(2,1)} custom-call(bf16[8,32,128]{2,1,0:T(8,128)(2,1)S(1)} %slice_dynamic-update-slice_fusion.right_ref, bf16[5,32,128]{2,1,0:T(8,128)(2,1)S(1)} %collective-permute-done.5.far_ref, bf16[32,128]{1,0:T(8,128)(2,1)S(1)} %get-tuple-element.33.left_ref, bf16[1024,128]{1,0:T(8,128)(2,1)S(1)} %get-tuple-element.18.sorted_w_ref, ...), custom_call_target="tpu_custom_call" | custom-call | tf_op jit(solution)/shard_map/pair/pallas_call | solution.py:676
  (15 shorter events, 0.1 us)
Async XLA Ops:
  0.6 5.6 %copy-start = (bf16[1024,128]{1,0:T(8,128)(2,1)S(1)}, bf16[1024,128]{1,0:T(8,128)(2,1)}, u32[]{:S(2)}) copy-start(bf16[1024,128]{1,0:T(8,128)(2,1)} %w_ref.1) | copy-start | bytes 786436
  0.6 1.9 %collective-permute-start = (bf16[4,16,128]{2,1,0:T(8,128)(2,1)}, bf16[4,16,128]{2,1,0:T(8,128)(2,1)S(1)}, u32[]{:S(2)}, u32[]{:S(2)}) collective-permute-start(bf16[4,16,128]{2,1,0:T(8,128)(2,1)} %cot_hbm.1), channel_id=1, source_target_pairs={{0,1},{1,0},{2,3},{3,2},{4,5},{5,4},{6,7},{7,6},{8,9},{9,8},{10,11... | collective-permute-start | bytes 49160 | tf_op jit(solution)/shard_map/ppermute | solution.py:564
  2.6 5.7 %collective-permute-start.1 = (bf16[4,32,128]{2,1,0:T(8,128)(2,1)S(1)}, bf16[4,32,128]{2,1,0:T(8,128)(2,1)S(1)}, u32[]{:S(2)}, u32[]{:S(2)}) collective-permute-start(bf16[4,32,128]{2,1,0:T(8,128)(2,1)S(1)} %pad_maximum_fusion.2), channel_id=1, source_target_pairs={{0,8},{2,10},{4,12},{6,14},{8,0},{10,2},{12,4},{14,6},{1,9},{3,11}... | collective-permute-start | bytes 98312 | tf_op jit(solution)/shard_map/ppermute | solution.py:609
  9.0 5.0 %collective-permute-start.2 = (bf16[3,32,128]{2,1,0:T(8,128)(2,1)S(1)}, bf16[3,32,128]{2,1,0:T(8,128)(2,1)S(1)}, u32[]{:S(2)}, u32[]{:S(2)}) collective-permute-start(bf16[3,32,128]{2,1,0:T(8,128)(2,1)S(1)} %get-tuple-element.32), channel_id=1, source_target_pairs={{0,6},{2,4},{4,2},{6,0},{8,14},{10,12},{12,10},{14,8},{1,7},{3,5},... | collective-permute-start | bytes 73736 | tf_op jit(solution)/shard_map/ppermute | solution.py:609
  11.7 3.8 %collective-permute-start.3 = (bf16[3,32,128]{2,1,0:T(8,128)(2,1)S(1)}, bf16[3,32,128]{2,1,0:T(8,128)(2,1)S(1)}, u32[]{:S(2)}, u32[]{:S(2)}) collective-permute-start(bf16[3,32,128]{2,1,0:T(8,128)(2,1)S(1)} %get-tuple-element.31), channel_id=1, source_target_pairs={{0,4},{2,6},{4,0},{6,2},{8,12},{10,14},{12,8},{14,10},{1,5},{3,7},... | collective-permute-start | bytes 73736 | tf_op jit(solution)/shard_map/ppermute | solution.py:609
  12.2 3.8 %collective-permute-start.4 = (bf16[3,32,128]{2,1,0:T(8,128)(2,1)S(1)}, bf16[3,32,128]{2,1,0:T(8,128)(2,1)S(1)}, u32[]{:S(2)}, u32[]{:S(2)}) collective-permute-start(bf16[3,32,128]{2,1,0:T(8,128)(2,1)S(1)} %get-tuple-element.30), channel_id=1, source_target_pairs={{0,2},{2,0},{4,6},{6,4},{8,10},{10,8},{12,14},{14,12},{1,3},{3,1},... | collective-permute-start | bytes 73736 | tf_op jit(solution)/shard_map/ppermute | solution.py:609
  16.0 1.3 %collective-permute-start.5 = (bf16[5,32,128]{2,1,0:T(8,128)(2,1)S(1)}, bf16[5,32,128]{2,1,0:T(8,128)(2,1)S(1)}, u32[]{:S(2)}, u32[]{:S(2)}) collective-permute-start(bf16[5,32,128]{2,1,0:T(8,128)(2,1)S(1)} %pad_maximum_fusion.1), channel_id=1, source_target_pairs={{0,1},{1,0},{2,3},{3,2},{4,5},{5,4},{6,7},{7,6},{8,9},{9,8},{10,11... | collective-permute-start | bytes 122888 | tf_op jit(solution)/shard_map/ppermute | solution.py:665

commit v11 on v10

--- a/solution.py
+++ b/solution.py
@@ -31,6 +31,11 @@
     middle = rest.astype(BF16)
     low = (rest - middle.astype(F32)).astype(BF16)
     return top, middle, low
+
+
+def split_two(value):
+    top = value.astype(BF16)
+    return top, (value - top.astype(F32)).astype(BF16)
 
 
 def normalise(rows):
@@ -348,47 +353,52 @@
     cot_hbm, both_ref, normed_ref, inv_std_ref, spread_w_ref, gain_ref, pair_offset_ref, cot_ref,
     x_ref, offset_ref, left_w_ref, left_b_ref, right_w_ref, right_b_ref, semaphores,
 ):
+    seqs, residues, _ = x_ref.shape
+    depth = left_w_ref.shape[0]
+    parts = 4
+    part = seqs // parts
     copies = start_copies(
-        (
-            (x_hbm, x_ref),
+        tuple(
+            (x_hbm.at[pl.ds(place * part, part)], x_ref.at[pl.ds(place * part, part)])
+            for place in range(parts)
+        )
+        + (
+            (left_w_hbm, left_w_ref),
+            (right_w_hbm, right_w_ref),
             (gain_hbm, gain_ref),
             (offset_hbm, offset_ref),
-            (left_w_hbm, left_w_ref),
             (left_b_hbm, left_b_ref),
-            (right_w_hbm, right_w_ref),
             (right_b_hbm, right_b_ref),
+            (cot_hbm, cot_ref),
             (pair_offset_hbm, pair_offset_ref),
-            (cot_hbm, cot_ref),
         ),
         semaphores,
     )
-    seqs, residues, _ = x_ref.shape
-    depth = left_w_ref.shape[0]
-    copies[0].wait()
+    for copy in copies[:parts]:
+        copy.wait()
     normed, inv_std = normalise(residue_rows(x_ref))
-    for copy in copies[1:]:
+    for copy in copies[parts:]:
         copy.wait()
     ln_out = (normed * gain_ref[...] + offset_ref[...]).astype(BF16)
     blocks = lane_block((seqs, LANES), depth)
-    spread = []
-    for place, (weight_ref, bias_ref) in enumerate(
-        ((left_w_ref, left_b_ref), (right_w_ref, right_b_ref))
-    ):
-        weight = jnp.concatenate([weight_ref[...]] * residues, axis=0)
-        spread.append(weight)
+    weight = jnp.concatenate(
+        [left_w_ref[...]] * residues + [right_w_ref[...]] * residues, axis=0
+    )
+    wide = lax.dot_general(ln_out, weight, NT, preferred_element_type=F32)
+    for place, bias_ref in enumerate((left_b_ref, right_b_ref)):
         bias = jnp.concatenate([bias_ref[...]] * residues, axis=1)
-        wide = lax.dot_general(ln_out, weight, NT, preferred_element_type=F32)
-        own = pick(blocks, [wide[p * seqs : (p + 1) * seqs] for p in range(residues)])
+        lanes = wide[:, place * LANES : (place + 1) * LANES]
+        own = pick(blocks, [lanes[p * seqs : (p + 1) * seqs] for p in range(residues)])
         both_ref[place] = (own + bias).astype(BF16)
     normed_ref[...] = normed
     inv_std_ref[...] = jnp.broadcast_to(inv_std, inv_std_ref.shape)
-    spread_w_ref[...] = jnp.concatenate(spread, axis=0)
-
-
-def outer_rows(scale, cot, residues, sorted_w_ref, turn_ref):
+    spread_w_ref[...] = weight
+
+
+def outer_rows(scale, cot, residues, sorted_wt_ref, turn_ref):
     columns = cot.shape[0] // residues
     depth = LANES // residues
-    flat = lax.dot_general(cot, sorted_w_ref[...], NT, preferred_element_type=F32) * scale
+    flat = jnp.dot(cot, sorted_wt_ref[...], preferred_element_type=F32) * scale
     blocks = lane_block((columns, LANES), depth)
     for tile in range(depth * depth // LANES):
         block = flat[:, tile * LANES : (tile + 1) * LANES]
@@ -405,7 +415,7 @@
 
 
 def small_own_kernel(scale, own_ref, other_ref, w_ref, both_ref,
-                     keep_ref, outer_near_ref, outer_far_ref, sorted_w_ref, turn_refs, wide_ref):
+                     keep_ref, outer_near_ref, outer_far_ref, sorted_w_ref, sorted_wt_ref, turn_refs, wide_ref):
     residues, columns, _ = own_ref.shape
     depth = LANES // residues
     wide_ref[...] = w_ref[...].astype(F32)
@@ -413,28 +423,29 @@
         sorted_w_ref[d * depth : (d + 1) * depth, :] = wide_ref[
             pl.ds(d, depth, stride=depth), :
         ].astype(BF16)
+    sorted_wt_ref[...] = sorted_w_ref[...].T
     rank = lax.axis_index("res")
     own_is_near = lax.axis_index("seq") == lax.shift_right_logical(rank, 2)
     own = own_ref[...].reshape(residues * columns, LANES)
     other = other_ref[...].reshape(residues * columns, LANES)
     near = outer_rows(
-        scale, jnp.where(own_is_near, own, other), residues, sorted_w_ref, turn_refs[0]
+        scale, jnp.where(own_is_near, own, other), residues, sorted_wt_ref, turn_refs[0]
     )
     outer_near_ref[...] = near
     partial = lax.dot_general(both_ref[0], near, NT, preferred_element_type=F32)
     for place in range(columns // residues):
         keep_ref[lax.bitwise_xor(rank & 3, place)] = partial[:, place * LANES : (place + 1) * LANES]
     outer_far_ref[...] = outer_rows(
-        scale, jnp.where(own_is_near, other, own), residues, sorted_w_ref, turn_refs[1]
-    )
-
-
-def small_partner_kernel(scale, residues, got_ref, sorted_w_ref, keep_ref, both_ref,
+        scale, jnp.where(own_is_near, other, own), residues, sorted_wt_ref, turn_refs[1]
+    )
+
+
+def small_partner_kernel(scale, residues, got_ref, sorted_wt_ref, keep_ref, both_ref,
                          leaving_ref, keep_out_ref, right_ref, turn_ref):
     rank = lax.axis_index("res")
     seqs = got_ref.shape[1]
     cot = got_ref[2:4].reshape(2 * seqs, LANES)
-    outer = outer_rows(scale, cot, residues, sorted_w_ref, turn_ref)
+    outer = outer_rows(scale, cot, residues, sorted_wt_ref, turn_ref)
     partial = lax.dot_general(got_ref[0], outer, NT, preferred_element_type=F32)
     right_ref[0] = both_ref[1]
     right_ref[1] = got_ref[1]
@@ -474,9 +485,9 @@
         axis=0,
     )
     rows = residues * seqs
-    parts = jnp.concatenate(split_three(spread), axis=0)
+    parts = jnp.concatenate(split_two(spread), axis=0)
     ln_cot = jnp.dot(parts, spread_w_ref[...], preferred_element_type=F32)
-    ln_cot = ln_cot[0:rows] + (ln_cot[rows : 2 * rows] + ln_cot[2 * rows : 3 * rows])
+    ln_cot = ln_cot[0:rows] + ln_cot[rows : 2 * rows]
     gained = ln_cot * gain_ref[...]
     normed = normed_ref[...]
     grad = inv_std_ref[:, 0:1] * (
@@ -531,9 +542,9 @@
         )
     flat = jnp.concatenate(tiles, axis=1)
     rows = residues * columns
-    parts = jnp.concatenate(split_three(flat), axis=0)
+    parts = jnp.concatenate(split_two(flat), axis=0)
     pair = jnp.dot(parts, sorted_w_ref[...], preferred_element_type=F32)
-    pair = pair[0:rows] + (pair[rows : 2 * rows] + pair[2 * rows : 3 * rows])
+    pair = pair[0:rows] + pair[rows : 2 * rows]
     pair_ref[...] = (pair + offset_ref[...]).astype(BF16).reshape(pair_ref.shape)
 
 
@@ -584,7 +595,7 @@
             pltpu.VMEM((1, depth), F32),
             pltpu.VMEM((depth, features), BF16),
             pltpu.VMEM((1, depth), F32),
-            pltpu.SemaphoreType.DMA((9,)),
+            pltpu.SemaphoreType.DMA((12,)),
         ],
         compiler_params=limit,
         name="project",
@@ -614,15 +625,16 @@
 
     half_rows = ranks // 2 * LANES
     turn = pltpu.VMEM((half_rows, LANES), F32)
-    keep, outer_near, outer_far, sorted_w = pl.pallas_call(
+    keep, outer_near, outer_far, sorted_w, sorted_wt = pl.pallas_call(
         functools.partial(small_own_kernel, scale),
         in_specs=[vmem] * 4,
-        out_specs=[vmem] * 4,
+        out_specs=[vmem] * 5,
         out_shape=(
             like((ranks // 2, seqs, LANES), F32),
             like((half_rows, LANES), BF16),
             like((half_rows, LANES), BF16),
             like(coupling_matrix.shape, BF16),
+            like(coupling_matrix.shape[::-1], BF16),
         ),
         scratch_shapes=[[turn, turn], pltpu.VMEM(coupling_matrix.shape, F32)],
         compiler_params=limit,
@@ -641,7 +653,7 @@
         scratch_shapes=[turn],
         compiler_params=limit,
         name="partner_pieces",
-    )(beyond_two, sorted_w, keep, both)
+    )(beyond_two, sorted_wt, keep, both)
 
     left = both[0]
     gathered = jnp.concatenate(

time: 18.8 us -> 18.7 us (level)
  no operation moved by 1% of the time
where the time goes in v11:
time: 18.7 us; the launch traced here: 18.6 us
  starting transfers between devices  7.83 us (42%)
  Pallas kernels  5.85 us (31%)
  waiting for transfers between devices  4.06 us (22%)
  between operations  0.73 us (4%)
    ppermute x4, starting transfers between devices, swap_over(): lax.ppermute(value, 'res', [(source, source ^ mask) for source in range(r...  7.24 us
    ppermute x4, waiting for transfers between devices, swap_over(): lax.ppermute(value, 'res', [(source, source ^ mask) for source in range(r...  3.96 us
    pallas_call x1, Pallas kernels, small_slice(): pl.pallas_call(functools.partial(small_own_kernel, scale), in_specs=[vmem...  1.49 us
    pallas_call x1, Pallas kernels, small_slice(): pl.pallas_call(small_project_kernel, in_specs=[hbm] * 9, out_specs=[vmem]...  1.32 us
    pallas_call x1, Pallas kernels, small_slice(): pl.pallas_call(functools.partial(small_pair_kernel, scale), in_specs=[vme...  1.3 us
    pallas_call x1, Pallas kernels, small_slice(): pl.pallas_call(small_grad_kernel, in_specs=[vmem] * 4 + [[vmem] * 3] + [v...  1.11 us
    pallas_call x1, Pallas kernels, small_slice(): pl.pallas_call(functools.partial(small_partner_kernel, scale, residues),...  0.63 us
    ppermute x1, starting transfers between devices, small_slice(): other_cot = lax.ppermute(coupling_cotangent, 'seq', swap)  0.52 us
  transfers between devices with their start and end apart: 6, of which 5 were waited for; matrix products, arithmetic and copies ran while one was open for 0% of the time, Pallas kernels for 21%

profile of v11, /device:TPU:0, one launch (start us, length us, event | category | flops | bytes accessed | tf_op | source)
XLA Modules:
  0.0 18.6 jit_solution(13719533410768263326)
XLA Ops:
  0.6 0.0 copy-start
  0.6 0.5 %collective-permute-start = (bf16[4,16,128]{2,1,0:T(8,128)(2,1)}, bf16[4,16,128]{2,1,0:T(8,128)(2,1)S(1)}, u32[]{:S(2)}, u32[]{:S(2)}) collective-permute-start(bf16[4,16,128]{2,1,0:T(8,128)(2,1)} %cot_hbm.1), channel_id=1, source_target_pairs={{0,1},{1,0},{2,3},{3,2},{4,5},{5,4},{6,7},{7,6},{8,9},{9,8},{10,11... | collective-permute-start | bytes 49160 | tf_op jit(solution)/shard_map/ppermute | solution.py:575
  1.2 1.3 %project.1 = (bf16[2,32,128]{2,1,0:T(8,128)(2,1)S(1)}, f32[128,256]{1,0:T(8,128)S(1)}, f32[128,128]{1,0:T(8,128)S(1)}, bf16[256,256]{1,0:T(8,128)(2,1)S(1)}, f32...) custom-call(bf16[32,4,256]{2,1,0:T(4,128)(2,1)} %x_hbm.1, f32[1,256]{1,0:T(1,128)} %bitcast.23, ...), custom_call_target="tpu_custom_call" | custom-call | tf_op jit(solution)/shard_map/project/pallas_call | solution.py:578
  2.5 0.0 collective-permute-done.other_ref
  2.5 3.7 %collective-permute-start.1 = (bf16[4,32,128]{2,1,0:T(8,128)(2,1)S(1)}, bf16[4,32,128]{2,1,0:T(8,128)(2,1)S(1)}, u32[]{:S(2)}, u32[]{:S(2)}) collective-permute-start(bf16[4,32,128]{2,1,0:T(8,128)(2,1)S(1)} %pad_maximum_fusion.2), channel_id=1, source_target_pairs={{0,8},{2,10},{4,12},{6,14},{8,0},{10,2},{12,4},{14,6},{1,9},{3,11}... | collective-permute-start | bytes 98312 | tf_op jit(solution)/shard_map/ppermute | solution.py:620
  6.2 0.0 copy-done
  6.2 1.5 %own_pieces.1 = (f32[4,32,128]{2,1,0:T(8,128)S(1)}, bf16[512,128]{1,0:T(8,128)(2,1)S(1)}, bf16[512,128]{1,0:T(8,128)(2,1)S(1)}, bf16[1024,128]{1,0:T(8,128)(2,1)S(1)}, bf16[128,1024]{1,0:T(8,128)(2,1)S(1)}) custom-call(bf16[4,16,128]{2,1,0:T(8,128)(2,1)S(1)} %get-tuple-element.18.own_ref, bf16[4,16,128]{2,1,0:T(8,128)(2,1)S(1)} %collective-permute-done.other_ref, ...), custom_call_target="tpu_custom_call" | custom-call | tf_op jit(solution)/shard_map/own_pieces/pallas_call | solution.py:628
  7.7 0.5 %collective-permute-done.1.got_ref = bf16[4,32,128]{2,1,0:T(8,128)(2,1)S(1)} collective-permute-done((bf16[4,32,128]{2,1,0:T(8,128)(2,1)S(1)}, bf16[4,32,128]{2,1,0:T(8,128)(2,1)S(1)}, u32[]{:S(2)}, u32[]{:S(2)}) %collective-permute-start.1) | collective-permute-done | bytes 32800 | tf_op jit(solution)/shard_map/ppermute | solution.py:620
  8.2 0.6 %partner_pieces.1 = (bf16[4,3,32,128]{3,2,1,0:T(8,128)(2,1)S(1)}, f32[4,32,128]{2,1,0:T(8,128)S(1)}, bf16[2,32,128]{2,1,0:T(8,128)(2,1)S(1)}) custom-call(bf16[4,32,128]{2,1,0:T(8,128)(2,1)S(1)} %collective-permute-done.1.got_ref, bf16[128,1024]{1,0:T(8,128)(2,1)S(1)} %get-tuple-element.19.sorted_wt_ref, f32[4,32,128]{2,1,0:T(8,128)S(1)} %get-tuple-element.20.keep_ref, ...), custom_call_target="tpu_custom_call" | custom-call | tf_op jit(solution)/shard_map/partner_pieces/pallas_call | solution.py:644
  8.9 2.8 %collective-permute-start.2 = (bf16[3,32,128]{2,1,0:T(8,128)(2,1)S(1)}, bf16[3,32,128]{2,1,0:T(8,128)(2,1)S(1)}, u32[]{:S(2)}, u32[]{:S(2)}) collective-permute-start(bf16[3,32,128]{2,1,0:T(8,128)(2,1)S(1)} %get-tuple-element.34), channel_id=1, source_target_pairs={{0,6},{2,4},{4,2},{6,0},{8,14},{10,12},{12,10},{14,8},{1,7},{3,5},... | collective-permute-start | bytes 73736 | tf_op jit(solution)/shard_map/ppermute | solution.py:620
  11.7 0.4 %collective-permute-start.3 = (bf16[3,32,128]{2,1,0:T(8,128)(2,1)S(1)}, bf16[3,32,128]{2,1,0:T(8,128)(2,1)S(1)}, u32[]{:S(2)}, u32[]{:S(2)}) collective-permute-start(bf16[3,32,128]{2,1,0:T(8,128)(2,1)S(1)} %get-tuple-element.33), channel_id=1, source_target_pairs={{0,4},{2,6},{4,0},{6,2},{8,12},{10,14},{12,8},{14,10},{1,5},{3,7},... | collective-permute-start | bytes 73736 | tf_op jit(solution)/shard_map/ppermute | solution.py:620
  12.1 0.3 %collective-permute-start.4 = (bf16[3,32,128]{2,1,0:T(8,128)(2,1)S(1)}, bf16[3,32,128]{2,1,0:T(8,128)(2,1)S(1)}, u32[]{:S(2)}, u32[]{:S(2)}) collective-permute-start(bf16[3,32,128]{2,1,0:T(8,128)(2,1)S(1)} %get-tuple-element.32), channel_id=1, source_target_pairs={{0,2},{2,0},{4,6},{6,4},{8,10},{10,8},{12,14},{14,12},{1,3},{3,1},... | collective-permute-start | bytes 73736 | tf_op jit(solution)/shard_map/ppermute | solution.py:620
  12.5 1.5 %collective-permute-done.2.near_refs_0_ = bf16[3,32,128]{2,1,0:T(8,128)(2,1)S(1)} collective-permute-done((bf16[3,32,128]{2,1,0:T(8,128)(2,1)S(1)}, bf16[3,32,128]{2,1,0:T(8,128)(2,1)S(1)}, u32[]{:S(2)}, u32[]{:S(2)}) %collective-permute-start.2) | collective-permute-done | bytes 24608 | tf_op jit(solution)/shard_map/ppermute | solution.py:620
  14.0 1.5 %collective-permute-done.3.near_refs_1_ = bf16[3,32,128]{2,1,0:T(8,128)(2,1)S(1)} collective-permute-done((bf16[3,32,128]{2,1,0:T(8,128)(2,1)S(1)}, bf16[3,32,128]{2,1,0:T(8,128)(2,1)S(1)}, u32[]{:S(2)}, u32[]{:S(2)}) %collective-permute-start.3) | collective-permute-done | bytes 24608 | tf_op jit(solution)/shard_map/ppermute | solution.py:620
  15.5 0.4 %collective-permute-done.4.near_refs_2_ = bf16[3,32,128]{2,1,0:T(8,128)(2,1)S(1)} collective-permute-done((bf16[3,32,128]{2,1,0:T(8,128)(2,1)S(1)}, bf16[3,32,128]{2,1,0:T(8,128)(2,1)S(1)}, u32[]{:S(2)}, u32[]{:S(2)}) %collective-permute-start.4) | collective-permute-done | bytes 24608 | tf_op jit(solution)/shard_map/ppermute | solution.py:620
  16.0 0.1 collective-permute-start.5
  16.1 1.1 %gradient.1 = bf16[32,4,256]{2,1,0:T(4,128)(2,1)} custom-call(bf16[8,32,128]{2,1,0:T(8,128)(2,1)S(1)} %slice_dynamic-update-slice_fusion.right_ref, bf16[512,128]{1,0:T(8,128)(2,1)S(1)} %get-tuple-element.25.outer_near_ref, bf16[512,128]{1,0:T(8,128)(2,1)S(1)} %get-tuple-element.26.outer_far_ref, f32[4,32,128]{2,1,0:T(8,128)S(1)} %get-tuple-element.27.keep_ref, ...), custom_call_target="tpu_custom_call" | custom-call | tf_op jit(solution)/shard_map/gradient/pallas_call | solution.py:679
  17.2 0.1 collective-permute-done.5.far_ref
  17.3 1.3 %pair.1 = bf16[4,16,128]{2,1,0:T(8,128)(2,1)} custom-call(bf16[8,32,128]{2,1,0:T(8,128)(2,1)S(1)} %slice_dynamic-update-slice_fusion.right_ref, bf16[5,32,128]{2,1,0:T(8,128)(2,1)S(1)} %collective-permute-done.5.far_ref, bf16[32,128]{1,0:T(8,128)(2,1)S(1)} %get-tuple-element.35.left_ref, bf16[1024,128]{1,0:T(8,128)(2,1)S(1)} %get-tuple-element.23.sorted_w_ref, ...), custom_call_target="tpu_custom_call" | custom-call | tf_op jit(solution)/shard_map/pair/pallas_call | solution.py:688
  (15 shorter events, 0.1 us)
Async XLA Ops:
  0.6 5.6 %copy-start = (bf16[1024,128]{1,0:T(8,128)(2,1)S(1)}, bf16[1024,128]{1,0:T(8,128)(2,1)}, u32[]{:S(2)}) copy-start(bf16[1024,128]{1,0:T(8,128)(2,1)} %w_ref.1) | copy-start | bytes 786436
  0.6 1.9 %collective-permute-start = (bf16[4,16,128]{2,1,0:T(8,128)(2,1)}, bf16[4,16,128]{2,1,0:T(8,128)(2,1)S(1)}, u32[]{:S(2)}, u32[]{:S(2)}) collective-permute-start(bf16[4,16,128]{2,1,0:T(8,128)(2,1)} %cot_hbm.1), channel_id=1, source_target_pairs={{0,1},{1,0},{2,3},{3,2},{4,5},{5,4},{6,7},{7,6},{8,9},{9,8},{10,11... | collective-permute-start | bytes 49160 | tf_op jit(solution)/shard_map/ppermute | solution.py:575
  2.5 5.7 %collective-permute-start.1 = (bf16[4,32,128]{2,1,0:T(8,128)(2,1)S(1)}, bf16[4,32,128]{2,1,0:T(8,128)(2,1)S(1)}, u32[]{:S(2)}, u32[]{:S(2)}) collective-permute-start(bf16[4,32,128]{2,1,0:T(8,128)(2,1)S(1)} %pad_maximum_fusion.2), channel_id=1, source_target_pairs={{0,8},{2,10},{4,12},{6,14},{8,0},{10,2},{12,4},{14,6},{1,9},{3,11}... | collective-permute-start | bytes 98312 | tf_op jit(solution)/shard_map/ppermute | solution.py:620
  8.9 5.0 %collective-permute-start.2 = (bf16[3,32,128]{2,1,0:T(8,128)(2,1)S(1)}, bf16[3,32,128]{2,1,0:T(8,128)(2,1)S(1)}, u32[]{:S(2)}, u32[]{:S(2)}) collective-permute-start(bf16[3,32,128]{2,1,0:T(8,128)(2,1)S(1)} %get-tuple-element.34), channel_id=1, source_target_pairs={{0,6},{2,4},{4,2},{6,0},{8,14},{10,12},{12,10},{14,8},{1,7},{3,5},... | collective-permute-start | bytes 73736 | tf_op jit(solution)/shard_map/ppermute | solution.py:620
  11.7 3.8 %collective-permute-start.3 = (bf16[3,32,128]{2,1,0:T(8,128)(2,1)S(1)}, bf16[3,32,128]{2,1,0:T(8,128)(2,1)S(1)}, u32[]{:S(2)}, u32[]{:S(2)}) collective-permute-start(bf16[3,32,128]{2,1,0:T(8,128)(2,1)S(1)} %get-tuple-element.33), channel_id=1, source_target_pairs={{0,4},{2,6},{4,0},{6,2},{8,12},{10,14},{12,8},{14,10},{1,5},{3,7},... | collective-permute-start | bytes 73736 | tf_op jit(solution)/shard_map/ppermute | solution.py:620
  12.1 3.8 %collective-permute-start.4 = (bf16[3,32,128]{2,1,0:T(8,128)(2,1)S(1)}, bf16[3,32,128]{2,1,0:T(8,128)(2,1)S(1)}, u32[]{:S(2)}, u32[]{:S(2)}) collective-permute-start(bf16[3,32,128]{2,1,0:T(8,128)(2,1)S(1)} %get-tuple-element.32), channel_id=1, source_target_pairs={{0,2},{2,0},{4,6},{6,4},{8,10},{10,8},{12,14},{14,12},{1,3},{3,1},... | collective-permute-start | bytes 73736 | tf_op jit(solution)/shard_map/ppermute | solution.py:620
  16.0 1.3 %collective-permute-start.5 = (bf16[5,32,128]{2,1,0:T(8,128)(2,1)S(1)}, bf16[5,32,128]{2,1,0:T(8,128)(2,1)S(1)}, u32[]{:S(2)}, u32[]{:S(2)}) collective-permute-start(bf16[5,32,128]{2,1,0:T(8,128)(2,1)S(1)} %pad_maximum_fusion.1), channel_id=1, source_target_pairs={{0,1},{1,0},{2,3},{3,2},{4,5},{5,4},{6,7},{7,6},{8,9},{9,8},{10,11... | collective-permute-start | bytes 122888 | tf_op jit(solution)/shard_map/ppermute | solution.py:677

commit v12 on v11

--- a/solution.py
+++ b/solution.py
@@ -441,7 +441,7 @@
 
 
 def small_partner_kernel(scale, residues, got_ref, sorted_wt_ref, keep_ref, both_ref,
-                         leaving_ref, keep_out_ref, right_ref, turn_ref):
+                         leaving_ref, keep_out_ref, right_ref, swap_ref, turn_ref):
     rank = lax.axis_index("res")
     seqs = got_ref.shape[1]
     cot = got_ref[2:4].reshape(2 * seqs, LANES)
@@ -449,6 +449,9 @@
     partial = lax.dot_general(got_ref[0], outer, NT, preferred_element_type=F32)
     right_ref[0] = both_ref[1]
     right_ref[1] = got_ref[1]
+    own_is_near = lax.axis_index("seq") == lax.shift_right_logical(rank, 2)
+    swap_ref[0] = jnp.where(own_is_near, got_ref[1], both_ref[1])
+    swap_ref[1] = both_ref[0]
     for place in range(leaving_ref.shape[0]):
         leaving_ref[place, 0] = both_ref[1]
         leaving_ref[place, 1] = got_ref[1]
@@ -459,21 +462,35 @@
         keep_out_ref[distance] = total
 
 
-def small_grad_kernel(right_ref, outer_near_ref, outer_far_ref, keep_ref, near_refs, normed_ref, inv_std_ref,
-                      gain_ref, spread_w_ref, grad_ref):
-    ranks, seqs, _ = right_ref.shape
-    residues = grad_ref.shape[1]
+def small_finish_kernel(
+    scale, right_ref, part_refs, swapped_ref, swapped_late_ref, both_ref, outer_near_ref, outer_far_ref,
+    keep_ref, normed_ref, inv_std_ref, gain_ref, spread_w_ref, sorted_w_ref, offset_ref,
+    grad_hbm, pair_hbm, grad_ref, pair_ref, near_ref, beyond_ref, turn_ref, semaphores,
+):
+    seqs, residues, _ = grad_ref.shape
+    columns = pair_ref.shape[1]
     depth = LANES // residues
+    ranks = columns // residues
     rank = lax.axis_index("res")
-    places = [lax.bitwise_xor(rank & 3, place) for place in range(ranks // 2)]
+    mine = lax.axis_index("seq")
+    here = rank & 3
+
+    blocks_of = [right_ref] + list(part_refs)
     right_all = jnp.concatenate(
-        [right_ref[place] for place in places] + [right_ref[4 + place] for place in places], axis=1
-    )
-    outer = jnp.concatenate([outer_near_ref[...], outer_far_ref[...]], axis=0)
+        [ref[0] for ref in blocks_of] + [ref[1] for ref in blocks_of], axis=1
+    )
+    spots = [
+        pl.ds(pl.multiple_of(lax.bitwise_xor(here, mask) * LANES, LANES), LANES)
+        for mask in range(ranks)
+    ]
+    outer = jnp.concatenate(
+        [outer_near_ref[spot, :] for spot in spots] + [outer_far_ref[spot, :] for spot in spots],
+        axis=0,
+    )
     left_cot = jnp.dot(right_all, outer, preferred_element_type=F32)
     right_cot = keep_ref[0]
-    for near_ref in near_refs:
-        right_cot = right_cot + near_ref[2].astype(F32)
+    for part_ref in part_refs:
+        right_cot = right_cot + part_ref[2].astype(F32)
     blocks = lane_block((seqs, LANES), depth)
     spread = jnp.concatenate(
         [
@@ -497,24 +514,25 @@
     )
     for place in range(residues):
         grad_ref[:, place, :] = grad[place * seqs : (place + 1) * seqs].astype(BF16)
-
-
-def small_pair_kernel(scale, right_ref, far_ref, left_ref, sorted_w_ref, offset_ref,
-                     pair_ref, turn_ref):
-    residues, columns, _ = pair_ref.shape
-    depth = LANES // residues
-    ranks = columns // residues
-    rank = lax.axis_index("res")
-    base = lax.axis_index("seq") * ranks
-    near, far = [], []
-    for place in range(ranks):
-        distance = lax.bitwise_xor(rank, base + place)
-        near.append(right_ref[distance])
-        far.append(far_ref[distance & (ranks - 1)])
+    grad_copy = pltpu.make_async_copy(grad_ref, grad_hbm, semaphores.at[0])
+    grad_copy.start()
+
+    half = jnp.where(mine == lax.shift_right_logical(rank, 2), 0, 1)
+    for mask, ref in enumerate(blocks_of):
+        near_ref[mask] = ref[half]
+    beyond_ref[0] = swapped_ref[0]
+    beyond_ref[1] = part_refs[0][3]
+    beyond_ref[2] = part_refs[1][3]
+    beyond_ref[3] = swapped_late_ref[...]
+    masks = [lax.bitwise_xor(here, place) for place in range(ranks)]
     right = jnp.concatenate(
-        [jnp.concatenate(near, axis=1), jnp.concatenate(far, axis=1)], axis=0
-    )
-    left = jnp.concatenate([left_ref[...], far_ref[ranks]], axis=0)
+        [
+            jnp.concatenate([ref[mask] for mask in masks], axis=1)
+            for ref in (near_ref, beyond_ref)
+        ],
+        axis=0,
+    )
+    left = jnp.concatenate([both_ref[0], swapped_ref[1]], axis=0)
     turn_ref[...] = lax.dot_general(right, left, TN, preferred_element_type=F32) * scale
     blocks = lane_block((columns, LANES), depth)
     tiles = []
@@ -523,8 +541,8 @@
             turn_ref[pl.ds(tile * residues + e, columns, stride=depth), :]
             for e in range(residues)
         ]
-        rows = jnp.concatenate(pieces, axis=0)
-        turned = [rows] + [pltpu.roll(rows, depth * t, 1) for t in range(1, residues)]
+        lines = jnp.concatenate(pieces, axis=0)
+        turned = [lines] + [pltpu.roll(lines, depth * t, 1) for t in range(1, residues)]
         tiles.append(
             jnp.concatenate(
                 [
@@ -546,6 +564,10 @@
     pair = jnp.dot(parts, sorted_w_ref[...], preferred_element_type=F32)
     pair = pair[0:rows] + pair[rows : 2 * rows]
     pair_ref[...] = (pair + offset_ref[...]).astype(BF16).reshape(pair_ref.shape)
+    pair_copy = pltpu.make_async_copy(pair_ref, pair_hbm, semaphores.at[1])
+    pair_copy.start()
+    grad_copy.wait()
+    pair_copy.wait()
 
 
 def small_slice(
@@ -641,13 +663,14 @@
         name="own_pieces",
     )(own_cot, other_cot, coupling_matrix, both)
 
-    leaving_parts, keep, right = pl.pallas_call(
+    leaving_parts, keep, right, leaving = pl.pallas_call(
         functools.partial(small_partner_kernel, scale, residues),
         in_specs=[vmem] * 4,
-        out_specs=[vmem] * 3,
+        out_specs=[vmem] * 4,
         out_shape=(
             like((ranks // 2, 3, seqs, LANES), BF16),
             like((ranks // 2, seqs, LANES), F32),
+            like((2, seqs, LANES), BF16),
             like((2, seqs, LANES), BF16),
         ),
         scratch_shapes=[turn],
@@ -655,45 +678,49 @@
         name="partner_pieces",
     )(beyond_two, sorted_wt, keep, both)
 
-    left = both[0]
-    gathered = jnp.concatenate(
-        [
-            right[0:1],
-            jnp.zeros((3, seqs, LANES), BF16),
-            right[1:2],
-            jnp.zeros((3, seqs, LANES), BF16),
-        ]
-    )
-    near_parts = []
-    for mask in (3, 2, 1):
-        part = swap_over(mask, leaving_parts[mask])
-        near_parts.append(part)
-        gathered = lax.dynamic_update_slice_in_dim(gathered, part[0:1], mask, 0)
-        gathered = lax.dynamic_update_slice_in_dim(gathered, part[1:2], 4 + mask, 0)
-
-    half = gathered.reshape(2, ranks // 2, seqs, LANES)
-    beyond = 1 - lax.bitwise_xor(lax.shift_right_logical(rank, 2), mine)
-    leaving = lax.dynamic_index_in_dim(half, beyond, 0, keepdims=False)
-    far = lax.ppermute(jnp.concatenate([leaving, left[None]]), "seq", swap)
-
-    gradient = pl.pallas_call(
-        small_grad_kernel,
-        in_specs=[vmem] * 4 + [[vmem] * 3] + [vmem] * 4,
-        out_specs=vmem,
-        out_shape=like(homolog_matrix.shape, BF16),
+    swapped = lax.ppermute(leaving, "seq", swap)
+    diagonal = swap_over(3, leaving_parts[3])
+    across, beside = [
+        swap_over(mask, jnp.concatenate([leaving_parts[mask], swapped[0:1]])) for mask in (2, 1)
+    ]
+    swapped_late = lax.ppermute(
+        jnp.where(own_is_near, diagonal[1], diagonal[0]), "seq", swap
+    )
+
+    pair_delta, gradient = pl.pallas_call(
+        functools.partial(small_finish_kernel, scale),
+        in_specs=[vmem, [vmem] * 3] + [vmem] * 12,
+        out_specs=[pl.BlockSpec(memory_space=pl.ANY)] * 2,
+        out_shape=(
+            like(homolog_matrix.shape, BF16),
+            like(coupling_cotangent.shape, BF16),
+        ),
+        scratch_shapes=[
+            pltpu.VMEM(homolog_matrix.shape, BF16),
+            pltpu.VMEM(coupling_cotangent.shape, BF16),
+            pltpu.VMEM((ranks // 2, seqs, LANES), BF16),
+            pltpu.VMEM((ranks // 2, seqs, LANES), BF16),
+            pltpu.VMEM((ranks // 2 * LANES, LANES), F32),
+            pltpu.SemaphoreType.DMA((2,)),
+        ],
         compiler_params=limit,
-        name="gradient",
-    )(gathered, outer_near, outer_far, keep, near_parts, normed, inv_std, gain, spread_w)
-
-    pair_delta = pl.pallas_call(
-        functools.partial(small_pair_kernel, scale),
-        in_specs=[vmem] * 5,
-        out_specs=vmem,
-        out_shape=like(coupling_cotangent.shape, BF16),
-        scratch_shapes=[pltpu.VMEM((ranks // 2 * LANES, LANES), F32)],
-        compiler_params=limit,
-        name="pair",
-    )(gathered, far, left, sorted_w, pair_offset)
+        name="finish",
+    )(
+        right,
+        [beside, across, diagonal],
+        swapped,
+        swapped_late,
+        both,
+        outer_near,
+        outer_far,
+        keep,
+        normed,
+        inv_std,
+        gain,
+        spread_w,
+        sorted_w,
+        pair_offset,
+    )[::-1]
     return (pair_delta, gradient)
 
 

time: 18.7 us -> 17.7 us (0.947)
  Pallas kernels: 5.85 us -> 4.79 us
  starting transfers between devices: 7.83 us -> 8.76 us
  waiting for transfers between devices: 4.06 us -> 3.23 us
    ppermute x4, waiting for transfers between devices: 3.96 us -> 2.06 us  [swap_over(): lax.ppermute(value, 'res', [(source, source ^ mask) for source in range(r...]
    ppermute x1 -> x2, waiting for transfers between devices: 0.1 us -> 1.17 us  [the longest x1 1.17 us: small_slice(): lax.ppermute(jnp.where(own_is_near, diagonal[1], diagonal[0]), 'seq', swap)]
    pallas_call x2 -> x1, Pallas kernels: 2.41 us -> 1.34 us  [small_slice(): pl.pallas_call(functools.partial(small_finish_kernel, scale), in_specs=[v...]
    ppermute x4, starting transfers between devices: 7.24 us -> 8.17 us  [swap_over(): lax.ppermute(value, 'res', [(source, source ^ mask) for source in range(r...]
  transfers between devices with their start and end apart: 6 -> 7, of which waited for: 5 -> 5; matrix products, arithmetic and copies ran while one was open for 0% -> 0% of each run, Pallas kernels for 21% -> 16%
where the time goes in v12:
time: 17.7 us; the launch traced here: 17.5 us
  starting transfers between devices  8.76 us (49%)
  Pallas kernels  4.79 us (27%)
  waiting for transfers between devices  3.23 us (18%)
  between operations  0.72 us (4%)
    ppermute x4, starting transfers between devices, swap_over(): lax.ppermute(value, 'res', [(source, source ^ mask) for source in range(r...  8.17 us
    ppermute x4, waiting for transfers between devices, swap_over(): lax.ppermute(value, 'res', [(source, source ^ mask) for source in range(r...  2.06 us
    pallas_call x1, Pallas kernels, small_slice(): pl.pallas_call(functools.partial(small_own_kernel, scale), in_specs=[vmem...  1.49 us
    pallas_call x1, Pallas kernels, small_slice(): pl.pallas_call(functools.partial(small_finish_kernel, scale), in_specs=[v...  1.34 us
    pallas_call x1, Pallas kernels, small_slice(): pl.pallas_call(small_project_kernel, in_specs=[hbm] * 9, out_specs=[vmem]...  1.32 us
    ppermute x1, waiting for transfers between devices, small_slice(): lax.ppermute(jnp.where(own_is_near, diagonal[1], diagonal[0]), 'seq', swap)  1.17 us
    pallas_call x1, Pallas kernels, small_slice(): pl.pallas_call(functools.partial(small_partner_kernel, scale, residues),...  0.63 us
    ppermute x1, starting transfers between devices, small_slice(): other_cot = lax.ppermute(coupling_cotangent, 'seq', swap)  0.52 us
  transfers between devices with their start and end apart: 7, of which 5 were waited for; matrix products, arithmetic and copies ran while one was open for 0% of the time, Pallas kernels for 16%

profile of v12, /device:TPU:0, one launch (start us, length us, event | category | flops | bytes accessed | tf_op | source)
XLA Modules:
  0.0 17.5 jit_solution(1072553382856663467)
XLA Ops:
  0.6 0.0 copy-start
  0.6 0.5 %collective-permute-start = (bf16[4,16,128]{2,1,0:T(8,128)(2,1)}, bf16[4,16,128]{2,1,0:T(8,128)(2,1)S(1)}, u32[]{:S(2)}, u32[]{:S(2)}) collective-permute-start(bf16[4,16,128]{2,1,0:T(8,128)(2,1)} %cot_hbm.1), channel_id=1, source_target_pairs={{0,1},{1,0},{2,3},{3,2},{4,5},{5,4},{6,7},{7,6},{8,9},{9,8},{10,11... | collective-permute-start | bytes 49160 | tf_op jit(solution)/shard_map/ppermute | solution.py:597
  1.2 1.3 %project.1 = (bf16[2,32,128]{2,1,0:T(8,128)(2,1)S(1)}, f32[128,256]{1,0:T(8,128)S(1)}, f32[128,128]{1,0:T(8,128)S(1)}, bf16[256,256]{1,0:T(8,128)(2,1)S(1)}, f32...) custom-call(bf16[32,4,256]{2,1,0:T(4,128)(2,1)} %x_hbm.1, f32[1,256]{1,0:T(1,128)} %bitcast.19, ...), custom_call_target="tpu_custom_call" | custom-call | tf_op jit(solution)/shard_map/project/pallas_call | solution.py:600
  2.5 0.0 collective-permute-done.other_ref
  2.5 3.7 %collective-permute-start.1 = (bf16[4,32,128]{2,1,0:T(8,128)(2,1)S(1)}, bf16[4,32,128]{2,1,0:T(8,128)(2,1)S(1)}, u32[]{:S(2)}, u32[]{:S(2)}) collective-permute-start(bf16[4,32,128]{2,1,0:T(8,128)(2,1)S(1)} %pad_maximum_fusion.2), channel_id=1, source_target_pairs={{0,8},{2,10},{4,12},{6,14},{8,0},{10,2},{12,4},{14,6},{1,9},{3,11}... | collective-permute-start | bytes 98312 | tf_op jit(solution)/shard_map/ppermute | solution.py:642
  6.2 0.0 copy-done
  6.2 1.5 %own_pieces.1 = (f32[4,32,128]{2,1,0:T(8,128)S(1)}, bf16[512,128]{1,0:T(8,128)(2,1)S(1)}, bf16[512,128]{1,0:T(8,128)(2,1)S(1)}, bf16[1024,128]{1,0:T(8,128)(2,1)S(1)}, bf16[128,1024]{1,0:T(8,128)(2,1)S(1)}) custom-call(bf16[4,16,128]{2,1,0:T(8,128)(2,1)S(1)} %get-tuple-element.21.own_ref, bf16[4,16,128]{2,1,0:T(8,128)(2,1)S(1)} %collective-permute-done.other_ref, ...), custom_call_target="tpu_custom_call" | custom-call | tf_op jit(solution)/shard_map/own_pieces/pallas_call | solution.py:650
  7.7 0.5 %collective-permute-done.1.got_ref = bf16[4,32,128]{2,1,0:T(8,128)(2,1)S(1)} collective-permute-done((bf16[4,32,128]{2,1,0:T(8,128)(2,1)S(1)}, bf16[4,32,128]{2,1,0:T(8,128)(2,1)S(1)}, u32[]{:S(2)}, u32[]{:S(2)}) %collective-permute-start.1) | collective-permute-done | bytes 32800 | tf_op jit(solution)/shard_map/ppermute | solution.py:642
  8.2 0.6 %partner_pieces.1 = (bf16[4,3,32,128]{3,2,1,0:T(8,128)(2,1)S(1)}, f32[4,32,128]{2,1,0:T(8,128)S(1)}, bf16[2,32,128]{2,1,0:T(8,128)(2,1)S(1)}, bf16[2,32,128]{2,1,0:T(8,128)(2,1)S(1)}) custom-call(bf16[4,32,128]{2,1,0:T(8,128)(2,1)S(1)} %collective-permute-done.1.got_ref, bf16[128,1024]{1,0:T(8,128)(2,1)S(1)} %get-tuple-element.22.sorted_wt_ref, ...), custom_call_target="tpu_custom_call" | custom-call | tf_op jit(solution)/shard_map/partner_pieces/pallas_call | solution.py:666
  8.9 0.1 collective-permute-start.2
  9.0 2.8 %collective-permute-start.5 = (bf16[3,32,128]{2,1,0:T(8,128)(2,1)S(1)}, bf16[3,32,128]{2,1,0:T(8,128)(2,1)S(1)}, u32[]{:S(2)}, u32[]{:S(2)}) collective-permute-start(bf16[3,32,128]{2,1,0:T(8,128)(2,1)S(1)} %get-tuple-element.38), channel_id=1, source_target_pairs={{0,6},{2,4},{4,2},{6,0},{8,14},{10,12},{12,10},{14,8},{1,7},{3,5},... | collective-permute-start | bytes 73736 | tf_op jit(solution)/shard_map/ppermute | solution.py:642
  11.8 0.0 collective-permute-done.2.swapped_ref
  11.8 0.5 %collective-permute-start.4 = (bf16[4,32,128]{2,1,0:T(8,128)(2,1)S(1)}, bf16[4,32,128]{2,1,0:T(8,128)(2,1)S(1)}, u32[]{:S(2)}, u32[]{:S(2)}) collective-permute-start(bf16[4,32,128]{2,1,0:T(8,128)(2,1)S(1)} %get-tuple-element.41), channel_id=1, source_target_pairs={{0,4},{2,6},{4,0},{6,2},{8,12},{10,14},{12,8},{14,10},{1,5},{3,7},... | collective-permute-start | bytes 98312 | tf_op jit(solution)/shard_map/ppermute | solution.py:642
  12.3 1.2 %collective-permute-start.3 = (bf16[4,32,128]{2,1,0:T(8,128)(2,1)S(1)}, bf16[4,32,128]{2,1,0:T(8,128)(2,1)S(1)}, u32[]{:S(2)}, u32[]{:S(2)}) collective-permute-start(bf16[4,32,128]{2,1,0:T(8,128)(2,1)S(1)} %get-tuple-element.42), channel_id=1, source_target_pairs={{0,2},{2,0},{4,6},{6,4},{8,10},{10,8},{12,14},{14,12},{1,3},{3,1},... | collective-permute-start | bytes 98312 | tf_op jit(solution)/shard_map/ppermute | solution.py:642
  13.5 0.3 %collective-permute-done.5.part_refs_2_ = bf16[3,32,128]{2,1,0:T(8,128)(2,1)S(1)} collective-permute-done((bf16[3,32,128]{2,1,0:T(8,128)(2,1)S(1)}, bf16[3,32,128]{2,1,0:T(8,128)(2,1)S(1)}, u32[]{:S(2)}, u32[]{:S(2)}) %collective-permute-start.5) | collective-permute-done | bytes 24608 | tf_op jit(solution)/shard_map/ppermute | solution.py:642
  13.8 0.0 collective-permute-start.6
  13.8 1.2 %collective-permute-done.6.swapped_late_ref = bf16[32,128]{1,0:T(8,128)(2,1)S(1)} collective-permute-done((bf16[32,128]{1,0:T(8,128)(2,1)S(1)}, bf16[32,128]{1,0:T(8,128)(2,1)S(1)}, u32[]{:S(2)}, u32[]{:S(2)}) %collective-permute-start.6) | collective-permute-done | bytes 8224 | tf_op jit(solution)/shard_map/ppermute | solution.py:686
  15.0 0.8 %collective-permute-done.4.part_refs_1_ = bf16[4,32,128]{2,1,0:T(8,128)(2,1)S(1)} collective-permute-done((bf16[4,32,128]{2,1,0:T(8,128)(2,1)S(1)}, bf16[4,32,128]{2,1,0:T(8,128)(2,1)S(1)}, u32[]{:S(2)}, u32[]{:S(2)}) %collective-permute-start.4) | collective-permute-done | bytes 32800 | tf_op jit(solution)/shard_map/ppermute | solution.py:642
  15.7 0.4 %collective-permute-done.3.part_refs_0_ = bf16[4,32,128]{2,1,0:T(8,128)(2,1)S(1)} collective-permute-done((bf16[4,32,128]{2,1,0:T(8,128)(2,1)S(1)}, bf16[4,32,128]{2,1,0:T(8,128)(2,1)S(1)}, u32[]{:S(2)}, u32[]{:S(2)}) %collective-permute-start.3) | collective-permute-done | bytes 32800 | tf_op jit(solution)/shard_map/ppermute | solution.py:642
  16.2 1.3 %finish.1 = (bf16[32,4,256]{2,1,0:T(4,128)(2,1)}, bf16[4,16,128]{2,1,0:T(8,128)(2,1)}) custom-call(bf16[2,32,128]{2,1,0:T(8,128)(2,1)S(1)} %get-tuple-element.24.right_ref, bf16[4,32,128]{2,1,0:T(8,128)(2,1)S(1)} %collective-permute-done.3.part_refs_0_, bf16[4,32,128]{2,1,0:T(8,128)(2,1)S(1)} %collective-permute-done.4.part_refs_1_, ...), custom_call_target="tpu_custom_call" | custom-call | tf_op jit(solution)/shard_map/finish/pallas_call | solution.py:690
  (6 shorter events, 0.0 us)
Async XLA Ops:
  0.6 5.6 %copy-start = (bf16[1024,128]{1,0:T(8,128)(2,1)S(1)}, bf16[1024,128]{1,0:T(8,128)(2,1)}, u32[]{:S(2)}) copy-start(bf16[1024,128]{1,0:T(8,128)(2,1)} %w_ref.1) | copy-start | bytes 786436
  0.6 1.9 %collective-permute-start = (bf16[4,16,128]{2,1,0:T(8,128)(2,1)}, bf16[4,16,128]{2,1,0:T(8,128)(2,1)S(1)}, u32[]{:S(2)}, u32[]{:S(2)}) collective-permute-start(bf16[4,16,128]{2,1,0:T(8,128)(2,1)} %cot_hbm.1), channel_id=1, source_target_pairs={{0,1},{1,0},{2,3},{3,2},{4,5},{5,4},{6,7},{7,6},{8,9},{9,8},{10,11... | collective-permute-start | bytes 49160 | tf_op jit(solution)/shard_map/ppermute | solution.py:597
  2.5 5.7 %collective-permute-start.1 = (bf16[4,32,128]{2,1,0:T(8,128)(2,1)S(1)}, bf16[4,32,128]{2,1,0:T(8,128)(2,1)S(1)}, u32[]{:S(2)}, u32[]{:S(2)}) collective-permute-start(bf16[4,32,128]{2,1,0:T(8,128)(2,1)S(1)} %pad_maximum_fusion.2), channel_id=1, source_target_pairs={{0,8},{2,10},{4,12},{6,14},{8,0},{10,2},{12,4},{14,6},{1,9},{3,11}... | collective-permute-start | bytes 98312 | tf_op jit(solution)/shard_map/ppermute | solution.py:642
  8.9 2.9 %collective-permute-start.2 = (bf16[2,32,128]{2,1,0:T(8,128)(2,1)S(1)}, bf16[2,32,128]{2,1,0:T(8,128)(2,1)S(1)}, u32[]{:S(2)}, u32[]{:S(2)}) collective-permute-start(bf16[2,32,128]{2,1,0:T(8,128)(2,1)S(1)} %get-tuple-element.26), channel_id=1, source_target_pairs={{0,1},{1,0},{2,3},{3,2},{4,5},{5,4},{6,7},{7,6},{8,9},{9,8},{10,11... | collective-permute-start | bytes 49160 | tf_op jit(solution)/shard_map/ppermute | solution.py:681
  9.0 4.8 %collective-permute-start.5 = (bf16[3,32,128]{2,1,0:T(8,128)(2,1)S(1)}, bf16[3,32,128]{2,1,0:T(8,128)(2,1)S(1)}, u32[]{:S(2)}, u32[]{:S(2)}) collective-permute-start(bf16[3,32,128]{2,1,0:T(8,128)(2,1)S(1)} %get-tuple-element.38), channel_id=1, source_target_pairs={{0,6},{2,4},{4,2},{6,0},{8,14},{10,12},{12,10},{14,8},{1,7},{3,5},... | collective-permute-start | bytes 73736 | tf_op jit(solution)/shard_map/ppermute | solution.py:642
  11.8 4.0 %collective-permute-start.4 = (bf16[4,32,128]{2,1,0:T(8,128)(2,1)S(1)}, bf16[4,32,128]{2,1,0:T(8,128)(2,1)S(1)}, u32[]{:S(2)}, u32[]{:S(2)}) collective-permute-start(bf16[4,32,128]{2,1,0:T(8,128)(2,1)S(1)} %get-tuple-element.41), channel_id=1, source_target_pairs={{0,4},{2,6},{4,0},{6,2},{8,12},{10,14},{12,8},{14,10},{1,5},{3,7},... | collective-permute-start | bytes 98312 | tf_op jit(solution)/shard_map/ppermute | solution.py:642
  12.3 3.9 %collective-permute-start.3 = (bf16[4,32,128]{2,1,0:T(8,128)(2,1)S(1)}, bf16[4,32,128]{2,1,0:T(8,128)(2,1)S(1)}, u32[]{:S(2)}, u32[]{:S(2)}) collective-permute-start(bf16[4,32,128]{2,1,0:T(8,128)(2,1)S(1)} %get-tuple-element.42), channel_id=1, source_target_pairs={{0,2},{2,0},{4,6},{6,4},{8,10},{10,8},{12,14},{14,12},{1,3},{3,1},... | collective-permute-start | bytes 98312 | tf_op jit(solution)/shard_map/ppermute | solution.py:642
  13.8 1.2 %collective-permute-start.6 = (bf16[32,128]{1,0:T(8,128)(2,1)S(1)}, bf16[32,128]{1,0:T(8,128)(2,1)S(1)}, u32[]{:S(2)}, u32[]{:S(2)}) collective-permute-start(bf16[32,128]{1,0:T(8,128)(2,1)S(1)} %fusion), channel_id=1, source_target_pairs={{0,1},{1,0},{2,3},{3,2},{4,5},{5,4},{6,7},{7,6},{8,9},{9,8},{10,11... | collective-permute-start | bytes 24584 | tf_op jit(solution)/shard_map/ppermute | solution.py:686

commit v13 on v12

--- a/solution.py
+++ b/solution.py
@@ -514,8 +514,6 @@
     )
     for place in range(residues):
         grad_ref[:, place, :] = grad[place * seqs : (place + 1) * seqs].astype(BF16)
-    grad_copy = pltpu.make_async_copy(grad_ref, grad_hbm, semaphores.at[0])
-    grad_copy.start()
 
     half = jnp.where(mine == lax.shift_right_logical(rank, 2), 0, 1)
     for mask, ref in enumerate(blocks_of):
@@ -564,10 +562,9 @@
     pair = jnp.dot(parts, sorted_w_ref[...], preferred_element_type=F32)
     pair = pair[0:rows] + pair[rows : 2 * rows]
     pair_ref[...] = (pair + offset_ref[...]).astype(BF16).reshape(pair_ref.shape)
-    pair_copy = pltpu.make_async_copy(pair_ref, pair_hbm, semaphores.at[1])
-    pair_copy.start()
-    grad_copy.wait()
-    pair_copy.wait()
+    copies = start_copies(((grad_ref, grad_hbm), (pair_ref, pair_hbm)), semaphores)
+    for copy in copies:
+        copy.wait()
 
 
 def small_slice(

time: 17.7 us -> 17.7 us (level)
  no operation moved by 1% of the time
where the time goes in v13:
time: 17.7 us; the launch traced here: 17.5 us
  starting transfers between devices  8.76 us (49%)
  Pallas kernels  4.79 us (27%)
  waiting for transfers between devices  3.23 us (18%)
  between operations  0.72 us (4%)
    ppermute x4, starting transfers between devices, swap_over(): lax.ppermute(value, 'res', [(source, source ^ mask) for source in range(r...  8.17 us
    ppermute x4, waiting for transfers between devices, swap_over(): lax.ppermute(value, 'res', [(source, source ^ mask) for source in range(r...  2.06 us
    pallas_call x1, Pallas kernels, small_slice(): pl.pallas_call(functools.partial(small_own_kernel, scale), in_specs=[vmem...  1.49 us
    pallas_call x1, Pallas kernels, small_slice(): pl.pallas_call(functools.partial(small_finish_kernel, scale), in_specs=[v...  1.34 us
    pallas_call x1, Pallas kernels, small_slice(): pl.pallas_call(small_project_kernel, in_specs=[hbm] * 9, out_specs=[vmem]...  1.32 us
    ppermute x1, waiting for transfers between devices, small_slice(): lax.ppermute(jnp.where(own_is_near, diagonal[1], diagonal[0]), 'seq', swap)  1.17 us
    pallas_call x1, Pallas kernels, small_slice(): pl.pallas_call(functools.partial(small_partner_kernel, scale, residues),...  0.63 us
    ppermute x1, starting transfers between devices, small_slice(): other_cot = lax.ppermute(coupling_cotangent, 'seq', swap)  0.52 us
  transfers between devices with their start and end apart: 7, of which 5 were waited for; matrix products, arithmetic and copies ran while one was open for 0% of the time, Pallas kernels for 16%

profile of v13, /device:TPU:0, one launch (start us, length us, event | category | flops | bytes accessed | tf_op | source)
XLA Modules:
  0.0 17.5 jit_solution(1072553382856663467)
XLA Ops:
  0.6 0.0 copy-start
  0.6 0.5 %collective-permute-start = (bf16[4,16,128]{2,1,0:T(8,128)(2,1)}, bf16[4,16,128]{2,1,0:T(8,128)(2,1)S(1)}, u32[]{:S(2)}, u32[]{:S(2)}) collective-permute-start(bf16[4,16,128]{2,1,0:T(8,128)(2,1)} %cot_hbm.1), channel_id=1, source_target_pairs={{0,1},{1,0},{2,3},{3,2},{4,5},{5,4},{6,7},{7,6},{8,9},{9,8},{10,11... | collective-permute-start | bytes 49160 | tf_op jit(solution)/shard_map/ppermute | solution.py:594
  1.2 1.3 %project.1 = (bf16[2,32,128]{2,1,0:T(8,128)(2,1)S(1)}, f32[128,256]{1,0:T(8,128)S(1)}, f32[128,128]{1,0:T(8,128)S(1)}, bf16[256,256]{1,0:T(8,128)(2,1)S(1)}, f32...) custom-call(bf16[32,4,256]{2,1,0:T(4,128)(2,1)} %x_hbm.1, f32[1,256]{1,0:T(1,128)} %bitcast.19, ...), custom_call_target="tpu_custom_call" | custom-call | tf_op jit(solution)/shard_map/project/pallas_call | solution.py:597
  2.5 0.0 collective-permute-done.other_ref
  2.5 3.7 %collective-permute-start.1 = (bf16[4,32,128]{2,1,0:T(8,128)(2,1)S(1)}, bf16[4,32,128]{2,1,0:T(8,128)(2,1)S(1)}, u32[]{:S(2)}, u32[]{:S(2)}) collective-permute-start(bf16[4,32,128]{2,1,0:T(8,128)(2,1)S(1)} %pad_maximum_fusion.2), channel_id=1, source_target_pairs={{0,8},{2,10},{4,12},{6,14},{8,0},{10,2},{12,4},{14,6},{1,9},{3,11}... | collective-permute-start | bytes 98312 | tf_op jit(solution)/shard_map/ppermute | solution.py:639
  6.2 0.0 copy-done
  6.2 1.5 %own_pieces.1 = (f32[4,32,128]{2,1,0:T(8,128)S(1)}, bf16[512,128]{1,0:T(8,128)(2,1)S(1)}, bf16[512,128]{1,0:T(8,128)(2,1)S(1)}, bf16[1024,128]{1,0:T(8,128)(2,1)S(1)}, bf16[128,1024]{1,0:T(8,128)(2,1)S(1)}) custom-call(bf16[4,16,128]{2,1,0:T(8,128)(2,1)S(1)} %get-tuple-element.21.own_ref, bf16[4,16,128]{2,1,0:T(8,128)(2,1)S(1)} %collective-permute-done.other_ref, ...), custom_call_target="tpu_custom_call" | custom-call | tf_op jit(solution)/shard_map/own_pieces/pallas_call | solution.py:647
  7.7 0.5 %collective-permute-done.1.got_ref = bf16[4,32,128]{2,1,0:T(8,128)(2,1)S(1)} collective-permute-done((bf16[4,32,128]{2,1,0:T(8,128)(2,1)S(1)}, bf16[4,32,128]{2,1,0:T(8,128)(2,1)S(1)}, u32[]{:S(2)}, u32[]{:S(2)}) %collective-permute-start.1) | collective-permute-done | bytes 32800 | tf_op jit(solution)/shard_map/ppermute | solution.py:639
  8.2 0.6 %partner_pieces.1 = (bf16[4,3,32,128]{3,2,1,0:T(8,128)(2,1)S(1)}, f32[4,32,128]{2,1,0:T(8,128)S(1)}, bf16[2,32,128]{2,1,0:T(8,128)(2,1)S(1)}, bf16[2,32,128]{2,1,0:T(8,128)(2,1)S(1)}) custom-call(bf16[4,32,128]{2,1,0:T(8,128)(2,1)S(1)} %collective-permute-done.1.got_ref, bf16[128,1024]{1,0:T(8,128)(2,1)S(1)} %get-tuple-element.22.sorted_wt_ref, ...), custom_call_target="tpu_custom_call" | custom-call | tf_op jit(solution)/shard_map/partner_pieces/pallas_call | solution.py:663
  8.9 0.1 collective-permute-start.2
  9.0 2.8 %collective-permute-start.5 = (bf16[3,32,128]{2,1,0:T(8,128)(2,1)S(1)}, bf16[3,32,128]{2,1,0:T(8,128)(2,1)S(1)}, u32[]{:S(2)}, u32[]{:S(2)}) collective-permute-start(bf16[3,32,128]{2,1,0:T(8,128)(2,1)S(1)} %get-tuple-element.38), channel_id=1, source_target_pairs={{0,6},{2,4},{4,2},{6,0},{8,14},{10,12},{12,10},{14,8},{1,7},{3,5},... | collective-permute-start | bytes 73736 | tf_op jit(solution)/shard_map/ppermute | solution.py:639
  11.8 0.0 collective-permute-done.2.swapped_ref
  11.8 0.5 %collective-permute-start.4 = (bf16[4,32,128]{2,1,0:T(8,128)(2,1)S(1)}, bf16[4,32,128]{2,1,0:T(8,128)(2,1)S(1)}, u32[]{:S(2)}, u32[]{:S(2)}) collective-permute-start(bf16[4,32,128]{2,1,0:T(8,128)(2,1)S(1)} %get-tuple-element.41), channel_id=1, source_target_pairs={{0,4},{2,6},{4,0},{6,2},{8,12},{10,14},{12,8},{14,10},{1,5},{3,7},... | collective-permute-start | bytes 98312 | tf_op jit(solution)/shard_map/ppermute | solution.py:639
  12.3 1.2 %collective-permute-start.3 = (bf16[4,32,128]{2,1,0:T(8,128)(2,1)S(1)}, bf16[4,32,128]{2,1,0:T(8,128)(2,1)S(1)}, u32[]{:S(2)}, u32[]{:S(2)}) collective-permute-start(bf16[4,32,128]{2,1,0:T(8,128)(2,1)S(1)} %get-tuple-element.42), channel_id=1, source_target_pairs={{0,2},{2,0},{4,6},{6,4},{8,10},{10,8},{12,14},{14,12},{1,3},{3,1},... | collective-permute-start | bytes 98312 | tf_op jit(solution)/shard_map/ppermute | solution.py:639
  13.5 0.3 %collective-permute-done.5.part_refs_2_ = bf16[3,32,128]{2,1,0:T(8,128)(2,1)S(1)} collective-permute-done((bf16[3,32,128]{2,1,0:T(8,128)(2,1)S(1)}, bf16[3,32,128]{2,1,0:T(8,128)(2,1)S(1)}, u32[]{:S(2)}, u32[]{:S(2)}) %collective-permute-start.5) | collective-permute-done | bytes 24608 | tf_op jit(solution)/shard_map/ppermute | solution.py:639
  13.8 0.0 collective-permute-start.6
  13.8 1.2 %collective-permute-done.6.swapped_late_ref = bf16[32,128]{1,0:T(8,128)(2,1)S(1)} collective-permute-done((bf16[32,128]{1,0:T(8,128)(2,1)S(1)}, bf16[32,128]{1,0:T(8,128)(2,1)S(1)}, u32[]{:S(2)}, u32[]{:S(2)}) %collective-permute-start.6) | collective-permute-done | bytes 8224 | tf_op jit(solution)/shard_map/ppermute | solution.py:683
  15.0 0.8 %collective-permute-done.4.part_refs_1_ = bf16[4,32,128]{2,1,0:T(8,128)(2,1)S(1)} collective-permute-done((bf16[4,32,128]{2,1,0:T(8,128)(2,1)S(1)}, bf16[4,32,128]{2,1,0:T(8,128)(2,1)S(1)}, u32[]{:S(2)}, u32[]{:S(2)}) %collective-permute-start.4) | collective-permute-done | bytes 32800 | tf_op jit(solution)/shard_map/ppermute | solution.py:639
  15.7 0.4 %collective-permute-done.3.part_refs_0_ = bf16[4,32,128]{2,1,0:T(8,128)(2,1)S(1)} collective-permute-done((bf16[4,32,128]{2,1,0:T(8,128)(2,1)S(1)}, bf16[4,32,128]{2,1,0:T(8,128)(2,1)S(1)}, u32[]{:S(2)}, u32[]{:S(2)}) %collective-permute-start.3) | collective-permute-done | bytes 32800 | tf_op jit(solution)/shard_map/ppermute | solution.py:639
  16.2 1.3 %finish.1 = (bf16[32,4,256]{2,1,0:T(4,128)(2,1)}, bf16[4,16,128]{2,1,0:T(8,128)(2,1)}) custom-call(bf16[2,32,128]{2,1,0:T(8,128)(2,1)S(1)} %get-tuple-element.24.right_ref, bf16[4,32,128]{2,1,0:T(8,128)(2,1)S(1)} %collective-permute-done.3.part_refs_0_, bf16[4,32,128]{2,1,0:T(8,128)(2,1)S(1)} %collective-permute-done.4.part_refs_1_, ...), custom_call_target="tpu_custom_call" | custom-call | tf_op jit(solution)/shard_map/finish/pallas_call | solution.py:687
  (6 shorter events, 0.0 us)
Async XLA Ops:
  0.6 5.6 %copy-start = (bf16[1024,128]{1,0:T(8,128)(2,1)S(1)}, bf16[1024,128]{1,0:T(8,128)(2,1)}, u32[]{:S(2)}) copy-start(bf16[1024,128]{1,0:T(8,128)(2,1)} %w_ref.1) | copy-start | bytes 786436
  0.6 1.9 %collective-permute-start = (bf16[4,16,128]{2,1,0:T(8,128)(2,1)}, bf16[4,16,128]{2,1,0:T(8,128)(2,1)S(1)}, u32[]{:S(2)}, u32[]{:S(2)}) collective-permute-start(bf16[4,16,128]{2,1,0:T(8,128)(2,1)} %cot_hbm.1), channel_id=1, source_target_pairs={{0,1},{1,0},{2,3},{3,2},{4,5},{5,4},{6,7},{7,6},{8,9},{9,8},{10,11... | collective-permute-start | bytes 49160 | tf_op jit(solution)/shard_map/ppermute | solution.py:594
  2.5 5.7 %collective-permute-start.1 = (bf16[4,32,128]{2,1,0:T(8,128)(2,1)S(1)}, bf16[4,32,128]{2,1,0:T(8,128)(2,1)S(1)}, u32[]{:S(2)}, u32[]{:S(2)}) collective-permute-start(bf16[4,32,128]{2,1,0:T(8,128)(2,1)S(1)} %pad_maximum_fusion.2), channel_id=1, source_target_pairs={{0,8},{2,10},{4,12},{6,14},{8,0},{10,2},{12,4},{14,6},{1,9},{3,11}... | collective-permute-start | bytes 98312 | tf_op jit(solution)/shard_map/ppermute | solution.py:639
  8.9 2.9 %collective-permute-start.2 = (bf16[2,32,128]{2,1,0:T(8,128)(2,1)S(1)}, bf16[2,32,128]{2,1,0:T(8,128)(2,1)S(1)}, u32[]{:S(2)}, u32[]{:S(2)}) collective-permute-start(bf16[2,32,128]{2,1,0:T(8,128)(2,1)S(1)} %get-tuple-element.26), channel_id=1, source_target_pairs={{0,1},{1,0},{2,3},{3,2},{4,5},{5,4},{6,7},{7,6},{8,9},{9,8},{10,11... | collective-permute-start | bytes 49160 | tf_op jit(solution)/shard_map/ppermute | solution.py:678
  9.0 4.8 %collective-permute-start.5 = (bf16[3,32,128]{2,1,0:T(8,128)(2,1)S(1)}, bf16[3,32,128]{2,1,0:T(8,128)(2,1)S(1)}, u32[]{:S(2)}, u32[]{:S(2)}) collective-permute-start(bf16[3,32,128]{2,1,0:T(8,128)(2,1)S(1)} %get-tuple-element.38), channel_id=1, source_target_pairs={{0,6},{2,4},{4,2},{6,0},{8,14},{10,12},{12,10},{14,8},{1,7},{3,5},... | collective-permute-start | bytes 73736 | tf_op jit(solution)/shard_map/ppermute | solution.py:639
  11.8 4.0 %collective-permute-start.4 = (bf16[4,32,128]{2,1,0:T(8,128)(2,1)S(1)}, bf16[4,32,128]{2,1,0:T(8,128)(2,1)S(1)}, u32[]{:S(2)}, u32[]{:S(2)}) collective-permute-start(bf16[4,32,128]{2,1,0:T(8,128)(2,1)S(1)} %get-tuple-element.41), channel_id=1, source_target_pairs={{0,4},{2,6},{4,0},{6,2},{8,12},{10,14},{12,8},{14,10},{1,5},{3,7},... | collective-permute-start | bytes 98312 | tf_op jit(solution)/shard_map/ppermute | solution.py:639
  12.3 3.9 %collective-permute-start.3 = (bf16[4,32,128]{2,1,0:T(8,128)(2,1)S(1)}, bf16[4,32,128]{2,1,0:T(8,128)(2,1)S(1)}, u32[]{:S(2)}, u32[]{:S(2)}) collective-permute-start(bf16[4,32,128]{2,1,0:T(8,128)(2,1)S(1)} %get-tuple-element.42), channel_id=1, source_target_pairs={{0,2},{2,0},{4,6},{6,4},{8,10},{10,8},{12,14},{14,12},{1,3},{3,1},... | collective-permute-start | bytes 98312 | tf_op jit(solution)/shard_map/ppermute | solution.py:639
  13.8 1.2 %collective-permute-start.6 = (bf16[32,128]{1,0:T(8,128)(2,1)S(1)}, bf16[32,128]{1,0:T(8,128)(2,1)S(1)}, u32[]{:S(2)}, u32[]{:S(2)}) collective-permute-start(bf16[32,128]{1,0:T(8,128)(2,1)S(1)} %fusion), channel_id=1, source_target_pairs={{0,1},{1,0},{2,3},{3,2},{4,5},{5,4},{6,7},{7,6},{8,9},{9,8},{10,11... | collective-permute-start | bytes 24584 | tf_op jit(solution)/shard_map/ppermute | solution.py:683

commit v14 on v12

--- a/solution.py
+++ b/solution.py
@@ -415,7 +415,8 @@
 
 
 def small_own_kernel(scale, own_ref, other_ref, w_ref, both_ref,
-                     keep_ref, outer_near_ref, outer_far_ref, sorted_w_ref, sorted_wt_ref, turn_refs, wide_ref):
+                     keep_ref, outer_near_ref, outer_far_ref, sorted_w_ref, sorted_wt_ref,
+                     order_ref, repeat_ref, turn_refs, wide_ref):
     residues, columns, _ = own_ref.shape
     depth = LANES // residues
     wide_ref[...] = w_ref[...].astype(F32)
@@ -438,15 +439,72 @@
     outer_far_ref[...] = outer_rows(
         scale, jnp.where(own_is_near, other, own), residues, sorted_wt_ref, turn_refs[1]
     )
-
-
-def small_partner_kernel(scale, residues, got_ref, sorted_wt_ref, keep_ref, both_ref,
-                         leaving_ref, keep_out_ref, right_ref, swap_ref, turn_ref):
+    order_ref[...] = one_hot(
+        lambda row: (
+            (2 * (row >> 6 & 1) + (row >> 2 & 1)) * LANES
+            + (row & 3) * depth + (row >> 3 & 7) * residues + (row >> 7)
+        ),
+        order_ref.shape,
+    )
+    for place in range(residues):
+        shape = (LANES, LANES)
+        row = lax.broadcasted_iota(jnp.int32, shape, 0)
+        lane = lax.broadcasted_iota(jnp.int32, shape, 1)
+        repeat_ref[:, place * LANES : (place + 1) * LANES] = jnp.where(
+            row == place * depth + lane % depth, 1.0, 0.0
+        ).astype(BF16)
+
+
+def one_hot(target, shape):
+    part = (shape[0], LANES)
+    wanted = target(lax.broadcasted_iota(jnp.int32, part, 0))
+    lane = lax.broadcasted_iota(jnp.int32, part, 1)
+    return jnp.concatenate(
+        [
+            jnp.where(wanted == lane + tile * LANES, 1.0, 0.0).astype(BF16)
+            for tile in range(shape[1] // LANES)
+        ],
+        axis=1,
+    )
+
+
+def blocks_apart(left, repeat, residues):
+    depth = LANES // residues
+    wide = jnp.dot(left, repeat, preferred_element_type=F32)
+    blocks = lane_block(wide.shape, depth) % residues
+    return jnp.concatenate(
+        [jnp.where(blocks == e, wide, 0.0).astype(BF16) for e in range(residues)], axis=0
+    )
+
+
+def small_partner_kernel(scale, residues, got_ref, sorted_wt_ref, keep_ref, both_ref, order_ref,
+                         repeat_ref, leaving_ref, keep_out_ref, right_ref, swap_ref):
     rank = lax.axis_index("res")
     seqs = got_ref.shape[1]
     cot = got_ref[2:4].reshape(2 * seqs, LANES)
-    outer = outer_rows(scale, cot, residues, sorted_wt_ref, turn_ref)
-    partial = lax.dot_general(got_ref[0], outer, NT, preferred_element_type=F32)
+    columns = cot.shape[0] // residues
+    tiles = sorted_wt_ref.shape[1] // LANES
+    flat = jnp.dot(cot, sorted_wt_ref[...], preferred_element_type=F32) * scale
+    outer = jnp.concatenate(
+        [
+            jnp.concatenate(
+                [
+                    flat[i * columns + start : i * columns + start + 8, tile * LANES : (tile + 1) * LANES]
+                    for start in range(0, columns, 8)
+                    for tile in range(tiles)
+                ],
+                axis=0,
+            )
+            for i in range(residues)
+        ],
+        axis=1,
+    ).astype(BF16)
+    apart = blocks_apart(got_ref[0], repeat_ref[...], residues)
+    partial = lax.dot_general(apart, outer, NT, preferred_element_type=F32).astype(BF16)
+    partial = jnp.concatenate(
+        [partial[e * seqs : (e + 1) * seqs] for e in range(residues)], axis=1
+    )
+    partial = jnp.dot(partial, order_ref[...], preferred_element_type=F32)
     right_ref[0] = both_ref[1]
     right_ref[1] = got_ref[1]
     own_is_near = lax.axis_index("seq") == lax.shift_right_logical(rank, 2)
@@ -647,16 +705,18 @@
 
     half_rows = ranks // 2 * LANES
     turn = pltpu.VMEM((half_rows, LANES), F32)
-    keep, outer_near, outer_far, sorted_w, sorted_wt = pl.pallas_call(
+    keep, outer_near, outer_far, sorted_w, sorted_wt, order, repeat = pl.pallas_call(
         functools.partial(small_own_kernel, scale),
         in_specs=[vmem] * 4,
-        out_specs=[vmem] * 5,
+        out_specs=[vmem] * 7,
         out_shape=(
             like((ranks // 2, seqs, LANES), F32),
             like((half_rows, LANES), BF16),
             like((half_rows, LANES), BF16),
             like(coupling_matrix.shape, BF16),
             like(coupling_matrix.shape[::-1], BF16),
+            like((half_rows, half_rows), BF16),
+            like((LANES, residues * LANES), BF16),
         ),
         scratch_shapes=[[turn, turn], pltpu.VMEM(coupling_matrix.shape, F32)],
         compiler_params=limit,
@@ -665,7 +725,7 @@
 
     leaving_parts, keep, right, leaving = pl.pallas_call(
         functools.partial(small_partner_kernel, scale, residues),
-        in_specs=[vmem] * 4,
+        in_specs=[vmem] * 6,
         out_specs=[vmem] * 4,
         out_shape=(
             like((ranks // 2, 3, seqs, LANES), BF16),
@@ -673,10 +733,9 @@
             like((2, seqs, LANES), BF16),
             like((2, seqs, LANES), BF16),
         ),
-        scratch_shapes=[turn],
         compiler_params=limit,
         name="partner_pieces",
-    )(beyond_two, sorted_wt, keep, both)
+    )(beyond_two, sorted_wt, keep, both, order, repeat)
 
     swapped = lax.ppermute(leaving, "seq", swap)
     diagonal = swap_over(3, leaving_parts[3])

time: 17.7 us -> 17.6 us (level)
  waiting for transfers between devices: 3.23 us -> 2.8 us
  Pallas kernels: 4.79 us -> 5.11 us
    ppermute x4, waiting for transfers between devices: 2.06 us -> 1.62 us  [swap_over(): lax.ppermute(value, 'res', [(source, source ^ mask) for source in range(r...]
    pallas_call x1, Pallas kernels: 1.49 us -> 1.93 us  [small_slice(): pl.pallas_call(functools.partial(small_own_kernel, scale), in_specs=[vmem...]
  transfers between devices with their start and end apart: 7 -> 7, of which waited for: 5 -> 5; matrix products, arithmetic and copies ran while one was open for 0% -> 0% of each run, Pallas kernels for 16% -> 19%
where the time goes in v14:
time: 17.6 us; the launch traced here: 17.4 us
  starting transfers between devices  8.78 us (50%)
  Pallas kernels  5.11 us (29%)
  waiting for transfers between devices  2.8 us (16%)
  between operations  0.7 us (4%)
    ppermute x4, starting transfers between devices, swap_over(): lax.ppermute(value, 'res', [(source, source ^ mask) for source in range(r...  8.07 us
    pallas_call x1, Pallas kernels, small_slice(): pl.pallas_call(functools.partial(small_own_kernel, scale), in_specs=[vmem...  1.93 us
    ppermute x4, waiting for transfers between devices, swap_over(): lax.ppermute(value, 'res', [(source, source ^ mask) for source in range(r...  1.62 us
    pallas_call x1, Pallas kernels, small_slice(): pl.pallas_call(functools.partial(small_finish_kernel, scale), in_specs=[v...  1.34 us
    pallas_call x1, Pallas kernels, small_slice(): pl.pallas_call(small_project_kernel, in_specs=[hbm] * 9, out_specs=[vmem]...  1.32 us
    ppermute x1, waiting for transfers between devices, small_slice(): lax.ppermute(jnp.where(own_is_near, diagonal[1], diagonal[0]), 'seq', swap)  1.17 us
    ppermute x1, starting transfers between devices, small_slice(): other_cot = lax.ppermute(coupling_cotangent, 'seq', swap)  0.52 us
    pallas_call x1, Pallas kernels, small_slice(): pl.pallas_call(functools.partial(small_partner_kernel, scale, residues),...  0.51 us
  transfers between devices with their start and end apart: 7, of which 5 were waited for; matrix products, arithmetic and copies ran while one was open for 0% of the time, Pallas kernels for 19%

profile of v14, /device:TPU:0, one launch (start us, length us, event | category | flops | bytes accessed | tf_op | source)
XLA Modules:
  0.0 17.4 jit_solution(1180013719915231573)
XLA Ops:
  0.6 0.0 copy-start
  0.6 0.5 %collective-permute-start = (bf16[4,16,128]{2,1,0:T(8,128)(2,1)}, bf16[4,16,128]{2,1,0:T(8,128)(2,1)S(1)}, u32[]{:S(2)}, u32[]{:S(2)}) collective-permute-start(bf16[4,16,128]{2,1,0:T(8,128)(2,1)} %cot_hbm.1), channel_id=1, source_target_pairs={{0,1},{1,0},{2,3},{3,2},{4,5},{5,4},{6,7},{7,6},{8,9},{9,8},{10,11... | collective-permute-start | bytes 49160 | tf_op jit(solution)/shard_map/ppermute | solution.py:655
  1.2 1.3 %project.1 = (bf16[2,32,128]{2,1,0:T(8,128)(2,1)S(1)}, f32[128,256]{1,0:T(8,128)S(1)}, f32[128,128]{1,0:T(8,128)S(1)}, bf16[256,256]{1,0:T(8,128)(2,1)S(1)}, f32...) custom-call(bf16[32,4,256]{2,1,0:T(4,128)(2,1)} %x_hbm.1, f32[1,256]{1,0:T(1,128)} %bitcast.19, ...), custom_call_target="tpu_custom_call" | custom-call | tf_op jit(solution)/shard_map/project/pallas_call | solution.py:658
  2.5 0.0 collective-permute-done.other_ref
  2.5 3.7 %collective-permute-start.1 = (bf16[4,32,128]{2,1,0:T(8,128)(2,1)S(1)}, bf16[4,32,128]{2,1,0:T(8,128)(2,1)S(1)}, u32[]{:S(2)}, u32[]{:S(2)}) collective-permute-start(bf16[4,32,128]{2,1,0:T(8,128)(2,1)S(1)} %pad_maximum_fusion.2), channel_id=1, source_target_pairs={{0,8},{2,10},{4,12},{6,14},{8,0},{10,2},{12,4},{14,6},{1,9},{3,11}... | collective-permute-start | bytes 98312 | tf_op jit(solution)/shard_map/ppermute | solution.py:700
  6.2 0.0 copy-done
  6.2 1.9 %own_pieces.1 = (f32[4,32,128]{2,1,0:T(8,128)S(1)}, bf16[512,128]{1,0:T(8,128)(2,1)S(1)}, bf16[512,128]{1,0:T(8,128)(2,1)S(1)}, bf16[1024,128]{1,0:T(8,128)(2,1)...) custom-call(bf16[4,16,128]{2,1,0:T(8,128)(2,1)S(1)} %get-tuple-element.23.own_ref, ...), custom_call_target="tpu_custom_call" | custom-call | tf_op jit(solution)/shard_map/own_pieces/pallas_call | solution.py:708
  8.2 0.1 collective-permute-done.1.got_ref
  8.2 0.5 %partner_pieces.1 = (bf16[4,3,32,128]{3,2,1,0:T(8,128)(2,1)S(1)}, f32[4,32,128]{2,1,0:T(8,128)S(1)}, bf16[2,32,128]{2,1,0:T(8,128)(2,1)S(1)}, bf16[2,32,128]{2,1,0:T(8,128)(2,1)S(1)}) custom-call(bf16[4,32,128]{2,1,0:T(8,128)(2,1)S(1)} %collective-permute-done.1.got_ref, bf16[128,1024]{1,0:T(8,128)(2,1)S(1)} %get-tuple-element.24.sorted_wt_ref, ...), custom_call_target="tpu_custom_call" | custom-call | tf_op jit(solution)/shard_map/partner_pieces/pallas_call | solution.py:726
  8.8 0.2 %collective-permute-start.2 = (bf16[2,32,128]{2,1,0:T(8,128)(2,1)S(1)}, bf16[2,32,128]{2,1,0:T(8,128)(2,1)S(1)}, u32[]{:S(2)}, u32[]{:S(2)}) collective-permute-start(bf16[2,32,128]{2,1,0:T(8,128)(2,1)S(1)} %get-tuple-element.30), channel_id=1, source_target_pairs={{0,1},{1,0},{2,3},{3,2},{4,5},{5,4},{6,7},{7,6},{8,9},{9,8},{10,11... | collective-permute-start | bytes 49160 | tf_op jit(solution)/shard_map/ppermute | solution.py:740
  9.0 2.7 %collective-permute-start.5 = (bf16[3,32,128]{2,1,0:T(8,128)(2,1)S(1)}, bf16[3,32,128]{2,1,0:T(8,128)(2,1)S(1)}, u32[]{:S(2)}, u32[]{:S(2)}) collective-permute-start(bf16[3,32,128]{2,1,0:T(8,128)(2,1)S(1)} %get-tuple-element.42), channel_id=1, source_target_pairs={{0,6},{2,4},{4,2},{6,0},{8,14},{10,12},{12,10},{14,8},{1,7},{3,5},... | collective-permute-start | bytes 73736 | tf_op jit(solution)/shard_map/ppermute | solution.py:700
  11.6 0.0 collective-permute-done.2.swapped_ref
  11.6 0.5 %collective-permute-start.4 = (bf16[4,32,128]{2,1,0:T(8,128)(2,1)S(1)}, bf16[4,32,128]{2,1,0:T(8,128)(2,1)S(1)}, u32[]{:S(2)}, u32[]{:S(2)}) collective-permute-start(bf16[4,32,128]{2,1,0:T(8,128)(2,1)S(1)} %get-tuple-element.45), channel_id=1, source_target_pairs={{0,4},{2,6},{4,0},{6,2},{8,12},{10,14},{12,8},{14,10},{1,5},{3,7},... | collective-permute-start | bytes 98312 | tf_op jit(solution)/shard_map/ppermute | solution.py:700
  12.2 1.2 %collective-permute-start.3 = (bf16[4,32,128]{2,1,0:T(8,128)(2,1)S(1)}, bf16[4,32,128]{2,1,0:T(8,128)(2,1)S(1)}, u32[]{:S(2)}, u32[]{:S(2)}) collective-permute-start(bf16[4,32,128]{2,1,0:T(8,128)(2,1)S(1)} %get-tuple-element.46), channel_id=1, source_target_pairs={{0,2},{2,0},{4,6},{6,4},{8,10},{10,8},{12,14},{14,12},{1,3},{3,1},... | collective-permute-start | bytes 98312 | tf_op jit(solution)/shard_map/ppermute | solution.py:700
  13.4 0.4 %collective-permute-done.5.part_refs_2_ = bf16[3,32,128]{2,1,0:T(8,128)(2,1)S(1)} collective-permute-done((bf16[3,32,128]{2,1,0:T(8,128)(2,1)S(1)}, bf16[3,32,128]{2,1,0:T(8,128)(2,1)S(1)}, u32[]{:S(2)}, u32[]{:S(2)}) %collective-permute-start.5) | collective-permute-done | bytes 24608 | tf_op jit(solution)/shard_map/ppermute | solution.py:700
  13.7 0.0 collective-permute-start.6
  13.7 1.2 %collective-permute-done.6.swapped_late_ref = bf16[32,128]{1,0:T(8,128)(2,1)S(1)} collective-permute-done((bf16[32,128]{1,0:T(8,128)(2,1)S(1)}, bf16[32,128]{1,0:T(8,128)(2,1)S(1)}, u32[]{:S(2)}, u32[]{:S(2)}) %collective-permute-start.6) | collective-permute-done | bytes 8224 | tf_op jit(solution)/shard_map/ppermute | solution.py:745
  14.9 0.7 %collective-permute-done.4.part_refs_1_ = bf16[4,32,128]{2,1,0:T(8,128)(2,1)S(1)} collective-permute-done((bf16[4,32,128]{2,1,0:T(8,128)(2,1)S(1)}, bf16[4,32,128]{2,1,0:T(8,128)(2,1)S(1)}, u32[]{:S(2)}, u32[]{:S(2)}) %collective-permute-start.4) | collective-permute-done | bytes 32800 | tf_op jit(solution)/shard_map/ppermute | solution.py:700
  15.6 0.4 %collective-permute-done.3.part_refs_0_ = bf16[4,32,128]{2,1,0:T(8,128)(2,1)S(1)} collective-permute-done((bf16[4,32,128]{2,1,0:T(8,128)(2,1)S(1)}, bf16[4,32,128]{2,1,0:T(8,128)(2,1)S(1)}, u32[]{:S(2)}, u32[]{:S(2)}) %collective-permute-start.3) | collective-permute-done | bytes 32800 | tf_op jit(solution)/shard_map/ppermute | solution.py:700
  16.1 1.3 %finish.1 = (bf16[32,4,256]{2,1,0:T(4,128)(2,1)}, bf16[4,16,128]{2,1,0:T(8,128)(2,1)}) custom-call(bf16[2,32,128]{2,1,0:T(8,128)(2,1)S(1)} %get-tuple-element.28.right_ref, bf16[4,32,128]{2,1,0:T(8,128)(2,1)S(1)} %collective-permute-done.3.part_refs_0_, bf16[4,32,128]{2,1,0:T(8,128)(2,1)S(1)} %collective-permute-done.4.part_refs_1_, ...), custom_call_target="tpu_custom_call" | custom-call | tf_op jit(solution)/shard_map/finish/pallas_call | solution.py:749
  (6 shorter events, 0.0 us)
Async XLA Ops:
  0.6 5.6 %copy-start = (bf16[1024,128]{1,0:T(8,128)(2,1)S(1)}, bf16[1024,128]{1,0:T(8,128)(2,1)}, u32[]{:S(2)}) copy-start(bf16[1024,128]{1,0:T(8,128)(2,1)} %w_ref.1) | copy-start | bytes 786436
  0.6 1.9 %collective-permute-start = (bf16[4,16,128]{2,1,0:T(8,128)(2,1)}, bf16[4,16,128]{2,1,0:T(8,128)(2,1)S(1)}, u32[]{:S(2)}, u32[]{:S(2)}) collective-permute-start(bf16[4,16,128]{2,1,0:T(8,128)(2,1)} %cot_hbm.1), channel_id=1, source_target_pairs={{0,1},{1,0},{2,3},{3,2},{4,5},{5,4},{6,7},{7,6},{8,9},{9,8},{10,11... | collective-permute-start | bytes 49160 | tf_op jit(solution)/shard_map/ppermute | solution.py:655
  2.5 5.7 %collective-permute-start.1 = (bf16[4,32,128]{2,1,0:T(8,128)(2,1)S(1)}, bf16[4,32,128]{2,1,0:T(8,128)(2,1)S(1)}, u32[]{:S(2)}, u32[]{:S(2)}) collective-permute-start(bf16[4,32,128]{2,1,0:T(8,128)(2,1)S(1)} %pad_maximum_fusion.2), channel_id=1, source_target_pairs={{0,8},{2,10},{4,12},{6,14},{8,0},{10,2},{12,4},{14,6},{1,9},{3,11}... | collective-permute-start | bytes 98312 | tf_op jit(solution)/shard_map/ppermute | solution.py:700
  8.8 2.9 %collective-permute-start.2 = (bf16[2,32,128]{2,1,0:T(8,128)(2,1)S(1)}, bf16[2,32,128]{2,1,0:T(8,128)(2,1)S(1)}, u32[]{:S(2)}, u32[]{:S(2)}) collective-permute-start(bf16[2,32,128]{2,1,0:T(8,128)(2,1)S(1)} %get-tuple-element.30), channel_id=1, source_target_pairs={{0,1},{1,0},{2,3},{3,2},{4,5},{5,4},{6,7},{7,6},{8,9},{9,8},{10,11... | collective-permute-start | bytes 49160 | tf_op jit(solution)/shard_map/ppermute | solution.py:740
  9.0 4.8 %collective-permute-start.5 = (bf16[3,32,128]{2,1,0:T(8,128)(2,1)S(1)}, bf16[3,32,128]{2,1,0:T(8,128)(2,1)S(1)}, u32[]{:S(2)}, u32[]{:S(2)}) collective-permute-start(bf16[3,32,128]{2,1,0:T(8,128)(2,1)S(1)} %get-tuple-element.42), channel_id=1, source_target_pairs={{0,6},{2,4},{4,2},{6,0},{8,14},{10,12},{12,10},{14,8},{1,7},{3,5},... | collective-permute-start | bytes 73736 | tf_op jit(solution)/shard_map/ppermute | solution.py:700
  11.6 4.0 %collective-permute-start.4 = (bf16[4,32,128]{2,1,0:T(8,128)(2,1)S(1)}, bf16[4,32,128]{2,1,0:T(8,128)(2,1)S(1)}, u32[]{:S(2)}, u32[]{:S(2)}) collective-permute-start(bf16[4,32,128]{2,1,0:T(8,128)(2,1)S(1)} %get-tuple-element.45), channel_id=1, source_target_pairs={{0,4},{2,6},{4,0},{6,2},{8,12},{10,14},{12,8},{14,10},{1,5},{3,7},... | collective-permute-start | bytes 98312 | tf_op jit(solution)/shard_map/ppermute | solution.py:700
  12.2 3.9 %collective-permute-start.3 = (bf16[4,32,128]{2,1,0:T(8,128)(2,1)S(1)}, bf16[4,32,128]{2,1,0:T(8,128)(2,1)S(1)}, u32[]{:S(2)}, u32[]{:S(2)}) collective-permute-start(bf16[4,32,128]{2,1,0:T(8,128)(2,1)S(1)} %get-tuple-element.46), channel_id=1, source_target_pairs={{0,2},{2,0},{4,6},{6,4},{8,10},{10,8},{12,14},{14,12},{1,3},{3,1},... | collective-permute-start | bytes 98312 | tf_op jit(solution)/shard_map/ppermute | solution.py:700
  13.7 1.2 %collective-permute-start.6 = (bf16[32,128]{1,0:T(8,128)(2,1)S(1)}, bf16[32,128]{1,0:T(8,128)(2,1)S(1)}, u32[]{:S(2)}, u32[]{:S(2)}) collective-permute-start(bf16[32,128]{1,0:T(8,128)(2,1)S(1)} %fusion), channel_id=1, source_target_pairs={{0,1},{1,0},{2,3},{3,2},{4,5},{5,4},{6,7},{7,6},{8,9},{9,8},{10,11... | collective-permute-start | bytes 24584 | tf_op jit(solution)/shard_map/ppermute | solution.py:745

commit v15 on v14

--- a/solution.py
+++ b/solution.py
@@ -520,10 +520,25 @@
         keep_out_ref[distance] = total
 
 
+def small_prepare_kernel(both_ref, swapped_ref, repeat_ref, keep_ref, part_ref,
+                         apart_ref, order_ref, right_cot_ref):
+    residues = apart_ref.shape[1] // LANES
+    depth = LANES // residues
+    left = jnp.concatenate([both_ref[0], swapped_ref[1]], axis=0)
+    apart_ref[...] = blocks_apart(left, repeat_ref[...], residues)
+    order_ref[...] = one_hot(
+        lambda row: (
+            (row & 3) * LANES + (row >> 2 & 7) * (4 * residues) + (row >> 7) * residues + (row >> 5 & 3)
+        ),
+        order_ref.shape,
+    )
+    right_cot_ref[...] = keep_ref[0] + part_ref[2].astype(F32)
+
+
 def small_finish_kernel(
-    scale, right_ref, part_refs, swapped_ref, swapped_late_ref, both_ref, outer_near_ref, outer_far_ref,
-    keep_ref, normed_ref, inv_std_ref, gain_ref, spread_w_ref, sorted_w_ref, offset_ref,
-    grad_hbm, pair_hbm, grad_ref, pair_ref, near_ref, beyond_ref, turn_ref, semaphores,
+    scale, right_ref, part_refs, swapped_ref, swapped_late_ref, outer_near_ref, outer_far_ref,
+    right_cot_ref, normed_ref, inv_std_ref, gain_ref, spread_w_ref, sorted_w_ref, offset_ref, apart_ref,
+    order_ref, grad_hbm, pair_hbm, grad_ref, pair_ref, near_ref, beyond_ref, semaphores,
 ):
     seqs, residues, _ = grad_ref.shape
     columns = pair_ref.shape[1]
@@ -546,8 +561,8 @@
         axis=0,
     )
     left_cot = jnp.dot(right_all, outer, preferred_element_type=F32)
-    right_cot = keep_ref[0]
-    for part_ref in part_refs:
+    right_cot = right_cot_ref[...]
+    for part_ref in part_refs[:2]:
         right_cot = right_cot + part_ref[2].astype(F32)
     blocks = lane_block((seqs, LANES), depth)
     spread = jnp.concatenate(
@@ -590,33 +605,24 @@
         ],
         axis=0,
     )
-    left = jnp.concatenate([both_ref[0], swapped_ref[1]], axis=0)
-    turn_ref[...] = lax.dot_general(right, left, TN, preferred_element_type=F32) * scale
-    blocks = lane_block((columns, LANES), depth)
-    tiles = []
-    for tile in range(depth * depth // LANES):
-        pieces = [
-            turn_ref[pl.ds(tile * residues + e, columns, stride=depth), :]
-            for e in range(residues)
-        ]
-        lines = jnp.concatenate(pieces, axis=0)
-        turned = [lines] + [pltpu.roll(lines, depth * t, 1) for t in range(1, residues)]
-        tiles.append(
+    right = jnp.dot(right, order_ref[...], preferred_element_type=F32).astype(BF16)
+    right = jnp.concatenate(
+        [right[:, e * LANES : (e + 1) * LANES] for e in range(residues)], axis=0
+    )
+    flat = lax.dot_general(right, apart_ref[...], TN, preferred_element_type=F32) * scale
+    flat = jnp.concatenate(
+        [
             jnp.concatenate(
                 [
-                    pick(
-                        blocks,
-                        [
-                            turned[(e - i) % residues][e * columns : (e + 1) * columns]
-                            for e in range(residues)
-                        ],
-                    )
-                    for i in range(residues)
+                    flat[tile * columns : (tile + 1) * columns, i * LANES : (i + 1) * LANES]
+                    for tile in range(depth * depth // LANES)
                 ],
-                axis=0,
+                axis=1,
             )
-        )
-    flat = jnp.concatenate(tiles, axis=1)
+            for i in range(residues)
+        ],
+        axis=0,
+    )
     rows = residues * columns
     parts = jnp.concatenate(split_two(flat), axis=0)
     pair = jnp.dot(parts, sorted_w_ref[...], preferred_element_type=F32)
@@ -746,9 +752,22 @@
         jnp.where(own_is_near, diagonal[1], diagonal[0]), "seq", swap
     )
 
+    apart, column_order, right_cot = pl.pallas_call(
+        small_prepare_kernel,
+        in_specs=[vmem] * 5,
+        out_specs=[vmem] * 3,
+        out_shape=(
+            like((2 * residues * seqs, residues * LANES), BF16),
+            like((half_rows, half_rows), BF16),
+            like((seqs, LANES), F32),
+        ),
+        compiler_params=limit,
+        name="prepare",
+    )(both, swapped, repeat, keep, diagonal)
+
     pair_delta, gradient = pl.pallas_call(
         functools.partial(small_finish_kernel, scale),
-        in_specs=[vmem, [vmem] * 3] + [vmem] * 12,
+        in_specs=[vmem, [vmem] * 3] + [vmem] * 13,
         out_specs=[pl.BlockSpec(memory_space=pl.ANY)] * 2,
         out_shape=(
             like(homolog_matrix.shape, BF16),
@@ -759,7 +778,6 @@
             pltpu.VMEM(coupling_cotangent.shape, BF16),
             pltpu.VMEM((ranks // 2, seqs, LANES), BF16),
             pltpu.VMEM((ranks // 2, seqs, LANES), BF16),
-            pltpu.VMEM((ranks // 2 * LANES, LANES), F32),
             pltpu.SemaphoreType.DMA((2,)),
         ],
         compiler_params=limit,
@@ -769,16 +787,17 @@
         [beside, across, diagonal],
         swapped,
         swapped_late,
-        both,
         outer_near,
         outer_far,
-        keep,
+        right_cot,
         normed,
         inv_std,
         gain,
         spread_w,
         sorted_w,
         pair_offset,
+        apart,
+        column_order,
     )[::-1]
     return (pair_delta, gradient)
 

time: 17.6 us -> 17.7 us (level)
  Pallas kernels: 5.11 us -> 5.68 us
  waiting for transfers between devices: 2.8 us -> 2.34 us
    ppermute x1, waiting for transfers between devices: 1.17 us -> 0.71 us  [small_slice(): lax.ppermute(jnp.where(own_is_near, diagonal[1], diagonal[0]), 'seq', swap)]
    pallas_call x0 -> x1, Pallas kernels: none -> 0.45 us  [small_slice(): pl.pallas_call(small_prepare_kernel, in_specs=[vmem] * 5, out_specs=[vmem...]
  transfers between devices with their start and end apart: 7 -> 7, of which waited for: 5 -> 5; matrix products, arithmetic and copies ran while one was open for 0% -> 0% of each run, Pallas kernels for 19% -> 21%
where the time goes in v15:
time: 17.7 us; the launch traced here: 17.5 us
  starting transfers between devices  8.77 us (50%)
  Pallas kernels  5.68 us (32%)
  waiting for transfers between devices  2.34 us (13%)
  between operations  0.71 us (4%)
    ppermute x4, starting transfers between devices, swap_over(): lax.ppermute(value, 'res', [(source, source ^ mask) for source in range(r...  8.07 us
    pallas_call x1, Pallas kernels, small_slice(): pl.pallas_call(functools.partial(small_own_kernel, scale), in_specs=[vmem...  1.93 us
    ppermute x4, waiting for transfers between devices, swap_over(): lax.ppermute(value, 'res', [(source, source ^ mask) for source in range(r...  1.62 us
    pallas_call x1, Pallas kernels, small_slice(): pl.pallas_call(functools.partial(small_finish_kernel, scale), in_specs=[v...  1.46 us
    pallas_call x1, Pallas kernels, small_slice(): pl.pallas_call(small_project_kernel, in_specs=[hbm] * 9, out_specs=[vmem]...  1.32 us
    ppermute x1, waiting for transfers between devices, small_slice(): lax.ppermute(jnp.where(own_is_near, diagonal[1], diagonal[0]), 'seq', swap)  0.71 us
    ppermute x1, starting transfers between devices, small_slice(): other_cot = lax.ppermute(coupling_cotangent, 'seq', swap)  0.52 us
    pallas_call x1, Pallas kernels, small_slice(): pl.pallas_call(functools.partial(small_partner_kernel, scale, residues),...  0.51 us
  transfers between devices with their start and end apart: 7, of which 5 were waited for; matrix products, arithmetic and copies ran while one was open for 0% of the time, Pallas kernels for 21%

profile of v15, /device:TPU:0, one launch (start us, length us, event | category | flops | bytes accessed | tf_op | source)
XLA Modules:
  0.0 17.5 jit_solution(16258400488839160080)
XLA Ops:
  0.6 0.0 copy-start
  0.6 0.5 %collective-permute-start = (bf16[4,16,128]{2,1,0:T(8,128)(2,1)}, bf16[4,16,128]{2,1,0:T(8,128)(2,1)S(1)}, u32[]{:S(2)}, u32[]{:S(2)}) collective-permute-start(bf16[4,16,128]{2,1,0:T(8,128)(2,1)} %cot_hbm.1), channel_id=1, source_target_pairs={{0,1},{1,0},{2,3},{3,2},{4,5},{5,4},{6,7},{7,6},{8,9},{9,8},{10,11... | collective-permute-start | bytes 49160 | tf_op jit(solution)/shard_map/ppermute | solution.py:661
  1.2 1.3 %project.1 = (bf16[2,32,128]{2,1,0:T(8,128)(2,1)S(1)}, f32[128,256]{1,0:T(8,128)S(1)}, f32[128,128]{1,0:T(8,128)S(1)}, bf16[256,256]{1,0:T(8,128)(2,1)S(1)}, f32...) custom-call(bf16[32,4,256]{2,1,0:T(4,128)(2,1)} %x_hbm.1, f32[1,256]{1,0:T(1,128)} %bitcast.19, ...), custom_call_target="tpu_custom_call" | custom-call | tf_op jit(solution)/shard_map/project/pallas_call | solution.py:664
  2.5 0.0 collective-permute-done.other_ref
  2.5 3.7 %collective-permute-start.1 = (bf16[4,32,128]{2,1,0:T(8,128)(2,1)S(1)}, bf16[4,32,128]{2,1,0:T(8,128)(2,1)S(1)}, u32[]{:S(2)}, u32[]{:S(2)}) collective-permute-start(bf16[4,32,128]{2,1,0:T(8,128)(2,1)S(1)} %pad_maximum_fusion.2), channel_id=1, source_target_pairs={{0,8},{2,10},{4,12},{6,14},{8,0},{10,2},{12,4},{14,6},{1,9},{3,11}... | collective-permute-start | bytes 98312 | tf_op jit(solution)/shard_map/ppermute | solution.py:706
  6.2 0.0 copy-done
  6.2 1.9 %own_pieces.1 = (f32[4,32,128]{2,1,0:T(8,128)S(1)}, bf16[512,128]{1,0:T(8,128)(2,1)S(1)}, bf16[512,128]{1,0:T(8,128)(2,1)S(1)}, bf16[1024,128]{1,0:T(8,128)(2,1)...) custom-call(bf16[4,16,128]{2,1,0:T(8,128)(2,1)S(1)} %get-tuple-element.26.own_ref, ...), custom_call_target="tpu_custom_call" | custom-call | tf_op jit(solution)/shard_map/own_pieces/pallas_call | solution.py:714
  8.2 0.1 collective-permute-done.1.got_ref
  8.2 0.5 %partner_pieces.1 = (bf16[4,3,32,128]{3,2,1,0:T(8,128)(2,1)S(1)}, f32[4,32,128]{2,1,0:T(8,128)S(1)}, bf16[2,32,128]{2,1,0:T(8,128)(2,1)S(1)}, bf16[2,32,128]{2,1,0:T(8,128)(2,1)S(1)}) custom-call(bf16[4,32,128]{2,1,0:T(8,128)(2,1)S(1)} %collective-permute-done.1.got_ref, bf16[128,1024]{1,0:T(8,128)(2,1)S(1)} %get-tuple-element.27.sorted_wt_ref, ...), custom_call_target="tpu_custom_call" | custom-call | tf_op jit(solution)/shard_map/partner_pieces/pallas_call | solution.py:732
  8.8 0.2 %collective-permute-start.2 = (bf16[2,32,128]{2,1,0:T(8,128)(2,1)S(1)}, bf16[2,32,128]{2,1,0:T(8,128)(2,1)S(1)}, u32[]{:S(2)}, u32[]{:S(2)}) collective-permute-start(bf16[2,32,128]{2,1,0:T(8,128)(2,1)S(1)} %get-tuple-element.33), channel_id=1, source_target_pairs={{0,1},{1,0},{2,3},{3,2},{4,5},{5,4},{6,7},{7,6},{8,9},{9,8},{10,11... | collective-permute-start | bytes 49160 | tf_op jit(solution)/shard_map/ppermute | solution.py:746
  9.0 2.7 %collective-permute-start.5 = (bf16[3,32,128]{2,1,0:T(8,128)(2,1)S(1)}, bf16[3,32,128]{2,1,0:T(8,128)(2,1)S(1)}, u32[]{:S(2)}, u32[]{:S(2)}) collective-permute-start(bf16[3,32,128]{2,1,0:T(8,128)(2,1)S(1)} %get-tuple-element.48), channel_id=1, source_target_pairs={{0,6},{2,4},{4,2},{6,0},{8,14},{10,12},{12,10},{14,8},{1,7},{3,5},... | collective-permute-start | bytes 73736 | tf_op jit(solution)/shard_map/ppermute | solution.py:706
  11.6 0.0 collective-permute-done.2.swapped_ref
  11.6 0.5 %collective-permute-start.4 = (bf16[4,32,128]{2,1,0:T(8,128)(2,1)S(1)}, bf16[4,32,128]{2,1,0:T(8,128)(2,1)S(1)}, u32[]{:S(2)}, u32[]{:S(2)}) collective-permute-start(bf16[4,32,128]{2,1,0:T(8,128)(2,1)S(1)} %get-tuple-element.51), channel_id=1, source_target_pairs={{0,4},{2,6},{4,0},{6,2},{8,12},{10,14},{12,8},{14,10},{1,5},{3,7},... | collective-permute-start | bytes 98312 | tf_op jit(solution)/shard_map/ppermute | solution.py:706
  12.2 1.2 %collective-permute-start.3 = (bf16[4,32,128]{2,1,0:T(8,128)(2,1)S(1)}, bf16[4,32,128]{2,1,0:T(8,128)(2,1)S(1)}, u32[]{:S(2)}, u32[]{:S(2)}) collective-permute-start(bf16[4,32,128]{2,1,0:T(8,128)(2,1)S(1)} %get-tuple-element.52), channel_id=1, source_target_pairs={{0,2},{2,0},{4,6},{6,4},{8,10},{10,8},{12,14},{14,12},{1,3},{3,1},... | collective-permute-start | bytes 98312 | tf_op jit(solution)/shard_map/ppermute | solution.py:706
  13.4 0.3 %collective-permute-done.5.part_ref.part_refs_2_ = bf16[3,32,128]{2,1,0:T(8,128)(2,1)S(1)} collective-permute-done((bf16[3,32,128]{2,1,0:T(8,128)(2,1)S(1)}, bf16[3,32,128]{2,1,0:T(8,128)(2,1)S(1)}, u32[]{:S(2)}, u32[]{:S(2)}) %collective-permute-start.5) | collective-permute-done | bytes 24608 | tf_op jit(solution)/shard_map/ppermute | solution.py:706
  13.7 0.0 collective-permute-start.6
  13.7 0.5 %prepare.1 = (bf16[256,512]{1,0:T(8,128)(2,1)S(1)}, bf16[512,512]{1,0:T(8,128)(2,1)S(1)}, f32[32,128]{1,0:T(8,128)S(1)}) custom-call(bf16[2,32,128]{2,1,0:T(8,128)(2,1)S(1)} %get-tuple-element.25.both_ref, bf16[2,32,128]{2,1,0:T(8,128)(2,1)S(1)} %collective-permute-done.2.swapped_ref, bf16[128,512]{1,0:T(8,128)(2,1)S(1)} %get-tuple-element.30.repeat_ref, ...), custom_call_target="tpu_custom_call" | custom-call | tf_op jit(solution)/shard_map/prepare/pallas_call | solution.py:755
  14.2 0.7 %collective-permute-done.6.swapped_late_ref = bf16[32,128]{1,0:T(8,128)(2,1)S(1)} collective-permute-done((bf16[32,128]{1,0:T(8,128)(2,1)S(1)}, bf16[32,128]{1,0:T(8,128)(2,1)S(1)}, u32[]{:S(2)}, u32[]{:S(2)}) %collective-permute-start.6) | collective-permute-done | bytes 8224 | tf_op jit(solution)/shard_map/ppermute | solution.py:751
  14.9 0.8 %collective-permute-done.4.part_refs_1_ = bf16[4,32,128]{2,1,0:T(8,128)(2,1)S(1)} collective-permute-done((bf16[4,32,128]{2,1,0:T(8,128)(2,1)S(1)}, bf16[4,32,128]{2,1,0:T(8,128)(2,1)S(1)}, u32[]{:S(2)}, u32[]{:S(2)}) %collective-permute-start.4) | collective-permute-done | bytes 32800 | tf_op jit(solution)/shard_map/ppermute | solution.py:706
  15.6 0.4 %collective-permute-done.3.part_refs_0_ = bf16[4,32,128]{2,1,0:T(8,128)(2,1)S(1)} collective-permute-done((bf16[4,32,128]{2,1,0:T(8,128)(2,1)S(1)}, bf16[4,32,128]{2,1,0:T(8,128)(2,1)S(1)}, u32[]{:S(2)}, u32[]{:S(2)}) %collective-permute-start.3) | collective-permute-done | bytes 32800 | tf_op jit(solution)/shard_map/ppermute | solution.py:706
  16.1 1.5 %finish.1 = (bf16[32,4,256]{2,1,0:T(4,128)(2,1)}, bf16[4,16,128]{2,1,0:T(8,128)(2,1)}) custom-call(bf16[2,32,128]{2,1,0:T(8,128)(2,1)S(1)} %get-tuple-element.31.right_ref, bf16[4,32,128]{2,1,0:T(8,128)(2,1)S(1)} %collective-permute-done.3.part_refs_0_, bf16[4,32,128]{2,1,0:T(8,128)(2,1)S(1)} %collective-permute-done.4.part_refs_1_, ...), custom_call_target="tpu_custom_call" | custom-call | tf_op jit(solution)/shard_map/finish/pallas_call | solution.py:768
  (6 shorter events, 0.0 us)
Async XLA Ops:
  0.6 5.6 %copy-start = (bf16[1024,128]{1,0:T(8,128)(2,1)S(1)}, bf16[1024,128]{1,0:T(8,128)(2,1)}, u32[]{:S(2)}) copy-start(bf16[1024,128]{1,0:T(8,128)(2,1)} %w_ref.1) | copy-start | bytes 786436
  0.6 1.9 %collective-permute-start = (bf16[4,16,128]{2,1,0:T(8,128)(2,1)}, bf16[4,16,128]{2,1,0:T(8,128)(2,1)S(1)}, u32[]{:S(2)}, u32[]{:S(2)}) collective-permute-start(bf16[4,16,128]{2,1,0:T(8,128)(2,1)} %cot_hbm.1), channel_id=1, source_target_pairs={{0,1},{1,0},{2,3},{3,2},{4,5},{5,4},{6,7},{7,6},{8,9},{9,8},{10,11... | collective-permute-start | bytes 49160 | tf_op jit(solution)/shard_map/ppermute | solution.py:661
  2.5 5.7 %collective-permute-start.1 = (bf16[4,32,128]{2,1,0:T(8,128)(2,1)S(1)}, bf16[4,32,128]{2,1,0:T(8,128)(2,1)S(1)}, u32[]{:S(2)}, u32[]{:S(2)}) collective-permute-start(bf16[4,32,128]{2,1,0:T(8,128)(2,1)S(1)} %pad_maximum_fusion.2), channel_id=1, source_target_pairs={{0,8},{2,10},{4,12},{6,14},{8,0},{10,2},{12,4},{14,6},{1,9},{3,11}... | collective-permute-start | bytes 98312 | tf_op jit(solution)/shard_map/ppermute | solution.py:706
  8.8 2.9 %collective-permute-start.2 = (bf16[2,32,128]{2,1,0:T(8,128)(2,1)S(1)}, bf16[2,32,128]{2,1,0:T(8,128)(2,1)S(1)}, u32[]{:S(2)}, u32[]{:S(2)}) collective-permute-start(bf16[2,32,128]{2,1,0:T(8,128)(2,1)S(1)} %get-tuple-element.33), channel_id=1, source_target_pairs={{0,1},{1,0},{2,3},{3,2},{4,5},{5,4},{6,7},{7,6},{8,9},{9,8},{10,11... | collective-permute-start | bytes 49160 | tf_op jit(solution)/shard_map/ppermute | solution.py:746
  9.0 4.7 %collective-permute-start.5 = (bf16[3,32,128]{2,1,0:T(8,128)(2,1)S(1)}, bf16[3,32,128]{2,1,0:T(8,128)(2,1)S(1)}, u32[]{:S(2)}, u32[]{:S(2)}) collective-permute-start(bf16[3,32,128]{2,1,0:T(8,128)(2,1)S(1)} %get-tuple-element.48), channel_id=1, source_target_pairs={{0,6},{2,4},{4,2},{6,0},{8,14},{10,12},{12,10},{14,8},{1,7},{3,5},... | collective-permute-start | bytes 73736 | tf_op jit(solution)/shard_map/ppermute | solution.py:706
  11.6 4.0 %collective-permute-start.4 = (bf16[4,32,128]{2,1,0:T(8,128)(2,1)S(1)}, bf16[4,32,128]{2,1,0:T(8,128)(2,1)S(1)}, u32[]{:S(2)}, u32[]{:S(2)}) collective-permute-start(bf16[4,32,128]{2,1,0:T(8,128)(2,1)S(1)} %get-tuple-element.51), channel_id=1, source_target_pairs={{0,4},{2,6},{4,0},{6,2},{8,12},{10,14},{12,8},{14,10},{1,5},{3,7},... | collective-permute-start | bytes 98312 | tf_op jit(solution)/shard_map/ppermute | solution.py:706
  12.2 3.9 %collective-permute-start.3 = (bf16[4,32,128]{2,1,0:T(8,128)(2,1)S(1)}, bf16[4,32,128]{2,1,0:T(8,128)(2,1)S(1)}, u32[]{:S(2)}, u32[]{:S(2)}) collective-permute-start(bf16[4,32,128]{2,1,0:T(8,128)(2,1)S(1)} %get-tuple-element.52), channel_id=1, source_target_pairs={{0,2},{2,0},{4,6},{6,4},{8,10},{10,8},{12,14},{14,12},{1,3},{3,1},... | collective-permute-start | bytes 98312 | tf_op jit(solution)/shard_map/ppermute | solution.py:706
  13.7 1.2 %collective-permute-start.6 = (bf16[32,128]{1,0:T(8,128)(2,1)S(1)}, bf16[32,128]{1,0:T(8,128)(2,1)S(1)}, u32[]{:S(2)}, u32[]{:S(2)}) collective-permute-start(bf16[32,128]{1,0:T(8,128)(2,1)S(1)} %fusion), channel_id=1, source_target_pairs={{0,1},{1,0},{2,3},{3,2},{4,5},{5,4},{6,7},{7,6},{8,9},{9,8},{10,11... | collective-permute-start | bytes 24584 | tf_op jit(solution)/shard_map/ppermute | solution.py:751

commit v16 on v15

--- a/solution.py
+++ b/solution.py
@@ -520,49 +520,101 @@
         keep_out_ref[distance] = total
 
 
-def small_prepare_kernel(both_ref, swapped_ref, repeat_ref, keep_ref, part_ref,
-                         apart_ref, order_ref, right_cot_ref):
-    residues = apart_ref.shape[1] // LANES
+def pair_rows(scale, right, left, residues, sorted_w_ref, turn_ref):
     depth = LANES // residues
+    columns = right.shape[1] // depth
+    turn_ref[...] = lax.dot_general(right, left, TN, preferred_element_type=F32) * scale
+    blocks = lane_block((columns, LANES), depth)
+    tiles = []
+    for tile in range(depth * depth // LANES):
+        pieces = [
+            turn_ref[pl.ds(tile * residues + e, columns, stride=depth), :]
+            for e in range(residues)
+        ]
+        lines = jnp.concatenate(pieces, axis=0)
+        turned = [lines] + [pltpu.roll(lines, depth * t, 1) for t in range(1, residues)]
+        tiles.append(
+            jnp.concatenate(
+                [
+                    pick(
+                        blocks,
+                        [
+                            turned[(e - i) % residues][e * columns : (e + 1) * columns]
+                            for e in range(residues)
+                        ],
+                    )
+                    for i in range(residues)
+                ],
+                axis=0,
+            )
+        )
+    flat = jnp.concatenate(tiles, axis=1)
+    rows = residues * columns
+    parts = jnp.concatenate(split_two(flat), axis=0)
+    pair = jnp.dot(parts, sorted_w_ref[...], preferred_element_type=F32)
+    return pair[0:rows] + pair[rows : 2 * rows]
+
+
+def left_share(block_refs, masks, outer_near_ref, outer_far_ref):
+    here = lax.axis_index("res") & 3
+    spots = [
+        pl.ds(pl.multiple_of(lax.bitwise_xor(here, mask) * LANES, LANES), LANES) for mask in masks
+    ]
+    right = jnp.concatenate([ref[0] for ref in block_refs] + [ref[1] for ref in block_refs], axis=1)
+    outer = jnp.concatenate(
+        [outer_near_ref[spot, :] for spot in spots] + [outer_far_ref[spot, :] for spot in spots],
+        axis=0,
+    )
+    return jnp.dot(right, outer, preferred_element_type=F32)
+
+
+def own_half():
+    near = lax.axis_index("seq") == lax.shift_right_logical(lax.axis_index("res"), 2)
+    return jnp.where(near, 0, 1)
+
+
+def small_early_kernel(
+    scale, right_ref, part_ref, swapped_ref, swapped_late_ref, both_ref, outer_near_ref, outer_far_ref,
+    keep_ref, sorted_w_ref,
+    pair_ref, left_cot_ref, right_cot_ref, turn_ref,
+):
+    residues = pair_ref.shape[1] // 4
+    left_cot_ref[...] = left_share([right_ref, part_ref], (0, 3), outer_near_ref, outer_far_ref)
+    right_cot_ref[...] = keep_ref[0] + part_ref[2].astype(F32)
+    half = own_half()
+    right = jnp.concatenate(
+        [
+            jnp.concatenate([right_ref[half], part_ref[half]], axis=1),
+            jnp.concatenate([swapped_ref[0], swapped_late_ref[...]], axis=1),
+        ],
+        axis=0,
+    )
     left = jnp.concatenate([both_ref[0], swapped_ref[1]], axis=0)
-    apart_ref[...] = blocks_apart(left, repeat_ref[...], residues)
-    order_ref[...] = one_hot(
-        lambda row: (
-            (row & 3) * LANES + (row >> 2 & 7) * (4 * residues) + (row >> 7) * residues + (row >> 5 & 3)
-        ),
-        order_ref.shape,
-    )
-    right_cot_ref[...] = keep_ref[0] + part_ref[2].astype(F32)
+    pair = pair_rows(scale, right, left, residues, sorted_w_ref, turn_ref)
+    store_pairs(pair, (0, 1), residues, pair_ref)
+
+
+def store_pairs(pair, spots, residues, pair_ref):
+    columns = pair.shape[0] // residues // len(spots)
+    for i in range(residues):
+        for place, spot in enumerate(spots):
+            start = (i * len(spots) + place) * columns
+            pair_ref[spot, i * columns : (i + 1) * columns, :] = pair[start : start + columns]
 
 
 def small_finish_kernel(
-    scale, right_ref, part_refs, swapped_ref, swapped_late_ref, outer_near_ref, outer_far_ref,
-    right_cot_ref, normed_ref, inv_std_ref, gain_ref, spread_w_ref, sorted_w_ref, offset_ref, apart_ref,
-    order_ref, grad_hbm, pair_hbm, grad_ref, pair_ref, near_ref, beyond_ref, semaphores,
+    scale, part_refs, swapped_ref, both_ref, outer_near_ref, outer_far_ref, early_pair_ref,
+    early_left_ref, early_right_ref, normed_ref, inv_std_ref, gain_ref, spread_w_ref, sorted_w_ref,
+    offset_ref, grad_hbm, pair_hbm, grad_ref, pair_ref, pairs_ref, turn_ref, semaphores,
 ):
     seqs, residues, _ = grad_ref.shape
     columns = pair_ref.shape[1]
     depth = LANES // residues
     ranks = columns // residues
-    rank = lax.axis_index("res")
-    mine = lax.axis_index("seq")
-    here = rank & 3
-
-    blocks_of = [right_ref] + list(part_refs)
-    right_all = jnp.concatenate(
-        [ref[0] for ref in blocks_of] + [ref[1] for ref in blocks_of], axis=1
-    )
-    spots = [
-        pl.ds(pl.multiple_of(lax.bitwise_xor(here, mask) * LANES, LANES), LANES)
-        for mask in range(ranks)
-    ]
-    outer = jnp.concatenate(
-        [outer_near_ref[spot, :] for spot in spots] + [outer_far_ref[spot, :] for spot in spots],
-        axis=0,
-    )
-    left_cot = jnp.dot(right_all, outer, preferred_element_type=F32)
-    right_cot = right_cot_ref[...]
-    for part_ref in part_refs[:2]:
+
+    left_cot = early_left_ref[...] + left_share(part_refs, (1, 2), outer_near_ref, outer_far_ref)
+    right_cot = early_right_ref[...]
+    for part_ref in part_refs:
         right_cot = right_cot + part_ref[2].astype(F32)
     blocks = lane_block((seqs, LANES), depth)
     spread = jnp.concatenate(
@@ -590,44 +642,24 @@
     grad_copy = pltpu.make_async_copy(grad_ref, grad_hbm, semaphores.at[0])
     grad_copy.start()
 
-    half = jnp.where(mine == lax.shift_right_logical(rank, 2), 0, 1)
-    for mask, ref in enumerate(blocks_of):
-        near_ref[mask] = ref[half]
-    beyond_ref[0] = swapped_ref[0]
-    beyond_ref[1] = part_refs[0][3]
-    beyond_ref[2] = part_refs[1][3]
-    beyond_ref[3] = swapped_late_ref[...]
-    masks = [lax.bitwise_xor(here, place) for place in range(ranks)]
+    half = own_half()
     right = jnp.concatenate(
         [
-            jnp.concatenate([ref[mask] for mask in masks], axis=1)
-            for ref in (near_ref, beyond_ref)
+            jnp.concatenate([ref[half] for ref in part_refs], axis=1),
+            jnp.concatenate([ref[3] for ref in part_refs], axis=1),
         ],
         axis=0,
     )
-    right = jnp.dot(right, order_ref[...], preferred_element_type=F32).astype(BF16)
-    right = jnp.concatenate(
-        [right[:, e * LANES : (e + 1) * LANES] for e in range(residues)], axis=0
-    )
-    flat = lax.dot_general(right, apart_ref[...], TN, preferred_element_type=F32) * scale
-    flat = jnp.concatenate(
-        [
-            jnp.concatenate(
-                [
-                    flat[tile * columns : (tile + 1) * columns, i * LANES : (i + 1) * LANES]
-                    for tile in range(depth * depth // LANES)
-                ],
-                axis=1,
-            )
-            for i in range(residues)
-        ],
-        axis=0,
-    )
-    rows = residues * columns
-    parts = jnp.concatenate(split_two(flat), axis=0)
-    pair = jnp.dot(parts, sorted_w_ref[...], preferred_element_type=F32)
-    pair = pair[0:rows] + pair[rows : 2 * rows]
-    pair_ref[...] = (pair + offset_ref[...]).astype(BF16).reshape(pair_ref.shape)
+    left = jnp.concatenate([both_ref[0], swapped_ref[1]], axis=0)
+    pair = pair_rows(scale, right, left, residues, sorted_w_ref, turn_ref)
+    pairs_ref[0] = early_pair_ref[0]
+    pairs_ref[3] = early_pair_ref[1]
+    store_pairs(pair, (1, 2), residues, pairs_ref)
+    here = lax.axis_index("res") & 3
+    placed = [pairs_ref[lax.bitwise_xor(here, place)] for place in range(ranks)]
+    for i in range(residues):
+        own = [block[i * residues : (i + 1) * residues] for block in placed]
+        pair_ref[i] = (jnp.concatenate(own, axis=0) + offset_ref[...]).astype(BF16)
     pair_copy = pltpu.make_async_copy(pair_ref, pair_hbm, semaphores.at[1])
     pair_copy.start()
     grad_copy.wait()
@@ -752,22 +784,24 @@
         jnp.where(own_is_near, diagonal[1], diagonal[0]), "seq", swap
     )
 
-    apart, column_order, right_cot = pl.pallas_call(
-        small_prepare_kernel,
-        in_specs=[vmem] * 5,
+    pair_turn = pltpu.VMEM((2 * LANES, LANES), F32)
+    early_pair, early_left, early_right = pl.pallas_call(
+        functools.partial(small_early_kernel, scale),
+        in_specs=[vmem] * 9,
         out_specs=[vmem] * 3,
         out_shape=(
-            like((2 * residues * seqs, residues * LANES), BF16),
-            like((half_rows, half_rows), BF16),
+            like((2, residues * residues, LANES), F32),
             like((seqs, LANES), F32),
-        ),
+            like((seqs, LANES), F32),
+        ),
+        scratch_shapes=[pair_turn],
         compiler_params=limit,
-        name="prepare",
-    )(both, swapped, repeat, keep, diagonal)
-
-    pair_delta, gradient = pl.pallas_call(
+        name="early",
+    )(right, diagonal, swapped, swapped_late, both, outer_near, outer_far, keep, sorted_w)
+
+    gradient, pair_delta = pl.pallas_call(
         functools.partial(small_finish_kernel, scale),
-        in_specs=[vmem, [vmem] * 3] + [vmem] * 13,
+        in_specs=[[vmem] * 2] + [vmem] * 13,
         out_specs=[pl.BlockSpec(memory_space=pl.ANY)] * 2,
         out_shape=(
             like(homolog_matrix.shape, BF16),
@@ -776,29 +810,28 @@
         scratch_shapes=[
             pltpu.VMEM(homolog_matrix.shape, BF16),
             pltpu.VMEM(coupling_cotangent.shape, BF16),
-            pltpu.VMEM((ranks // 2, seqs, LANES), BF16),
-            pltpu.VMEM((ranks // 2, seqs, LANES), BF16),
+            pltpu.VMEM((ranks // 2, residues * residues, LANES), F32),
+            pair_turn,
             pltpu.SemaphoreType.DMA((2,)),
         ],
         compiler_params=limit,
         name="finish",
     )(
-        right,
-        [beside, across, diagonal],
+        [beside, across],
         swapped,
-        swapped_late,
+        both,
         outer_near,
         outer_far,
-        right_cot,
+        early_pair,
+        early_left,
+        early_right,
         normed,
         inv_std,
         gain,
         spread_w,
         sorted_w,
         pair_offset,
-        apart,
-        column_order,
-    )[::-1]
+    )
     return (pair_delta, gradient)
 
 

time: 17.7 us -> 17.6 us (level)
    ppermute x4, waiting for transfers between devices: 1.62 us -> 1.09 us  [swap_over(): lax.ppermute(value, 'res', [(source, source ^ mask) for source in range(r...]
    ppermute x1, waiting for transfers between devices: 0.71 us -> 1.17 us  [small_slice(): lax.ppermute(jnp.where(own_is_near, diagonal[1], diagonal[0]), 'seq', swap)]
  transfers between devices with their start and end apart: 7 -> 7, of which waited for: 5 -> 5; matrix products, arithmetic and copies ran while one was open for 0% -> 0% of each run, Pallas kernels for 21% -> 22%
where the time goes in v16:
time: 17.6 us; the launch traced here: 17.4 us
  starting transfers between devices  8.78 us (50%)
  Pallas kernels  5.63 us (32%)
  waiting for transfers between devices  2.26 us (13%)
  between operations  0.71 us (4%)
    ppermute x4, starting transfers between devices, swap_over(): lax.ppermute(value, 'res', [(source, source ^ mask) for source in range(r...  8.07 us
    pallas_call x1, Pallas kernels, small_slice(): pl.pallas_call(functools.partial(small_own_kernel, scale), in_specs=[vmem...  1.93 us
    pallas_call x1, Pallas kernels, small_slice(): pl.pallas_call(functools.partial(small_finish_kernel, scale), in_specs=[[...  1.34 us
    pallas_call x1, Pallas kernels, small_slice(): pl.pallas_call(small_project_kernel, in_specs=[hbm] * 9, out_specs=[vmem]...  1.32 us
    ppermute x1, waiting for transfers between devices, small_slice(): lax.ppermute(jnp.where(own_is_near, diagonal[1], diagonal[0]), 'seq', swap)  1.17 us
    ppermute x4, waiting for transfers between devices, swap_over(): lax.ppermute(value, 'res', [(source, source ^ mask) for source in range(r...  1.09 us
    pallas_call x1, Pallas kernels, small_slice(): pl.pallas_call(functools.partial(small_early_kernel, scale), in_specs=[vm...  0.53 us
    ppermute x1, starting transfers between devices, small_slice(): other_cot = lax.ppermute(coupling_cotangent, 'seq', swap)  0.52 us
  transfers between devices with their start and end apart: 7, of which 5 were waited for; matrix products, arithmetic and copies ran while one was open for 0% of the time, Pallas kernels for 22%

profile of v16, /device:TPU:0, one launch (start us, length us, event | category | flops | bytes accessed | tf_op | source)
XLA Modules:
  0.0 17.4 jit_solution(8654469495292995763)
XLA Ops:
  0.6 0.0 copy-start
  0.6 0.5 %collective-permute-start = (bf16[4,16,128]{2,1,0:T(8,128)(2,1)}, bf16[4,16,128]{2,1,0:T(8,128)(2,1)S(1)}, u32[]{:S(2)}, u32[]{:S(2)}) collective-permute-start(bf16[4,16,128]{2,1,0:T(8,128)(2,1)} %cot_hbm.1), channel_id=1, source_target_pairs={{0,1},{1,0},{2,3},{3,2},{4,5},{5,4},{6,7},{7,6},{8,9},{9,8},{10,11... | collective-permute-start | bytes 49160 | tf_op jit(solution)/shard_map/ppermute | solution.py:693
  1.2 1.3 %project.1 = (bf16[2,32,128]{2,1,0:T(8,128)(2,1)S(1)}, f32[128,256]{1,0:T(8,128)S(1)}, f32[128,128]{1,0:T(8,128)S(1)}, bf16[256,256]{1,0:T(8,128)(2,1)S(1)}, f32...) custom-call(bf16[32,4,256]{2,1,0:T(4,128)(2,1)} %x_hbm.1, f32[1,256]{1,0:T(1,128)} %bitcast.19, ...), custom_call_target="tpu_custom_call" | custom-call | tf_op jit(solution)/shard_map/project/pallas_call | solution.py:696
  2.5 0.0 collective-permute-done.other_ref
  2.5 3.7 %collective-permute-start.1 = (bf16[4,32,128]{2,1,0:T(8,128)(2,1)S(1)}, bf16[4,32,128]{2,1,0:T(8,128)(2,1)S(1)}, u32[]{:S(2)}, u32[]{:S(2)}) collective-permute-start(bf16[4,32,128]{2,1,0:T(8,128)(2,1)S(1)} %pad_maximum_fusion.2), channel_id=1, source_target_pairs={{0,8},{2,10},{4,12},{6,14},{8,0},{10,2},{12,4},{14,6},{1,9},{3,11}... | collective-permute-start | bytes 98312 | tf_op jit(solution)/shard_map/ppermute | solution.py:738
  6.2 0.0 copy-done
  6.2 1.9 %own_pieces.1 = (f32[4,32,128]{2,1,0:T(8,128)S(1)}, bf16[512,128]{1,0:T(8,128)(2,1)S(1)}, bf16[512,128]{1,0:T(8,128)(2,1)S(1)}, bf16[1024,128]{1,0:T(8,128)(2,1)...) custom-call(bf16[4,16,128]{2,1,0:T(8,128)(2,1)S(1)} %get-tuple-element.26.own_ref, ...), custom_call_target="tpu_custom_call" | custom-call | tf_op jit(solution)/shard_map/own_pieces/pallas_call | solution.py:746
  8.2 0.1 collective-permute-done.1.got_ref
  8.2 0.5 %partner_pieces.1 = (bf16[4,3,32,128]{3,2,1,0:T(8,128)(2,1)S(1)}, f32[4,32,128]{2,1,0:T(8,128)S(1)}, bf16[2,32,128]{2,1,0:T(8,128)(2,1)S(1)}, bf16[2,32,128]{2,1,0:T(8,128)(2,1)S(1)}) custom-call(bf16[4,32,128]{2,1,0:T(8,128)(2,1)S(1)} %collective-permute-done.1.got_ref, bf16[128,1024]{1,0:T(8,128)(2,1)S(1)} %get-tuple-element.27.sorted_wt_ref, ...), custom_call_target="tpu_custom_call" | custom-call | tf_op jit(solution)/shard_map/partner_pieces/pallas_call | solution.py:764
  8.8 0.2 %collective-permute-start.2 = (bf16[2,32,128]{2,1,0:T(8,128)(2,1)S(1)}, bf16[2,32,128]{2,1,0:T(8,128)(2,1)S(1)}, u32[]{:S(2)}, u32[]{:S(2)}) collective-permute-start(bf16[2,32,128]{2,1,0:T(8,128)(2,1)S(1)} %get-tuple-element.32), channel_id=1, source_target_pairs={{0,1},{1,0},{2,3},{3,2},{4,5},{5,4},{6,7},{7,6},{8,9},{9,8},{10,11... | collective-permute-start | bytes 49160 | tf_op jit(solution)/shard_map/ppermute | solution.py:778
  9.0 2.7 %collective-permute-start.5 = (bf16[3,32,128]{2,1,0:T(8,128)(2,1)S(1)}, bf16[3,32,128]{2,1,0:T(8,128)(2,1)S(1)}, u32[]{:S(2)}, u32[]{:S(2)}) collective-permute-start(bf16[3,32,128]{2,1,0:T(8,128)(2,1)S(1)} %get-tuple-element.48), channel_id=1, source_target_pairs={{0,6},{2,4},{4,2},{6,0},{8,14},{10,12},{12,10},{14,8},{1,7},{3,5},... | collective-permute-start | bytes 73736 | tf_op jit(solution)/shard_map/ppermute | solution.py:738
  11.6 0.0 collective-permute-done.2.swapped_ref
  11.6 0.5 %collective-permute-start.4 = (bf16[4,32,128]{2,1,0:T(8,128)(2,1)S(1)}, bf16[4,32,128]{2,1,0:T(8,128)(2,1)S(1)}, u32[]{:S(2)}, u32[]{:S(2)}) collective-permute-start(bf16[4,32,128]{2,1,0:T(8,128)(2,1)S(1)} %get-tuple-element.51), channel_id=1, source_target_pairs={{0,4},{2,6},{4,0},{6,2},{8,12},{10,14},{12,8},{14,10},{1,5},{3,7},... | collective-permute-start | bytes 98312 | tf_op jit(solution)/shard_map/ppermute | solution.py:738
  12.2 1.2 %collective-permute-start.3 = (bf16[4,32,128]{2,1,0:T(8,128)(2,1)S(1)}, bf16[4,32,128]{2,1,0:T(8,128)(2,1)S(1)}, u32[]{:S(2)}, u32[]{:S(2)}) collective-permute-start(bf16[4,32,128]{2,1,0:T(8,128)(2,1)S(1)} %get-tuple-element.52), channel_id=1, source_target_pairs={{0,2},{2,0},{4,6},{6,4},{8,10},{10,8},{12,14},{14,12},{1,3},{3,1},... | collective-permute-start | bytes 98312 | tf_op jit(solution)/shard_map/ppermute | solution.py:738
  13.4 0.4 %collective-permute-done.5.part_ref = bf16[3,32,128]{2,1,0:T(8,128)(2,1)S(1)} collective-permute-done((bf16[3,32,128]{2,1,0:T(8,128)(2,1)S(1)}, bf16[3,32,128]{2,1,0:T(8,128)(2,1)S(1)}, u32[]{:S(2)}, u32[]{:S(2)}) %collective-permute-start.5) | collective-permute-done | bytes 24608 | tf_op jit(solution)/shard_map/ppermute | solution.py:738
  13.7 0.0 collective-permute-start.6
  13.7 1.2 %collective-permute-done.6.swapped_late_ref = bf16[32,128]{1,0:T(8,128)(2,1)S(1)} collective-permute-done((bf16[32,128]{1,0:T(8,128)(2,1)S(1)}, bf16[32,128]{1,0:T(8,128)(2,1)S(1)}, u32[]{:S(2)}, u32[]{:S(2)}) %collective-permute-start.6) | collective-permute-done | bytes 8224 | tf_op jit(solution)/shard_map/ppermute | solution.py:783
  14.9 0.5 %early.1 = (f32[2,16,128]{2,1,0:T(8,128)S(1)}, f32[32,128]{1,0:T(8,128)S(1)}, f32[32,128]{1,0:T(8,128)S(1)}) custom-call(bf16[2,32,128]{2,1,0:T(8,128)(2,1)S(1)} %get-tuple-element.35.right_ref, bf16[3,32,128]{2,1,0:T(8,128)(2,1)S(1)} %collective-permute-done.5.part_ref, bf16[2,32,128]{2,1,0:T(8,128)(2,1)S(1)} %collective-permute-done.2.swapped_ref, ...), custom_call_target="tpu_custom_call" | custom-call | tf_op jit(solution)/shard_map/early/pallas_call | solution.py:788
  15.4 0.2 %collective-permute-done.4.part_refs_1_ = bf16[4,32,128]{2,1,0:T(8,128)(2,1)S(1)} collective-permute-done((bf16[4,32,128]{2,1,0:T(8,128)(2,1)S(1)}, bf16[4,32,128]{2,1,0:T(8,128)(2,1)S(1)}, u32[]{:S(2)}, u32[]{:S(2)}) %collective-permute-start.4) | collective-permute-done | bytes 32800 | tf_op jit(solution)/shard_map/ppermute | solution.py:738
  15.6 0.4 %collective-permute-done.3.part_refs_0_ = bf16[4,32,128]{2,1,0:T(8,128)(2,1)S(1)} collective-permute-done((bf16[4,32,128]{2,1,0:T(8,128)(2,1)S(1)}, bf16[4,32,128]{2,1,0:T(8,128)(2,1)S(1)}, u32[]{:S(2)}, u32[]{:S(2)}) %collective-permute-start.3) | collective-permute-done | bytes 32800 | tf_op jit(solution)/shard_map/ppermute | solution.py:738
  16.1 1.3 %finish.1 = (bf16[32,4,256]{2,1,0:T(4,128)(2,1)}, bf16[4,16,128]{2,1,0:T(8,128)(2,1)}) custom-call(bf16[4,32,128]{2,1,0:T(8,128)(2,1)S(1)} %collective-permute-done.3.part_refs_0_, bf16[4,32,128]{2,1,0:T(8,128)(2,1)S(1)} %collective-permute-done.4.part_refs_1_, bf16[2,32,128]{2,1,0:T(8,128)(2,1)S(1)} %collective-permute-done.2.swapped_ref, ...), custom_call_target="tpu_custom_call" | custom-call | tf_op jit(solution)/shard_map/finish/pallas_call | solution.py:802
  (6 shorter events, 0.0 us)
Async XLA Ops:
  0.6 5.6 %copy-start = (bf16[1024,128]{1,0:T(8,128)(2,1)S(1)}, bf16[1024,128]{1,0:T(8,128)(2,1)}, u32[]{:S(2)}) copy-start(bf16[1024,128]{1,0:T(8,128)(2,1)} %w_ref.1) | copy-start | bytes 786436
  0.6 1.9 %collective-permute-start = (bf16[4,16,128]{2,1,0:T(8,128)(2,1)}, bf16[4,16,128]{2,1,0:T(8,128)(2,1)S(1)}, u32[]{:S(2)}, u32[]{:S(2)}) collective-permute-start(bf16[4,16,128]{2,1,0:T(8,128)(2,1)} %cot_hbm.1), channel_id=1, source_target_pairs={{0,1},{1,0},{2,3},{3,2},{4,5},{5,4},{6,7},{7,6},{8,9},{9,8},{10,11... | collective-permute-start | bytes 49160 | tf_op jit(solution)/shard_map/ppermute | solution.py:693
  2.5 5.7 %collective-permute-start.1 = (bf16[4,32,128]{2,1,0:T(8,128)(2,1)S(1)}, bf16[4,32,128]{2,1,0:T(8,128)(2,1)S(1)}, u32[]{:S(2)}, u32[]{:S(2)}) collective-permute-start(bf16[4,32,128]{2,1,0:T(8,128)(2,1)S(1)} %pad_maximum_fusion.2), channel_id=1, source_target_pairs={{0,8},{2,10},{4,12},{6,14},{8,0},{10,2},{12,4},{14,6},{1,9},{3,11}... | collective-permute-start | bytes 98312 | tf_op jit(solution)/shard_map/ppermute | solution.py:738
  8.8 2.9 %collective-permute-start.2 = (bf16[2,32,128]{2,1,0:T(8,128)(2,1)S(1)}, bf16[2,32,128]{2,1,0:T(8,128)(2,1)S(1)}, u32[]{:S(2)}, u32[]{:S(2)}) collective-permute-start(bf16[2,32,128]{2,1,0:T(8,128)(2,1)S(1)} %get-tuple-element.32), channel_id=1, source_target_pairs={{0,1},{1,0},{2,3},{3,2},{4,5},{5,4},{6,7},{7,6},{8,9},{9,8},{10,11... | collective-permute-start | bytes 49160 | tf_op jit(solution)/shard_map/ppermute | solution.py:778
  9.0 4.8 %collective-permute-start.5 = (bf16[3,32,128]{2,1,0:T(8,128)(2,1)S(1)}, bf16[3,32,128]{2,1,0:T(8,128)(2,1)S(1)}, u32[]{:S(2)}, u32[]{:S(2)}) collective-permute-start(bf16[3,32,128]{2,1,0:T(8,128)(2,1)S(1)} %get-tuple-element.48), channel_id=1, source_target_pairs={{0,6},{2,4},{4,2},{6,0},{8,14},{10,12},{12,10},{14,8},{1,7},{3,5},... | collective-permute-start | bytes 73736 | tf_op jit(solution)/shard_map/ppermute | solution.py:738
  11.6 4.0 %collective-permute-start.4 = (bf16[4,32,128]{2,1,0:T(8,128)(2,1)S(1)}, bf16[4,32,128]{2,1,0:T(8,128)(2,1)S(1)}, u32[]{:S(2)}, u32[]{:S(2)}) collective-permute-start(bf16[4,32,128]{2,1,0:T(8,128)(2,1)S(1)} %get-tuple-element.51), channel_id=1, source_target_pairs={{0,4},{2,6},{4,0},{6,2},{8,12},{10,14},{12,8},{14,10},{1,5},{3,7},... | collective-permute-start | bytes 98312 | tf_op jit(solution)/shard_map/ppermute | solution.py:738
  12.2 3.9 %collective-permute-start.3 = (bf16[4,32,128]{2,1,0:T(8,128)(2,1)S(1)}, bf16[4,32,128]{2,1,0:T(8,128)(2,1)S(1)}, u32[]{:S(2)}, u32[]{:S(2)}) collective-permute-start(bf16[4,32,128]{2,1,0:T(8,128)(2,1)S(1)} %get-tuple-element.52), channel_id=1, source_target_pairs={{0,2},{2,0},{4,6},{6,4},{8,10},{10,8},{12,14},{14,12},{1,3},{3,1},... | collective-permute-start | bytes 98312 | tf_op jit(solution)/shard_map/ppermute | solution.py:738
  13.7 1.2 %collective-permute-start.6 = (bf16[32,128]{1,0:T(8,128)(2,1)S(1)}, bf16[32,128]{1,0:T(8,128)(2,1)S(1)}, u32[]{:S(2)}, u32[]{:S(2)}) collective-permute-start(bf16[32,128]{1,0:T(8,128)(2,1)S(1)} %fusion), channel_id=1, source_target_pairs={{0,1},{1,0},{2,3},{3,2},{4,5},{5,4},{6,7},{7,6},{8,9},{9,8},{10,11... | collective-permute-start | bytes 24584 | tf_op jit(solution)/shard_map/ppermute | solution.py:783

commit v17 on v16

--- a/solution.py
+++ b/solution.py
@@ -639,8 +639,15 @@
     )
     for place in range(residues):
         grad_ref[:, place, :] = grad[place * seqs : (place + 1) * seqs].astype(BF16)
-    grad_copy = pltpu.make_async_copy(grad_ref, grad_hbm, semaphores.at[0])
-    grad_copy.start()
+    parts = 4
+    part = seqs // parts
+    copies = start_copies(
+        tuple(
+            (grad_ref.at[pl.ds(place * part, part)], grad_hbm.at[pl.ds(place * part, part)])
+            for place in range(parts)
+        ),
+        semaphores,
+    )
 
     half = own_half()
     right = jnp.concatenate(
@@ -660,9 +667,10 @@
     for i in range(residues):
         own = [block[i * residues : (i + 1) * residues] for block in placed]
         pair_ref[i] = (jnp.concatenate(own, axis=0) + offset_ref[...]).astype(BF16)
-    pair_copy = pltpu.make_async_copy(pair_ref, pair_hbm, semaphores.at[1])
+    pair_copy = pltpu.make_async_copy(pair_ref, pair_hbm, semaphores.at[parts])
     pair_copy.start()
-    grad_copy.wait()
+    for copy in copies:
+        copy.wait()
     pair_copy.wait()
 
 
@@ -812,7 +820,7 @@
             pltpu.VMEM(coupling_cotangent.shape, BF16),
             pltpu.VMEM((ranks // 2, residues * residues, LANES), F32),
             pair_turn,
-            pltpu.SemaphoreType.DMA((2,)),
+            pltpu.SemaphoreType.DMA((5,)),
         ],
         compiler_params=limit,
         name="finish",

time: 17.6 us -> 17.6 us (level)
  no operation moved by 1% of the time
where the time goes in v17:
time: 17.6 us; the launch traced here: 17.4 us
  starting transfers between devices  8.78 us (50%)
  Pallas kernels  5.65 us (32%)
  waiting for transfers between devices  2.26 us (13%)
  between operations  0.71 us (4%)
    ppermute x4, starting transfers between devices, swap_over(): lax.ppermute(value, 'res', [(source, source ^ mask) for source in range(r...  8.07 us
    pallas_call x1, Pallas kernels, small_slice(): pl.pallas_call(functools.partial(small_own_kernel, scale), in_specs=[vmem...  1.93 us
    pallas_call x1, Pallas kernels, small_slice(): pl.pallas_call(functools.partial(small_finish_kernel, scale), in_specs=[[...  1.36 us
    pallas_call x1, Pallas kernels, small_slice(): pl.pallas_call(small_project_kernel, in_specs=[hbm] * 9, out_specs=[vmem]...  1.32 us
    ppermute x1, waiting for transfers between devices, small_slice(): lax.ppermute(jnp.where(own_is_near, diagonal[1], diagonal[0]), 'seq', swap)  1.17 us
    ppermute x4, waiting for transfers between devices, swap_over(): lax.ppermute(value, 'res', [(source, source ^ mask) for source in range(r...  1.09 us
    pallas_call x1, Pallas kernels, small_slice(): pl.pallas_call(functools.partial(small_early_kernel, scale), in_specs=[vm...  0.53 us
    ppermute x1, starting transfers between devices, small_slice(): other_cot = lax.ppermute(coupling_cotangent, 'seq', swap)  0.52 us
  transfers between devices with their start and end apart: 7, of which 5 were waited for; matrix products, arithmetic and copies ran while one was open for 0% of the time, Pallas kernels for 22%

profile of v17, /device:TPU:0, one launch (start us, length us, event | category | flops | bytes accessed | tf_op | source)
XLA Modules:
  0.0 17.4 jit_solution(10261558691341810094)
XLA Ops:
  0.6 0.0 copy-start
  0.6 0.5 %collective-permute-start = (bf16[4,16,128]{2,1,0:T(8,128)(2,1)}, bf16[4,16,128]{2,1,0:T(8,128)(2,1)S(1)}, u32[]{:S(2)}, u32[]{:S(2)}) collective-permute-start(bf16[4,16,128]{2,1,0:T(8,128)(2,1)} %cot_hbm.1), channel_id=1, source_target_pairs={{0,1},{1,0},{2,3},{3,2},{4,5},{5,4},{6,7},{7,6},{8,9},{9,8},{10,11... | collective-permute-start | bytes 49160 | tf_op jit(solution)/shard_map/ppermute | solution.py:701
  1.2 1.3 %project.1 = (bf16[2,32,128]{2,1,0:T(8,128)(2,1)S(1)}, f32[128,256]{1,0:T(8,128)S(1)}, f32[128,128]{1,0:T(8,128)S(1)}, bf16[256,256]{1,0:T(8,128)(2,1)S(1)}, f32...) custom-call(bf16[32,4,256]{2,1,0:T(4,128)(2,1)} %x_hbm.1, f32[1,256]{1,0:T(1,128)} %bitcast.19, ...), custom_call_target="tpu_custom_call" | custom-call | tf_op jit(solution)/shard_map/project/pallas_call | solution.py:704
  2.5 0.0 collective-permute-done.other_ref
  2.5 3.7 %collective-permute-start.1 = (bf16[4,32,128]{2,1,0:T(8,128)(2,1)S(1)}, bf16[4,32,128]{2,1,0:T(8,128)(2,1)S(1)}, u32[]{:S(2)}, u32[]{:S(2)}) collective-permute-start(bf16[4,32,128]{2,1,0:T(8,128)(2,1)S(1)} %pad_maximum_fusion.2), channel_id=1, source_target_pairs={{0,8},{2,10},{4,12},{6,14},{8,0},{10,2},{12,4},{14,6},{1,9},{3,11}... | collective-permute-start | bytes 98312 | tf_op jit(solution)/shard_map/ppermute | solution.py:746
  6.2 0.0 copy-done
  6.2 1.9 %own_pieces.1 = (f32[4,32,128]{2,1,0:T(8,128)S(1)}, bf16[512,128]{1,0:T(8,128)(2,1)S(1)}, bf16[512,128]{1,0:T(8,128)(2,1)S(1)}, bf16[1024,128]{1,0:T(8,128)(2,1)...) custom-call(bf16[4,16,128]{2,1,0:T(8,128)(2,1)S(1)} %get-tuple-element.26.own_ref, ...), custom_call_target="tpu_custom_call" | custom-call | tf_op jit(solution)/shard_map/own_pieces/pallas_call | solution.py:754
  8.2 0.1 collective-permute-done.1.got_ref
  8.2 0.5 %partner_pieces.1 = (bf16[4,3,32,128]{3,2,1,0:T(8,128)(2,1)S(1)}, f32[4,32,128]{2,1,0:T(8,128)S(1)}, bf16[2,32,128]{2,1,0:T(8,128)(2,1)S(1)}, bf16[2,32,128]{2,1,0:T(8,128)(2,1)S(1)}) custom-call(bf16[4,32,128]{2,1,0:T(8,128)(2,1)S(1)} %collective-permute-done.1.got_ref, bf16[128,1024]{1,0:T(8,128)(2,1)S(1)} %get-tuple-element.27.sorted_wt_ref, ...), custom_call_target="tpu_custom_call" | custom-call | tf_op jit(solution)/shard_map/partner_pieces/pallas_call | solution.py:772
  8.8 0.2 %collective-permute-start.2 = (bf16[2,32,128]{2,1,0:T(8,128)(2,1)S(1)}, bf16[2,32,128]{2,1,0:T(8,128)(2,1)S(1)}, u32[]{:S(2)}, u32[]{:S(2)}) collective-permute-start(bf16[2,32,128]{2,1,0:T(8,128)(2,1)S(1)} %get-tuple-element.32), channel_id=1, source_target_pairs={{0,1},{1,0},{2,3},{3,2},{4,5},{5,4},{6,7},{7,6},{8,9},{9,8},{10,11... | collective-permute-start | bytes 49160 | tf_op jit(solution)/shard_map/ppermute | solution.py:786
  9.0 2.7 %collective-permute-start.5 = (bf16[3,32,128]{2,1,0:T(8,128)(2,1)S(1)}, bf16[3,32,128]{2,1,0:T(8,128)(2,1)S(1)}, u32[]{:S(2)}, u32[]{:S(2)}) collective-permute-start(bf16[3,32,128]{2,1,0:T(8,128)(2,1)S(1)} %get-tuple-element.48), channel_id=1, source_target_pairs={{0,6},{2,4},{4,2},{6,0},{8,14},{10,12},{12,10},{14,8},{1,7},{3,5},... | collective-permute-start | bytes 73736 | tf_op jit(solution)/shard_map/ppermute | solution.py:746
  11.6 0.0 collective-permute-done.2.swapped_ref
  11.6 0.5 %collective-permute-start.4 = (bf16[4,32,128]{2,1,0:T(8,128)(2,1)S(1)}, bf16[4,32,128]{2,1,0:T(8,128)(2,1)S(1)}, u32[]{:S(2)}, u32[]{:S(2)}) collective-permute-start(bf16[4,32,128]{2,1,0:T(8,128)(2,1)S(1)} %get-tuple-element.51), channel_id=1, source_target_pairs={{0,4},{2,6},{4,0},{6,2},{8,12},{10,14},{12,8},{14,10},{1,5},{3,7},... | collective-permute-start | bytes 98312 | tf_op jit(solution)/shard_map/ppermute | solution.py:746
  12.2 1.2 %collective-permute-start.3 = (bf16[4,32,128]{2,1,0:T(8,128)(2,1)S(1)}, bf16[4,32,128]{2,1,0:T(8,128)(2,1)S(1)}, u32[]{:S(2)}, u32[]{:S(2)}) collective-permute-start(bf16[4,32,128]{2,1,0:T(8,128)(2,1)S(1)} %get-tuple-element.52), channel_id=1, source_target_pairs={{0,2},{2,0},{4,6},{6,4},{8,10},{10,8},{12,14},{14,12},{1,3},{3,1},... | collective-permute-start | bytes 98312 | tf_op jit(solution)/shard_map/ppermute | solution.py:746
  13.4 0.4 %collective-permute-done.5.part_ref = bf16[3,32,128]{2,1,0:T(8,128)(2,1)S(1)} collective-permute-done((bf16[3,32,128]{2,1,0:T(8,128)(2,1)S(1)}, bf16[3,32,128]{2,1,0:T(8,128)(2,1)S(1)}, u32[]{:S(2)}, u32[]{:S(2)}) %collective-permute-start.5) | collective-permute-done | bytes 24608 | tf_op jit(solution)/shard_map/ppermute | solution.py:746
  13.7 0.0 collective-permute-start.6
  13.7 1.2 %collective-permute-done.6.swapped_late_ref = bf16[32,128]{1,0:T(8,128)(2,1)S(1)} collective-permute-done((bf16[32,128]{1,0:T(8,128)(2,1)S(1)}, bf16[32,128]{1,0:T(8,128)(2,1)S(1)}, u32[]{:S(2)}, u32[]{:S(2)}) %collective-permute-start.6) | collective-permute-done | bytes 8224 | tf_op jit(solution)/shard_map/ppermute | solution.py:791
  14.9 0.5 %early.1 = (f32[2,16,128]{2,1,0:T(8,128)S(1)}, f32[32,128]{1,0:T(8,128)S(1)}, f32[32,128]{1,0:T(8,128)S(1)}) custom-call(bf16[2,32,128]{2,1,0:T(8,128)(2,1)S(1)} %get-tuple-element.35.right_ref, bf16[3,32,128]{2,1,0:T(8,128)(2,1)S(1)} %collective-permute-done.5.part_ref, bf16[2,32,128]{2,1,0:T(8,128)(2,1)S(1)} %collective-permute-done.2.swapped_ref, ...), custom_call_target="tpu_custom_call" | custom-call | tf_op jit(solution)/shard_map/early/pallas_call | solution.py:796
  15.4 0.2 %collective-permute-done.4.part_refs_1_ = bf16[4,32,128]{2,1,0:T(8,128)(2,1)S(1)} collective-permute-done((bf16[4,32,128]{2,1,0:T(8,128)(2,1)S(1)}, bf16[4,32,128]{2,1,0:T(8,128)(2,1)S(1)}, u32[]{:S(2)}, u32[]{:S(2)}) %collective-permute-start.4) | collective-permute-done | bytes 32800 | tf_op jit(solution)/shard_map/ppermute | solution.py:746
  15.6 0.4 %collective-permute-done.3.part_refs_0_ = bf16[4,32,128]{2,1,0:T(8,128)(2,1)S(1)} collective-permute-done((bf16[4,32,128]{2,1,0:T(8,128)(2,1)S(1)}, bf16[4,32,128]{2,1,0:T(8,128)(2,1)S(1)}, u32[]{:S(2)}, u32[]{:S(2)}) %collective-permute-start.3) | collective-permute-done | bytes 32800 | tf_op jit(solution)/shard_map/ppermute | solution.py:746
  16.1 1.4 %finish.1 = (bf16[32,4,256]{2,1,0:T(4,128)(2,1)}, bf16[4,16,128]{2,1,0:T(8,128)(2,1)}) custom-call(bf16[4,32,128]{2,1,0:T(8,128)(2,1)S(1)} %collective-permute-done.3.part_refs_0_, bf16[4,32,128]{2,1,0:T(8,128)(2,1)S(1)} %collective-permute-done.4.part_refs_1_, bf16[2,32,128]{2,1,0:T(8,128)(2,1)S(1)} %collective-permute-done.2.swapped_ref, ...), custom_call_target="tpu_custom_call" | custom-call | tf_op jit(solution)/shard_map/finish/pallas_call | solution.py:810
  (6 shorter events, 0.0 us)
Async XLA Ops:
  0.6 5.6 %copy-start = (bf16[1024,128]{1,0:T(8,128)(2,1)S(1)}, bf16[1024,128]{1,0:T(8,128)(2,1)}, u32[]{:S(2)}) copy-start(bf16[1024,128]{1,0:T(8,128)(2,1)} %w_ref.1) | copy-start | bytes 786436
  0.6 1.9 %collective-permute-start = (bf16[4,16,128]{2,1,0:T(8,128)(2,1)}, bf16[4,16,128]{2,1,0:T(8,128)(2,1)S(1)}, u32[]{:S(2)}, u32[]{:S(2)}) collective-permute-start(bf16[4,16,128]{2,1,0:T(8,128)(2,1)} %cot_hbm.1), channel_id=1, source_target_pairs={{0,1},{1,0},{2,3},{3,2},{4,5},{5,4},{6,7},{7,6},{8,9},{9,8},{10,11... | collective-permute-start | bytes 49160 | tf_op jit(solution)/shard_map/ppermute | solution.py:701
  2.5 5.7 %collective-permute-start.1 = (bf16[4,32,128]{2,1,0:T(8,128)(2,1)S(1)}, bf16[4,32,128]{2,1,0:T(8,128)(2,1)S(1)}, u32[]{:S(2)}, u32[]{:S(2)}) collective-permute-start(bf16[4,32,128]{2,1,0:T(8,128)(2,1)S(1)} %pad_maximum_fusion.2), channel_id=1, source_target_pairs={{0,8},{2,10},{4,12},{6,14},{8,0},{10,2},{12,4},{14,6},{1,9},{3,11}... | collective-permute-start | bytes 98312 | tf_op jit(solution)/shard_map/ppermute | solution.py:746
  8.8 2.9 %collective-permute-start.2 = (bf16[2,32,128]{2,1,0:T(8,128)(2,1)S(1)}, bf16[2,32,128]{2,1,0:T(8,128)(2,1)S(1)}, u32[]{:S(2)}, u32[]{:S(2)}) collective-permute-start(bf16[2,32,128]{2,1,0:T(8,128)(2,1)S(1)} %get-tuple-element.32), channel_id=1, source_target_pairs={{0,1},{1,0},{2,3},{3,2},{4,5},{5,4},{6,7},{7,6},{8,9},{9,8},{10,11... | collective-permute-start | bytes 49160 | tf_op jit(solution)/shard_map/ppermute | solution.py:786
  9.0 4.8 %collective-permute-start.5 = (bf16[3,32,128]{2,1,0:T(8,128)(2,1)S(1)}, bf16[3,32,128]{2,1,0:T(8,128)(2,1)S(1)}, u32[]{:S(2)}, u32[]{:S(2)}) collective-permute-start(bf16[3,32,128]{2,1,0:T(8,128)(2,1)S(1)} %get-tuple-element.48), channel_id=1, source_target_pairs={{0,6},{2,4},{4,2},{6,0},{8,14},{10,12},{12,10},{14,8},{1,7},{3,5},... | collective-permute-start | bytes 73736 | tf_op jit(solution)/shard_map/ppermute | solution.py:746
  11.6 4.0 %collective-permute-start.4 = (bf16[4,32,128]{2,1,0:T(8,128)(2,1)S(1)}, bf16[4,32,128]{2,1,0:T(8,128)(2,1)S(1)}, u32[]{:S(2)}, u32[]{:S(2)}) collective-permute-start(bf16[4,32,128]{2,1,0:T(8,128)(2,1)S(1)} %get-tuple-element.51), channel_id=1, source_target_pairs={{0,4},{2,6},{4,0},{6,2},{8,12},{10,14},{12,8},{14,10},{1,5},{3,7},... | collective-permute-start | bytes 98312 | tf_op jit(solution)/shard_map/ppermute | solution.py:746
  12.2 3.9 %collective-permute-start.3 = (bf16[4,32,128]{2,1,0:T(8,128)(2,1)S(1)}, bf16[4,32,128]{2,1,0:T(8,128)(2,1)S(1)}, u32[]{:S(2)}, u32[]{:S(2)}) collective-permute-start(bf16[4,32,128]{2,1,0:T(8,128)(2,1)S(1)} %get-tuple-element.52), channel_id=1, source_target_pairs={{0,2},{2,0},{4,6},{6,4},{8,10},{10,8},{12,14},{14,12},{1,3},{3,1},... | collective-permute-start | bytes 98312 | tf_op jit(solution)/shard_map/ppermute | solution.py:746
  13.7 1.2 %collective-permute-start.6 = (bf16[32,128]{1,0:T(8,128)(2,1)S(1)}, bf16[32,128]{1,0:T(8,128)(2,1)S(1)}, u32[]{:S(2)}, u32[]{:S(2)}) collective-permute-start(bf16[32,128]{1,0:T(8,128)(2,1)S(1)} %fusion), channel_id=1, source_target_pairs={{0,1},{1,0},{2,3},{3,2},{4,5},{5,4},{6,7},{7,6},{8,9},{9,8},{10,11... | collective-permute-start | bytes 24584 | tf_op jit(solution)/shard_map/ppermute | solution.py:791

commit v18 on v16

--- a/solution.py
+++ b/solution.py
@@ -639,9 +639,6 @@
     )
     for place in range(residues):
         grad_ref[:, place, :] = grad[place * seqs : (place + 1) * seqs].astype(BF16)
-    grad_copy = pltpu.make_async_copy(grad_ref, grad_hbm, semaphores.at[0])
-    grad_copy.start()
-
     half = own_half()
     right = jnp.concatenate(
         [
@@ -660,10 +657,18 @@
     for i in range(residues):
         own = [block[i * residues : (i + 1) * residues] for block in placed]
         pair_ref[i] = (jnp.concatenate(own, axis=0) + offset_ref[...]).astype(BF16)
-    pair_copy = pltpu.make_async_copy(pair_ref, pair_hbm, semaphores.at[1])
-    pair_copy.start()
-    grad_copy.wait()
-    pair_copy.wait()
+    parts = 4
+    part = seqs // parts
+    copies = start_copies(
+        ((pair_ref, pair_hbm),)
+        + tuple(
+            (grad_ref.at[pl.ds(place * part, part)], grad_hbm.at[pl.ds(place * part, part)])
+            for place in range(parts)
+        ),
+        semaphores,
+    )
+    for copy in copies:
+        copy.wait()
 
 
 def small_slice(
@@ -812,7 +817,7 @@
             pltpu.VMEM(coupling_cotangent.shape, BF16),
             pltpu.VMEM((ranks // 2, residues * residues, LANES), F32),
             pair_turn,
-            pltpu.SemaphoreType.DMA((2,)),
+            pltpu.SemaphoreType.DMA((5,)),
         ],
         compiler_params=limit,
         name="finish",

time: 17.6 us -> 17.6 us (level)
  no operation moved by 1% of the time
where the time goes in v18:
time: 17.6 us; the launch traced here: 17.5 us
  starting transfers between devices  8.78 us (50%)
  Pallas kernels  5.67 us (32%)
  waiting for transfers between devices  2.26 us (13%)
  between operations  0.71 us (4%)
    ppermute x4, starting transfers between devices, swap_over(): lax.ppermute(value, 'res', [(source, source ^ mask) for source in range(r...  8.07 us
    pallas_call x1, Pallas kernels, small_slice(): pl.pallas_call(functools.partial(small_own_kernel, scale), in_specs=[vmem...  1.93 us
    pallas_call x1, Pallas kernels, small_slice(): pl.pallas_call(functools.partial(small_finish_kernel, scale), in_specs=[[...  1.37 us
    pallas_call x1, Pallas kernels, small_slice(): pl.pallas_call(small_project_kernel, in_specs=[hbm] * 9, out_specs=[vmem]...  1.32 us
    ppermute x1, waiting for transfers between devices, small_slice(): lax.ppermute(jnp.where(own_is_near, diagonal[1], diagonal[0]), 'seq', swap)  1.17 us
    ppermute x4, waiting for transfers between devices, swap_over(): lax.ppermute(value, 'res', [(source, source ^ mask) for source in range(r...  1.09 us
    pallas_call x1, Pallas kernels, small_slice(): pl.pallas_call(functools.partial(small_early_kernel, scale), in_specs=[vm...  0.53 us
    ppermute x1, starting transfers between devices, small_slice(): other_cot = lax.ppermute(coupling_cotangent, 'seq', swap)  0.52 us
  transfers between devices with their start and end apart: 7, of which 5 were waited for; matrix products, arithmetic and copies ran while one was open for 0% of the time, Pallas kernels for 22%

profile of v18, /device:TPU:0, one launch (start us, length us, event | category | flops | bytes accessed | tf_op | source)
XLA Modules:
  0.0 17.5 jit_solution(2031383530579232227)
XLA Ops:
  0.6 0.0 copy-start
  0.6 0.5 %collective-permute-start = (bf16[4,16,128]{2,1,0:T(8,128)(2,1)}, bf16[4,16,128]{2,1,0:T(8,128)(2,1)S(1)}, u32[]{:S(2)}, u32[]{:S(2)}) collective-permute-start(bf16[4,16,128]{2,1,0:T(8,128)(2,1)} %cot_hbm.1), channel_id=1, source_target_pairs={{0,1},{1,0},{2,3},{3,2},{4,5},{5,4},{6,7},{7,6},{8,9},{9,8},{10,11... | collective-permute-start | bytes 49160 | tf_op jit(solution)/shard_map/ppermute | solution.py:698
  1.2 1.3 %project.1 = (bf16[2,32,128]{2,1,0:T(8,128)(2,1)S(1)}, f32[128,256]{1,0:T(8,128)S(1)}, f32[128,128]{1,0:T(8,128)S(1)}, bf16[256,256]{1,0:T(8,128)(2,1)S(1)}, f32...) custom-call(bf16[32,4,256]{2,1,0:T(4,128)(2,1)} %x_hbm.1, f32[1,256]{1,0:T(1,128)} %bitcast.19, ...), custom_call_target="tpu_custom_call" | custom-call | tf_op jit(solution)/shard_map/project/pallas_call | solution.py:701
  2.5 0.0 collective-permute-done.other_ref
  2.5 3.7 %collective-permute-start.1 = (bf16[4,32,128]{2,1,0:T(8,128)(2,1)S(1)}, bf16[4,32,128]{2,1,0:T(8,128)(2,1)S(1)}, u32[]{:S(2)}, u32[]{:S(2)}) collective-permute-start(bf16[4,32,128]{2,1,0:T(8,128)(2,1)S(1)} %pad_maximum_fusion.2), channel_id=1, source_target_pairs={{0,8},{2,10},{4,12},{6,14},{8,0},{10,2},{12,4},{14,6},{1,9},{3,11}... | collective-permute-start | bytes 98312 | tf_op jit(solution)/shard_map/ppermute | solution.py:743
  6.2 0.0 copy-done
  6.2 1.9 %own_pieces.1 = (f32[4,32,128]{2,1,0:T(8,128)S(1)}, bf16[512,128]{1,0:T(8,128)(2,1)S(1)}, bf16[512,128]{1,0:T(8,128)(2,1)S(1)}, bf16[1024,128]{1,0:T(8,128)(2,1)...) custom-call(bf16[4,16,128]{2,1,0:T(8,128)(2,1)S(1)} %get-tuple-element.26.own_ref, ...), custom_call_target="tpu_custom_call" | custom-call | tf_op jit(solution)/shard_map/own_pieces/pallas_call | solution.py:751
  8.2 0.1 collective-permute-done.1.got_ref
  8.2 0.5 %partner_pieces.1 = (bf16[4,3,32,128]{3,2,1,0:T(8,128)(2,1)S(1)}, f32[4,32,128]{2,1,0:T(8,128)S(1)}, bf16[2,32,128]{2,1,0:T(8,128)(2,1)S(1)}, bf16[2,32,128]{2,1,0:T(8,128)(2,1)S(1)}) custom-call(bf16[4,32,128]{2,1,0:T(8,128)(2,1)S(1)} %collective-permute-done.1.got_ref, bf16[128,1024]{1,0:T(8,128)(2,1)S(1)} %get-tuple-element.27.sorted_wt_ref, ...), custom_call_target="tpu_custom_call" | custom-call | tf_op jit(solution)/shard_map/partner_pieces/pallas_call | solution.py:769
  8.8 0.2 %collective-permute-start.2 = (bf16[2,32,128]{2,1,0:T(8,128)(2,1)S(1)}, bf16[2,32,128]{2,1,0:T(8,128)(2,1)S(1)}, u32[]{:S(2)}, u32[]{:S(2)}) collective-permute-start(bf16[2,32,128]{2,1,0:T(8,128)(2,1)S(1)} %get-tuple-element.32), channel_id=1, source_target_pairs={{0,1},{1,0},{2,3},{3,2},{4,5},{5,4},{6,7},{7,6},{8,9},{9,8},{10,11... | collective-permute-start | bytes 49160 | tf_op jit(solution)/shard_map/ppermute | solution.py:783
  9.0 2.7 %collective-permute-start.5 = (bf16[3,32,128]{2,1,0:T(8,128)(2,1)S(1)}, bf16[3,32,128]{2,1,0:T(8,128)(2,1)S(1)}, u32[]{:S(2)}, u32[]{:S(2)}) collective-permute-start(bf16[3,32,128]{2,1,0:T(8,128)(2,1)S(1)} %get-tuple-element.48), channel_id=1, source_target_pairs={{0,6},{2,4},{4,2},{6,0},{8,14},{10,12},{12,10},{14,8},{1,7},{3,5},... | collective-permute-start | bytes 73736 | tf_op jit(solution)/shard_map/ppermute | solution.py:743
  11.6 0.0 collective-permute-done.2.swapped_ref
  11.6 0.5 %collective-permute-start.4 = (bf16[4,32,128]{2,1,0:T(8,128)(2,1)S(1)}, bf16[4,32,128]{2,1,0:T(8,128)(2,1)S(1)}, u32[]{:S(2)}, u32[]{:S(2)}) collective-permute-start(bf16[4,32,128]{2,1,0:T(8,128)(2,1)S(1)} %get-tuple-element.51), channel_id=1, source_target_pairs={{0,4},{2,6},{4,0},{6,2},{8,12},{10,14},{12,8},{14,10},{1,5},{3,7},... | collective-permute-start | bytes 98312 | tf_op jit(solution)/shard_map/ppermute | solution.py:743
  12.2 1.2 %collective-permute-start.3 = (bf16[4,32,128]{2,1,0:T(8,128)(2,1)S(1)}, bf16[4,32,128]{2,1,0:T(8,128)(2,1)S(1)}, u32[]{:S(2)}, u32[]{:S(2)}) collective-permute-start(bf16[4,32,128]{2,1,0:T(8,128)(2,1)S(1)} %get-tuple-element.52), channel_id=1, source_target_pairs={{0,2},{2,0},{4,6},{6,4},{8,10},{10,8},{12,14},{14,12},{1,3},{3,1},... | collective-permute-start | bytes 98312 | tf_op jit(solution)/shard_map/ppermute | solution.py:743
  13.4 0.4 %collective-permute-done.5.part_ref = bf16[3,32,128]{2,1,0:T(8,128)(2,1)S(1)} collective-permute-done((bf16[3,32,128]{2,1,0:T(8,128)(2,1)S(1)}, bf16[3,32,128]{2,1,0:T(8,128)(2,1)S(1)}, u32[]{:S(2)}, u32[]{:S(2)}) %collective-permute-start.5) | collective-permute-done | bytes 24608 | tf_op jit(solution)/shard_map/ppermute | solution.py:743
  13.7 0.0 collective-permute-start.6
  13.7 1.2 %collective-permute-done.6.swapped_late_ref = bf16[32,128]{1,0:T(8,128)(2,1)S(1)} collective-permute-done((bf16[32,128]{1,0:T(8,128)(2,1)S(1)}, bf16[32,128]{1,0:T(8,128)(2,1)S(1)}, u32[]{:S(2)}, u32[]{:S(2)}) %collective-permute-start.6) | collective-permute-done | bytes 8224 | tf_op jit(solution)/shard_map/ppermute | solution.py:788
  14.9 0.5 %early.1 = (f32[2,16,128]{2,1,0:T(8,128)S(1)}, f32[32,128]{1,0:T(8,128)S(1)}, f32[32,128]{1,0:T(8,128)S(1)}) custom-call(bf16[2,32,128]{2,1,0:T(8,128)(2,1)S(1)} %get-tuple-element.35.right_ref, bf16[3,32,128]{2,1,0:T(8,128)(2,1)S(1)} %collective-permute-done.5.part_ref, bf16[2,32,128]{2,1,0:T(8,128)(2,1)S(1)} %collective-permute-done.2.swapped_ref, ...), custom_call_target="tpu_custom_call" | custom-call | tf_op jit(solution)/shard_map/early/pallas_call | solution.py:793
  15.4 0.2 %collective-permute-done.4.part_refs_1_ = bf16[4,32,128]{2,1,0:T(8,128)(2,1)S(1)} collective-permute-done((bf16[4,32,128]{2,1,0:T(8,128)(2,1)S(1)}, bf16[4,32,128]{2,1,0:T(8,128)(2,1)S(1)}, u32[]{:S(2)}, u32[]{:S(2)}) %collective-permute-start.4) | collective-permute-done | bytes 32800 | tf_op jit(solution)/shard_map/ppermute | solution.py:743
  15.6 0.4 %collective-permute-done.3.part_refs_0_ = bf16[4,32,128]{2,1,0:T(8,128)(2,1)S(1)} collective-permute-done((bf16[4,32,128]{2,1,0:T(8,128)(2,1)S(1)}, bf16[4,32,128]{2,1,0:T(8,128)(2,1)S(1)}, u32[]{:S(2)}, u32[]{:S(2)}) %collective-permute-start.3) | collective-permute-done | bytes 32800 | tf_op jit(solution)/shard_map/ppermute | solution.py:743
  16.1 1.4 %finish.1 = (bf16[32,4,256]{2,1,0:T(4,128)(2,1)}, bf16[4,16,128]{2,1,0:T(8,128)(2,1)}) custom-call(bf16[4,32,128]{2,1,0:T(8,128)(2,1)S(1)} %collective-permute-done.3.part_refs_0_, bf16[4,32,128]{2,1,0:T(8,128)(2,1)S(1)} %collective-permute-done.4.part_refs_1_, bf16[2,32,128]{2,1,0:T(8,128)(2,1)S(1)} %collective-permute-done.2.swapped_ref, ...), custom_call_target="tpu_custom_call" | custom-call | tf_op jit(solution)/shard_map/finish/pallas_call | solution.py:807
  (6 shorter events, 0.0 us)
Async XLA Ops:
  0.6 5.6 %copy-start = (bf16[1024,128]{1,0:T(8,128)(2,1)S(1)}, bf16[1024,128]{1,0:T(8,128)(2,1)}, u32[]{:S(2)}) copy-start(bf16[1024,128]{1,0:T(8,128)(2,1)} %w_ref.1) | copy-start | bytes 786436
  0.6 1.9 %collective-permute-start = (bf16[4,16,128]{2,1,0:T(8,128)(2,1)}, bf16[4,16,128]{2,1,0:T(8,128)(2,1)S(1)}, u32[]{:S(2)}, u32[]{:S(2)}) collective-permute-start(bf16[4,16,128]{2,1,0:T(8,128)(2,1)} %cot_hbm.1), channel_id=1, source_target_pairs={{0,1},{1,0},{2,3},{3,2},{4,5},{5,4},{6,7},{7,6},{8,9},{9,8},{10,11... | collective-permute-start | bytes 49160 | tf_op jit(solution)/shard_map/ppermute | solution.py:698
  2.5 5.7 %collective-permute-start.1 = (bf16[4,32,128]{2,1,0:T(8,128)(2,1)S(1)}, bf16[4,32,128]{2,1,0:T(8,128)(2,1)S(1)}, u32[]{:S(2)}, u32[]{:S(2)}) collective-permute-start(bf16[4,32,128]{2,1,0:T(8,128)(2,1)S(1)} %pad_maximum_fusion.2), channel_id=1, source_target_pairs={{0,8},{2,10},{4,12},{6,14},{8,0},{10,2},{12,4},{14,6},{1,9},{3,11}... | collective-permute-start | bytes 98312 | tf_op jit(solution)/shard_map/ppermute | solution.py:743
  8.8 2.9 %collective-permute-start.2 = (bf16[2,32,128]{2,1,0:T(8,128)(2,1)S(1)}, bf16[2,32,128]{2,1,0:T(8,128)(2,1)S(1)}, u32[]{:S(2)}, u32[]{:S(2)}) collective-permute-start(bf16[2,32,128]{2,1,0:T(8,128)(2,1)S(1)} %get-tuple-element.32), channel_id=1, source_target_pairs={{0,1},{1,0},{2,3},{3,2},{4,5},{5,4},{6,7},{7,6},{8,9},{9,8},{10,11... | collective-permute-start | bytes 49160 | tf_op jit(solution)/shard_map/ppermute | solution.py:783
  9.0 4.8 %collective-permute-start.5 = (bf16[3,32,128]{2,1,0:T(8,128)(2,1)S(1)}, bf16[3,32,128]{2,1,0:T(8,128)(2,1)S(1)}, u32[]{:S(2)}, u32[]{:S(2)}) collective-permute-start(bf16[3,32,128]{2,1,0:T(8,128)(2,1)S(1)} %get-tuple-element.48), channel_id=1, source_target_pairs={{0,6},{2,4},{4,2},{6,0},{8,14},{10,12},{12,10},{14,8},{1,7},{3,5},... | collective-permute-start | bytes 73736 | tf_op jit(solution)/shard_map/ppermute | solution.py:743
  11.6 4.0 %collective-permute-start.4 = (bf16[4,32,128]{2,1,0:T(8,128)(2,1)S(1)}, bf16[4,32,128]{2,1,0:T(8,128)(2,1)S(1)}, u32[]{:S(2)}, u32[]{:S(2)}) collective-permute-start(bf16[4,32,128]{2,1,0:T(8,128)(2,1)S(1)} %get-tuple-element.51), channel_id=1, source_target_pairs={{0,4},{2,6},{4,0},{6,2},{8,12},{10,14},{12,8},{14,10},{1,5},{3,7},... | collective-permute-start | bytes 98312 | tf_op jit(solution)/shard_map/ppermute | solution.py:743
  12.2 3.9 %collective-permute-start.3 = (bf16[4,32,128]{2,1,0:T(8,128)(2,1)S(1)}, bf16[4,32,128]{2,1,0:T(8,128)(2,1)S(1)}, u32[]{:S(2)}, u32[]{:S(2)}) collective-permute-start(bf16[4,32,128]{2,1,0:T(8,128)(2,1)S(1)} %get-tuple-element.52), channel_id=1, source_target_pairs={{0,2},{2,0},{4,6},{6,4},{8,10},{10,8},{12,14},{14,12},{1,3},{3,1},... | collective-permute-start | bytes 98312 | tf_op jit(solution)/shard_map/ppermute | solution.py:743
  13.7 1.2 %collective-permute-start.6 = (bf16[32,128]{1,0:T(8,128)(2,1)S(1)}, bf16[32,128]{1,0:T(8,128)(2,1)S(1)}, u32[]{:S(2)}, u32[]{:S(2)}) collective-permute-start(bf16[32,128]{1,0:T(8,128)(2,1)S(1)} %fusion), channel_id=1, source_target_pairs={{0,1},{1,0},{2,3},{3,2},{4,5},{5,4},{6,7},{7,6},{8,9},{9,8},{10,11... | collective-permute-start | bytes 24584 | tf_op jit(solution)/shard_map/ppermute | solution.py:788

commit v19 on v14

--- a/solution.py
+++ b/solution.py
@@ -31,6 +31,21 @@
     middle = rest.astype(BF16)
     low = (rest - middle.astype(F32)).astype(BF16)
     return top, middle, low
+
+
+def exchange_blocks(pieces, width):
+    first, second, third, fourth = pieces
+    blocks = lane_block(first.shape, width)
+    odd, high = blocks % 2 == 1, blocks >= 2
+    roll = lambda value, count: pltpu.roll(value, count * width, 1)
+    first, second = jnp.where(odd, roll(second, 1), first), jnp.where(odd, second, roll(first, 3))
+    third, fourth = jnp.where(odd, roll(fourth, 1), third), jnp.where(odd, fourth, roll(third, 3))
+    return [
+        jnp.where(high, roll(third, 2), first),
+        jnp.where(high, roll(fourth, 2), second),
+        jnp.where(high, third, roll(first, 2)),
+        jnp.where(high, fourth, roll(second, 2)),
+    ]
 
 
 def split_two(value):
@@ -351,7 +366,7 @@
 def small_project_kernel(
     x_hbm, gain_hbm, offset_hbm, left_w_hbm, left_b_hbm, right_w_hbm, right_b_hbm, pair_offset_hbm,
     cot_hbm, both_ref, normed_ref, inv_std_ref, spread_w_ref, gain_ref, pair_offset_ref, cot_ref,
-    x_ref, offset_ref, left_w_ref, left_b_ref, right_w_ref, right_b_ref, semaphores,
+    x_ref, offset_ref, left_w_ref, left_b_ref, right_w_ref, right_b_ref, wide_ref, semaphores,
 ):
     seqs, residues, _ = x_ref.shape
     depth = left_w_ref.shape[0]
@@ -376,7 +391,8 @@
     )
     for copy in copies[:parts]:
         copy.wait()
-    normed, inv_std = normalise(residue_rows(x_ref))
+    rows = x_ref[...].astype(F32).reshape(seqs * residues, x_ref.shape[2])
+    normed, inv_std = normalise(rows)
     for copy in copies[parts:]:
         copy.wait()
     ln_out = (normed * gain_ref[...] + offset_ref[...]).astype(BF16)
@@ -387,8 +403,10 @@
     wide = lax.dot_general(ln_out, weight, NT, preferred_element_type=F32)
     for place, bias_ref in enumerate((left_b_ref, right_b_ref)):
         bias = jnp.concatenate([bias_ref[...]] * residues, axis=1)
-        lanes = wide[:, place * LANES : (place + 1) * LANES]
-        own = pick(blocks, [lanes[p * seqs : (p + 1) * seqs] for p in range(residues)])
+        wide_ref[place] = wide[:, place * LANES : (place + 1) * LANES]
+        own = pick(
+            blocks, [wide_ref[place, pl.ds(p, seqs, stride=residues), :] for p in range(residues)]
+        )
         both_ref[place] = (own + bias).astype(BF16)
     normed_ref[...] = normed
     inv_std_ref[...] = jnp.broadcast_to(inv_std, inv_std_ref.shape)
@@ -399,18 +417,13 @@
     columns = cot.shape[0] // residues
     depth = LANES // residues
     flat = jnp.dot(cot, sorted_wt_ref[...], preferred_element_type=F32) * scale
-    blocks = lane_block((columns, LANES), depth)
     for tile in range(depth * depth // LANES):
         block = flat[:, tile * LANES : (tile + 1) * LANES]
-        turned = [block] + [pltpu.roll(block, depth * t, 1) for t in range(1, residues)]
+        turned = exchange_blocks(
+            [block[i * columns : (i + 1) * columns] for i in range(residues)], depth
+        )
         for e in range(residues):
-            turn_ref[pl.ds(tile * residues + e, columns, stride=depth), :] = pick(
-                blocks,
-                [
-                    turned[(i - e) % residues][i * columns : (i + 1) * columns]
-                    for i in range(residues)
-                ],
-            )
+            turn_ref[pl.ds(tile * residues + e, columns, stride=depth), :] = turned[e]
     return turn_ref[...].astype(BF16)
 
 
@@ -523,7 +536,7 @@
 def small_finish_kernel(
     scale, right_ref, part_refs, swapped_ref, swapped_late_ref, both_ref, outer_near_ref, outer_far_ref,
     keep_ref, normed_ref, inv_std_ref, gain_ref, spread_w_ref, sorted_w_ref, offset_ref,
-    grad_hbm, pair_hbm, grad_ref, pair_ref, near_ref, beyond_ref, turn_ref, semaphores,
+    grad_hbm, pair_hbm, grad_ref, pair_ref, near_ref, beyond_ref, turn_ref, lines_ref, semaphores,
 ):
     seqs, residues, _ = grad_ref.shape
     columns = pair_ref.shape[1]
@@ -563,15 +576,20 @@
     parts = jnp.concatenate(split_two(spread), axis=0)
     ln_cot = jnp.dot(parts, spread_w_ref[...], preferred_element_type=F32)
     ln_cot = ln_cot[0:rows] + ln_cot[rows : 2 * rows]
-    gained = ln_cot * gain_ref[...]
+    tiles = range(lines_ref.shape[0])
+    for place in range(residues):
+        for tile in tiles:
+            lines_ref[tile, pl.ds(place, seqs, stride=residues), :] = ln_cot[
+                place * seqs : (place + 1) * seqs, tile * LANES : (tile + 1) * LANES
+            ]
+    gained = jnp.concatenate([lines_ref[tile] for tile in tiles], axis=1) * gain_ref[...]
     normed = normed_ref[...]
     grad = inv_std_ref[:, 0:1] * (
         gained
         - jnp.mean(gained, axis=-1, keepdims=True)
         - normed * jnp.mean(gained * normed, axis=-1, keepdims=True)
     )
-    for place in range(residues):
-        grad_ref[:, place, :] = grad[place * seqs : (place + 1) * seqs].astype(BF16)
+    grad_ref[...] = grad.reshape(grad_ref.shape).astype(BF16)
     grad_copy = pltpu.make_async_copy(grad_ref, grad_hbm, semaphores.at[0])
     grad_copy.start()
 
@@ -592,30 +610,16 @@
     )
     left = jnp.concatenate([both_ref[0], swapped_ref[1]], axis=0)
     turn_ref[...] = lax.dot_general(right, left, TN, preferred_element_type=F32) * scale
-    blocks = lane_block((columns, LANES), depth)
     tiles = []
     for tile in range(depth * depth // LANES):
-        pieces = [
-            turn_ref[pl.ds(tile * residues + e, columns, stride=depth), :]
-            for e in range(residues)
-        ]
-        lines = jnp.concatenate(pieces, axis=0)
-        turned = [lines] + [pltpu.roll(lines, depth * t, 1) for t in range(1, residues)]
-        tiles.append(
-            jnp.concatenate(
-                [
-                    pick(
-                        blocks,
-                        [
-                            turned[(e - i) % residues][e * columns : (e + 1) * columns]
-                            for e in range(residues)
-                        ],
-                    )
-                    for i in range(residues)
-                ],
-                axis=0,
-            )
+        turned = exchange_blocks(
+            [
+                turn_ref[pl.ds(tile * residues + e, columns, stride=depth), :]
+                for e in range(residues)
+            ],
+            depth,
         )
+        tiles.append(jnp.concatenate(turned, axis=0))
     flat = jnp.concatenate(tiles, axis=1)
     rows = residues * columns
     parts = jnp.concatenate(split_two(flat), axis=0)
@@ -675,6 +679,7 @@
             pltpu.VMEM((1, depth), F32),
             pltpu.VMEM((depth, features), BF16),
             pltpu.VMEM((1, depth), F32),
+            pltpu.VMEM((2, rows, LANES), F32),
             pltpu.SemaphoreType.DMA((12,)),
         ],
         compiler_params=limit,
@@ -760,6 +765,7 @@
             pltpu.VMEM((ranks // 2, seqs, LANES), BF16),
             pltpu.VMEM((ranks // 2, seqs, LANES), BF16),
             pltpu.VMEM((ranks // 2 * LANES, LANES), F32),
+            pltpu.VMEM((features // LANES, rows, LANES), F32),
             pltpu.SemaphoreType.DMA((2,)),
         ],
         compiler_params=limit,

time: 17.6 us -> 17.6 us (level)
  transfers between devices with their start and end apart: 7 -> 7, of which waited for: 5 -> 5; matrix products, arithmetic and copies ran while one was open for 0% -> 0% of each run, Pallas kernels for 19% -> 18%
where the time goes in v19:
time: 17.6 us; the launch traced here: 17.4 us
  starting transfers between devices  8.82 us (50%)
  Pallas kernels  4.96 us (28%)
  waiting for transfers between devices  2.87 us (16%)
  between operations  0.71 us (4%)
    ppermute x4, starting transfers between devices, swap_over(): lax.ppermute(value, 'res', [(source, source ^ mask) for source in range(r...  8.22 us
    pallas_call x1, Pallas kernels, small_slice(): pl.pallas_call(functools.partial(small_own_kernel, scale), in_specs=[vmem...  1.83 us
    ppermute x4, waiting for transfers between devices, swap_over(): lax.ppermute(value, 'res', [(source, source ^ mask) for source in range(r...  1.7 us
    pallas_call x1, Pallas kernels, small_slice(): pl.pallas_call(functools.partial(small_finish_kernel, scale), in_specs=[v...  1.33 us
    pallas_call x1, Pallas kernels, small_slice(): pl.pallas_call(small_project_kernel, in_specs=[hbm] * 9, out_specs=[vmem]...  1.3 us
    ppermute x1, waiting for transfers between devices, small_slice(): lax.ppermute(jnp.where(own_is_near, diagonal[1], diagonal[0]), 'seq', swap)  1.17 us
    ppermute x1, starting transfers between devices, small_slice(): other_cot = lax.ppermute(coupling_cotangent, 'seq', swap)  0.52 us
    pallas_call x1, Pallas kernels, small_slice(): pl.pallas_call(functools.partial(small_partner_kernel, scale, residues),...  0.51 us
  transfers between devices with their start and end apart: 7, of which 5 were waited for; matrix products, arithmetic and copies ran while one was open for 0% of the time, Pallas kernels for 18%

profile of v19, /device:TPU:0, one launch (start us, length us, event | category | flops | bytes accessed | tf_op | source)
XLA Modules:
  0.0 17.4 jit_solution(12845539569323401368)
XLA Ops:
  0.6 0.0 copy-start
  0.6 0.5 %collective-permute-start = (bf16[4,16,128]{2,1,0:T(8,128)(2,1)}, bf16[4,16,128]{2,1,0:T(8,128)(2,1)S(1)}, u32[]{:S(2)}, u32[]{:S(2)}) collective-permute-start(bf16[4,16,128]{2,1,0:T(8,128)(2,1)} %cot_hbm.1), channel_id=1, source_target_pairs={{0,1},{1,0},{2,3},{3,2},{4,5},{5,4},{6,7},{7,6},{8,9},{9,8},{10,11... | collective-permute-start | bytes 49160 | tf_op jit(solution)/shard_map/ppermute | solution.py:659
  1.2 1.3 %project.1 = (bf16[2,32,128]{2,1,0:T(8,128)(2,1)S(1)}, f32[128,256]{1,0:T(8,128)S(1)}, f32[128,128]{1,0:T(8,128)S(1)}, bf16[256,256]{1,0:T(8,128)(2,1)S(1)}, f32...) custom-call(bf16[32,4,256]{2,1,0:T(4,128)(2,1)} %x_hbm.1, f32[1,256]{1,0:T(1,128)} %bitcast.19, ...), custom_call_target="tpu_custom_call" | custom-call | tf_op jit(solution)/shard_map/project/pallas_call | solution.py:662
  2.5 0.0 collective-permute-done.other_ref
  2.5 3.7 %collective-permute-start.1 = (bf16[4,32,128]{2,1,0:T(8,128)(2,1)S(1)}, bf16[4,32,128]{2,1,0:T(8,128)(2,1)S(1)}, u32[]{:S(2)}, u32[]{:S(2)}) collective-permute-start(bf16[4,32,128]{2,1,0:T(8,128)(2,1)S(1)} %pad_maximum_fusion.2), channel_id=1, source_target_pairs={{0,8},{2,10},{4,12},{6,14},{8,0},{10,2},{12,4},{14,6},{1,9},{3,11}... | collective-permute-start | bytes 98312 | tf_op jit(solution)/shard_map/ppermute | solution.py:705
  6.2 0.0 copy-done
  6.2 1.8 %own_pieces.1 = (f32[4,32,128]{2,1,0:T(8,128)S(1)}, bf16[512,128]{1,0:T(8,128)(2,1)S(1)}, bf16[512,128]{1,0:T(8,128)(2,1)S(1)}, bf16[1024,128]{1,0:T(8,128)(2,1)...) custom-call(bf16[4,16,128]{2,1,0:T(8,128)(2,1)S(1)} %get-tuple-element.23.own_ref, ...), custom_call_target="tpu_custom_call" | custom-call | tf_op jit(solution)/shard_map/own_pieces/pallas_call | solution.py:713
  8.1 0.2 collective-permute-done.1.got_ref
  8.2 0.5 %partner_pieces.1 = (bf16[4,3,32,128]{3,2,1,0:T(8,128)(2,1)S(1)}, f32[4,32,128]{2,1,0:T(8,128)S(1)}, bf16[2,32,128]{2,1,0:T(8,128)(2,1)S(1)}, bf16[2,32,128]{2,1,0:T(8,128)(2,1)S(1)}) custom-call(bf16[4,32,128]{2,1,0:T(8,128)(2,1)S(1)} %collective-permute-done.1.got_ref, bf16[128,1024]{1,0:T(8,128)(2,1)S(1)} %get-tuple-element.24.sorted_wt_ref, ...), custom_call_target="tpu_custom_call" | custom-call | tf_op jit(solution)/shard_map/partner_pieces/pallas_call | solution.py:731
  8.7 0.1 collective-permute-start.2
  8.8 2.8 %collective-permute-start.5 = (bf16[3,32,128]{2,1,0:T(8,128)(2,1)S(1)}, bf16[3,32,128]{2,1,0:T(8,128)(2,1)S(1)}, u32[]{:S(2)}, u32[]{:S(2)}) collective-permute-start(bf16[3,32,128]{2,1,0:T(8,128)(2,1)S(1)} %get-tuple-element.42), channel_id=1, source_target_pairs={{0,6},{2,4},{4,2},{6,0},{8,14},{10,12},{12,10},{14,8},{1,7},{3,5},... | collective-permute-start | bytes 73736 | tf_op jit(solution)/shard_map/ppermute | solution.py:705
  11.6 0.0 collective-permute-done.2.swapped_ref
  11.6 0.5 %collective-permute-start.4 = (bf16[4,32,128]{2,1,0:T(8,128)(2,1)S(1)}, bf16[4,32,128]{2,1,0:T(8,128)(2,1)S(1)}, u32[]{:S(2)}, u32[]{:S(2)}) collective-permute-start(bf16[4,32,128]{2,1,0:T(8,128)(2,1)S(1)} %get-tuple-element.45), channel_id=1, source_target_pairs={{0,4},{2,6},{4,0},{6,2},{8,12},{10,14},{12,8},{14,10},{1,5},{3,7},... | collective-permute-start | bytes 98312 | tf_op jit(solution)/shard_map/ppermute | solution.py:705
  12.2 1.2 %collective-permute-start.3 = (bf16[4,32,128]{2,1,0:T(8,128)(2,1)S(1)}, bf16[4,32,128]{2,1,0:T(8,128)(2,1)S(1)}, u32[]{:S(2)}, u32[]{:S(2)}) collective-permute-start(bf16[4,32,128]{2,1,0:T(8,128)(2,1)S(1)} %get-tuple-element.46), channel_id=1, source_target_pairs={{0,2},{2,0},{4,6},{6,4},{8,10},{10,8},{12,14},{14,12},{1,3},{3,1},... | collective-permute-start | bytes 98312 | tf_op jit(solution)/shard_map/ppermute | solution.py:705
  13.4 0.3 %collective-permute-done.5.part_refs_2_ = bf16[3,32,128]{2,1,0:T(8,128)(2,1)S(1)} collective-permute-done((bf16[3,32,128]{2,1,0:T(8,128)(2,1)S(1)}, bf16[3,32,128]{2,1,0:T(8,128)(2,1)S(1)}, u32[]{:S(2)}, u32[]{:S(2)}) %collective-permute-start.5) | collective-permute-done | bytes 24608 | tf_op jit(solution)/shard_map/ppermute | solution.py:705
  13.6 0.0 collective-permute-start.6
  13.6 1.2 %collective-permute-done.6.swapped_late_ref = bf16[32,128]{1,0:T(8,128)(2,1)S(1)} collective-permute-done((bf16[32,128]{1,0:T(8,128)(2,1)S(1)}, bf16[32,128]{1,0:T(8,128)(2,1)S(1)}, u32[]{:S(2)}, u32[]{:S(2)}) %collective-permute-start.6) | collective-permute-done | bytes 8224 | tf_op jit(solution)/shard_map/ppermute | solution.py:750
  14.8 0.8 %collective-permute-done.4.part_refs_1_ = bf16[4,32,128]{2,1,0:T(8,128)(2,1)S(1)} collective-permute-done((bf16[4,32,128]{2,1,0:T(8,128)(2,1)S(1)}, bf16[4,32,128]{2,1,0:T(8,128)(2,1)S(1)}, u32[]{:S(2)}, u32[]{:S(2)}) %collective-permute-start.4) | collective-permute-done | bytes 32800 | tf_op jit(solution)/shard_map/ppermute | solution.py:705
  15.6 0.4 %collective-permute-done.3.part_refs_0_ = bf16[4,32,128]{2,1,0:T(8,128)(2,1)S(1)} collective-permute-done((bf16[4,32,128]{2,1,0:T(8,128)(2,1)S(1)}, bf16[4,32,128]{2,1,0:T(8,128)(2,1)S(1)}, u32[]{:S(2)}, u32[]{:S(2)}) %collective-permute-start.3) | collective-permute-done | bytes 32800 | tf_op jit(solution)/shard_map/ppermute | solution.py:705
  16.1 1.3 %finish.1 = (bf16[32,4,256]{2,1,0:T(4,128)(2,1)}, bf16[4,16,128]{2,1,0:T(8,128)(2,1)}) custom-call(bf16[2,32,128]{2,1,0:T(8,128)(2,1)S(1)} %get-tuple-element.28.right_ref, bf16[4,32,128]{2,1,0:T(8,128)(2,1)S(1)} %collective-permute-done.3.part_refs_0_, bf16[4,32,128]{2,1,0:T(8,128)(2,1)S(1)} %collective-permute-done.4.part_refs_1_, ...), custom_call_target="tpu_custom_call" | custom-call | tf_op jit(solution)/shard_map/finish/pallas_call | solution.py:754
  (6 shorter events, 0.0 us)
Async XLA Ops:
  0.6 5.6 %copy-start = (bf16[1024,128]{1,0:T(8,128)(2,1)S(1)}, bf16[1024,128]{1,0:T(8,128)(2,1)}, u32[]{:S(2)}) copy-start(bf16[1024,128]{1,0:T(8,128)(2,1)} %w_ref.1) | copy-start | bytes 786436
  0.6 1.8 %collective-permute-start = (bf16[4,16,128]{2,1,0:T(8,128)(2,1)}, bf16[4,16,128]{2,1,0:T(8,128)(2,1)S(1)}, u32[]{:S(2)}, u32[]{:S(2)}) collective-permute-start(bf16[4,16,128]{2,1,0:T(8,128)(2,1)} %cot_hbm.1), channel_id=1, source_target_pairs={{0,1},{1,0},{2,3},{3,2},{4,5},{5,4},{6,7},{7,6},{8,9},{9,8},{10,11... | collective-permute-start | bytes 49160 | tf_op jit(solution)/shard_map/ppermute | solution.py:659
  2.5 5.7 %collective-permute-start.1 = (bf16[4,32,128]{2,1,0:T(8,128)(2,1)S(1)}, bf16[4,32,128]{2,1,0:T(8,128)(2,1)S(1)}, u32[]{:S(2)}, u32[]{:S(2)}) collective-permute-start(bf16[4,32,128]{2,1,0:T(8,128)(2,1)S(1)} %pad_maximum_fusion.2), channel_id=1, source_target_pairs={{0,8},{2,10},{4,12},{6,14},{8,0},{10,2},{12,4},{14,6},{1,9},{3,11}... | collective-permute-start | bytes 98312 | tf_op jit(solution)/shard_map/ppermute | solution.py:705
  8.7 2.9 %collective-permute-start.2 = (bf16[2,32,128]{2,1,0:T(8,128)(2,1)S(1)}, bf16[2,32,128]{2,1,0:T(8,128)(2,1)S(1)}, u32[]{:S(2)}, u32[]{:S(2)}) collective-permute-start(bf16[2,32,128]{2,1,0:T(8,128)(2,1)S(1)} %get-tuple-element.30), channel_id=1, source_target_pairs={{0,1},{1,0},{2,3},{3,2},{4,5},{5,4},{6,7},{7,6},{8,9},{9,8},{10,11... | collective-permute-start | bytes 49160 | tf_op jit(solution)/shard_map/ppermute | solution.py:745
  8.8 4.8 %collective-permute-start.5 = (bf16[3,32,128]{2,1,0:T(8,128)(2,1)S(1)}, bf16[3,32,128]{2,1,0:T(8,128)(2,1)S(1)}, u32[]{:S(2)}, u32[]{:S(2)}) collective-permute-start(bf16[3,32,128]{2,1,0:T(8,128)(2,1)S(1)} %get-tuple-element.42), channel_id=1, source_target_pairs={{0,6},{2,4},{4,2},{6,0},{8,14},{10,12},{12,10},{14,8},{1,7},{3,5},... | collective-permute-start | bytes 73736 | tf_op jit(solution)/shard_map/ppermute | solution.py:705
  11.6 4.0 %collective-permute-start.4 = (bf16[4,32,128]{2,1,0:T(8,128)(2,1)S(1)}, bf16[4,32,128]{2,1,0:T(8,128)(2,1)S(1)}, u32[]{:S(2)}, u32[]{:S(2)}) collective-permute-start(bf16[4,32,128]{2,1,0:T(8,128)(2,1)S(1)} %get-tuple-element.45), channel_id=1, source_target_pairs={{0,4},{2,6},{4,0},{6,2},{8,12},{10,14},{12,8},{14,10},{1,5},{3,7},... | collective-permute-start | bytes 98312 | tf_op jit(solution)/shard_map/ppermute | solution.py:705
  12.2 3.9 %collective-permute-start.3 = (bf16[4,32,128]{2,1,0:T(8,128)(2,1)S(1)}, bf16[4,32,128]{2,1,0:T(8,128)(2,1)S(1)}, u32[]{:S(2)}, u32[]{:S(2)}) collective-permute-start(bf16[4,32,128]{2,1,0:T(8,128)(2,1)S(1)} %get-tuple-element.46), channel_id=1, source_target_pairs={{0,2},{2,0},{4,6},{6,4},{8,10},{10,8},{12,14},{14,12},{1,3},{3,1},... | collective-permute-start | bytes 98312 | tf_op jit(solution)/shard_map/ppermute | solution.py:705
  13.6 1.2 %collective-permute-start.6 = (bf16[32,128]{1,0:T(8,128)(2,1)S(1)}, bf16[32,128]{1,0:T(8,128)(2,1)S(1)}, u32[]{:S(2)}, u32[]{:S(2)}) collective-permute-start(bf16[32,128]{1,0:T(8,128)(2,1)S(1)} %fusion), channel_id=1, source_target_pairs={{0,1},{1,0},{2,3},{3,2},{4,5},{5,4},{6,7},{7,6},{8,9},{9,8},{10,11... | collective-permute-start | bytes 24584 | tf_op jit(solution)/shard_map/ppermute | solution.py:750

commit v20 on v19

--- a/solution.py
+++ b/solution.py
@@ -403,7 +403,7 @@
     wide = lax.dot_general(ln_out, weight, NT, preferred_element_type=F32)
     for place, bias_ref in enumerate((left_b_ref, right_b_ref)):
         bias = jnp.concatenate([bias_ref[...]] * residues, axis=1)
-        wide_ref[place] = wide[:, place * LANES : (place + 1) * LANES]
+        wide_ref[place, 0 : seqs * residues, :] = wide[:, place * LANES : (place + 1) * LANES]
         own = pick(
             blocks, [wide_ref[place, pl.ds(p, seqs, stride=residues), :] for p in range(residues)]
         )
@@ -413,10 +413,13 @@
     spread_w_ref[...] = weight
 
 
-def outer_rows(scale, cot, residues, sorted_wt_ref, turn_ref):
-    columns = cot.shape[0] // residues
+def outer_flat(scale, cot, sorted_wt_ref):
+    return jnp.dot(cot, sorted_wt_ref[...], preferred_element_type=F32) * scale
+
+
+def outer_rows(flat, residues, turn_ref):
+    columns = flat.shape[0] // residues
     depth = LANES // residues
-    flat = jnp.dot(cot, sorted_wt_ref[...], preferred_element_type=F32) * scale
     for tile in range(depth * depth // LANES):
         block = flat[:, tile * LANES : (tile + 1) * LANES]
         turned = exchange_blocks(
@@ -424,87 +427,18 @@
         )
         for e in range(residues):
             turn_ref[pl.ds(tile * residues + e, columns, stride=depth), :] = turned[e]
-    return turn_ref[...].astype(BF16)
-
-
-def small_own_kernel(scale, own_ref, other_ref, w_ref, both_ref,
-                     keep_ref, outer_near_ref, outer_far_ref, sorted_w_ref, sorted_wt_ref,
-                     order_ref, repeat_ref, turn_refs, wide_ref):
-    residues, columns, _ = own_ref.shape
-    depth = LANES // residues
-    wide_ref[...] = w_ref[...].astype(F32)
-    for d in range(depth):
-        sorted_w_ref[d * depth : (d + 1) * depth, :] = wide_ref[
-            pl.ds(d, depth, stride=depth), :
-        ].astype(BF16)
-    sorted_wt_ref[...] = sorted_w_ref[...].T
-    rank = lax.axis_index("res")
-    own_is_near = lax.axis_index("seq") == lax.shift_right_logical(rank, 2)
-    own = own_ref[...].reshape(residues * columns, LANES)
-    other = other_ref[...].reshape(residues * columns, LANES)
-    near = outer_rows(
-        scale, jnp.where(own_is_near, own, other), residues, sorted_wt_ref, turn_refs[0]
-    )
-    outer_near_ref[...] = near
-    partial = lax.dot_general(both_ref[0], near, NT, preferred_element_type=F32)
-    for place in range(columns // residues):
-        keep_ref[lax.bitwise_xor(rank & 3, place)] = partial[:, place * LANES : (place + 1) * LANES]
-    outer_far_ref[...] = outer_rows(
-        scale, jnp.where(own_is_near, other, own), residues, sorted_wt_ref, turn_refs[1]
-    )
-    order_ref[...] = one_hot(
-        lambda row: (
-            (2 * (row >> 6 & 1) + (row >> 2 & 1)) * LANES
-            + (row & 3) * depth + (row >> 3 & 7) * residues + (row >> 7)
-        ),
-        order_ref.shape,
-    )
-    for place in range(residues):
-        shape = (LANES, LANES)
-        row = lax.broadcasted_iota(jnp.int32, shape, 0)
-        lane = lax.broadcasted_iota(jnp.int32, shape, 1)
-        repeat_ref[:, place * LANES : (place + 1) * LANES] = jnp.where(
-            row == place * depth + lane % depth, 1.0, 0.0
-        ).astype(BF16)
-
-
-def one_hot(target, shape):
-    part = (shape[0], LANES)
-    wanted = target(lax.broadcasted_iota(jnp.int32, part, 0))
-    lane = lax.broadcasted_iota(jnp.int32, part, 1)
+    return turn_ref[0 : columns * depth, :].astype(BF16)
+
+
+def outer_tiles(flat, residues):
+    columns = flat.shape[0] // residues
     return jnp.concatenate(
-        [
-            jnp.where(wanted == lane + tile * LANES, 1.0, 0.0).astype(BF16)
-            for tile in range(shape[1] // LANES)
-        ],
-        axis=1,
-    )
-
-
-def blocks_apart(left, repeat, residues):
-    depth = LANES // residues
-    wide = jnp.dot(left, repeat, preferred_element_type=F32)
-    blocks = lane_block(wide.shape, depth) % residues
-    return jnp.concatenate(
-        [jnp.where(blocks == e, wide, 0.0).astype(BF16) for e in range(residues)], axis=0
-    )
-
-
-def small_partner_kernel(scale, residues, got_ref, sorted_wt_ref, keep_ref, both_ref, order_ref,
-                         repeat_ref, leaving_ref, keep_out_ref, right_ref, swap_ref):
-    rank = lax.axis_index("res")
-    seqs = got_ref.shape[1]
-    cot = got_ref[2:4].reshape(2 * seqs, LANES)
-    columns = cot.shape[0] // residues
-    tiles = sorted_wt_ref.shape[1] // LANES
-    flat = jnp.dot(cot, sorted_wt_ref[...], preferred_element_type=F32) * scale
-    outer = jnp.concatenate(
         [
             jnp.concatenate(
                 [
-                    flat[i * columns + start : i * columns + start + 8, tile * LANES : (tile + 1) * LANES]
+                    flat[i * columns + start : i * columns + start + 8, tile : tile + LANES]
                     for start in range(0, columns, 8)
-                    for tile in range(tiles)
+                    for tile in range(0, flat.shape[1], LANES)
                 ],
                 axis=0,
             )
@@ -512,30 +446,100 @@
         ],
         axis=1,
     ).astype(BF16)
-    apart = blocks_apart(got_ref[0], repeat_ref[...], residues)
-    partial = lax.dot_general(apart, outer, NT, preferred_element_type=F32).astype(BF16)
-    partial = jnp.concatenate(
-        [partial[e * seqs : (e + 1) * seqs] for e in range(residues)], axis=1
-    )
-    partial = jnp.dot(partial, order_ref[...], preferred_element_type=F32)
+
+
+def blocks_apart(left, repeat, residues):
+    depth = LANES // residues
+    wide = jnp.dot(left, repeat, preferred_element_type=F32)
+    blocks = lane_block(wide.shape, depth) % residues
+    return jnp.concatenate(
+        [jnp.where(blocks == e, wide, 0.0).astype(BF16) for e in range(residues)], axis=0
+    )
+
+
+def column_pieces(left, outer, repeat, residues):
+    seqs = left.shape[0]
+    partial = lax.dot_general(
+        blocks_apart(left, repeat, residues), outer, NT, preferred_element_type=F32
+    )
+    rows = [partial[e * seqs : (e + 1) * seqs] for e in range(residues)]
+    turned = [pltpu.roll(row, LANES // 2, 1) for row in rows]
+    low = lane_block(rows[0].shape, LANES // 2) == 0
+    return [
+        [jnp.where(low, rows[e], turned[e + 1]) for e in (0, 2)],
+        [jnp.where(low, turned[e], rows[e + 1]) for e in (0, 2)],
+    ]
+
+
+def small_own_kernel(scale, own_ref, other_ref, w_ref, both_ref, spread_w_ref,
+                     keep_ref, outer_near_ref, outer_far_ref, sorted_w_ref, sorted_wt_ref,
+                     repeat_ref, columns_w_ref, turn_refs, wide_ref):
+    residues, columns, _ = own_ref.shape
+    depth = LANES // residues
+    wide_ref[0 : w_ref.shape[0], :] = w_ref[...].astype(F32)
+    for d in range(depth):
+        sorted_w_ref[d * depth : (d + 1) * depth, :] = wide_ref[
+            pl.ds(d, depth, stride=depth), :
+        ].astype(BF16)
+    sorted_wt_ref[...] = sorted_w_ref[...].T
+    shape = (LANES, LANES)
+    row = lax.broadcasted_iota(jnp.int32, shape, 0)
+    lane = lax.broadcasted_iota(jnp.int32, shape, 1)
+    for place in range(residues):
+        repeat_ref[:, place * LANES : (place + 1) * LANES] = jnp.where(
+            row == place * depth + lane % depth, 1.0, 0.0
+        ).astype(BF16)
+    shape = (columns_w_ref.shape[0], depth)
+    row = lax.broadcasted_iota(jnp.int32, shape, 0)
+    lane = lax.broadcasted_iota(jnp.int32, shape, 1)
+    chosen = jnp.where(lane == (row >> 3 & 7) * residues + (row >> 6), 1.0, 0.0).astype(BF16)
+    columns_w_ref[...] = jnp.dot(
+        chosen, spread_w_ref[LANES : LANES + depth, :], preferred_element_type=F32
+    ).astype(BF16)
+
+    rank = lax.axis_index("res")
+    own_is_near = lax.axis_index("seq") == lax.shift_right_logical(rank, 2)
+    own = own_ref[...].reshape(residues * columns, LANES)
+    other = other_ref[...].reshape(residues * columns, LANES)
+    flat = outer_flat(scale, jnp.where(own_is_near, own, other), sorted_wt_ref)
+    pieces = column_pieces(both_ref[0], outer_tiles(flat, residues), repeat_ref[...], residues)
+    for block in range(2):
+        for tile in range(2):
+            keep_ref[block, tile] = pieces[block][tile]
+    outer_near_ref[...] = outer_rows(flat, residues, turn_refs[0])
+    flat = outer_flat(scale, jnp.where(own_is_near, other, own), sorted_wt_ref)
+    outer_far_ref[...] = outer_rows(flat, residues, turn_refs[1])
+
+
+def small_partner_kernel(scale, residues, got_ref, sorted_wt_ref, keep_ref, both_ref, repeat_ref,
+                         leaving_ref, keep_out_ref, right_ref, swap_ref):
+    rank = lax.axis_index("res")
+    seqs = got_ref.shape[1]
+    cot = got_ref[2:4].reshape(2 * seqs, LANES)
+    outer = outer_tiles(outer_flat(scale, cot, sorted_wt_ref), residues)
+    pieces = column_pieces(got_ref[0], outer, repeat_ref[...], residues)
     right_ref[0] = both_ref[1]
     right_ref[1] = got_ref[1]
     own_is_near = lax.axis_index("seq") == lax.shift_right_logical(rank, 2)
     swap_ref[0] = jnp.where(own_is_near, got_ref[1], both_ref[1])
     swap_ref[1] = both_ref[0]
+    first = lax.shift_right_logical(rank & 3, 1)
+    for block in range(2):
+        distance = 2 * lax.bitwise_xor(first, block)
+        for tile in range(2):
+            total = keep_ref[block, tile] + pieces[block][tile]
+            keep_out_ref[distance, tile] = total
+            total = total.astype(BF16)
+            leaving_ref[distance, 2 + tile] = total
+            leaving_ref[distance + 1, 2 + tile] = total
     for place in range(leaving_ref.shape[0]):
         leaving_ref[place, 0] = both_ref[1]
         leaving_ref[place, 1] = got_ref[1]
-    for place in range(leaving_ref.shape[0]):
-        distance = lax.bitwise_xor(rank & 3, place)
-        total = keep_ref[distance] + partial[:, place * LANES : (place + 1) * LANES]
-        leaving_ref[distance, 2] = total.astype(BF16)
-        keep_out_ref[distance] = total
 
 
 def small_finish_kernel(
     scale, right_ref, part_refs, swapped_ref, swapped_late_ref, both_ref, outer_near_ref, outer_far_ref,
-    keep_ref, normed_ref, inv_std_ref, gain_ref, spread_w_ref, sorted_w_ref, offset_ref,
+    keep_ref, normed_ref, inv_std_ref, gain_ref, spread_w_ref, columns_w_ref, sorted_w_ref, offset_ref,
     grad_hbm, pair_hbm, grad_ref, pair_ref, near_ref, beyond_ref, turn_ref, lines_ref, semaphores,
 ):
     seqs, residues, _ = grad_ref.shape
@@ -559,14 +563,20 @@
         axis=0,
     )
     left_cot = jnp.dot(right_all, outer, preferred_element_type=F32)
-    right_cot = keep_ref[0]
-    for part_ref in part_refs:
-        right_cot = right_cot + part_ref[2].astype(F32)
+    right_cot = []
+    for tile in range(2):
+        total = keep_ref[0, tile]
+        for part_ref in part_refs:
+            total = total + part_ref[2 + tile].astype(F32)
+        right_cot.append(total)
     blocks = lane_block((seqs, LANES), depth)
+    column = lane_block((seqs, LANES), 1) % 8 - residues * (rank & 1)
     spread = jnp.concatenate(
         [
             jnp.concatenate(
-                [jnp.where(blocks == place, cot, 0.0) for cot in (left_cot, right_cot)], axis=1
+                [jnp.where(blocks == place, left_cot, 0.0)]
+                + [jnp.where(column == place, cot, 0.0) for cot in right_cot],
+                axis=1,
             )
             for place in range(residues)
         ],
@@ -574,7 +584,8 @@
     )
     rows = residues * seqs
     parts = jnp.concatenate(split_two(spread), axis=0)
-    ln_cot = jnp.dot(parts, spread_w_ref[...], preferred_element_type=F32)
+    weight = jnp.concatenate([spread_w_ref[0:LANES, :], columns_w_ref[...]], axis=0)
+    ln_cot = jnp.dot(parts, weight, preferred_element_type=F32)
     ln_cot = ln_cot[0:rows] + ln_cot[rows : 2 * rows]
     tiles = range(lines_ref.shape[0])
     for place in range(residues):
@@ -582,7 +593,7 @@
             lines_ref[tile, pl.ds(place, seqs, stride=residues), :] = ln_cot[
                 place * seqs : (place + 1) * seqs, tile * LANES : (tile + 1) * LANES
             ]
-    gained = jnp.concatenate([lines_ref[tile] for tile in tiles], axis=1) * gain_ref[...]
+    gained = jnp.concatenate([lines_ref[tile, 0:rows, :] for tile in tiles], axis=1) * gain_ref[...]
     normed = normed_ref[...]
     grad = inv_std_ref[:, 0:1] * (
         gained
@@ -597,8 +608,8 @@
     for mask, ref in enumerate(blocks_of):
         near_ref[mask] = ref[half]
     beyond_ref[0] = swapped_ref[0]
-    beyond_ref[1] = part_refs[0][3]
-    beyond_ref[2] = part_refs[1][3]
+    beyond_ref[1] = part_refs[0][4]
+    beyond_ref[2] = part_refs[1][4]
     beyond_ref[3] = swapped_late_ref[...]
     masks = [lax.bitwise_xor(here, place) for place in range(ranks)]
     right = jnp.concatenate(
@@ -609,7 +620,7 @@
         axis=0,
     )
     left = jnp.concatenate([both_ref[0], swapped_ref[1]], axis=0)
-    turn_ref[...] = lax.dot_general(right, left, TN, preferred_element_type=F32) * scale
+    turn_ref[0 : columns * depth, :] = lax.dot_general(right, left, TN, preferred_element_type=F32) * scale
     tiles = []
     for tile in range(depth * depth // LANES):
         turned = exchange_blocks(
@@ -679,7 +690,7 @@
             pltpu.VMEM((1, depth), F32),
             pltpu.VMEM((depth, features), BF16),
             pltpu.VMEM((1, depth), F32),
-            pltpu.VMEM((2, rows, LANES), F32),
+            pltpu.VMEM((2, rows + 8, LANES), F32),
             pltpu.SemaphoreType.DMA((12,)),
         ],
         compiler_params=limit,
@@ -709,38 +720,41 @@
     beyond_two = swap_over(4, jnp.concatenate([both, far_cot]))
 
     half_rows = ranks // 2 * LANES
-    turn = pltpu.VMEM((half_rows, LANES), F32)
-    keep, outer_near, outer_far, sorted_w, sorted_wt, order, repeat = pl.pallas_call(
+    turn = pltpu.VMEM((half_rows + depth, LANES), F32)
+    keep, outer_near, outer_far, sorted_w, sorted_wt, repeat, columns_w = pl.pallas_call(
         functools.partial(small_own_kernel, scale),
-        in_specs=[vmem] * 4,
+        in_specs=[vmem] * 5,
         out_specs=[vmem] * 7,
         out_shape=(
-            like((ranks // 2, seqs, LANES), F32),
+            like((2, 2, seqs, LANES), F32),
             like((half_rows, LANES), BF16),
             like((half_rows, LANES), BF16),
             like(coupling_matrix.shape, BF16),
             like(coupling_matrix.shape[::-1], BF16),
-            like((half_rows, half_rows), BF16),
             like((LANES, residues * LANES), BF16),
+            like((2 * LANES, features), BF16),
         ),
-        scratch_shapes=[[turn, turn], pltpu.VMEM(coupling_matrix.shape, F32)],
+        scratch_shapes=[
+            [turn, turn],
+            pltpu.VMEM((coupling_matrix.shape[0] + depth, LANES), F32),
+        ],
         compiler_params=limit,
         name="own_pieces",
-    )(own_cot, other_cot, coupling_matrix, both)
+    )(own_cot, other_cot, coupling_matrix, both, spread_w)
 
     leaving_parts, keep, right, leaving = pl.pallas_call(
         functools.partial(small_partner_kernel, scale, residues),
-        in_specs=[vmem] * 6,
+        in_specs=[vmem] * 5,
         out_specs=[vmem] * 4,
         out_shape=(
-            like((ranks // 2, 3, seqs, LANES), BF16),
-            like((ranks // 2, seqs, LANES), F32),
+            like((ranks // 2, 4, seqs, LANES), BF16),
+            like((ranks // 2, 2, seqs, LANES), F32),
             like((2, seqs, LANES), BF16),
             like((2, seqs, LANES), BF16),
         ),
         compiler_params=limit,
         name="partner_pieces",
-    )(beyond_two, sorted_wt, keep, both, order, repeat)
+    )(beyond_two, sorted_wt, keep, both, repeat)
 
     swapped = lax.ppermute(leaving, "seq", swap)
     diagonal = swap_over(3, leaving_parts[3])
@@ -753,7 +767,7 @@
 
     pair_delta, gradient = pl.pallas_call(
         functools.partial(small_finish_kernel, scale),
-        in_specs=[vmem, [vmem] * 3] + [vmem] * 12,
+        in_specs=[vmem, [vmem] * 3] + [vmem] * 13,
         out_specs=[pl.BlockSpec(memory_space=pl.ANY)] * 2,
         out_shape=(
             like(homolog_matrix.shape, BF16),
@@ -764,8 +778,8 @@
             pltpu.VMEM(coupling_cotangent.shape, BF16),
             pltpu.VMEM((ranks // 2, seqs, LANES), BF16),
             pltpu.VMEM((ranks // 2, seqs, LANES), BF16),
-            pltpu.VMEM((ranks // 2 * LANES, LANES), F32),
-            pltpu.VMEM((features // LANES, rows, LANES), F32),
+            turn,
+            pltpu.VMEM((features // LANES, rows + 8, LANES), F32),
             pltpu.SemaphoreType.DMA((2,)),
         ],
         compiler_params=limit,
@@ -783,6 +797,7 @@
         inv_std,
         gain,
         spread_w,
+        columns_w,
         sorted_w,
         pair_offset,
     )[::-1]

time: 17.6 us -> 17.6 us (level)
  waiting for transfers between devices: 2.87 us -> 3.57 us
  Pallas kernels: 4.96 us -> 4.3 us
    ppermute x4, waiting for transfers between devices: 1.7 us -> 2.4 us  [swap_over(): lax.ppermute(value, 'res', [(source, source ^ mask) for source in range(r...]
    pallas_call x1, Pallas kernels: 1.83 us -> 1.21 us  [small_slice(): pl.pallas_call(functools.partial(small_own_kernel, scale), in_specs=[vmem...]
  transfers between devices with their start and end apart: 7 -> 7, of which waited for: 5 -> 5; matrix products, arithmetic and copies ran while one was open for 0% -> 0% of each run, Pallas kernels for 18% -> 14%
where the time goes in v20:
time: 17.6 us; the launch traced here: 17.4 us
  starting transfers between devices  8.81 us (50%)
  Pallas kernels  4.3 us (24%)
  waiting for transfers between devices  3.57 us (20%)
  between operations  0.72 us (4%)
    ppermute x4, starting transfers between devices, swap_over(): lax.ppermute(value, 'res', [(source, source ^ mask) for source in range(r...  8.22 us
    ppermute x4, waiting for transfers between devices, swap_over(): lax.ppermute(value, 'res', [(source, source ^ mask) for source in range(r...  2.4 us
    pallas_call x1, Pallas kernels, small_slice(): pl.pallas_call(functools.partial(small_finish_kernel, scale), in_specs=[v...  1.35 us
    pallas_call x1, Pallas kernels, small_slice(): pl.pallas_call(small_project_kernel, in_specs=[hbm] * 9, out_specs=[vmem]...  1.3 us
    pallas_call x1, Pallas kernels, small_slice(): pl.pallas_call(functools.partial(small_own_kernel, scale), in_specs=[vmem...  1.21 us
    ppermute x1, waiting for transfers between devices, small_slice(): lax.ppermute(jnp.where(own_is_near, diagonal[1], diagonal[0]), 'seq', swap)  1.17 us
    ppermute x1, starting transfers between devices, small_slice(): other_cot = lax.ppermute(coupling_cotangent, 'seq', swap)  0.52 us
    pallas_call x1, Pallas kernels, small_slice(): pl.pallas_call(functools.partial(small_partner_kernel, scale, residues),...  0.44 us
  transfers between devices with their start and end apart: 7, of which 5 were waited for; matrix products, arithmetic and copies ran while one was open for 0% of the time, Pallas kernels for 14%

profile of v20, /device:TPU:0, one launch (start us, length us, event | category | flops | bytes accessed | tf_op | source)
XLA Modules:
  0.0 17.4 jit_solution(5709981200614406390)
XLA Ops:
  0.6 0.0 copy-start
  0.6 0.5 %collective-permute-start = (bf16[4,16,128]{2,1,0:T(8,128)(2,1)}, bf16[4,16,128]{2,1,0:T(8,128)(2,1)S(1)}, u32[]{:S(2)}, u32[]{:S(2)}) collective-permute-start(bf16[4,16,128]{2,1,0:T(8,128)(2,1)} %cot_hbm.1), channel_id=1, source_target_pairs={{0,1},{1,0},{2,3},{3,2},{4,5},{5,4},{6,7},{7,6},{8,9},{9,8},{10,11... | collective-permute-start | bytes 49160 | tf_op jit(solution)/shard_map/ppermute | solution.py:670
  1.2 1.3 %project.1 = (bf16[2,32,128]{2,1,0:T(8,128)(2,1)S(1)}, f32[128,256]{1,0:T(8,128)S(1)}, f32[128,128]{1,0:T(8,128)S(1)}, bf16[256,256]{1,0:T(8,128)(2,1)S(1)}, f32...) custom-call(bf16[32,4,256]{2,1,0:T(4,128)(2,1)} %x_hbm.1, f32[1,256]{1,0:T(1,128)} %bitcast.19, ...), custom_call_target="tpu_custom_call" | custom-call | tf_op jit(solution)/shard_map/project/pallas_call | solution.py:673
  2.5 0.0 collective-permute-done.other_ref
  2.5 3.7 %collective-permute-start.1 = (bf16[4,32,128]{2,1,0:T(8,128)(2,1)S(1)}, bf16[4,32,128]{2,1,0:T(8,128)(2,1)S(1)}, u32[]{:S(2)}, u32[]{:S(2)}) collective-permute-start(bf16[4,32,128]{2,1,0:T(8,128)(2,1)S(1)} %pad_maximum_fusion.2), channel_id=1, source_target_pairs={{0,8},{2,10},{4,12},{6,14},{8,0},{10,2},{12,4},{14,6},{1,9},{3,11}... | collective-permute-start | bytes 98312 | tf_op jit(solution)/shard_map/ppermute | solution.py:716
  6.2 0.0 copy-done
  6.2 1.2 %own_pieces.1 = (f32[2,2,32,128]{3,2,1,0:T(8,128)S(1)}, bf16[512,128]{1,0:T(8,128)(2,1)S(1)}, bf16[512,128]{1,0:T(8,128)(2,1)S(1)}, bf16[1024,128]{1,0:T(8,128)(...) custom-call(bf16[4,16,128]{2,1,0:T(8,128)(2,1)S(1)} %get-tuple-element.23.own_re, ...), custom_call_target="tpu_custom_call" | custom-call | tf_op jit(solution)/shard_map/own_pieces/pallas_call | solution.py:724
  7.4 0.8 %collective-permute-done.1.got_ref = bf16[4,32,128]{2,1,0:T(8,128)(2,1)S(1)} collective-permute-done((bf16[4,32,128]{2,1,0:T(8,128)(2,1)S(1)}, bf16[4,32,128]{2,1,0:T(8,128)(2,1)S(1)}, u32[]{:S(2)}, u32[]{:S(2)}) %collective-permute-start.1) | collective-permute-done | bytes 32800 | tf_op jit(solution)/shard_map/ppermute | solution.py:716
  8.2 0.4 %partner_pieces.1 = (bf16[4,4,32,128]{3,2,1,0:T(8,128)(2,1)S(1)}, f32[4,2,32,128]{3,2,1,0:T(8,128)S(1)}, bf16[2,32,128]{2,1,0:T(8,128)(2,1)S(1)}, bf16[2,32,128]{2,1,0:T(8,128)(2,1)S(1)}) custom-call(bf16[4,32,128]{2,1,0:T(8,128)(2,1)S(1)} %collective-permute-done.1.got_ref, bf16[128,1024]{1,0:T(8,128)(2,1)S(1)} %get-tuple-element.25.sorted_wt_ref, ...), custom_call_target="tpu_custom_call" | custom-call | tf_op jit(solution)/shard_map/partner_pieces/pallas_call | solution.py:745
  8.7 0.1 collective-permute-start.2
  8.8 2.8 %collective-permute-start.5 = (bf16[4,32,128]{2,1,0:T(8,128)(2,1)S(1)}, bf16[4,32,128]{2,1,0:T(8,128)(2,1)S(1)}, u32[]{:S(2)}, u32[]{:S(2)}) collective-permute-start(bf16[4,32,128]{2,1,0:T(8,128)(2,1)S(1)} %get-tuple-element.42), channel_id=1, source_target_pairs={{0,6},{2,4},{4,2},{6,0},{8,14},{10,12},{12,10},{14,8},{1,7},{3,5},... | collective-permute-start | bytes 98312 | tf_op jit(solution)/shard_map/ppermute | solution.py:716
  11.6 0.0 collective-permute-done.2.swapped_ref
  11.6 0.5 %collective-permute-start.4 = (bf16[5,32,128]{2,1,0:T(8,128)(2,1)S(1)}, bf16[5,32,128]{2,1,0:T(8,128)(2,1)S(1)}, u32[]{:S(2)}, u32[]{:S(2)}) collective-permute-start(bf16[5,32,128]{2,1,0:T(8,128)(2,1)S(1)} %get-tuple-element.45), channel_id=1, source_target_pairs={{0,4},{2,6},{4,0},{6,2},{8,12},{10,14},{12,8},{14,10},{1,5},{3,7},... | collective-permute-start | bytes 122888 | tf_op jit(solution)/shard_map/ppermute | solution.py:716
  12.1 1.2 %collective-permute-start.3 = (bf16[5,32,128]{2,1,0:T(8,128)(2,1)S(1)}, bf16[5,32,128]{2,1,0:T(8,128)(2,1)S(1)}, u32[]{:S(2)}, u32[]{:S(2)}) collective-permute-start(bf16[5,32,128]{2,1,0:T(8,128)(2,1)S(1)} %get-tuple-element.46), channel_id=1, source_target_pairs={{0,2},{2,0},{4,6},{6,4},{8,10},{10,8},{12,14},{14,12},{1,3},{3,1},... | collective-permute-start | bytes 122888 | tf_op jit(solution)/shard_map/ppermute | solution.py:716
  13.3 0.4 %collective-permute-done.5.part_refs_2_ = bf16[4,32,128]{2,1,0:T(8,128)(2,1)S(1)} collective-permute-done((bf16[4,32,128]{2,1,0:T(8,128)(2,1)S(1)}, bf16[4,32,128]{2,1,0:T(8,128)(2,1)S(1)}, u32[]{:S(2)}, u32[]{:S(2)}) %collective-permute-start.5) | collective-permute-done | bytes 32800 | tf_op jit(solution)/shard_map/ppermute | solution.py:716
  13.7 0.0 collective-permute-start.6
  13.7 1.2 %collective-permute-done.6.swapped_late_ref = bf16[32,128]{1,0:T(8,128)(2,1)S(1)} collective-permute-done((bf16[32,128]{1,0:T(8,128)(2,1)S(1)}, bf16[32,128]{1,0:T(8,128)(2,1)S(1)}, u32[]{:S(2)}, u32[]{:S(2)}) %collective-permute-start.6) | collective-permute-done | bytes 8224 | tf_op jit(solution)/shard_map/ppermute | solution.py:764
  14.8 0.8 %collective-permute-done.4.part_refs_1_ = bf16[5,32,128]{2,1,0:T(8,128)(2,1)S(1)} collective-permute-done((bf16[5,32,128]{2,1,0:T(8,128)(2,1)S(1)}, bf16[5,32,128]{2,1,0:T(8,128)(2,1)S(1)}, u32[]{:S(2)}, u32[]{:S(2)}) %collective-permute-start.4) | collective-permute-done | bytes 40992 | tf_op jit(solution)/shard_map/ppermute | solution.py:716
  15.6 0.4 %collective-permute-done.3.part_refs_0_ = bf16[5,32,128]{2,1,0:T(8,128)(2,1)S(1)} collective-permute-done((bf16[5,32,128]{2,1,0:T(8,128)(2,1)S(1)}, bf16[5,32,128]{2,1,0:T(8,128)(2,1)S(1)}, u32[]{:S(2)}, u32[]{:S(2)}) %collective-permute-start.3) | collective-permute-done | bytes 40992 | tf_op jit(solution)/shard_map/ppermute | solution.py:716
  16.1 1.3 %finish.1 = (bf16[32,4,256]{2,1,0:T(4,128)(2,1)}, bf16[4,16,128]{2,1,0:T(8,128)(2,1)}) custom-call(bf16[2,32,128]{2,1,0:T(8,128)(2,1)S(1)} %get-tuple-element.28.right_ref, bf16[5,32,128]{2,1,0:T(8,128)(2,1)S(1)} %collective-permute-done.3.part_refs_0_, bf16[5,32,128]{2,1,0:T(8,128)(2,1)S(1)} %collective-permute-done.4.part_refs_1_, ...), custom_call_target="tpu_custom_call" | custom-call | tf_op jit(solution)/shard_map/finish/pallas_call | solution.py:768
  (6 shorter events, 0.0 us)
Async XLA Ops:
  0.6 5.6 %copy-start = (bf16[1024,128]{1,0:T(8,128)(2,1)S(1)}, bf16[1024,128]{1,0:T(8,128)(2,1)}, u32[]{:S(2)}) copy-start(bf16[1024,128]{1,0:T(8,128)(2,1)} %w_ref.1) | copy-start | bytes 786436
  0.6 1.8 %collective-permute-start = (bf16[4,16,128]{2,1,0:T(8,128)(2,1)}, bf16[4,16,128]{2,1,0:T(8,128)(2,1)S(1)}, u32[]{:S(2)}, u32[]{:S(2)}) collective-permute-start(bf16[4,16,128]{2,1,0:T(8,128)(2,1)} %cot_hbm.1), channel_id=1, source_target_pairs={{0,1},{1,0},{2,3},{3,2},{4,5},{5,4},{6,7},{7,6},{8,9},{9,8},{10,11... | collective-permute-start | bytes 49160 | tf_op jit(solution)/shard_map/ppermute | solution.py:670
  2.5 5.7 %collective-permute-start.1 = (bf16[4,32,128]{2,1,0:T(8,128)(2,1)S(1)}, bf16[4,32,128]{2,1,0:T(8,128)(2,1)S(1)}, u32[]{:S(2)}, u32[]{:S(2)}) collective-permute-start(bf16[4,32,128]{2,1,0:T(8,128)(2,1)S(1)} %pad_maximum_fusion.2), channel_id=1, source_target_pairs={{0,8},{2,10},{4,12},{6,14},{8,0},{10,2},{12,4},{14,6},{1,9},{3,11}... | collective-permute-start | bytes 98312 | tf_op jit(solution)/shard_map/ppermute | solution.py:716
  8.7 2.9 %collective-permute-start.2 = (bf16[2,32,128]{2,1,0:T(8,128)(2,1)S(1)}, bf16[2,32,128]{2,1,0:T(8,128)(2,1)S(1)}, u32[]{:S(2)}, u32[]{:S(2)}) collective-permute-start(bf16[2,32,128]{2,1,0:T(8,128)(2,1)S(1)} %get-tuple-element.30), channel_id=1, source_target_pairs={{0,1},{1,0},{2,3},{3,2},{4,5},{5,4},{6,7},{7,6},{8,9},{9,8},{10,11... | collective-permute-start | bytes 49160 | tf_op jit(solution)/shard_map/ppermute | solution.py:759
  8.8 4.9 %collective-permute-start.5 = (bf16[4,32,128]{2,1,0:T(8,128)(2,1)S(1)}, bf16[4,32,128]{2,1,0:T(8,128)(2,1)S(1)}, u32[]{:S(2)}, u32[]{:S(2)}) collective-permute-start(bf16[4,32,128]{2,1,0:T(8,128)(2,1)S(1)} %get-tuple-element.42), channel_id=1, source_target_pairs={{0,6},{2,4},{4,2},{6,0},{8,14},{10,12},{12,10},{14,8},{1,7},{3,5},... | collective-permute-start | bytes 98312 | tf_op jit(solution)/shard_map/ppermute | solution.py:716
  11.6 4.1 %collective-permute-start.4 = (bf16[5,32,128]{2,1,0:T(8,128)(2,1)S(1)}, bf16[5,32,128]{2,1,0:T(8,128)(2,1)S(1)}, u32[]{:S(2)}, u32[]{:S(2)}) collective-permute-start(bf16[5,32,128]{2,1,0:T(8,128)(2,1)S(1)} %get-tuple-element.45), channel_id=1, source_target_pairs={{0,4},{2,6},{4,0},{6,2},{8,12},{10,14},{12,8},{14,10},{1,5},{3,7},... | collective-permute-start | bytes 122888 | tf_op jit(solution)/shard_map/ppermute | solution.py:716
  12.1 4.0 %collective-permute-start.3 = (bf16[5,32,128]{2,1,0:T(8,128)(2,1)S(1)}, bf16[5,32,128]{2,1,0:T(8,128)(2,1)S(1)}, u32[]{:S(2)}, u32[]{:S(2)}) collective-permute-start(bf16[5,32,128]{2,1,0:T(8,128)(2,1)S(1)} %get-tuple-element.46), channel_id=1, source_target_pairs={{0,2},{2,0},{4,6},{6,4},{8,10},{10,8},{12,14},{14,12},{1,3},{3,1},... | collective-permute-start | bytes 122888 | tf_op jit(solution)/shard_map/ppermute | solution.py:716
  13.7 1.2 %collective-permute-start.6 = (bf16[32,128]{1,0:T(8,128)(2,1)S(1)}, bf16[32,128]{1,0:T(8,128)(2,1)S(1)}, u32[]{:S(2)}, u32[]{:S(2)}) collective-permute-start(bf16[32,128]{1,0:T(8,128)(2,1)S(1)} %fusion), channel_id=1, source_target_pairs={{0,1},{1,0},{2,3},{3,2},{4,5},{5,4},{6,7},{7,6},{8,9},{9,8},{10,11... | collective-permute-start | bytes 24584 | tf_op jit(solution)/shard_map/ppermute | solution.py:764

commit v21 on v20

--- a/solution.py
+++ b/solution.py
@@ -465,10 +465,15 @@
     rows = [partial[e * seqs : (e + 1) * seqs] for e in range(residues)]
     turned = [pltpu.roll(row, LANES // 2, 1) for row in rows]
     low = lane_block(rows[0].shape, LANES // 2) == 0
-    return [
+    first = lane_block(rows[0].shape, residues) % 2 == 0
+    pieces = []
+    for block in (
         [jnp.where(low, rows[e], turned[e + 1]) for e in (0, 2)],
         [jnp.where(low, turned[e], rows[e + 1]) for e in (0, 2)],
-    ]
+    ):
+        pieces.append(jnp.where(first, block[0], pltpu.roll(block[1], residues, 1)))
+        pieces.append(jnp.where(first, pltpu.roll(block[0], LANES - residues, 1), block[1]))
+    return pieces
 
 
 def small_own_kernel(scale, own_ref, other_ref, w_ref, both_ref, spread_w_ref,
@@ -492,7 +497,8 @@
     shape = (columns_w_ref.shape[0], depth)
     row = lax.broadcasted_iota(jnp.int32, shape, 0)
     lane = lax.broadcasted_iota(jnp.int32, shape, 1)
-    chosen = jnp.where(lane == (row >> 3 & 7) * residues + (row >> 6), 1.0, 0.0).astype(BF16)
+    place = (row >> 3 & 7) * residues + 2 * (row >> 2 & 1) + (row >> 6)
+    chosen = jnp.where(lane == place, 1.0, 0.0).astype(BF16)
     columns_w_ref[...] = jnp.dot(
         chosen, spread_w_ref[LANES : LANES + depth, :], preferred_element_type=F32
     ).astype(BF16)
@@ -503,9 +509,8 @@
     other = other_ref[...].reshape(residues * columns, LANES)
     flat = outer_flat(scale, jnp.where(own_is_near, own, other), sorted_wt_ref)
     pieces = column_pieces(both_ref[0], outer_tiles(flat, residues), repeat_ref[...], residues)
-    for block in range(2):
-        for tile in range(2):
-            keep_ref[block, tile] = pieces[block][tile]
+    for place, piece in enumerate(pieces):
+        keep_ref[place] = piece
     outer_near_ref[...] = outer_rows(flat, residues, turn_refs[0])
     flat = outer_flat(scale, jnp.where(own_is_near, other, own), sorted_wt_ref)
     outer_far_ref[...] = outer_rows(flat, residues, turn_refs[1])
@@ -523,15 +528,11 @@
     own_is_near = lax.axis_index("seq") == lax.shift_right_logical(rank, 2)
     swap_ref[0] = jnp.where(own_is_near, got_ref[1], both_ref[1])
     swap_ref[1] = both_ref[0]
-    first = lax.shift_right_logical(rank & 3, 1)
-    for block in range(2):
-        distance = 2 * lax.bitwise_xor(first, block)
-        for tile in range(2):
-            total = keep_ref[block, tile] + pieces[block][tile]
-            keep_out_ref[distance, tile] = total
-            total = total.astype(BF16)
-            leaving_ref[distance, 2 + tile] = total
-            leaving_ref[distance + 1, 2 + tile] = total
+    for place, piece in enumerate(pieces):
+        distance = lax.bitwise_xor(rank & 3, place)
+        total = keep_ref[place] + piece
+        keep_out_ref[distance] = total
+        leaving_ref[distance, 2] = total.astype(BF16)
     for place in range(leaving_ref.shape[0]):
         leaving_ref[place, 0] = both_ref[1]
         leaving_ref[place, 1] = got_ref[1]
@@ -563,19 +564,18 @@
         axis=0,
     )
     left_cot = jnp.dot(right_all, outer, preferred_element_type=F32)
-    right_cot = []
-    for tile in range(2):
-        total = keep_ref[0, tile]
-        for part_ref in part_refs:
-            total = total + part_ref[2 + tile].astype(F32)
-        right_cot.append(total)
+    right_cot = keep_ref[0]
+    for part_ref in part_refs:
+        right_cot = right_cot + part_ref[2].astype(F32)
     blocks = lane_block((seqs, LANES), depth)
-    column = lane_block((seqs, LANES), 1) % 8 - residues * (rank & 1)
+    column = lane_block((seqs, LANES), 1) % residues
     spread = jnp.concatenate(
         [
             jnp.concatenate(
-                [jnp.where(blocks == place, left_cot, 0.0)]
-                + [jnp.where(column == place, cot, 0.0) for cot in right_cot],
+                [
+                    jnp.where(blocks == place, left_cot, 0.0),
+                    jnp.where(column == place, right_cot, 0.0),
+                ],
                 axis=1,
             )
             for place in range(residues)
@@ -608,8 +608,8 @@
     for mask, ref in enumerate(blocks_of):
         near_ref[mask] = ref[half]
     beyond_ref[0] = swapped_ref[0]
-    beyond_ref[1] = part_refs[0][4]
-    beyond_ref[2] = part_refs[1][4]
+    beyond_ref[1] = part_refs[0][3]
+    beyond_ref[2] = part_refs[1][3]
     beyond_ref[3] = swapped_late_ref[...]
     masks = [lax.bitwise_xor(here, place) for place in range(ranks)]
     right = jnp.concatenate(
@@ -726,13 +726,13 @@
         in_specs=[vmem] * 5,
         out_specs=[vmem] * 7,
         out_shape=(
-            like((2, 2, seqs, LANES), F32),
+            like((ranks // 2, seqs, LANES), F32),
             like((half_rows, LANES), BF16),
             like((half_rows, LANES), BF16),
             like(coupling_matrix.shape, BF16),
             like(coupling_matrix.shape[::-1], BF16),
             like((LANES, residues * LANES), BF16),
-            like((2 * LANES, features), BF16),
+            like((LANES, features), BF16),
         ),
         scratch_shapes=[
             [turn, turn],
@@ -747,8 +747,8 @@
         in_specs=[vmem] * 5,
         out_specs=[vmem] * 4,
         out_shape=(
-            like((ranks // 2, 4, seqs, LANES), BF16),
-            like((ranks // 2, 2, seqs, LANES), F32),
+            like((ranks // 2, 3, seqs, LANES), BF16),
+            like((ranks // 2, seqs, LANES), F32),
             like((2, seqs, LANES), BF16),
             like((2, seqs, LANES), BF16),
         ),

time: 17.6 us -> 17.6 us (level)
  transfers between devices with their start and end apart: 7 -> 7, of which waited for: 5 -> 5; matrix products, arithmetic and copies ran while one was open for 0% -> 0% of each run, Pallas kernels for 14% -> 15%
where the time goes in v21:
time: 17.6 us; the launch traced here: 17.4 us
  starting transfers between devices  8.81 us (50%)
  Pallas kernels  4.42 us (25%)
  waiting for transfers between devices  3.41 us (19%)
  between operations  0.72 us (4%)
    ppermute x4, starting transfers between devices, swap_over(): lax.ppermute(value, 'res', [(source, source ^ mask) for source in range(r...  8.22 us
    ppermute x4, waiting for transfers between devices, swap_over(): lax.ppermute(value, 'res', [(source, source ^ mask) for source in range(r...  2.24 us
    pallas_call x1, Pallas kernels, small_slice(): pl.pallas_call(functools.partial(small_finish_kernel, scale), in_specs=[v...  1.33 us
    pallas_call x1, Pallas kernels, small_slice(): pl.pallas_call(small_project_kernel, in_specs=[hbm] * 9, out_specs=[vmem]...  1.3 us
    pallas_call x1, Pallas kernels, small_slice(): pl.pallas_call(functools.partial(small_own_kernel, scale), in_specs=[vmem...  1.28 us
    ppermute x1, waiting for transfers between devices, small_slice(): lax.ppermute(jnp.where(own_is_near, diagonal[1], diagonal[0]), 'seq', swap)  1.17 us
    ppermute x1, starting transfers between devices, small_slice(): other_cot = lax.ppermute(coupling_cotangent, 'seq', swap)  0.52 us
    pallas_call x1, Pallas kernels, small_slice(): pl.pallas_call(functools.partial(small_partner_kernel, scale, residues),...  0.51 us
  transfers between devices with their start and end apart: 7, of which 5 were waited for; matrix products, arithmetic and copies ran while one was open for 0% of the time, Pallas kernels for 15%

profile of v21, /device:TPU:0, one launch (start us, length us, event | category | flops | bytes accessed | tf_op | source)
XLA Modules:
  0.0 17.4 jit_solution(14114022393489558345)
XLA Ops:
  0.6 0.0 copy-start
  0.6 0.5 %collective-permute-start = (bf16[4,16,128]{2,1,0:T(8,128)(2,1)}, bf16[4,16,128]{2,1,0:T(8,128)(2,1)S(1)}, u32[]{:S(2)}, u32[]{:S(2)}) collective-permute-start(bf16[4,16,128]{2,1,0:T(8,128)(2,1)} %cot_hbm.1), channel_id=1, source_target_pairs={{0,1},{1,0},{2,3},{3,2},{4,5},{5,4},{6,7},{7,6},{8,9},{9,8},{10,11... | collective-permute-start | bytes 49160 | tf_op jit(solution)/shard_map/ppermute | solution.py:670
  1.2 1.3 %project.1 = (bf16[2,32,128]{2,1,0:T(8,128)(2,1)S(1)}, f32[128,256]{1,0:T(8,128)S(1)}, f32[128,128]{1,0:T(8,128)S(1)}, bf16[256,256]{1,0:T(8,128)(2,1)S(1)}, f32...) custom-call(bf16[32,4,256]{2,1,0:T(4,128)(2,1)} %x_hbm.1, f32[1,256]{1,0:T(1,128)} %bitcast.19, ...), custom_call_target="tpu_custom_call" | custom-call | tf_op jit(solution)/shard_map/project/pallas_call | solution.py:673
  2.5 0.0 collective-permute-done.other_ref
  2.5 3.7 %collective-permute-start.1 = (bf16[4,32,128]{2,1,0:T(8,128)(2,1)S(1)}, bf16[4,32,128]{2,1,0:T(8,128)(2,1)S(1)}, u32[]{:S(2)}, u32[]{:S(2)}) collective-permute-start(bf16[4,32,128]{2,1,0:T(8,128)(2,1)S(1)} %pad_maximum_fusion.2), channel_id=1, source_target_pairs={{0,8},{2,10},{4,12},{6,14},{8,0},{10,2},{12,4},{14,6},{1,9},{3,11}... | collective-permute-start | bytes 98312 | tf_op jit(solution)/shard_map/ppermute | solution.py:716
  6.2 0.0 copy-done
  6.2 1.3 %own_pieces.1 = (f32[4,32,128]{2,1,0:T(8,128)S(1)}, bf16[512,128]{1,0:T(8,128)(2,1)S(1)}, bf16[512,128]{1,0:T(8,128)(2,1)S(1)}, bf16[1024,128]{1,0:T(8,128)(2,1)...) custom-call(bf16[4,16,128]{2,1,0:T(8,128)(2,1)S(1)} %get-tuple-element.23.own_ref, ...), custom_call_target="tpu_custom_call" | custom-call | tf_op jit(solution)/shard_map/own_pieces/pallas_call | solution.py:724
  7.5 0.7 %collective-permute-done.1.got_ref = bf16[4,32,128]{2,1,0:T(8,128)(2,1)S(1)} collective-permute-done((bf16[4,32,128]{2,1,0:T(8,128)(2,1)S(1)}, bf16[4,32,128]{2,1,0:T(8,128)(2,1)S(1)}, u32[]{:S(2)}, u32[]{:S(2)}) %collective-permute-start.1) | collective-permute-done | bytes 32800 | tf_op jit(solution)/shard_map/ppermute | solution.py:716
  8.2 0.5 %partner_pieces.1 = (bf16[4,3,32,128]{3,2,1,0:T(8,128)(2,1)S(1)}, f32[4,32,128]{2,1,0:T(8,128)S(1)}, bf16[2,32,128]{2,1,0:T(8,128)(2,1)S(1)}, bf16[2,32,128]{2,1,0:T(8,128)(2,1)S(1)}) custom-call(bf16[4,32,128]{2,1,0:T(8,128)(2,1)S(1)} %collective-permute-done.1.got_ref, bf16[128,1024]{1,0:T(8,128)(2,1)S(1)} %get-tuple-element.25.sorted_wt_ref, ...), custom_call_target="tpu_custom_call" | custom-call | tf_op jit(solution)/shard_map/partner_pieces/pallas_call | solution.py:745
  8.7 0.1 collective-permute-start.2
  8.8 2.8 %collective-permute-start.5 = (bf16[3,32,128]{2,1,0:T(8,128)(2,1)S(1)}, bf16[3,32,128]{2,1,0:T(8,128)(2,1)S(1)}, u32[]{:S(2)}, u32[]{:S(2)}) collective-permute-start(bf16[3,32,128]{2,1,0:T(8,128)(2,1)S(1)} %get-tuple-element.42), channel_id=1, source_target_pairs={{0,6},{2,4},{4,2},{6,0},{8,14},{10,12},{12,10},{14,8},{1,7},{3,5},... | collective-permute-start | bytes 73736 | tf_op jit(solution)/shard_map/ppermute | solution.py:716
  11.6 0.0 collective-permute-done.2.swapped_ref
  11.6 0.5 %collective-permute-start.4 = (bf16[4,32,128]{2,1,0:T(8,128)(2,1)S(1)}, bf16[4,32,128]{2,1,0:T(8,128)(2,1)S(1)}, u32[]{:S(2)}, u32[]{:S(2)}) collective-permute-start(bf16[4,32,128]{2,1,0:T(8,128)(2,1)S(1)} %get-tuple-element.45), channel_id=1, source_target_pairs={{0,4},{2,6},{4,0},{6,2},{8,12},{10,14},{12,8},{14,10},{1,5},{3,7},... | collective-permute-start | bytes 98312 | tf_op jit(solution)/shard_map/ppermute | solution.py:716
  12.2 1.2 %collective-permute-start.3 = (bf16[4,32,128]{2,1,0:T(8,128)(2,1)S(1)}, bf16[4,32,128]{2,1,0:T(8,128)(2,1)S(1)}, u32[]{:S(2)}, u32[]{:S(2)}) collective-permute-start(bf16[4,32,128]{2,1,0:T(8,128)(2,1)S(1)} %get-tuple-element.46), channel_id=1, source_target_pairs={{0,2},{2,0},{4,6},{6,4},{8,10},{10,8},{12,14},{14,12},{1,3},{3,1},... | collective-permute-start | bytes 98312 | tf_op jit(solution)/shard_map/ppermute | solution.py:716
  13.4 0.3 %collective-permute-done.5.part_refs_2_ = bf16[3,32,128]{2,1,0:T(8,128)(2,1)S(1)} collective-permute-done((bf16[3,32,128]{2,1,0:T(8,128)(2,1)S(1)}, bf16[3,32,128]{2,1,0:T(8,128)(2,1)S(1)}, u32[]{:S(2)}, u32[]{:S(2)}) %collective-permute-start.5) | collective-permute-done | bytes 24608 | tf_op jit(solution)/shard_map/ppermute | solution.py:716
  13.6 0.0 collective-permute-start.6
  13.6 1.2 %collective-permute-done.6.swapped_late_ref = bf16[32,128]{1,0:T(8,128)(2,1)S(1)} collective-permute-done((bf16[32,128]{1,0:T(8,128)(2,1)S(1)}, bf16[32,128]{1,0:T(8,128)(2,1)S(1)}, u32[]{:S(2)}, u32[]{:S(2)}) %collective-permute-start.6) | collective-permute-done | bytes 8224 | tf_op jit(solution)/shard_map/ppermute | solution.py:764
  14.8 0.8 %collective-permute-done.4.part_refs_1_ = bf16[4,32,128]{2,1,0:T(8,128)(2,1)S(1)} collective-permute-done((bf16[4,32,128]{2,1,0:T(8,128)(2,1)S(1)}, bf16[4,32,128]{2,1,0:T(8,128)(2,1)S(1)}, u32[]{:S(2)}, u32[]{:S(2)}) %collective-permute-start.4) | collective-permute-done | bytes 32800 | tf_op jit(solution)/shard_map/ppermute | solution.py:716
  15.6 0.4 %collective-permute-done.3.part_refs_0_ = bf16[4,32,128]{2,1,0:T(8,128)(2,1)S(1)} collective-permute-done((bf16[4,32,128]{2,1,0:T(8,128)(2,1)S(1)}, bf16[4,32,128]{2,1,0:T(8,128)(2,1)S(1)}, u32[]{:S(2)}, u32[]{:S(2)}) %collective-permute-start.3) | collective-permute-done | bytes 32800 | tf_op jit(solution)/shard_map/ppermute | solution.py:716
  16.1 1.3 %finish.1 = (bf16[32,4,256]{2,1,0:T(4,128)(2,1)}, bf16[4,16,128]{2,1,0:T(8,128)(2,1)}) custom-call(bf16[2,32,128]{2,1,0:T(8,128)(2,1)S(1)} %get-tuple-element.28.right_ref, bf16[4,32,128]{2,1,0:T(8,128)(2,1)S(1)} %collective-permute-done.3.part_refs_0_, bf16[4,32,128]{2,1,0:T(8,128)(2,1)S(1)} %collective-permute-done.4.part_refs_1_, ...), custom_call_target="tpu_custom_call" | custom-call | tf_op jit(solution)/shard_map/finish/pallas_call | solution.py:768
  (6 shorter events, 0.0 us)
Async XLA Ops:
  0.6 5.6 %copy-start = (bf16[1024,128]{1,0:T(8,128)(2,1)S(1)}, bf16[1024,128]{1,0:T(8,128)(2,1)}, u32[]{:S(2)}) copy-start(bf16[1024,128]{1,0:T(8,128)(2,1)} %w_ref.1) | copy-start | bytes 786436
  0.6 1.8 %collective-permute-start = (bf16[4,16,128]{2,1,0:T(8,128)(2,1)}, bf16[4,16,128]{2,1,0:T(8,128)(2,1)S(1)}, u32[]{:S(2)}, u32[]{:S(2)}) collective-permute-start(bf16[4,16,128]{2,1,0:T(8,128)(2,1)} %cot_hbm.1), channel_id=1, source_target_pairs={{0,1},{1,0},{2,3},{3,2},{4,5},{5,4},{6,7},{7,6},{8,9},{9,8},{10,11... | collective-permute-start | bytes 49160 | tf_op jit(solution)/shard_map/ppermute | solution.py:670
  2.5 5.7 %collective-permute-start.1 = (bf16[4,32,128]{2,1,0:T(8,128)(2,1)S(1)}, bf16[4,32,128]{2,1,0:T(8,128)(2,1)S(1)}, u32[]{:S(2)}, u32[]{:S(2)}) collective-permute-start(bf16[4,32,128]{2,1,0:T(8,128)(2,1)S(1)} %pad_maximum_fusion.2), channel_id=1, source_target_pairs={{0,8},{2,10},{4,12},{6,14},{8,0},{10,2},{12,4},{14,6},{1,9},{3,11}... | collective-permute-start | bytes 98312 | tf_op jit(solution)/shard_map/ppermute | solution.py:716
  8.7 2.9 %collective-permute-start.2 = (bf16[2,32,128]{2,1,0:T(8,128)(2,1)S(1)}, bf16[2,32,128]{2,1,0:T(8,128)(2,1)S(1)}, u32[]{:S(2)}, u32[]{:S(2)}) collective-permute-start(bf16[2,32,128]{2,1,0:T(8,128)(2,1)S(1)} %get-tuple-element.30), channel_id=1, source_target_pairs={{0,1},{1,0},{2,3},{3,2},{4,5},{5,4},{6,7},{7,6},{8,9},{9,8},{10,11... | collective-permute-start | bytes 49160 | tf_op jit(solution)/shard_map/ppermute | solution.py:759
  8.8 4.8 %collective-permute-start.5 = (bf16[3,32,128]{2,1,0:T(8,128)(2,1)S(1)}, bf16[3,32,128]{2,1,0:T(8,128)(2,1)S(1)}, u32[]{:S(2)}, u32[]{:S(2)}) collective-permute-start(bf16[3,32,128]{2,1,0:T(8,128)(2,1)S(1)} %get-tuple-element.42), channel_id=1, source_target_pairs={{0,6},{2,4},{4,2},{6,0},{8,14},{10,12},{12,10},{14,8},{1,7},{3,5},... | collective-permute-start | bytes 73736 | tf_op jit(solution)/shard_map/ppermute | solution.py:716
  11.6 4.0 %collective-permute-start.4 = (bf16[4,32,128]{2,1,0:T(8,128)(2,1)S(1)}, bf16[4,32,128]{2,1,0:T(8,128)(2,1)S(1)}, u32[]{:S(2)}, u32[]{:S(2)}) collective-permute-start(bf16[4,32,128]{2,1,0:T(8,128)(2,1)S(1)} %get-tuple-element.45), channel_id=1, source_target_pairs={{0,4},{2,6},{4,0},{6,2},{8,12},{10,14},{12,8},{14,10},{1,5},{3,7},... | collective-permute-start | bytes 98312 | tf_op jit(solution)/shard_map/ppermute | solution.py:716
  12.2 3.9 %collective-permute-start.3 = (bf16[4,32,128]{2,1,0:T(8,128)(2,1)S(1)}, bf16[4,32,128]{2,1,0:T(8,128)(2,1)S(1)}, u32[]{:S(2)}, u32[]{:S(2)}) collective-permute-start(bf16[4,32,128]{2,1,0:T(8,128)(2,1)S(1)} %get-tuple-element.46), channel_id=1, source_target_pairs={{0,2},{2,0},{4,6},{6,4},{8,10},{10,8},{12,14},{14,12},{1,3},{3,1},... | collective-permute-start | bytes 98312 | tf_op jit(solution)/shard_map/ppermute | solution.py:716
  13.6 1.2 %collective-permute-start.6 = (bf16[32,128]{1,0:T(8,128)(2,1)S(1)}, bf16[32,128]{1,0:T(8,128)(2,1)S(1)}, u32[]{:S(2)}, u32[]{:S(2)}) collective-permute-start(bf16[32,128]{1,0:T(8,128)(2,1)S(1)} %fusion), channel_id=1, source_target_pairs={{0,1},{1,0},{2,3},{3,2},{4,5},{5,4},{6,7},{7,6},{8,9},{9,8},{10,11... | collective-permute-start | bytes 24584 | tf_op jit(solution)/shard_map/ppermute | solution.py:764

commit v22 on v21

--- a/solution.py
+++ b/solution.py
@@ -538,33 +538,89 @@
         leaving_ref[place, 1] = got_ref[1]
 
 
+def pair_rows(scale, right, left, residues, sorted_w_ref, turn_ref):
+    depth = LANES // residues
+    columns = right.shape[1] // depth
+    turn_ref[0 : columns * depth, :] = (
+        lax.dot_general(right, left, TN, preferred_element_type=F32) * scale
+    )
+    tiles = []
+    for tile in range(depth * depth // LANES):
+        turned = exchange_blocks(
+            [
+                turn_ref[pl.ds(tile * residues + e, columns, stride=depth), :]
+                for e in range(residues)
+            ],
+            depth,
+        )
+        tiles.append(jnp.concatenate(turned, axis=0))
+    flat = jnp.concatenate(tiles, axis=1)
+    rows = residues * columns
+    parts = jnp.concatenate(split_two(flat), axis=0)
+    pair = jnp.dot(parts, sorted_w_ref[...], preferred_element_type=F32)
+    return pair[0:rows] + pair[rows : 2 * rows]
+
+
+def store_pairs(pair, spots, residues, pair_ref):
+    columns = pair.shape[0] // residues // len(spots)
+    for i in range(residues):
+        for place, spot in enumerate(spots):
+            start = (i * len(spots) + place) * columns
+            pair_ref[spot, i * columns : (i + 1) * columns, :] = pair[start : start + columns]
+
+
+def left_share(block_refs, masks, outer_near_ref, outer_far_ref):
+    here = lax.axis_index("res") & 3
+    spots = [
+        pl.ds(pl.multiple_of(lax.bitwise_xor(here, mask) * LANES, LANES), LANES) for mask in masks
+    ]
+    right = jnp.concatenate([ref[0] for ref in block_refs] + [ref[1] for ref in block_refs], axis=1)
+    outer = jnp.concatenate(
+        [outer_near_ref[spot, :] for spot in spots] + [outer_far_ref[spot, :] for spot in spots],
+        axis=0,
+    )
+    return jnp.dot(right, outer, preferred_element_type=F32)
+
+
+def own_half():
+    near = lax.axis_index("seq") == lax.shift_right_logical(lax.axis_index("res"), 2)
+    return jnp.where(near, 0, 1)
+
+
+def small_early_kernel(
+    scale, right_ref, part_ref, swapped_ref, swapped_late_ref, both_ref, outer_near_ref, outer_far_ref,
+    keep_ref, sorted_w_ref,
+    pair_ref, left_cot_ref, right_cot_ref, turn_ref,
+):
+    residues = pair_ref.shape[1] // 4
+    left_cot_ref[...] = left_share([right_ref, part_ref], (0, 3), outer_near_ref, outer_far_ref)
+    right_cot_ref[...] = keep_ref[0] + part_ref[2].astype(F32)
+    half = own_half()
+    right = jnp.concatenate(
+        [
+            jnp.concatenate([right_ref[half], part_ref[half]], axis=1),
+            jnp.concatenate([swapped_ref[0], swapped_late_ref[...]], axis=1),
+        ],
+        axis=0,
+    )
+    left = jnp.concatenate([both_ref[0], swapped_ref[1]], axis=0)
+    pair = pair_rows(scale, right, left, residues, sorted_w_ref, turn_ref)
+    store_pairs(pair, (0, 1), residues, pair_ref)
+
+
 def small_finish_kernel(
-    scale, right_ref, part_refs, swapped_ref, swapped_late_ref, both_ref, outer_near_ref, outer_far_ref,
-    keep_ref, normed_ref, inv_std_ref, gain_ref, spread_w_ref, columns_w_ref, sorted_w_ref, offset_ref,
-    grad_hbm, pair_hbm, grad_ref, pair_ref, near_ref, beyond_ref, turn_ref, lines_ref, semaphores,
+    scale, part_refs, swapped_ref, both_ref, outer_near_ref, outer_far_ref, early_pair_ref,
+    early_left_ref, early_right_ref, normed_ref, inv_std_ref, gain_ref, spread_w_ref, columns_w_ref,
+    sorted_w_ref, offset_ref, grad_hbm, pair_hbm, grad_ref, pair_ref, pairs_ref, turn_ref, lines_ref,
+    semaphores,
 ):
     seqs, residues, _ = grad_ref.shape
     columns = pair_ref.shape[1]
     depth = LANES // residues
     ranks = columns // residues
-    rank = lax.axis_index("res")
-    mine = lax.axis_index("seq")
-    here = rank & 3
-
-    blocks_of = [right_ref] + list(part_refs)
-    right_all = jnp.concatenate(
-        [ref[0] for ref in blocks_of] + [ref[1] for ref in blocks_of], axis=1
-    )
-    spots = [
-        pl.ds(pl.multiple_of(lax.bitwise_xor(here, mask) * LANES, LANES), LANES)
-        for mask in range(ranks)
-    ]
-    outer = jnp.concatenate(
-        [outer_near_ref[spot, :] for spot in spots] + [outer_far_ref[spot, :] for spot in spots],
-        axis=0,
-    )
-    left_cot = jnp.dot(right_all, outer, preferred_element_type=F32)
-    right_cot = keep_ref[0]
+
+    left_cot = early_left_ref[...] + left_share(part_refs, (1, 2), outer_near_ref, outer_far_ref)
+    right_cot = early_right_ref[...]
     for part_ref in part_refs:
         right_cot = right_cot + part_ref[2].astype(F32)
     blocks = lane_block((seqs, LANES), depth)
@@ -593,54 +649,44 @@
             lines_ref[tile, pl.ds(place, seqs, stride=residues), :] = ln_cot[
                 place * seqs : (place + 1) * seqs, tile * LANES : (tile + 1) * LANES
             ]
-    gained = jnp.concatenate([lines_ref[tile, 0:rows, :] for tile in tiles], axis=1) * gain_ref[...]
-    normed = normed_ref[...]
-    grad = inv_std_ref[:, 0:1] * (
-        gained
-        - jnp.mean(gained, axis=-1, keepdims=True)
-        - normed * jnp.mean(gained * normed, axis=-1, keepdims=True)
-    )
-    grad_ref[...] = grad.reshape(grad_ref.shape).astype(BF16)
-    grad_copy = pltpu.make_async_copy(grad_ref, grad_hbm, semaphores.at[0])
-    grad_copy.start()
-
-    half = jnp.where(mine == lax.shift_right_logical(rank, 2), 0, 1)
-    for mask, ref in enumerate(blocks_of):
-        near_ref[mask] = ref[half]
-    beyond_ref[0] = swapped_ref[0]
-    beyond_ref[1] = part_refs[0][3]
-    beyond_ref[2] = part_refs[1][3]
-    beyond_ref[3] = swapped_late_ref[...]
-    masks = [lax.bitwise_xor(here, place) for place in range(ranks)]
+    copies = []
+    for half in range(2):
+        some = pl.ds(half * rows // 2, rows // 2)
+        gained = jnp.concatenate([lines_ref[tile, some, :] for tile in tiles], axis=1) * gain_ref[...]
+        normed = normed_ref[some, :]
+        grad = inv_std_ref[some, 0:1] * (
+            gained
+            - jnp.mean(gained, axis=-1, keepdims=True)
+            - normed * jnp.mean(gained * normed, axis=-1, keepdims=True)
+        )
+        some = pl.ds(half * seqs // 2, seqs // 2)
+        grad_ref[some] = grad.reshape(seqs // 2, residues, grad.shape[1]).astype(BF16)
+        copy = pltpu.make_async_copy(grad_ref.at[some], grad_hbm.at[some], semaphores.at[half])
+        copy.start()
+        copies.append(copy)
+
+    half = own_half()
     right = jnp.concatenate(
         [
-            jnp.concatenate([ref[mask] for mask in masks], axis=1)
-            for ref in (near_ref, beyond_ref)
+            jnp.concatenate([ref[half] for ref in part_refs], axis=1),
+            jnp.concatenate([ref[3] for ref in part_refs], axis=1),
         ],
         axis=0,
     )
     left = jnp.concatenate([both_ref[0], swapped_ref[1]], axis=0)
-    turn_ref[0 : columns * depth, :] = lax.dot_general(right, left, TN, preferred_element_type=F32) * scale
-    tiles = []
-    for tile in range(depth * depth // LANES):
-        turned = exchange_blocks(
-            [
-                turn_ref[pl.ds(tile * residues + e, columns, stride=depth), :]
-                for e in range(residues)
-            ],
-            depth,
-        )
-        tiles.append(jnp.concatenate(turned, axis=0))
-    flat = jnp.concatenate(tiles, axis=1)
-    rows = residues * columns
-    parts = jnp.concatenate(split_two(flat), axis=0)
-    pair = jnp.dot(parts, sorted_w_ref[...], preferred_element_type=F32)
-    pair = pair[0:rows] + pair[rows : 2 * rows]
-    pair_ref[...] = (pair + offset_ref[...]).astype(BF16).reshape(pair_ref.shape)
-    pair_copy = pltpu.make_async_copy(pair_ref, pair_hbm, semaphores.at[1])
-    pair_copy.start()
-    grad_copy.wait()
-    pair_copy.wait()
+    pair = pair_rows(scale, right, left, residues, sorted_w_ref, turn_ref)
+    pairs_ref[0] = early_pair_ref[0]
+    pairs_ref[3] = early_pair_ref[1]
+    store_pairs(pair, (1, 2), residues, pairs_ref)
+    here = lax.axis_index("res") & 3
+    placed = [pairs_ref[lax.bitwise_xor(here, place)] for place in range(ranks)]
+    for i in range(residues):
+        own = [block[i * residues : (i + 1) * residues] for block in placed]
+        pair_ref[i] = (jnp.concatenate(own, axis=0) + offset_ref[...]).astype(BF16)
+    copy = pltpu.make_async_copy(pair_ref, pair_hbm, semaphores.at[2])
+    copy.start()
+    for copy in copies + [copy]:
+        copy.wait()
 
 
 def small_slice(
@@ -765,9 +811,24 @@
         jnp.where(own_is_near, diagonal[1], diagonal[0]), "seq", swap
     )
 
-    pair_delta, gradient = pl.pallas_call(
+    pair_turn = pltpu.VMEM((2 * LANES + depth, LANES), F32)
+    early_pair, early_left, early_right = pl.pallas_call(
+        functools.partial(small_early_kernel, scale),
+        in_specs=[vmem] * 9,
+        out_specs=[vmem] * 3,
+        out_shape=(
+            like((2, residues * residues, LANES), F32),
+            like((seqs, LANES), F32),
+            like((seqs, LANES), F32),
+        ),
+        scratch_shapes=[pair_turn],
+        compiler_params=limit,
+        name="early",
+    )(right, diagonal, swapped, swapped_late, both, outer_near, outer_far, keep, sorted_w)
+
+    gradient, pair_delta = pl.pallas_call(
         functools.partial(small_finish_kernel, scale),
-        in_specs=[vmem, [vmem] * 3] + [vmem] * 13,
+        in_specs=[[vmem] * 2] + [vmem] * 14,
         out_specs=[pl.BlockSpec(memory_space=pl.ANY)] * 2,
         out_shape=(
             like(homolog_matrix.shape, BF16),
@@ -776,23 +837,22 @@
         scratch_shapes=[
             pltpu.VMEM(homolog_matrix.shape, BF16),
             pltpu.VMEM(coupling_cotangent.shape, BF16),
-            pltpu.VMEM((ranks // 2, seqs, LANES), BF16),
-            pltpu.VMEM((ranks // 2, seqs, LANES), BF16),
-            turn,
+            pltpu.VMEM((ranks // 2, residues * residues, LANES), F32),
+            pair_turn,
             pltpu.VMEM((features // LANES, rows + 8, LANES), F32),
-            pltpu.SemaphoreType.DMA((2,)),
+            pltpu.SemaphoreType.DMA((3,)),
         ],
         compiler_params=limit,
         name="finish",
     )(
-        right,
-        [beside, across, diagonal],
+        [beside, across],
         swapped,
-        swapped_late,
         both,
         outer_near,
         outer_far,
-        keep,
+        early_pair,
+        early_left,
+        early_right,
         normed,
         inv_std,
         gain,
@@ -800,7 +860,7 @@
         columns_w,
         sorted_w,
         pair_offset,
-    )[::-1]
+    )
     return (pair_delta, gradient)
 
 

time: 17.6 us -> 17.6 us (level)
  Pallas kernels: 4.42 us -> 5 us
  waiting for transfers between devices: 3.41 us -> 2.86 us
    pallas_call x1 -> x2, Pallas kernels: 1.33 us -> 1.9 us  [the longest x1 1.35 us: small_slice(): pl.pallas_call(functools.partial(small_finish_kernel, scale), in_specs=[[...]
    ppermute x4, waiting for transfers between devices: 2.24 us -> 1.68 us  [swap_over(): lax.ppermute(value, 'res', [(source, source ^ mask) for source in range(r...]
  transfers between devices with their start and end apart: 7 -> 7, of which waited for: 5 -> 5; matrix products, arithmetic and copies ran while one was open for 0% -> 0% of each run, Pallas kernels for 15% -> 18%
where the time goes in v22:
time: 17.6 us; the launch traced here: 17.4 us
  starting transfers between devices  8.81 us (50%)
  Pallas kernels  5 us (28%)
  waiting for transfers between devices  2.86 us (16%)
  between operations  0.72 us (4%)
    ppermute x4, starting transfers between devices, swap_over(): lax.ppermute(value, 'res', [(source, source ^ mask) for source in range(r...  8.22 us
    ppermute x4, waiting for transfers between devices, swap_over(): lax.ppermute(value, 'res', [(source, source ^ mask) for source in range(r...  1.68 us
    pallas_call x1, Pallas kernels, small_slice(): pl.pallas_call(functools.partial(small_finish_kernel, scale), in_specs=[[...  1.35 us
    pallas_call x1, Pallas kernels, small_slice(): pl.pallas_call(small_project_kernel, in_specs=[hbm] * 9, out_specs=[vmem]...  1.3 us
    pallas_call x1, Pallas kernels, small_slice(): pl.pallas_call(functools.partial(small_own_kernel, scale), in_specs=[vmem...  1.28 us
    ppermute x1, waiting for transfers between devices, small_slice(): lax.ppermute(jnp.where(own_is_near, diagonal[1], diagonal[0]), 'seq', swap)  1.17 us
    pallas_call x1, Pallas kernels, small_slice(): pl.pallas_call(functools.partial(small_early_kernel, scale), in_specs=[vm...  0.55 us
    ppermute x1, starting transfers between devices, small_slice(): other_cot = lax.ppermute(coupling_cotangent, 'seq', swap)  0.52 us
  transfers between devices with their start and end apart: 7, of which 5 were waited for; matrix products, arithmetic and copies ran while one was open for 0% of the time, Pallas kernels for 18%

profile of v22, /device:TPU:0, one launch (start us, length us, event | category | flops | bytes accessed | tf_op | source)
XLA Modules:
  0.0 17.4 jit_solution(6315069407965796038)
XLA Ops:
  0.6 0.0 copy-start
  0.6 0.5 %collective-permute-start = (bf16[4,16,128]{2,1,0:T(8,128)(2,1)}, bf16[4,16,128]{2,1,0:T(8,128)(2,1)S(1)}, u32[]{:S(2)}, u32[]{:S(2)}) collective-permute-start(bf16[4,16,128]{2,1,0:T(8,128)(2,1)} %cot_hbm.1), channel_id=1, source_target_pairs={{0,1},{1,0},{2,3},{3,2},{4,5},{5,4},{6,7},{7,6},{8,9},{9,8},{10,11... | collective-permute-start | bytes 49160 | tf_op jit(solution)/shard_map/ppermute | solution.py:716
  1.2 1.3 %project.1 = (bf16[2,32,128]{2,1,0:T(8,128)(2,1)S(1)}, f32[128,256]{1,0:T(8,128)S(1)}, f32[128,128]{1,0:T(8,128)S(1)}, bf16[256,256]{1,0:T(8,128)(2,1)S(1)}, f32...) custom-call(bf16[32,4,256]{2,1,0:T(4,128)(2,1)} %x_hbm.1, f32[1,256]{1,0:T(1,128)} %bitcast.19, ...), custom_call_target="tpu_custom_call" | custom-call | tf_op jit(solution)/shard_map/project/pallas_call | solution.py:719
  2.5 0.0 collective-permute-done.other_ref
  2.5 3.7 %collective-permute-start.1 = (bf16[4,32,128]{2,1,0:T(8,128)(2,1)S(1)}, bf16[4,32,128]{2,1,0:T(8,128)(2,1)S(1)}, u32[]{:S(2)}, u32[]{:S(2)}) collective-permute-start(bf16[4,32,128]{2,1,0:T(8,128)(2,1)S(1)} %pad_maximum_fusion.2), channel_id=1, source_target_pairs={{0,8},{2,10},{4,12},{6,14},{8,0},{10,2},{12,4},{14,6},{1,9},{3,11}... | collective-permute-start | bytes 98312 | tf_op jit(solution)/shard_map/ppermute | solution.py:762
  6.2 0.0 copy-done
  6.2 1.3 %own_pieces.1 = (f32[4,32,128]{2,1,0:T(8,128)S(1)}, bf16[512,128]{1,0:T(8,128)(2,1)S(1)}, bf16[512,128]{1,0:T(8,128)(2,1)S(1)}, bf16[1024,128]{1,0:T(8,128)(2,1)...) custom-call(bf16[4,16,128]{2,1,0:T(8,128)(2,1)S(1)} %get-tuple-element.26.own_ref, ...), custom_call_target="tpu_custom_call" | custom-call | tf_op jit(solution)/shard_map/own_pieces/pallas_call | solution.py:770
  7.5 0.7 %collective-permute-done.1.got_ref = bf16[4,32,128]{2,1,0:T(8,128)(2,1)S(1)} collective-permute-done((bf16[4,32,128]{2,1,0:T(8,128)(2,1)S(1)}, bf16[4,32,128]{2,1,0:T(8,128)(2,1)S(1)}, u32[]{:S(2)}, u32[]{:S(2)}) %collective-permute-start.1) | collective-permute-done | bytes 32800 | tf_op jit(solution)/shard_map/ppermute | solution.py:762
  8.2 0.5 %partner_pieces.1 = (bf16[4,3,32,128]{3,2,1,0:T(8,128)(2,1)S(1)}, f32[4,32,128]{2,1,0:T(8,128)S(1)}, bf16[2,32,128]{2,1,0:T(8,128)(2,1)S(1)}, bf16[2,32,128]{2,1,0:T(8,128)(2,1)S(1)}) custom-call(bf16[4,32,128]{2,1,0:T(8,128)(2,1)S(1)} %collective-permute-done.1.got_ref, bf16[128,1024]{1,0:T(8,128)(2,1)S(1)} %get-tuple-element.28.sorted_wt_ref, ...), custom_call_target="tpu_custom_call" | custom-call | tf_op jit(solution)/shard_map/partner_pieces/pallas_call | solution.py:791
  8.7 0.1 collective-permute-start.2
  8.8 2.8 %collective-permute-start.5 = (bf16[3,32,128]{2,1,0:T(8,128)(2,1)S(1)}, bf16[3,32,128]{2,1,0:T(8,128)(2,1)S(1)}, u32[]{:S(2)}, u32[]{:S(2)}) collective-permute-start(bf16[3,32,128]{2,1,0:T(8,128)(2,1)S(1)} %get-tuple-element.48), channel_id=1, source_target_pairs={{0,6},{2,4},{4,2},{6,0},{8,14},{10,12},{12,10},{14,8},{1,7},{3,5},... | collective-permute-start | bytes 73736 | tf_op jit(solution)/shard_map/ppermute | solution.py:762
  11.6 0.0 collective-permute-done.2.swapped_ref
  11.6 0.5 %collective-permute-start.4 = (bf16[4,32,128]{2,1,0:T(8,128)(2,1)S(1)}, bf16[4,32,128]{2,1,0:T(8,128)(2,1)S(1)}, u32[]{:S(2)}, u32[]{:S(2)}) collective-permute-start(bf16[4,32,128]{2,1,0:T(8,128)(2,1)S(1)} %get-tuple-element.51), channel_id=1, source_target_pairs={{0,4},{2,6},{4,0},{6,2},{8,12},{10,14},{12,8},{14,10},{1,5},{3,7},... | collective-permute-start | bytes 98312 | tf_op jit(solution)/shard_map/ppermute | solution.py:762
  12.2 1.2 %collective-permute-start.3 = (bf16[4,32,128]{2,1,0:T(8,128)(2,1)S(1)}, bf16[4,32,128]{2,1,0:T(8,128)(2,1)S(1)}, u32[]{:S(2)}, u32[]{:S(2)}) collective-permute-start(bf16[4,32,128]{2,1,0:T(8,128)(2,1)S(1)} %get-tuple-element.52), channel_id=1, source_target_pairs={{0,2},{2,0},{4,6},{6,4},{8,10},{10,8},{12,14},{14,12},{1,3},{3,1},... | collective-permute-start | bytes 98312 | tf_op jit(solution)/shard_map/ppermute | solution.py:762
  13.4 0.3 %collective-permute-done.5.part_ref = bf16[3,32,128]{2,1,0:T(8,128)(2,1)S(1)} collective-permute-done((bf16[3,32,128]{2,1,0:T(8,128)(2,1)S(1)}, bf16[3,32,128]{2,1,0:T(8,128)(2,1)S(1)}, u32[]{:S(2)}, u32[]{:S(2)}) %collective-permute-start.5) | collective-permute-done | bytes 24608 | tf_op jit(solution)/shard_map/ppermute | solution.py:762
  13.6 0.0 collective-permute-start.6
  13.6 1.2 %collective-permute-done.6.swapped_late_ref = bf16[32,128]{1,0:T(8,128)(2,1)S(1)} collective-permute-done((bf16[32,128]{1,0:T(8,128)(2,1)S(1)}, bf16[32,128]{1,0:T(8,128)(2,1)S(1)}, u32[]{:S(2)}, u32[]{:S(2)}) %collective-permute-start.6) | collective-permute-done | bytes 8224 | tf_op jit(solution)/shard_map/ppermute | solution.py:810
  14.8 0.6 %early.1 = (f32[2,16,128]{2,1,0:T(8,128)S(1)}, f32[32,128]{1,0:T(8,128)S(1)}, f32[32,128]{1,0:T(8,128)S(1)}) custom-call(bf16[2,32,128]{2,1,0:T(8,128)(2,1)S(1)} %get-tuple-element.35.right_ref, bf16[3,32,128]{2,1,0:T(8,128)(2,1)S(1)} %collective-permute-done.5.part_ref, bf16[2,32,128]{2,1,0:T(8,128)(2,1)S(1)} %collective-permute-done.2.swapped_ref, ...), custom_call_target="tpu_custom_call" | custom-call | tf_op jit(solution)/shard_map/early/pallas_call | solution.py:815
  15.4 0.3 %collective-permute-done.4.part_refs_1_ = bf16[4,32,128]{2,1,0:T(8,128)(2,1)S(1)} collective-permute-done((bf16[4,32,128]{2,1,0:T(8,128)(2,1)S(1)}, bf16[4,32,128]{2,1,0:T(8,128)(2,1)S(1)}, u32[]{:S(2)}, u32[]{:S(2)}) %collective-permute-start.4) | collective-permute-done | bytes 32800 | tf_op jit(solution)/shard_map/ppermute | solution.py:762
  15.6 0.4 %collective-permute-done.3.part_refs_0_ = bf16[4,32,128]{2,1,0:T(8,128)(2,1)S(1)} collective-permute-done((bf16[4,32,128]{2,1,0:T(8,128)(2,1)S(1)}, bf16[4,32,128]{2,1,0:T(8,128)(2,1)S(1)}, u32[]{:S(2)}, u32[]{:S(2)}) %collective-permute-start.3) | collective-permute-done | bytes 32800 | tf_op jit(solution)/shard_map/ppermute | solution.py:762
  16.1 1.3 %finish.1 = (bf16[32,4,256]{2,1,0:T(4,128)(2,1)}, bf16[4,16,128]{2,1,0:T(8,128)(2,1)}) custom-call(bf16[4,32,128]{2,1,0:T(8,128)(2,1)S(1)} %collective-permute-done.3.part_refs_0_, bf16[4,32,128]{2,1,0:T(8,128)(2,1)S(1)} %collective-permute-done.4.part_refs_1_, bf16[2,32,128]{2,1,0:T(8,128)(2,1)S(1)} %collective-permute-done.2.swapped_ref, ...), custom_call_target="tpu_custom_call" | custom-call | tf_op jit(solution)/shard_map/finish/pallas_call | solution.py:829
  (6 shorter events, 0.0 us)
Async XLA Ops:
  0.6 5.6 %copy-start = (bf16[1024,128]{1,0:T(8,128)(2,1)S(1)}, bf16[1024,128]{1,0:T(8,128)(2,1)}, u32[]{:S(2)}) copy-start(bf16[1024,128]{1,0:T(8,128)(2,1)} %w_ref.1) | copy-start | bytes 786436
  0.6 1.8 %collective-permute-start = (bf16[4,16,128]{2,1,0:T(8,128)(2,1)}, bf16[4,16,128]{2,1,0:T(8,128)(2,1)S(1)}, u32[]{:S(2)}, u32[]{:S(2)}) collective-permute-start(bf16[4,16,128]{2,1,0:T(8,128)(2,1)} %cot_hbm.1), channel_id=1, source_target_pairs={{0,1},{1,0},{2,3},{3,2},{4,5},{5,4},{6,7},{7,6},{8,9},{9,8},{10,11... | collective-permute-start | bytes 49160 | tf_op jit(solution)/shard_map/ppermute | solution.py:716
  2.5 5.7 %collective-permute-start.1 = (bf16[4,32,128]{2,1,0:T(8,128)(2,1)S(1)}, bf16[4,32,128]{2,1,0:T(8,128)(2,1)S(1)}, u32[]{:S(2)}, u32[]{:S(2)}) collective-permute-start(bf16[4,32,128]{2,1,0:T(8,128)(2,1)S(1)} %pad_maximum_fusion.2), channel_id=1, source_target_pairs={{0,8},{2,10},{4,12},{6,14},{8,0},{10,2},{12,4},{14,6},{1,9},{3,11}... | collective-permute-start | bytes 98312 | tf_op jit(solution)/shard_map/ppermute | solution.py:762
  8.7 2.9 %collective-permute-start.2 = (bf16[2,32,128]{2,1,0:T(8,128)(2,1)S(1)}, bf16[2,32,128]{2,1,0:T(8,128)(2,1)S(1)}, u32[]{:S(2)}, u32[]{:S(2)}) collective-permute-start(bf16[2,32,128]{2,1,0:T(8,128)(2,1)S(1)} %get-tuple-element.32), channel_id=1, source_target_pairs={{0,1},{1,0},{2,3},{3,2},{4,5},{5,4},{6,7},{7,6},{8,9},{9,8},{10,11... | collective-permute-start | bytes 49160 | tf_op jit(solution)/shard_map/ppermute | solution.py:805
  8.8 4.8 %collective-permute-start.5 = (bf16[3,32,128]{2,1,0:T(8,128)(2,1)S(1)}, bf16[3,32,128]{2,1,0:T(8,128)(2,1)S(1)}, u32[]{:S(2)}, u32[]{:S(2)}) collective-permute-start(bf16[3,32,128]{2,1,0:T(8,128)(2,1)S(1)} %get-tuple-element.48), channel_id=1, source_target_pairs={{0,6},{2,4},{4,2},{6,0},{8,14},{10,12},{12,10},{14,8},{1,7},{3,5},... | collective-permute-start | bytes 73736 | tf_op jit(solution)/shard_map/ppermute | solution.py:762
  11.6 4.0 %collective-permute-start.4 = (bf16[4,32,128]{2,1,0:T(8,128)(2,1)S(1)}, bf16[4,32,128]{2,1,0:T(8,128)(2,1)S(1)}, u32[]{:S(2)}, u32[]{:S(2)}) collective-permute-start(bf16[4,32,128]{2,1,0:T(8,128)(2,1)S(1)} %get-tuple-element.51), channel_id=1, source_target_pairs={{0,4},{2,6},{4,0},{6,2},{8,12},{10,14},{12,8},{14,10},{1,5},{3,7},... | collective-permute-start | bytes 98312 | tf_op jit(solution)/shard_map/ppermute | solution.py:762
  12.2 3.9 %collective-permute-start.3 = (bf16[4,32,128]{2,1,0:T(8,128)(2,1)S(1)}, bf16[4,32,128]{2,1,0:T(8,128)(2,1)S(1)}, u32[]{:S(2)}, u32[]{:S(2)}) collective-permute-start(bf16[4,32,128]{2,1,0:T(8,128)(2,1)S(1)} %get-tuple-element.52), channel_id=1, source_target_pairs={{0,2},{2,0},{4,6},{6,4},{8,10},{10,8},{12,14},{14,12},{1,3},{3,1},... | collective-permute-start | bytes 98312 | tf_op jit(solution)/shard_map/ppermute | solution.py:762
  13.6 1.2 %collective-permute-start.6 = (bf16[32,128]{1,0:T(8,128)(2,1)S(1)}, bf16[32,128]{1,0:T(8,128)(2,1)S(1)}, u32[]{:S(2)}, u32[]{:S(2)}) collective-permute-start(bf16[32,128]{1,0:T(8,128)(2,1)S(1)} %fusion), channel_id=1, source_target_pairs={{0,1},{1,0},{2,3},{3,2},{4,5},{5,4},{6,7},{7,6},{8,9},{9,8},{10,11... | collective-permute-start | bytes 24584 | tf_op jit(solution)/shard_map/ppermute | solution.py:810

commit v23 on v21

--- a/solution.py
+++ b/solution.py
@@ -465,15 +465,10 @@
     rows = [partial[e * seqs : (e + 1) * seqs] for e in range(residues)]
     turned = [pltpu.roll(row, LANES // 2, 1) for row in rows]
     low = lane_block(rows[0].shape, LANES // 2) == 0
-    first = lane_block(rows[0].shape, residues) % 2 == 0
-    pieces = []
-    for block in (
+    return [
         [jnp.where(low, rows[e], turned[e + 1]) for e in (0, 2)],
         [jnp.where(low, turned[e], rows[e + 1]) for e in (0, 2)],
-    ):
-        pieces.append(jnp.where(first, block[0], pltpu.roll(block[1], residues, 1)))
-        pieces.append(jnp.where(first, pltpu.roll(block[0], LANES - residues, 1), block[1]))
-    return pieces
+    ]
 
 
 def small_own_kernel(scale, own_ref, other_ref, w_ref, both_ref, spread_w_ref,
@@ -509,15 +504,16 @@
     other = other_ref[...].reshape(residues * columns, LANES)
     flat = outer_flat(scale, jnp.where(own_is_near, own, other), sorted_wt_ref)
     pieces = column_pieces(both_ref[0], outer_tiles(flat, residues), repeat_ref[...], residues)
-    for place, piece in enumerate(pieces):
-        keep_ref[place] = piece
+    for block in range(2):
+        for tile in range(2):
+            keep_ref[block, tile] = pieces[block][tile]
     outer_near_ref[...] = outer_rows(flat, residues, turn_refs[0])
     flat = outer_flat(scale, jnp.where(own_is_near, other, own), sorted_wt_ref)
     outer_far_ref[...] = outer_rows(flat, residues, turn_refs[1])
 
 
 def small_partner_kernel(scale, residues, got_ref, sorted_wt_ref, keep_ref, both_ref, repeat_ref,
-                         leaving_ref, keep_out_ref, right_ref, swap_ref):
+                         leaving_ref, right_ref, swap_ref):
     rank = lax.axis_index("res")
     seqs = got_ref.shape[1]
     cot = got_ref[2:4].reshape(2 * seqs, LANES)
@@ -528,11 +524,17 @@
     own_is_near = lax.axis_index("seq") == lax.shift_right_logical(rank, 2)
     swap_ref[0] = jnp.where(own_is_near, got_ref[1], both_ref[1])
     swap_ref[1] = both_ref[0]
-    for place, piece in enumerate(pieces):
-        distance = lax.bitwise_xor(rank & 3, place)
-        total = keep_ref[place] + piece
-        keep_out_ref[distance] = total
-        leaving_ref[distance, 2] = total.astype(BF16)
+    first = lane_block((seqs, LANES), residues) % 2 == 0
+    for block in range(2):
+        low, high = [
+            (keep_ref[block, tile] + pieces[block][tile]).astype(BF16) for tile in range(2)
+        ]
+        chips = (
+            jnp.where(first, low, pltpu.roll(high, residues, 1)),
+            jnp.where(first, pltpu.roll(low, LANES - residues, 1), high),
+        )
+        for chip in range(2):
+            leaving_ref[lax.bitwise_xor(rank & 3, 2 * block + chip), 2] = chips[chip]
     for place in range(leaving_ref.shape[0]):
         leaving_ref[place, 0] = both_ref[1]
         leaving_ref[place, 1] = got_ref[1]
@@ -540,7 +542,7 @@
 
 def small_finish_kernel(
     scale, right_ref, part_refs, swapped_ref, swapped_late_ref, both_ref, outer_near_ref, outer_far_ref,
-    keep_ref, normed_ref, inv_std_ref, gain_ref, spread_w_ref, columns_w_ref, sorted_w_ref, offset_ref,
+    own_part_ref, normed_ref, inv_std_ref, gain_ref, spread_w_ref, columns_w_ref, sorted_w_ref, offset_ref,
     grad_hbm, pair_hbm, grad_ref, pair_ref, near_ref, beyond_ref, turn_ref, lines_ref, semaphores,
 ):
     seqs, residues, _ = grad_ref.shape
@@ -564,7 +566,7 @@
         axis=0,
     )
     left_cot = jnp.dot(right_all, outer, preferred_element_type=F32)
-    right_cot = keep_ref[0]
+    right_cot = own_part_ref[2].astype(F32)
     for part_ref in part_refs:
         right_cot = right_cot + part_ref[2].astype(F32)
     blocks = lane_block((seqs, LANES), depth)
@@ -726,7 +728,7 @@
         in_specs=[vmem] * 5,
         out_specs=[vmem] * 7,
         out_shape=(
-            like((ranks // 2, seqs, LANES), F32),
+            like((2, 2, seqs, LANES), F32),
             like((half_rows, LANES), BF16),
             like((half_rows, LANES), BF16),
             like(coupling_matrix.shape, BF16),
@@ -742,13 +744,12 @@
         name="own_pieces",
     )(own_cot, other_cot, coupling_matrix, both, spread_w)
 
-    leaving_parts, keep, right, leaving = pl.pallas_call(
+    leaving_parts, right, leaving = pl.pallas_call(
         functools.partial(small_partner_kernel, scale, residues),
         in_specs=[vmem] * 5,
-        out_specs=[vmem] * 4,
+        out_specs=[vmem] * 3,
         out_shape=(
             like((ranks // 2, 3, seqs, LANES), BF16),
-            like((ranks // 2, seqs, LANES), F32),
             like((2, seqs, LANES), BF16),
             like((2, seqs, LANES), BF16),
         ),
@@ -792,7 +793,7 @@
         both,
         outer_near,
         outer_far,
-        keep,
+        leaving_parts[0],
         normed,
         inv_std,
         gain,

time: 17.6 us -> 17.6 us (level)
  no operation moved by 1% of the time
where the time goes in v23:
time: 17.6 us; the launch traced here: 17.4 us
  starting transfers between devices  8.81 us (50%)
  Pallas kernels  4.38 us (25%)
  waiting for transfers between devices  3.46 us (20%)
  between operations  0.72 us (4%)
    ppermute x4, starting transfers between devices, swap_over(): lax.ppermute(value, 'res', [(source, source ^ mask) for source in range(r...  8.22 us
    ppermute x4, waiting for transfers between devices, swap_over(): lax.ppermute(value, 'res', [(source, source ^ mask) for source in range(r...  2.29 us
    pallas_call x1, Pallas kernels, small_slice(): pl.pallas_call(functools.partial(small_finish_kernel, scale), in_specs=[v...  1.33 us
    pallas_call x1, Pallas kernels, small_slice(): pl.pallas_call(small_project_kernel, in_specs=[hbm] * 9, out_specs=[vmem]...  1.3 us
    pallas_call x1, Pallas kernels, small_slice(): pl.pallas_call(functools.partial(small_own_kernel, scale), in_specs=[vmem...  1.24 us
    ppermute x1, waiting for transfers between devices, small_slice(): lax.ppermute(jnp.where(own_is_near, diagonal[1], diagonal[0]), 'seq', swap)  1.17 us
    ppermute x1, starting transfers between devices, small_slice(): other_cot = lax.ppermute(coupling_cotangent, 'seq', swap)  0.52 us
    pallas_call x1, Pallas kernels, small_slice(): pl.pallas_call(functools.partial(small_partner_kernel, scale, residues),...  0.51 us
  transfers between devices with their start and end apart: 7, of which 5 were waited for; matrix products, arithmetic and copies ran while one was open for 0% of the time, Pallas kernels for 15%

profile of v23, /device:TPU:0, one launch (start us, length us, event | category | flops | bytes accessed | tf_op | source)
XLA Modules:
  0.0 17.4 jit_solution(100824732056961234)
XLA Ops:
  0.6 0.0 copy-start
  0.6 0.5 %collective-permute-start = (bf16[4,16,128]{2,1,0:T(8,128)(2,1)}, bf16[4,16,128]{2,1,0:T(8,128)(2,1)S(1)}, u32[]{:S(2)}, u32[]{:S(2)}) collective-permute-start(bf16[4,16,128]{2,1,0:T(8,128)(2,1)} %cot_hbm.1), channel_id=1, source_target_pairs={{0,1},{1,0},{2,3},{3,2},{4,5},{5,4},{6,7},{7,6},{8,9},{9,8},{10,11... | collective-permute-start | bytes 49160 | tf_op jit(solution)/shard_map/ppermute | solution.py:672
  1.2 1.3 %project.1 = (bf16[2,32,128]{2,1,0:T(8,128)(2,1)S(1)}, f32[128,256]{1,0:T(8,128)S(1)}, f32[128,128]{1,0:T(8,128)S(1)}, bf16[256,256]{1,0:T(8,128)(2,1)S(1)}, f32...) custom-call(bf16[32,4,256]{2,1,0:T(4,128)(2,1)} %x_hbm.1, f32[1,256]{1,0:T(1,128)} %bitcast.21, ...), custom_call_target="tpu_custom_call" | custom-call | tf_op jit(solution)/shard_map/project/pallas_call | solution.py:675
  2.5 0.0 collective-permute-done.other_ref
  2.5 3.7 %collective-permute-start.1 = (bf16[4,32,128]{2,1,0:T(8,128)(2,1)S(1)}, bf16[4,32,128]{2,1,0:T(8,128)(2,1)S(1)}, u32[]{:S(2)}, u32[]{:S(2)}) collective-permute-start(bf16[4,32,128]{2,1,0:T(8,128)(2,1)S(1)} %pad_maximum_fusion.2), channel_id=1, source_target_pairs={{0,8},{2,10},{4,12},{6,14},{8,0},{10,2},{12,4},{14,6},{1,9},{3,11}... | collective-permute-start | bytes 98312 | tf_op jit(solution)/shard_map/ppermute | solution.py:718
  6.2 0.0 copy-done
  6.2 1.2 %own_pieces.1 = (f32[2,2,32,128]{3,2,1,0:T(8,128)S(1)}, bf16[512,128]{1,0:T(8,128)(2,1)S(1)}, bf16[512,128]{1,0:T(8,128)(2,1)S(1)}, bf16[1024,128]{1,0:T(8,128)(...) custom-call(bf16[4,16,128]{2,1,0:T(8,128)(2,1)S(1)} %get-tuple-element.22.own_re, ...), custom_call_target="tpu_custom_call" | custom-call | tf_op jit(solution)/shard_map/own_pieces/pallas_call | solution.py:726
  7.5 0.8 %collective-permute-done.1.got_ref = bf16[4,32,128]{2,1,0:T(8,128)(2,1)S(1)} collective-permute-done((bf16[4,32,128]{2,1,0:T(8,128)(2,1)S(1)}, bf16[4,32,128]{2,1,0:T(8,128)(2,1)S(1)}, u32[]{:S(2)}, u32[]{:S(2)}) %collective-permute-start.1) | collective-permute-done | bytes 32800 | tf_op jit(solution)/shard_map/ppermute | solution.py:718
  8.2 0.5 %partner_pieces.1 = (bf16[4,3,32,128]{3,2,1,0:T(8,128)(2,1)S(1)}, bf16[2,32,128]{2,1,0:T(8,128)(2,1)S(1)}, bf16[2,32,128]{2,1,0:T(8,128)(2,1)S(1)}) custom-call(bf16[4,32,128]{2,1,0:T(8,128)(2,1)S(1)} %collective-permute-done.1.got_ref, bf16[128,1024]{1,0:T(8,128)(2,1)S(1)} %get-tuple-element.24.sorted_wt_ref, ...), custom_call_target="tpu_custom_call" | custom-call | tf_op jit(solution)/shard_map/partner_pieces/pallas_call | solution.py:747
  8.7 0.1 collective-permute-start.2
  8.8 2.8 %collective-permute-start.5 = (bf16[3,32,128]{2,1,0:T(8,128)(2,1)S(1)}, bf16[3,32,128]{2,1,0:T(8,128)(2,1)S(1)}, u32[]{:S(2)}, u32[]{:S(2)}) collective-permute-start(bf16[3,32,128]{2,1,0:T(8,128)(2,1)S(1)} %get-tuple-element.41), channel_id=1, source_target_pairs={{0,6},{2,4},{4,2},{6,0},{8,14},{10,12},{12,10},{14,8},{1,7},{3,5},... | collective-permute-start | bytes 73736 | tf_op jit(solution)/shard_map/ppermute | solution.py:718
  11.6 0.0 collective-permute-done.2.swapped_ref
  11.6 0.5 %collective-permute-start.4 = (bf16[4,32,128]{2,1,0:T(8,128)(2,1)S(1)}, bf16[4,32,128]{2,1,0:T(8,128)(2,1)S(1)}, u32[]{:S(2)}, u32[]{:S(2)}) collective-permute-start(bf16[4,32,128]{2,1,0:T(8,128)(2,1)S(1)} %get-tuple-element.44), channel_id=1, source_target_pairs={{0,4},{2,6},{4,0},{6,2},{8,12},{10,14},{12,8},{14,10},{1,5},{3,7},... | collective-permute-start | bytes 98312 | tf_op jit(solution)/shard_map/ppermute | solution.py:718
  12.2 1.2 %collective-permute-start.3 = (bf16[4,32,128]{2,1,0:T(8,128)(2,1)S(1)}, bf16[4,32,128]{2,1,0:T(8,128)(2,1)S(1)}, u32[]{:S(2)}, u32[]{:S(2)}) collective-permute-start(bf16[4,32,128]{2,1,0:T(8,128)(2,1)S(1)} %get-tuple-element.45), channel_id=1, source_target_pairs={{0,2},{2,0},{4,6},{6,4},{8,10},{10,8},{12,14},{14,12},{1,3},{3,1},... | collective-permute-start | bytes 98312 | tf_op jit(solution)/shard_map/ppermute | solution.py:718
  13.4 0.3 %collective-permute-done.5.part_refs_2_ = bf16[3,32,128]{2,1,0:T(8,128)(2,1)S(1)} collective-permute-done((bf16[3,32,128]{2,1,0:T(8,128)(2,1)S(1)}, bf16[3,32,128]{2,1,0:T(8,128)(2,1)S(1)}, u32[]{:S(2)}, u32[]{:S(2)}) %collective-permute-start.5) | collective-permute-done | bytes 24608 | tf_op jit(solution)/shard_map/ppermute | solution.py:718
  13.6 0.0 collective-permute-start.6
  13.6 1.2 %collective-permute-done.6.swapped_late_ref = bf16[32,128]{1,0:T(8,128)(2,1)S(1)} collective-permute-done((bf16[32,128]{1,0:T(8,128)(2,1)S(1)}, bf16[32,128]{1,0:T(8,128)(2,1)S(1)}, u32[]{:S(2)}, u32[]{:S(2)}) %collective-permute-start.6) | collective-permute-done | bytes 8224 | tf_op jit(solution)/shard_map/ppermute | solution.py:765
  14.8 0.8 %collective-permute-done.4.part_refs_1_ = bf16[4,32,128]{2,1,0:T(8,128)(2,1)S(1)} collective-permute-done((bf16[4,32,128]{2,1,0:T(8,128)(2,1)S(1)}, bf16[4,32,128]{2,1,0:T(8,128)(2,1)S(1)}, u32[]{:S(2)}, u32[]{:S(2)}) %collective-permute-start.4) | collective-permute-done | bytes 32800 | tf_op jit(solution)/shard_map/ppermute | solution.py:718
  15.6 0.4 %collective-permute-done.3.part_refs_0_ = bf16[4,32,128]{2,1,0:T(8,128)(2,1)S(1)} collective-permute-done((bf16[4,32,128]{2,1,0:T(8,128)(2,1)S(1)}, bf16[4,32,128]{2,1,0:T(8,128)(2,1)S(1)}, u32[]{:S(2)}, u32[]{:S(2)}) %collective-permute-start.3) | collective-permute-done | bytes 32800 | tf_op jit(solution)/shard_map/ppermute | solution.py:718
  16.1 1.3 %finish.1 = (bf16[32,4,256]{2,1,0:T(4,128)(2,1)}, bf16[4,16,128]{2,1,0:T(8,128)(2,1)}) custom-call(bf16[2,32,128]{2,1,0:T(8,128)(2,1)S(1)} %get-tuple-element.27.right_ref, bf16[4,32,128]{2,1,0:T(8,128)(2,1)S(1)} %collective-permute-done.3.part_refs_0_, bf16[4,32,128]{2,1,0:T(8,128)(2,1)S(1)} %collective-permute-done.4.part_refs_1_, ...), custom_call_target="tpu_custom_call" | custom-call | tf_op jit(solution)/shard_map/finish/pallas_call | solution.py:769
  (6 shorter events, 0.0 us)
Async XLA Ops:
  0.6 5.6 %copy-start = (bf16[1024,128]{1,0:T(8,128)(2,1)S(1)}, bf16[1024,128]{1,0:T(8,128)(2,1)}, u32[]{:S(2)}) copy-start(bf16[1024,128]{1,0:T(8,128)(2,1)} %w_ref.1) | copy-start | bytes 786436
  0.6 1.8 %collective-permute-start = (bf16[4,16,128]{2,1,0:T(8,128)(2,1)}, bf16[4,16,128]{2,1,0:T(8,128)(2,1)S(1)}, u32[]{:S(2)}, u32[]{:S(2)}) collective-permute-start(bf16[4,16,128]{2,1,0:T(8,128)(2,1)} %cot_hbm.1), channel_id=1, source_target_pairs={{0,1},{1,0},{2,3},{3,2},{4,5},{5,4},{6,7},{7,6},{8,9},{9,8},{10,11... | collective-permute-start | bytes 49160 | tf_op jit(solution)/shard_map/ppermute | solution.py:672
  2.5 5.7 %collective-permute-start.1 = (bf16[4,32,128]{2,1,0:T(8,128)(2,1)S(1)}, bf16[4,32,128]{2,1,0:T(8,128)(2,1)S(1)}, u32[]{:S(2)}, u32[]{:S(2)}) collective-permute-start(bf16[4,32,128]{2,1,0:T(8,128)(2,1)S(1)} %pad_maximum_fusion.2), channel_id=1, source_target_pairs={{0,8},{2,10},{4,12},{6,14},{8,0},{10,2},{12,4},{14,6},{1,9},{3,11}... | collective-permute-start | bytes 98312 | tf_op jit(solution)/shard_map/ppermute | solution.py:718
  8.7 2.9 %collective-permute-start.2 = (bf16[2,32,128]{2,1,0:T(8,128)(2,1)S(1)}, bf16[2,32,128]{2,1,0:T(8,128)(2,1)S(1)}, u32[]{:S(2)}, u32[]{:S(2)}) collective-permute-start(bf16[2,32,128]{2,1,0:T(8,128)(2,1)S(1)} %get-tuple-element.29), channel_id=1, source_target_pairs={{0,1},{1,0},{2,3},{3,2},{4,5},{5,4},{6,7},{7,6},{8,9},{9,8},{10,11... | collective-permute-start | bytes 49160 | tf_op jit(solution)/shard_map/ppermute | solution.py:760
  8.8 4.8 %collective-permute-start.5 = (bf16[3,32,128]{2,1,0:T(8,128)(2,1)S(1)}, bf16[3,32,128]{2,1,0:T(8,128)(2,1)S(1)}, u32[]{:S(2)}, u32[]{:S(2)}) collective-permute-start(bf16[3,32,128]{2,1,0:T(8,128)(2,1)S(1)} %get-tuple-element.41), channel_id=1, source_target_pairs={{0,6},{2,4},{4,2},{6,0},{8,14},{10,12},{12,10},{14,8},{1,7},{3,5},... | collective-permute-start | bytes 73736 | tf_op jit(solution)/shard_map/ppermute | solution.py:718
  11.6 4.0 %collective-permute-start.4 = (bf16[4,32,128]{2,1,0:T(8,128)(2,1)S(1)}, bf16[4,32,128]{2,1,0:T(8,128)(2,1)S(1)}, u32[]{:S(2)}, u32[]{:S(2)}) collective-permute-start(bf16[4,32,128]{2,1,0:T(8,128)(2,1)S(1)} %get-tuple-element.44), channel_id=1, source_target_pairs={{0,4},{2,6},{4,0},{6,2},{8,12},{10,14},{12,8},{14,10},{1,5},{3,7},... | collective-permute-start | bytes 98312 | tf_op jit(solution)/shard_map/ppermute | solution.py:718
  12.2 3.9 %collective-permute-start.3 = (bf16[4,32,128]{2,1,0:T(8,128)(2,1)S(1)}, bf16[4,32,128]{2,1,0:T(8,128)(2,1)S(1)}, u32[]{:S(2)}, u32[]{:S(2)}) collective-permute-start(bf16[4,32,128]{2,1,0:T(8,128)(2,1)S(1)} %get-tuple-element.45), channel_id=1, source_target_pairs={{0,2},{2,0},{4,6},{6,4},{8,10},{10,8},{12,14},{14,12},{1,3},{3,1},... | collective-permute-start | bytes 98312 | tf_op jit(solution)/shard_map/ppermute | solution.py:718
  13.6 1.2 %collective-permute-start.6 = (bf16[32,128]{1,0:T(8,128)(2,1)S(1)}, bf16[32,128]{1,0:T(8,128)(2,1)S(1)}, u32[]{:S(2)}, u32[]{:S(2)}) collective-permute-start(bf16[32,128]{1,0:T(8,128)(2,1)S(1)} %fusion), channel_id=1, source_target_pairs={{0,1},{1,0},{2,3},{3,2},{4,5},{5,4},{6,7},{7,6},{8,9},{9,8},{10,11... | collective-permute-start | bytes 24584 | tf_op jit(solution)/shard_map/ppermute | solution.py:765

commit v24 on v21

--- a/solution.py
+++ b/solution.py
@@ -413,8 +413,8 @@
     spread_w_ref[...] = weight
 
 
-def outer_flat(scale, cot, sorted_wt_ref):
-    return jnp.dot(cot, sorted_wt_ref[...], preferred_element_type=F32) * scale
+def outer_flat(cot, sorted_wt_ref):
+    return jnp.dot(cot, sorted_wt_ref[...], preferred_element_type=F32)
 
 
 def outer_rows(flat, residues, turn_ref):
@@ -448,19 +448,30 @@
     ).astype(BF16)
 
 
-def blocks_apart(left, repeat, residues):
+def blocks_apart(left, residues):
     depth = LANES // residues
-    wide = jnp.dot(left, repeat, preferred_element_type=F32)
-    blocks = lane_block(wide.shape, depth) % residues
+    left = left.astype(F32)
+    turned = [left] + [pltpu.roll(left, depth * t, 1) for t in range(1, residues)]
+    blocks = lane_block(left.shape, depth)
     return jnp.concatenate(
-        [jnp.where(blocks == e, wide, 0.0).astype(BF16) for e in range(residues)], axis=0
-    )
-
-
-def column_pieces(left, outer, repeat, residues):
+        [
+            jnp.concatenate(
+                [
+                    jnp.where(blocks == e, turned[(e - i) % residues], 0.0).astype(BF16)
+                    for i in range(residues)
+                ],
+                axis=1,
+            )
+            for e in range(residues)
+        ],
+        axis=0,
+    )
+
+
+def column_pieces(left, outer, residues):
     seqs = left.shape[0]
     partial = lax.dot_general(
-        blocks_apart(left, repeat, residues), outer, NT, preferred_element_type=F32
+        blocks_apart(left, residues), outer, NT, preferred_element_type=F32
     )
     rows = [partial[e * seqs : (e + 1) * seqs] for e in range(residues)]
     turned = [pltpu.roll(row, LANES // 2, 1) for row in rows]
@@ -478,7 +489,7 @@
 
 def small_own_kernel(scale, own_ref, other_ref, w_ref, both_ref, spread_w_ref,
                      keep_ref, outer_near_ref, outer_far_ref, sorted_w_ref, sorted_wt_ref,
-                     repeat_ref, columns_w_ref, turn_refs, wide_ref):
+                     columns_w_ref, turn_refs, wide_ref):
     residues, columns, _ = own_ref.shape
     depth = LANES // residues
     wide_ref[0 : w_ref.shape[0], :] = w_ref[...].astype(F32)
@@ -486,14 +497,7 @@
         sorted_w_ref[d * depth : (d + 1) * depth, :] = wide_ref[
             pl.ds(d, depth, stride=depth), :
         ].astype(BF16)
-    sorted_wt_ref[...] = sorted_w_ref[...].T
-    shape = (LANES, LANES)
-    row = lax.broadcasted_iota(jnp.int32, shape, 0)
-    lane = lax.broadcasted_iota(jnp.int32, shape, 1)
-    for place in range(residues):
-        repeat_ref[:, place * LANES : (place + 1) * LANES] = jnp.where(
-            row == place * depth + lane % depth, 1.0, 0.0
-        ).astype(BF16)
+    sorted_wt_ref[...] = (sorted_w_ref[...].astype(F32) * scale).astype(BF16).T
     shape = (columns_w_ref.shape[0], depth)
     row = lax.broadcasted_iota(jnp.int32, shape, 0)
     lane = lax.broadcasted_iota(jnp.int32, shape, 1)
@@ -507,22 +511,22 @@
     own_is_near = lax.axis_index("seq") == lax.shift_right_logical(rank, 2)
     own = own_ref[...].reshape(residues * columns, LANES)
     other = other_ref[...].reshape(residues * columns, LANES)
-    flat = outer_flat(scale, jnp.where(own_is_near, own, other), sorted_wt_ref)
-    pieces = column_pieces(both_ref[0], outer_tiles(flat, residues), repeat_ref[...], residues)
+    flat = outer_flat(jnp.where(own_is_near, own, other), sorted_wt_ref)
+    pieces = column_pieces(both_ref[0], outer_tiles(flat, residues), residues)
     for place, piece in enumerate(pieces):
         keep_ref[place] = piece
     outer_near_ref[...] = outer_rows(flat, residues, turn_refs[0])
-    flat = outer_flat(scale, jnp.where(own_is_near, other, own), sorted_wt_ref)
+    flat = outer_flat(jnp.where(own_is_near, other, own), sorted_wt_ref)
     outer_far_ref[...] = outer_rows(flat, residues, turn_refs[1])
 
 
-def small_partner_kernel(scale, residues, got_ref, sorted_wt_ref, keep_ref, both_ref, repeat_ref,
+def small_partner_kernel(residues, got_ref, sorted_wt_ref, keep_ref, both_ref,
                          leaving_ref, keep_out_ref, right_ref, swap_ref):
     rank = lax.axis_index("res")
     seqs = got_ref.shape[1]
     cot = got_ref[2:4].reshape(2 * seqs, LANES)
-    outer = outer_tiles(outer_flat(scale, cot, sorted_wt_ref), residues)
-    pieces = column_pieces(got_ref[0], outer, repeat_ref[...], residues)
+    outer = outer_tiles(outer_flat(cot, sorted_wt_ref), residues)
+    pieces = column_pieces(got_ref[0], outer, residues)
     right_ref[0] = both_ref[1]
     right_ref[1] = got_ref[1]
     own_is_near = lax.axis_index("seq") == lax.shift_right_logical(rank, 2)
@@ -721,17 +725,16 @@
 
     half_rows = ranks // 2 * LANES
     turn = pltpu.VMEM((half_rows + depth, LANES), F32)
-    keep, outer_near, outer_far, sorted_w, sorted_wt, repeat, columns_w = pl.pallas_call(
+    keep, outer_near, outer_far, sorted_w, sorted_wt, columns_w = pl.pallas_call(
         functools.partial(small_own_kernel, scale),
         in_specs=[vmem] * 5,
-        out_specs=[vmem] * 7,
+        out_specs=[vmem] * 6,
         out_shape=(
             like((ranks // 2, seqs, LANES), F32),
             like((half_rows, LANES), BF16),
             like((half_rows, LANES), BF16),
             like(coupling_matrix.shape, BF16),
             like(coupling_matrix.shape[::-1], BF16),
-            like((LANES, residues * LANES), BF16),
             like((LANES, features), BF16),
         ),
         scratch_shapes=[
@@ -743,8 +746,8 @@
     )(own_cot, other_cot, coupling_matrix, both, spread_w)
 
     leaving_parts, keep, right, leaving = pl.pallas_call(
-        functools.partial(small_partner_kernel, scale, residues),
-        in_specs=[vmem] * 5,
+        functools.partial(small_partner_kernel, residues),
+        in_specs=[vmem] * 4,
         out_specs=[vmem] * 4,
         out_shape=(
             like((ranks // 2, 3, seqs, LANES), BF16),
@@ -754,7 +757,7 @@
         ),
         compiler_params=limit,
         name="partner_pieces",
-    )(beyond_two, sorted_wt, keep, both, repeat)
+    )(beyond_two, sorted_wt, keep, both)
 
     swapped = lax.ppermute(leaving, "seq", swap)
     diagonal = swap_over(3, leaving_parts[3])
@@ -805,7 +808,8 @@
 
 
 def body(*arrays):
-    if lax.axis_size("res") == 8:
+    sequences = arrays[0].shape[0] * lax.axis_size("seq")
+    if lax.axis_size("res") == 8 and sequences & (sequences - 1) == 0:
         return small_slice(*arrays)
     return wide_slice(*arrays)
 

time: 17.6 us -> 17.6 us (level)
  transfers between devices with their start and end apart: 7 -> 7, of which waited for: 5 -> 5; matrix products, arithmetic and copies ran while one was open for 0% -> 0% of each run, Pallas kernels for 15% -> 14%
where the time goes in v24:
time: 17.6 us; the launch traced here: 17.4 us
  starting transfers between devices  8.81 us (50%)
  Pallas kernels  4.31 us (24%)
  waiting for transfers between devices  3.52 us (20%)
  between operations  0.72 us (4%)
    ppermute x4, starting transfers between devices, swap_over(): lax.ppermute(value, 'res', [(source, source ^ mask) for source in range(r...  8.22 us
    ppermute x4, waiting for transfers between devices, swap_over(): lax.ppermute(value, 'res', [(source, source ^ mask) for source in range(r...  2.35 us
    pallas_call x1, Pallas kernels, small_slice(): pl.pallas_call(functools.partial(small_finish_kernel, scale), in_specs=[v...  1.33 us
    pallas_call x1, Pallas kernels, small_slice(): pl.pallas_call(small_project_kernel, in_specs=[hbm] * 9, out_specs=[vmem]...  1.3 us
    pallas_call x1, Pallas kernels, small_slice(): pl.pallas_call(functools.partial(small_own_kernel, scale), in_specs=[vmem...  1.18 us
    ppermute x1, waiting for transfers between devices, small_slice(): lax.ppermute(jnp.where(own_is_near, diagonal[1], diagonal[0]), 'seq', swap)  1.17 us
    ppermute x1, starting transfers between devices, small_slice(): other_cot = lax.ppermute(coupling_cotangent, 'seq', swap)  0.52 us
    pallas_call x1, Pallas kernels, small_slice(): pl.pallas_call(functools.partial(small_partner_kernel, residues), in_spec...  0.5 us
  transfers between devices with their start and end apart: 7, of which 5 were waited for; matrix products, arithmetic and copies ran while one was open for 0% of the time, Pallas kernels for 14%

profile of v24, /device:TPU:0, one launch (start us, length us, event | category | flops | bytes accessed | tf_op | source)
XLA Modules:
  0.0 17.4 jit_solution(8387504520750703175)
XLA Ops:
  0.6 0.0 copy-start
  0.6 0.5 %collective-permute-start = (bf16[4,16,128]{2,1,0:T(8,128)(2,1)}, bf16[4,16,128]{2,1,0:T(8,128)(2,1)S(1)}, u32[]{:S(2)}, u32[]{:S(2)}) collective-permute-start(bf16[4,16,128]{2,1,0:T(8,128)(2,1)} %cot_hbm.1), channel_id=1, source_target_pairs={{0,1},{1,0},{2,3},{3,2},{4,5},{5,4},{6,7},{7,6},{8,9},{9,8},{10,11... | collective-permute-start | bytes 49160 | tf_op jit(solution)/shard_map/ppermute | solution.py:674
  1.2 1.3 %project.1 = (bf16[2,32,128]{2,1,0:T(8,128)(2,1)S(1)}, f32[128,256]{1,0:T(8,128)S(1)}, f32[128,128]{1,0:T(8,128)S(1)}, bf16[256,256]{1,0:T(8,128)(2,1)S(1)}, f32...) custom-call(bf16[32,4,256]{2,1,0:T(4,128)(2,1)} %x_hbm.1, f32[1,256]{1,0:T(1,128)} %bitcast.19, ...), custom_call_target="tpu_custom_call" | custom-call | tf_op jit(solution)/shard_map/project/pallas_call | solution.py:677
  2.5 0.0 collective-permute-done.other_ref
  2.5 3.7 %collective-permute-start.1 = (bf16[4,32,128]{2,1,0:T(8,128)(2,1)S(1)}, bf16[4,32,128]{2,1,0:T(8,128)(2,1)S(1)}, u32[]{:S(2)}, u32[]{:S(2)}) collective-permute-start(bf16[4,32,128]{2,1,0:T(8,128)(2,1)S(1)} %pad_maximum_fusion.2), channel_id=1, source_target_pairs={{0,8},{2,10},{4,12},{6,14},{8,0},{10,2},{12,4},{14,6},{1,9},{3,11}... | collective-permute-start | bytes 98312 | tf_op jit(solution)/shard_map/ppermute | solution.py:720
  6.2 0.0 copy-done
  6.2 1.2 %own_pieces.1 = (f32[4,32,128]{2,1,0:T(8,128)S(1)}, bf16[512,128]{1,0:T(8,128)(2,1)S(1)}, bf16[512,128]{1,0:T(8,128)(2,1)S(1)}, bf16[1024,128]{1,0:T(8,128)(2,1)...) custom-call(bf16[4,16,128]{2,1,0:T(8,128)(2,1)S(1)} %get-tuple-element.22.own_ref, ...), custom_call_target="tpu_custom_call" | custom-call | tf_op jit(solution)/shard_map/own_pieces/pallas_call | solution.py:728
  7.4 0.8 %collective-permute-done.1.got_ref = bf16[4,32,128]{2,1,0:T(8,128)(2,1)S(1)} collective-permute-done((bf16[4,32,128]{2,1,0:T(8,128)(2,1)S(1)}, bf16[4,32,128]{2,1,0:T(8,128)(2,1)S(1)}, u32[]{:S(2)}, u32[]{:S(2)}) %collective-permute-start.1) | collective-permute-done | bytes 32800 | tf_op jit(solution)/shard_map/ppermute | solution.py:720
  8.2 0.5 %partner_pieces.1 = (bf16[4,3,32,128]{3,2,1,0:T(8,128)(2,1)S(1)}, f32[4,32,128]{2,1,0:T(8,128)S(1)}, bf16[2,32,128]{2,1,0:T(8,128)(2,1)S(1)}, bf16[2,32,128]{2,1,0:T(8,128)(2,1)S(1)}) custom-call(bf16[4,32,128]{2,1,0:T(8,128)(2,1)S(1)} %collective-permute-done.1.got_ref, bf16[128,1024]{1,0:T(8,128)(2,1)S(1)} %get-tuple-element.24.sorted_wt_ref, ...), custom_call_target="tpu_custom_call" | custom-call | tf_op jit(solution)/shard_map/partner_pieces/pallas_call | solution.py:748
  8.7 0.1 collective-permute-start.2
  8.8 2.8 %collective-permute-start.5 = (bf16[3,32,128]{2,1,0:T(8,128)(2,1)S(1)}, bf16[3,32,128]{2,1,0:T(8,128)(2,1)S(1)}, u32[]{:S(2)}, u32[]{:S(2)}) collective-permute-start(bf16[3,32,128]{2,1,0:T(8,128)(2,1)S(1)} %get-tuple-element.40), channel_id=1, source_target_pairs={{0,6},{2,4},{4,2},{6,0},{8,14},{10,12},{12,10},{14,8},{1,7},{3,5},... | collective-permute-start | bytes 73736 | tf_op jit(solution)/shard_map/ppermute | solution.py:720
  11.6 0.0 collective-permute-done.2.swapped_ref
  11.6 0.5 %collective-permute-start.4 = (bf16[4,32,128]{2,1,0:T(8,128)(2,1)S(1)}, bf16[4,32,128]{2,1,0:T(8,128)(2,1)S(1)}, u32[]{:S(2)}, u32[]{:S(2)}) collective-permute-start(bf16[4,32,128]{2,1,0:T(8,128)(2,1)S(1)} %get-tuple-element.43), channel_id=1, source_target_pairs={{0,4},{2,6},{4,0},{6,2},{8,12},{10,14},{12,8},{14,10},{1,5},{3,7},... | collective-permute-start | bytes 98312 | tf_op jit(solution)/shard_map/ppermute | solution.py:720
  12.2 1.2 %collective-permute-start.3 = (bf16[4,32,128]{2,1,0:T(8,128)(2,1)S(1)}, bf16[4,32,128]{2,1,0:T(8,128)(2,1)S(1)}, u32[]{:S(2)}, u32[]{:S(2)}) collective-permute-start(bf16[4,32,128]{2,1,0:T(8,128)(2,1)S(1)} %get-tuple-element.44), channel_id=1, source_target_pairs={{0,2},{2,0},{4,6},{6,4},{8,10},{10,8},{12,14},{14,12},{1,3},{3,1},... | collective-permute-start | bytes 98312 | tf_op jit(solution)/shard_map/ppermute | solution.py:720
  13.4 0.3 %collective-permute-done.5.part_refs_2_ = bf16[3,32,128]{2,1,0:T(8,128)(2,1)S(1)} collective-permute-done((bf16[3,32,128]{2,1,0:T(8,128)(2,1)S(1)}, bf16[3,32,128]{2,1,0:T(8,128)(2,1)S(1)}, u32[]{:S(2)}, u32[]{:S(2)}) %collective-permute-start.5) | collective-permute-done | bytes 24608 | tf_op jit(solution)/shard_map/ppermute | solution.py:720
  13.6 0.0 collective-permute-start.6
  13.6 1.2 %collective-permute-done.6.swapped_late_ref = bf16[32,128]{1,0:T(8,128)(2,1)S(1)} collective-permute-done((bf16[32,128]{1,0:T(8,128)(2,1)S(1)}, bf16[32,128]{1,0:T(8,128)(2,1)S(1)}, u32[]{:S(2)}, u32[]{:S(2)}) %collective-permute-start.6) | collective-permute-done | bytes 8224 | tf_op jit(solution)/shard_map/ppermute | solution.py:767
  14.8 0.8 %collective-permute-done.4.part_refs_1_ = bf16[4,32,128]{2,1,0:T(8,128)(2,1)S(1)} collective-permute-done((bf16[4,32,128]{2,1,0:T(8,128)(2,1)S(1)}, bf16[4,32,128]{2,1,0:T(8,128)(2,1)S(1)}, u32[]{:S(2)}, u32[]{:S(2)}) %collective-permute-start.4) | collective-permute-done | bytes 32800 | tf_op jit(solution)/shard_map/ppermute | solution.py:720
  15.6 0.4 %collective-permute-done.3.part_refs_0_ = bf16[4,32,128]{2,1,0:T(8,128)(2,1)S(1)} collective-permute-done((bf16[4,32,128]{2,1,0:T(8,128)(2,1)S(1)}, bf16[4,32,128]{2,1,0:T(8,128)(2,1)S(1)}, u32[]{:S(2)}, u32[]{:S(2)}) %collective-permute-start.3) | collective-permute-done | bytes 32800 | tf_op jit(solution)/shard_map/ppermute | solution.py:720
  16.1 1.3 %finish.1 = (bf16[32,4,256]{2,1,0:T(4,128)(2,1)}, bf16[4,16,128]{2,1,0:T(8,128)(2,1)}) custom-call(bf16[2,32,128]{2,1,0:T(8,128)(2,1)S(1)} %get-tuple-element.26.right_ref, bf16[4,32,128]{2,1,0:T(8,128)(2,1)S(1)} %collective-permute-done.3.part_refs_0_, bf16[4,32,128]{2,1,0:T(8,128)(2,1)S(1)} %collective-permute-done.4.part_refs_1_, ...), custom_call_target="tpu_custom_call" | custom-call | tf_op jit(solution)/shard_map/finish/pallas_call | solution.py:771
  (6 shorter events, 0.0 us)
Async XLA Ops:
  0.6 5.6 %copy-start = (bf16[1024,128]{1,0:T(8,128)(2,1)S(1)}, bf16[1024,128]{1,0:T(8,128)(2,1)}, u32[]{:S(2)}) copy-start(bf16[1024,128]{1,0:T(8,128)(2,1)} %w_ref.1) | copy-start | bytes 786436
  0.6 1.8 %collective-permute-start = (bf16[4,16,128]{2,1,0:T(8,128)(2,1)}, bf16[4,16,128]{2,1,0:T(8,128)(2,1)S(1)}, u32[]{:S(2)}, u32[]{:S(2)}) collective-permute-start(bf16[4,16,128]{2,1,0:T(8,128)(2,1)} %cot_hbm.1), channel_id=1, source_target_pairs={{0,1},{1,0},{2,3},{3,2},{4,5},{5,4},{6,7},{7,6},{8,9},{9,8},{10,11... | collective-permute-start | bytes 49160 | tf_op jit(solution)/shard_map/ppermute | solution.py:674
  2.5 5.7 %collective-permute-start.1 = (bf16[4,32,128]{2,1,0:T(8,128)(2,1)S(1)}, bf16[4,32,128]{2,1,0:T(8,128)(2,1)S(1)}, u32[]{:S(2)}, u32[]{:S(2)}) collective-permute-start(bf16[4,32,128]{2,1,0:T(8,128)(2,1)S(1)} %pad_maximum_fusion.2), channel_id=1, source_target_pairs={{0,8},{2,10},{4,12},{6,14},{8,0},{10,2},{12,4},{14,6},{1,9},{3,11}... | collective-permute-start | bytes 98312 | tf_op jit(solution)/shard_map/ppermute | solution.py:720
  8.7 2.9 %collective-permute-start.2 = (bf16[2,32,128]{2,1,0:T(8,128)(2,1)S(1)}, bf16[2,32,128]{2,1,0:T(8,128)(2,1)S(1)}, u32[]{:S(2)}, u32[]{:S(2)}) collective-permute-start(bf16[2,32,128]{2,1,0:T(8,128)(2,1)S(1)} %get-tuple-element.28), channel_id=1, source_target_pairs={{0,1},{1,0},{2,3},{3,2},{4,5},{5,4},{6,7},{7,6},{8,9},{9,8},{10,11... | collective-permute-start | bytes 49160 | tf_op jit(solution)/shard_map/ppermute | solution.py:762
  8.8 4.8 %collective-permute-start.5 = (bf16[3,32,128]{2,1,0:T(8,128)(2,1)S(1)}, bf16[3,32,128]{2,1,0:T(8,128)(2,1)S(1)}, u32[]{:S(2)}, u32[]{:S(2)}) collective-permute-start(bf16[3,32,128]{2,1,0:T(8,128)(2,1)S(1)} %get-tuple-element.40), channel_id=1, source_target_pairs={{0,6},{2,4},{4,2},{6,0},{8,14},{10,12},{12,10},{14,8},{1,7},{3,5},... | collective-permute-start | bytes 73736 | tf_op jit(solution)/shard_map/ppermute | solution.py:720
  11.6 4.0 %collective-permute-start.4 = (bf16[4,32,128]{2,1,0:T(8,128)(2,1)S(1)}, bf16[4,32,128]{2,1,0:T(8,128)(2,1)S(1)}, u32[]{:S(2)}, u32[]{:S(2)}) collective-permute-start(bf16[4,32,128]{2,1,0:T(8,128)(2,1)S(1)} %get-tuple-element.43), channel_id=1, source_target_pairs={{0,4},{2,6},{4,0},{6,2},{8,12},{10,14},{12,8},{14,10},{1,5},{3,7},... | collective-permute-start | bytes 98312 | tf_op jit(solution)/shard_map/ppermute | solution.py:720
  12.2 3.9 %collective-permute-start.3 = (bf16[4,32,128]{2,1,0:T(8,128)(2,1)S(1)}, bf16[4,32,128]{2,1,0:T(8,128)(2,1)S(1)}, u32[]{:S(2)}, u32[]{:S(2)}) collective-permute-start(bf16[4,32,128]{2,1,0:T(8,128)(2,1)S(1)} %get-tuple-element.44), channel_id=1, source_target_pairs={{0,2},{2,0},{4,6},{6,4},{8,10},{10,8},{12,14},{14,12},{1,3},{3,1},... | collective-permute-start | bytes 98312 | tf_op jit(solution)/shard_map/ppermute | solution.py:720
  13.6 1.2 %collective-permute-start.6 = (bf16[32,128]{1,0:T(8,128)(2,1)S(1)}, bf16[32,128]{1,0:T(8,128)(2,1)S(1)}, u32[]{:S(2)}, u32[]{:S(2)}) collective-permute-start(bf16[32,128]{1,0:T(8,128)(2,1)S(1)} %fusion), channel_id=1, source_target_pairs={{0,1},{1,0},{2,3},{3,2},{4,5},{5,4},{6,7},{7,6},{8,9},{9,8},{10,11... | collective-permute-start | bytes 24584 | tf_op jit(solution)/shard_map/ppermute | solution.py:767

commit v25 on v24

--- a/solution.py
+++ b/solution.py
@@ -474,16 +474,15 @@
         blocks_apart(left, residues), outer, NT, preferred_element_type=F32
     )
     rows = [partial[e * seqs : (e + 1) * seqs] for e in range(residues)]
-    turned = [pltpu.roll(row, LANES // 2, 1) for row in rows]
-    low = lane_block(rows[0].shape, LANES // 2) == 0
-    first = lane_block(rows[0].shape, residues) % 2 == 0
+    half = lane_block(rows[0].shape, LANES // 2)
+    source = 2 * (lane_block(rows[0].shape, residues) % 2) + half
     pieces = []
-    for block in (
-        [jnp.where(low, rows[e], turned[e + 1]) for e in (0, 2)],
-        [jnp.where(low, turned[e], rows[e + 1]) for e in (0, 2)],
-    ):
-        pieces.append(jnp.where(first, block[0], pltpu.roll(block[1], residues, 1)))
-        pieces.append(jnp.where(first, pltpu.roll(block[0], LANES - residues, 1), block[1]))
+    for chip in range(residues):
+        turned = []
+        for e, row in enumerate(rows):
+            count = (LANES // 2 * (e % 2 - chip // 2) + residues * (e // 2 - chip % 2)) % LANES
+            turned.append(pltpu.roll(row, count, 1) if count else row)
+        pieces.append(pick(source, turned))
     return pieces
 
 

time: 17.6 us -> 17.5 us (level)
  no operation moved by 1% of the time
where the time goes in v25:
time: 17.5 us; the launch traced here: 17.3 us
  starting transfers between devices  8.81 us (50%)
  Pallas kernels  4.24 us (24%)
  waiting for transfers between devices  3.53 us (20%)
  between operations  0.72 us (4%)
    ppermute x4, starting transfers between devices, swap_over(): lax.ppermute(value, 'res', [(source, source ^ mask) for source in range(r...  8.22 us
    ppermute x4, waiting for transfers between devices, swap_over(): lax.ppermute(value, 'res', [(source, source ^ mask) for source in range(r...  2.36 us
    pallas_call x1, Pallas kernels, small_slice(): pl.pallas_call(functools.partial(small_finish_kernel, scale), in_specs=[v...  1.33 us
    pallas_call x1, Pallas kernels, small_slice(): pl.pallas_call(small_project_kernel, in_specs=[hbm] * 9, out_specs=[vmem]...  1.3 us
    ppermute x1, waiting for transfers between devices, small_slice(): lax.ppermute(jnp.where(own_is_near, diagonal[1], diagonal[0]), 'seq', swap)  1.17 us
    pallas_call x1, Pallas kernels, small_slice(): pl.pallas_call(functools.partial(small_own_kernel, scale), in_specs=[vmem...  1.16 us
    ppermute x1, starting transfers between devices, small_slice(): other_cot = lax.ppermute(coupling_cotangent, 'seq', swap)  0.52 us
    pallas_call x1, Pallas kernels, small_slice(): pl.pallas_call(functools.partial(small_partner_kernel, residues), in_spec...  0.45 us
  transfers between devices with their start and end apart: 7, of which 5 were waited for; matrix products, arithmetic and copies ran while one was open for 0% of the time, Pallas kernels for 14%

profile of v25, /device:TPU:0, one launch (start us, length us, event | category | flops | bytes accessed | tf_op | source)
XLA Modules:
  0.0 17.3 jit_solution(11033018893388425610)
XLA Ops:
  0.6 0.0 copy-start
  0.6 0.5 %collective-permute-start = (bf16[4,16,128]{2,1,0:T(8,128)(2,1)}, bf16[4,16,128]{2,1,0:T(8,128)(2,1)S(1)}, u32[]{:S(2)}, u32[]{:S(2)}) collective-permute-start(bf16[4,16,128]{2,1,0:T(8,128)(2,1)} %cot_hbm.1), channel_id=1, source_target_pairs={{0,1},{1,0},{2,3},{3,2},{4,5},{5,4},{6,7},{7,6},{8,9},{9,8},{10,11... | collective-permute-start | bytes 49160 | tf_op jit(solution)/shard_map/ppermute | solution.py:673
  1.2 1.3 %project.1 = (bf16[2,32,128]{2,1,0:T(8,128)(2,1)S(1)}, f32[128,256]{1,0:T(8,128)S(1)}, f32[128,128]{1,0:T(8,128)S(1)}, bf16[256,256]{1,0:T(8,128)(2,1)S(1)}, f32...) custom-call(bf16[32,4,256]{2,1,0:T(4,128)(2,1)} %x_hbm.1, f32[1,256]{1,0:T(1,128)} %bitcast.19, ...), custom_call_target="tpu_custom_call" | custom-call | tf_op jit(solution)/shard_map/project/pallas_call | solution.py:676
  2.5 0.0 collective-permute-done.other_ref
  2.5 3.7 %collective-permute-start.1 = (bf16[4,32,128]{2,1,0:T(8,128)(2,1)S(1)}, bf16[4,32,128]{2,1,0:T(8,128)(2,1)S(1)}, u32[]{:S(2)}, u32[]{:S(2)}) collective-permute-start(bf16[4,32,128]{2,1,0:T(8,128)(2,1)S(1)} %pad_maximum_fusion.2), channel_id=1, source_target_pairs={{0,8},{2,10},{4,12},{6,14},{8,0},{10,2},{12,4},{14,6},{1,9},{3,11}... | collective-permute-start | bytes 98312 | tf_op jit(solution)/shard_map/ppermute | solution.py:719
  6.2 0.0 copy-done
  6.2 1.2 %own_pieces.1 = (f32[4,32,128]{2,1,0:T(8,128)S(1)}, bf16[512,128]{1,0:T(8,128)(2,1)S(1)}, bf16[512,128]{1,0:T(8,128)(2,1)S(1)}, bf16[1024,128]{1,0:T(8,128)(2,1)...) custom-call(bf16[4,16,128]{2,1,0:T(8,128)(2,1)S(1)} %get-tuple-element.22.own_ref, ...), custom_call_target="tpu_custom_call" | custom-call | tf_op jit(solution)/shard_map/own_pieces/pallas_call | solution.py:727
  7.4 0.8 %collective-permute-done.1.got_ref = bf16[4,32,128]{2,1,0:T(8,128)(2,1)S(1)} collective-permute-done((bf16[4,32,128]{2,1,0:T(8,128)(2,1)S(1)}, bf16[4,32,128]{2,1,0:T(8,128)(2,1)S(1)}, u32[]{:S(2)}, u32[]{:S(2)}) %collective-permute-start.1) | collective-permute-done | bytes 32800 | tf_op jit(solution)/shard_map/ppermute | solution.py:719
  8.2 0.4 %partner_pieces.1 = (bf16[4,3,32,128]{3,2,1,0:T(8,128)(2,1)S(1)}, f32[4,32,128]{2,1,0:T(8,128)S(1)}, bf16[2,32,128]{2,1,0:T(8,128)(2,1)S(1)}, bf16[2,32,128]{2,1,0:T(8,128)(2,1)S(1)}) custom-call(bf16[4,32,128]{2,1,0:T(8,128)(2,1)S(1)} %collective-permute-done.1.got_ref, bf16[128,1024]{1,0:T(8,128)(2,1)S(1)} %get-tuple-element.24.sorted_wt_ref, ...), custom_call_target="tpu_custom_call" | custom-call | tf_op jit(solution)/shard_map/partner_pieces/pallas_call | solution.py:747
  8.7 0.1 collective-permute-start.2
  8.8 2.8 %collective-permute-start.5 = (bf16[3,32,128]{2,1,0:T(8,128)(2,1)S(1)}, bf16[3,32,128]{2,1,0:T(8,128)(2,1)S(1)}, u32[]{:S(2)}, u32[]{:S(2)}) collective-permute-start(bf16[3,32,128]{2,1,0:T(8,128)(2,1)S(1)} %get-tuple-element.40), channel_id=1, source_target_pairs={{0,6},{2,4},{4,2},{6,0},{8,14},{10,12},{12,10},{14,8},{1,7},{3,5},... | collective-permute-start | bytes 73736 | tf_op jit(solution)/shard_map/ppermute | solution.py:719
  11.6 0.0 collective-permute-done.2.swapped_ref
  11.6 0.5 %collective-permute-start.4 = (bf16[4,32,128]{2,1,0:T(8,128)(2,1)S(1)}, bf16[4,32,128]{2,1,0:T(8,128)(2,1)S(1)}, u32[]{:S(2)}, u32[]{:S(2)}) collective-permute-start(bf16[4,32,128]{2,1,0:T(8,128)(2,1)S(1)} %get-tuple-element.43), channel_id=1, source_target_pairs={{0,4},{2,6},{4,0},{6,2},{8,12},{10,14},{12,8},{14,10},{1,5},{3,7},... | collective-permute-start | bytes 98312 | tf_op jit(solution)/shard_map/ppermute | solution.py:719
  12.1 1.2 %collective-permute-start.3 = (bf16[4,32,128]{2,1,0:T(8,128)(2,1)S(1)}, bf16[4,32,128]{2,1,0:T(8,128)(2,1)S(1)}, u32[]{:S(2)}, u32[]{:S(2)}) collective-permute-start(bf16[4,32,128]{2,1,0:T(8,128)(2,1)S(1)} %get-tuple-element.44), channel_id=1, source_target_pairs={{0,2},{2,0},{4,6},{6,4},{8,10},{10,8},{12,14},{14,12},{1,3},{3,1},... | collective-permute-start | bytes 98312 | tf_op jit(solution)/shard_map/ppermute | solution.py:719
  13.3 0.3 %collective-permute-done.5.part_refs_2_ = bf16[3,32,128]{2,1,0:T(8,128)(2,1)S(1)} collective-permute-done((bf16[3,32,128]{2,1,0:T(8,128)(2,1)S(1)}, bf16[3,32,128]{2,1,0:T(8,128)(2,1)S(1)}, u32[]{:S(2)}, u32[]{:S(2)}) %collective-permute-start.5) | collective-permute-done | bytes 24608 | tf_op jit(solution)/shard_map/ppermute | solution.py:719
  13.6 0.0 collective-permute-start.6
  13.6 1.2 %collective-permute-done.6.swapped_late_ref = bf16[32,128]{1,0:T(8,128)(2,1)S(1)} collective-permute-done((bf16[32,128]{1,0:T(8,128)(2,1)S(1)}, bf16[32,128]{1,0:T(8,128)(2,1)S(1)}, u32[]{:S(2)}, u32[]{:S(2)}) %collective-permute-start.6) | collective-permute-done | bytes 8224 | tf_op jit(solution)/shard_map/ppermute | solution.py:766
  14.7 0.8 %collective-permute-done.4.part_refs_1_ = bf16[4,32,128]{2,1,0:T(8,128)(2,1)S(1)} collective-permute-done((bf16[4,32,128]{2,1,0:T(8,128)(2,1)S(1)}, bf16[4,32,128]{2,1,0:T(8,128)(2,1)S(1)}, u32[]{:S(2)}, u32[]{:S(2)}) %collective-permute-start.4) | collective-permute-done | bytes 32800 | tf_op jit(solution)/shard_map/ppermute | solution.py:719
  15.6 0.4 %collective-permute-done.3.part_refs_0_ = bf16[4,32,128]{2,1,0:T(8,128)(2,1)S(1)} collective-permute-done((bf16[4,32,128]{2,1,0:T(8,128)(2,1)S(1)}, bf16[4,32,128]{2,1,0:T(8,128)(2,1)S(1)}, u32[]{:S(2)}, u32[]{:S(2)}) %collective-permute-start.3) | collective-permute-done | bytes 32800 | tf_op jit(solution)/shard_map/ppermute | solution.py:719
  16.0 1.3 %finish.1 = (bf16[32,4,256]{2,1,0:T(4,128)(2,1)}, bf16[4,16,128]{2,1,0:T(8,128)(2,1)}) custom-call(bf16[2,32,128]{2,1,0:T(8,128)(2,1)S(1)} %get-tuple-element.26.right_ref, bf16[4,32,128]{2,1,0:T(8,128)(2,1)S(1)} %collective-permute-done.3.part_refs_0_, bf16[4,32,128]{2,1,0:T(8,128)(2,1)S(1)} %collective-permute-done.4.part_refs_1_, ...), custom_call_target="tpu_custom_call" | custom-call | tf_op jit(solution)/shard_map/finish/pallas_call | solution.py:770
  (6 shorter events, 0.0 us)
Async XLA Ops:
  0.6 5.6 %copy-start = (bf16[1024,128]{1,0:T(8,128)(2,1)S(1)}, bf16[1024,128]{1,0:T(8,128)(2,1)}, u32[]{:S(2)}) copy-start(bf16[1024,128]{1,0:T(8,128)(2,1)} %w_ref.1) | copy-start | bytes 786436
  0.6 1.8 %collective-permute-start = (bf16[4,16,128]{2,1,0:T(8,128)(2,1)}, bf16[4,16,128]{2,1,0:T(8,128)(2,1)S(1)}, u32[]{:S(2)}, u32[]{:S(2)}) collective-permute-start(bf16[4,16,128]{2,1,0:T(8,128)(2,1)} %cot_hbm.1), channel_id=1, source_target_pairs={{0,1},{1,0},{2,3},{3,2},{4,5},{5,4},{6,7},{7,6},{8,9},{9,8},{10,11... | collective-permute-start | bytes 49160 | tf_op jit(solution)/shard_map/ppermute | solution.py:673
  2.5 5.7 %collective-permute-start.1 = (bf16[4,32,128]{2,1,0:T(8,128)(2,1)S(1)}, bf16[4,32,128]{2,1,0:T(8,128)(2,1)S(1)}, u32[]{:S(2)}, u32[]{:S(2)}) collective-permute-start(bf16[4,32,128]{2,1,0:T(8,128)(2,1)S(1)} %pad_maximum_fusion.2), channel_id=1, source_target_pairs={{0,8},{2,10},{4,12},{6,14},{8,0},{10,2},{12,4},{14,6},{1,9},{3,11}... | collective-permute-start | bytes 98312 | tf_op jit(solution)/shard_map/ppermute | solution.py:719
  8.7 2.9 %collective-permute-start.2 = (bf16[2,32,128]{2,1,0:T(8,128)(2,1)S(1)}, bf16[2,32,128]{2,1,0:T(8,128)(2,1)S(1)}, u32[]{:S(2)}, u32[]{:S(2)}) collective-permute-start(bf16[2,32,128]{2,1,0:T(8,128)(2,1)S(1)} %get-tuple-element.28), channel_id=1, source_target_pairs={{0,1},{1,0},{2,3},{3,2},{4,5},{5,4},{6,7},{7,6},{8,9},{9,8},{10,11... | collective-permute-start | bytes 49160 | tf_op jit(solution)/shard_map/ppermute | solution.py:761
  8.8 4.8 %collective-permute-start.5 = (bf16[3,32,128]{2,1,0:T(8,128)(2,1)S(1)}, bf16[3,32,128]{2,1,0:T(8,128)(2,1)S(1)}, u32[]{:S(2)}, u32[]{:S(2)}) collective-permute-start(bf16[3,32,128]{2,1,0:T(8,128)(2,1)S(1)} %get-tuple-element.40), channel_id=1, source_target_pairs={{0,6},{2,4},{4,2},{6,0},{8,14},{10,12},{12,10},{14,8},{1,7},{3,5},... | collective-permute-start | bytes 73736 | tf_op jit(solution)/shard_map/ppermute | solution.py:719
  11.6 4.0 %collective-permute-start.4 = (bf16[4,32,128]{2,1,0:T(8,128)(2,1)S(1)}, bf16[4,32,128]{2,1,0:T(8,128)(2,1)S(1)}, u32[]{:S(2)}, u32[]{:S(2)}) collective-permute-start(bf16[4,32,128]{2,1,0:T(8,128)(2,1)S(1)} %get-tuple-element.43), channel_id=1, source_target_pairs={{0,4},{2,6},{4,0},{6,2},{8,12},{10,14},{12,8},{14,10},{1,5},{3,7},... | collective-permute-start | bytes 98312 | tf_op jit(solution)/shard_map/ppermute | solution.py:719
  12.1 3.9 %collective-permute-start.3 = (bf16[4,32,128]{2,1,0:T(8,128)(2,1)S(1)}, bf16[4,32,128]{2,1,0:T(8,128)(2,1)S(1)}, u32[]{:S(2)}, u32[]{:S(2)}) collective-permute-start(bf16[4,32,128]{2,1,0:T(8,128)(2,1)S(1)} %get-tuple-element.44), channel_id=1, source_target_pairs={{0,2},{2,0},{4,6},{6,4},{8,10},{10,8},{12,14},{14,12},{1,3},{3,1},... | collective-permute-start | bytes 98312 | tf_op jit(solution)/shard_map/ppermute | solution.py:719
  13.6 1.2 %collective-permute-start.6 = (bf16[32,128]{1,0:T(8,128)(2,1)S(1)}, bf16[32,128]{1,0:T(8,128)(2,1)S(1)}, u32[]{:S(2)}, u32[]{:S(2)}) collective-permute-start(bf16[32,128]{1,0:T(8,128)(2,1)S(1)} %fusion), channel_id=1, source_target_pairs={{0,1},{1,0},{2,3},{3,2},{4,5},{5,4},{6,7},{7,6},{8,9},{9,8},{10,11... | collective-permute-start | bytes 24584 | tf_op jit(solution)/shard_map/ppermute | solution.py:766

commit v26 on v25

--- a/solution.py
+++ b/solution.py
@@ -34,17 +34,17 @@
 
 
 def exchange_blocks(pieces, width):
-    first, second, third, fourth = pieces
-    blocks = lane_block(first.shape, width)
-    odd, high = blocks % 2 == 1, blocks >= 2
-    roll = lambda value, count: pltpu.roll(value, count * width, 1)
-    first, second = jnp.where(odd, roll(second, 1), first), jnp.where(odd, second, roll(first, 3))
-    third, fourth = jnp.where(odd, roll(fourth, 1), third), jnp.where(odd, fourth, roll(third, 3))
+    count = len(pieces)
+    blocks = lane_block(pieces[0].shape, width)
     return [
-        jnp.where(high, roll(third, 2), first),
-        jnp.where(high, roll(fourth, 2), second),
-        jnp.where(high, third, roll(first, 2)),
-        jnp.where(high, fourth, roll(second, 2)),
+        pick(
+            blocks,
+            [
+                pltpu.roll(piece, width * ((e - i) % count), 1) if e != i else piece
+                for e, piece in enumerate(pieces)
+            ],
+        )
+        for i in range(count)
     ]
 
 
@@ -598,7 +598,8 @@
             ]
     gained = jnp.concatenate([lines_ref[tile, 0:rows, :] for tile in tiles], axis=1) * gain_ref[...]
     normed = normed_ref[...]
-    grad = inv_std_ref[:, 0:1] * (
+    inv_std = jnp.concatenate([inv_std_ref[...]] * len(tiles), axis=1)
+    grad = inv_std * (
         gained
         - jnp.mean(gained, axis=-1, keepdims=True)
         - normed * jnp.mean(gained * normed, axis=-1, keepdims=True)

time: 17.5 us -> 17.5 us (level)
  transfers between devices with their start and end apart: 7 -> 7, of which waited for: 5 -> 5; matrix products, arithmetic and copies ran while one was open for 0% -> 0% of each run, Pallas kernels for 14% -> 15%
where the time goes in v26:
time: 17.5 us; the launch traced here: 17.4 us
  starting transfers between devices  8.81 us (50%)
  Pallas kernels  4.34 us (25%)
  waiting for transfers between devices  3.44 us (20%)
  between operations  0.72 us (4%)
    ppermute x4, starting transfers between devices, swap_over(): lax.ppermute(value, 'res', [(source, source ^ mask) for source in range(r...  8.22 us
    ppermute x4, waiting for transfers between devices, swap_over(): lax.ppermute(value, 'res', [(source, source ^ mask) for source in range(r...  2.27 us
    pallas_call x1, Pallas kernels, small_slice(): pl.pallas_call(functools.partial(small_finish_kernel, scale), in_specs=[v...  1.34 us
    pallas_call x1, Pallas kernels, small_slice(): pl.pallas_call(small_project_kernel, in_specs=[hbm] * 9, out_specs=[vmem]...  1.3 us
    pallas_call x1, Pallas kernels, small_slice(): pl.pallas_call(functools.partial(small_own_kernel, scale), in_specs=[vmem...  1.25 us
    ppermute x1, waiting for transfers between devices, small_slice(): lax.ppermute(jnp.where(own_is_near, diagonal[1], diagonal[0]), 'seq', swap)  1.17 us
    ppermute x1, starting transfers between devices, small_slice(): other_cot = lax.ppermute(coupling_cotangent, 'seq', swap)  0.52 us
    pallas_call x1, Pallas kernels, small_slice(): pl.pallas_call(functools.partial(small_partner_kernel, residues), in_spec...  0.45 us
  transfers between devices with their start and end apart: 7, of which 5 were waited for; matrix products, arithmetic and copies ran while one was open for 0% of the time, Pallas kernels for 15%

profile of v26, /device:TPU:0, one launch (start us, length us, event | category | flops | bytes accessed | tf_op | source)
XLA Modules:
  0.0 17.4 jit_solution(17485810137766545306)
XLA Ops:
  0.6 0.0 copy-start
  0.6 0.5 %collective-permute-start = (bf16[4,16,128]{2,1,0:T(8,128)(2,1)}, bf16[4,16,128]{2,1,0:T(8,128)(2,1)S(1)}, u32[]{:S(2)}, u32[]{:S(2)}) collective-permute-start(bf16[4,16,128]{2,1,0:T(8,128)(2,1)} %cot_hbm.1), channel_id=1, source_target_pairs={{0,1},{1,0},{2,3},{3,2},{4,5},{5,4},{6,7},{7,6},{8,9},{9,8},{10,11... | collective-permute-start | bytes 49160 | tf_op jit(solution)/shard_map/ppermute | solution.py:674
  1.2 1.3 %project.1 = (bf16[2,32,128]{2,1,0:T(8,128)(2,1)S(1)}, f32[128,256]{1,0:T(8,128)S(1)}, f32[128,128]{1,0:T(8,128)S(1)}, bf16[256,256]{1,0:T(8,128)(2,1)S(1)}, f32...) custom-call(bf16[32,4,256]{2,1,0:T(4,128)(2,1)} %x_hbm.1, f32[1,256]{1,0:T(1,128)} %bitcast.19, ...), custom_call_target="tpu_custom_call" | custom-call | tf_op jit(solution)/shard_map/project/pallas_call | solution.py:677
  2.5 0.0 collective-permute-done.other_ref
  2.5 3.7 %collective-permute-start.1 = (bf16[4,32,128]{2,1,0:T(8,128)(2,1)S(1)}, bf16[4,32,128]{2,1,0:T(8,128)(2,1)S(1)}, u32[]{:S(2)}, u32[]{:S(2)}) collective-permute-start(bf16[4,32,128]{2,1,0:T(8,128)(2,1)S(1)} %pad_maximum_fusion.2), channel_id=1, source_target_pairs={{0,8},{2,10},{4,12},{6,14},{8,0},{10,2},{12,4},{14,6},{1,9},{3,11}... | collective-permute-start | bytes 98312 | tf_op jit(solution)/shard_map/ppermute | solution.py:720
  6.2 0.0 copy-done
  6.2 1.3 %own_pieces.1 = (f32[4,32,128]{2,1,0:T(8,128)S(1)}, bf16[512,128]{1,0:T(8,128)(2,1)S(1)}, bf16[512,128]{1,0:T(8,128)(2,1)S(1)}, bf16[1024,128]{1,0:T(8,128)(2,1)...) custom-call(bf16[4,16,128]{2,1,0:T(8,128)(2,1)S(1)} %get-tuple-element.22.own_ref, ...), custom_call_target="tpu_custom_call" | custom-call | tf_op jit(solution)/shard_map/own_pieces/pallas_call | solution.py:728
  7.5 0.7 %collective-permute-done.1.got_ref = bf16[4,32,128]{2,1,0:T(8,128)(2,1)S(1)} collective-permute-done((bf16[4,32,128]{2,1,0:T(8,128)(2,1)S(1)}, bf16[4,32,128]{2,1,0:T(8,128)(2,1)S(1)}, u32[]{:S(2)}, u32[]{:S(2)}) %collective-permute-start.1) | collective-permute-done | bytes 32800 | tf_op jit(solution)/shard_map/ppermute | solution.py:720
  8.2 0.4 %partner_pieces.1 = (bf16[4,3,32,128]{3,2,1,0:T(8,128)(2,1)S(1)}, f32[4,32,128]{2,1,0:T(8,128)S(1)}, bf16[2,32,128]{2,1,0:T(8,128)(2,1)S(1)}, bf16[2,32,128]{2,1,0:T(8,128)(2,1)S(1)}) custom-call(bf16[4,32,128]{2,1,0:T(8,128)(2,1)S(1)} %collective-permute-done.1.got_ref, bf16[128,1024]{1,0:T(8,128)(2,1)S(1)} %get-tuple-element.24.sorted_wt_ref, ...), custom_call_target="tpu_custom_call" | custom-call | tf_op jit(solution)/shard_map/partner_pieces/pallas_call | solution.py:748
  8.7 0.1 collective-permute-start.2
  8.8 2.8 %collective-permute-start.5 = (bf16[3,32,128]{2,1,0:T(8,128)(2,1)S(1)}, bf16[3,32,128]{2,1,0:T(8,128)(2,1)S(1)}, u32[]{:S(2)}, u32[]{:S(2)}) collective-permute-start(bf16[3,32,128]{2,1,0:T(8,128)(2,1)S(1)} %get-tuple-element.40), channel_id=1, source_target_pairs={{0,6},{2,4},{4,2},{6,0},{8,14},{10,12},{12,10},{14,8},{1,7},{3,5},... | collective-permute-start | bytes 73736 | tf_op jit(solution)/shard_map/ppermute | solution.py:720
  11.6 0.0 collective-permute-done.2.swapped_ref
  11.6 0.5 %collective-permute-start.4 = (bf16[4,32,128]{2,1,0:T(8,128)(2,1)S(1)}, bf16[4,32,128]{2,1,0:T(8,128)(2,1)S(1)}, u32[]{:S(2)}, u32[]{:S(2)}) collective-permute-start(bf16[4,32,128]{2,1,0:T(8,128)(2,1)S(1)} %get-tuple-element.43), channel_id=1, source_target_pairs={{0,4},{2,6},{4,0},{6,2},{8,12},{10,14},{12,8},{14,10},{1,5},{3,7},... | collective-permute-start | bytes 98312 | tf_op jit(solution)/shard_map/ppermute | solution.py:720
  12.1 1.2 %collective-permute-start.3 = (bf16[4,32,128]{2,1,0:T(8,128)(2,1)S(1)}, bf16[4,32,128]{2,1,0:T(8,128)(2,1)S(1)}, u32[]{:S(2)}, u32[]{:S(2)}) collective-permute-start(bf16[4,32,128]{2,1,0:T(8,128)(2,1)S(1)} %get-tuple-element.44), channel_id=1, source_target_pairs={{0,2},{2,0},{4,6},{6,4},{8,10},{10,8},{12,14},{14,12},{1,3},{3,1},... | collective-permute-start | bytes 98312 | tf_op jit(solution)/shard_map/ppermute | solution.py:720
  13.3 0.3 %collective-permute-done.5.part_refs_2_ = bf16[3,32,128]{2,1,0:T(8,128)(2,1)S(1)} collective-permute-done((bf16[3,32,128]{2,1,0:T(8,128)(2,1)S(1)}, bf16[3,32,128]{2,1,0:T(8,128)(2,1)S(1)}, u32[]{:S(2)}, u32[]{:S(2)}) %collective-permute-start.5) | collective-permute-done | bytes 24608 | tf_op jit(solution)/shard_map/ppermute | solution.py:720
  13.6 0.0 collective-permute-start.6
  13.6 1.2 %collective-permute-done.6.swapped_late_ref = bf16[32,128]{1,0:T(8,128)(2,1)S(1)} collective-permute-done((bf16[32,128]{1,0:T(8,128)(2,1)S(1)}, bf16[32,128]{1,0:T(8,128)(2,1)S(1)}, u32[]{:S(2)}, u32[]{:S(2)}) %collective-permute-start.6) | collective-permute-done | bytes 8224 | tf_op jit(solution)/shard_map/ppermute | solution.py:767
  14.7 0.8 %collective-permute-done.4.part_refs_1_ = bf16[4,32,128]{2,1,0:T(8,128)(2,1)S(1)} collective-permute-done((bf16[4,32,128]{2,1,0:T(8,128)(2,1)S(1)}, bf16[4,32,128]{2,1,0:T(8,128)(2,1)S(1)}, u32[]{:S(2)}, u32[]{:S(2)}) %collective-permute-start.4) | collective-permute-done | bytes 32800 | tf_op jit(solution)/shard_map/ppermute | solution.py:720
  15.6 0.4 %collective-permute-done.3.part_refs_0_ = bf16[4,32,128]{2,1,0:T(8,128)(2,1)S(1)} collective-permute-done((bf16[4,32,128]{2,1,0:T(8,128)(2,1)S(1)}, bf16[4,32,128]{2,1,0:T(8,128)(2,1)S(1)}, u32[]{:S(2)}, u32[]{:S(2)}) %collective-permute-start.3) | collective-permute-done | bytes 32800 | tf_op jit(solution)/shard_map/ppermute | solution.py:720
  16.0 1.3 %finish.1 = (bf16[32,4,256]{2,1,0:T(4,128)(2,1)}, bf16[4,16,128]{2,1,0:T(8,128)(2,1)}) custom-call(bf16[2,32,128]{2,1,0:T(8,128)(2,1)S(1)} %get-tuple-element.26.right_ref, bf16[4,32,128]{2,1,0:T(8,128)(2,1)S(1)} %collective-permute-done.3.part_refs_0_, bf16[4,32,128]{2,1,0:T(8,128)(2,1)S(1)} %collective-permute-done.4.part_refs_1_, ...), custom_call_target="tpu_custom_call" | custom-call | tf_op jit(solution)/shard_map/finish/pallas_call | solution.py:771
  (6 shorter events, 0.0 us)
Async XLA Ops:
  0.6 5.6 %copy-start = (bf16[1024,128]{1,0:T(8,128)(2,1)S(1)}, bf16[1024,128]{1,0:T(8,128)(2,1)}, u32[]{:S(2)}) copy-start(bf16[1024,128]{1,0:T(8,128)(2,1)} %w_ref.1) | copy-start | bytes 786436
  0.6 1.8 %collective-permute-start = (bf16[4,16,128]{2,1,0:T(8,128)(2,1)}, bf16[4,16,128]{2,1,0:T(8,128)(2,1)S(1)}, u32[]{:S(2)}, u32[]{:S(2)}) collective-permute-start(bf16[4,16,128]{2,1,0:T(8,128)(2,1)} %cot_hbm.1), channel_id=1, source_target_pairs={{0,1},{1,0},{2,3},{3,2},{4,5},{5,4},{6,7},{7,6},{8,9},{9,8},{10,11... | collective-permute-start | bytes 49160 | tf_op jit(solution)/shard_map/ppermute | solution.py:674
  2.5 5.7 %collective-permute-start.1 = (bf16[4,32,128]{2,1,0:T(8,128)(2,1)S(1)}, bf16[4,32,128]{2,1,0:T(8,128)(2,1)S(1)}, u32[]{:S(2)}, u32[]{:S(2)}) collective-permute-start(bf16[4,32,128]{2,1,0:T(8,128)(2,1)S(1)} %pad_maximum_fusion.2), channel_id=1, source_target_pairs={{0,8},{2,10},{4,12},{6,14},{8,0},{10,2},{12,4},{14,6},{1,9},{3,11}... | collective-permute-start | bytes 98312 | tf_op jit(solution)/shard_map/ppermute | solution.py:720
  8.7 2.9 %collective-permute-start.2 = (bf16[2,32,128]{2,1,0:T(8,128)(2,1)S(1)}, bf16[2,32,128]{2,1,0:T(8,128)(2,1)S(1)}, u32[]{:S(2)}, u32[]{:S(2)}) collective-permute-start(bf16[2,32,128]{2,1,0:T(8,128)(2,1)S(1)} %get-tuple-element.28), channel_id=1, source_target_pairs={{0,1},{1,0},{2,3},{3,2},{4,5},{5,4},{6,7},{7,6},{8,9},{9,8},{10,11... | collective-permute-start | bytes 49160 | tf_op jit(solution)/shard_map/ppermute | solution.py:762
  8.8 4.8 %collective-permute-start.5 = (bf16[3,32,128]{2,1,0:T(8,128)(2,1)S(1)}, bf16[3,32,128]{2,1,0:T(8,128)(2,1)S(1)}, u32[]{:S(2)}, u32[]{:S(2)}) collective-permute-start(bf16[3,32,128]{2,1,0:T(8,128)(2,1)S(1)} %get-tuple-element.40), channel_id=1, source_target_pairs={{0,6},{2,4},{4,2},{6,0},{8,14},{10,12},{12,10},{14,8},{1,7},{3,5},... | collective-permute-start | bytes 73736 | tf_op jit(solution)/shard_map/ppermute | solution.py:720
  11.6 4.0 %collective-permute-start.4 = (bf16[4,32,128]{2,1,0:T(8,128)(2,1)S(1)}, bf16[4,32,128]{2,1,0:T(8,128)(2,1)S(1)}, u32[]{:S(2)}, u32[]{:S(2)}) collective-permute-start(bf16[4,32,128]{2,1,0:T(8,128)(2,1)S(1)} %get-tuple-element.43), channel_id=1, source_target_pairs={{0,4},{2,6},{4,0},{6,2},{8,12},{10,14},{12,8},{14,10},{1,5},{3,7},... | collective-permute-start | bytes 98312 | tf_op jit(solution)/shard_map/ppermute | solution.py:720
  12.1 3.9 %collective-permute-start.3 = (bf16[4,32,128]{2,1,0:T(8,128)(2,1)S(1)}, bf16[4,32,128]{2,1,0:T(8,128)(2,1)S(1)}, u32[]{:S(2)}, u32[]{:S(2)}) collective-permute-start(bf16[4,32,128]{2,1,0:T(8,128)(2,1)S(1)} %get-tuple-element.44), channel_id=1, source_target_pairs={{0,2},{2,0},{4,6},{6,4},{8,10},{10,8},{12,14},{14,12},{1,3},{3,1},... | collective-permute-start | bytes 98312 | tf_op jit(solution)/shard_map/ppermute | solution.py:720
  13.6 1.2 %collective-permute-start.6 = (bf16[32,128]{1,0:T(8,128)(2,1)S(1)}, bf16[32,128]{1,0:T(8,128)(2,1)S(1)}, u32[]{:S(2)}, u32[]{:S(2)}) collective-permute-start(bf16[32,128]{1,0:T(8,128)(2,1)S(1)} %fusion), channel_id=1, source_target_pairs={{0,1},{1,0},{2,3},{3,2},{4,5},{5,4},{6,7},{7,6},{8,9},{9,8},{10,11... | collective-permute-start | bytes 24584 | tf_op jit(solution)/shard_map/ppermute | solution.py:767

commit v27 on v25

--- a/solution.py
+++ b/solution.py
@@ -520,7 +520,7 @@
 
 
 def small_partner_kernel(residues, got_ref, sorted_wt_ref, keep_ref, both_ref,
-                         leaving_ref, keep_out_ref, right_ref, swap_ref):
+                         leaving_ref, keep_out_ref, right_ref):
     rank = lax.axis_index("res")
     seqs = got_ref.shape[1]
     cot = got_ref[2:4].reshape(2 * seqs, LANES)
@@ -528,9 +528,6 @@
     pieces = column_pieces(got_ref[0], outer, residues)
     right_ref[0] = both_ref[1]
     right_ref[1] = got_ref[1]
-    own_is_near = lax.axis_index("seq") == lax.shift_right_logical(rank, 2)
-    swap_ref[0] = jnp.where(own_is_near, got_ref[1], both_ref[1])
-    swap_ref[1] = both_ref[0]
     for place, piece in enumerate(pieces):
         distance = lax.bitwise_xor(rank & 3, place)
         total = keep_ref[place] + piece
@@ -546,6 +543,7 @@
     keep_ref, normed_ref, inv_std_ref, gain_ref, spread_w_ref, columns_w_ref, sorted_w_ref, offset_ref,
     grad_hbm, pair_hbm, grad_ref, pair_ref, near_ref, beyond_ref, turn_ref, lines_ref, semaphores,
 ):
+    part_refs = [part_refs[1], part_refs[0], part_refs[2]]
     seqs, residues, _ = grad_ref.shape
     columns = pair_ref.shape[1]
     depth = LANES // residues
@@ -744,24 +742,25 @@
         name="own_pieces",
     )(own_cot, other_cot, coupling_matrix, both, spread_w)
 
-    leaving_parts, keep, right, leaving = pl.pallas_call(
+    needed = jnp.where(own_is_near, beyond_two[1], both[1])
+    swapped = lax.ppermute(jnp.stack([needed, both[0]]), "seq", swap)
+
+    leaving_parts, keep, right = pl.pallas_call(
         functools.partial(small_partner_kernel, residues),
         in_specs=[vmem] * 4,
-        out_specs=[vmem] * 4,
+        out_specs=[vmem] * 3,
         out_shape=(
             like((ranks // 2, 3, seqs, LANES), BF16),
             like((ranks // 2, seqs, LANES), F32),
-            like((2, seqs, LANES), BF16),
             like((2, seqs, LANES), BF16),
         ),
         compiler_params=limit,
         name="partner_pieces",
     )(beyond_two, sorted_wt, keep, both)
 
-    swapped = lax.ppermute(leaving, "seq", swap)
     diagonal = swap_over(3, leaving_parts[3])
-    across, beside = [
-        swap_over(mask, jnp.concatenate([leaving_parts[mask], swapped[0:1]])) for mask in (2, 1)
+    beside, across = [
+        swap_over(mask, jnp.concatenate([leaving_parts[mask], swapped[0:1]])) for mask in (1, 2)
     ]
     swapped_late = lax.ppermute(
         jnp.where(own_is_near, diagonal[1], diagonal[0]), "seq", swap
@@ -788,7 +787,7 @@
         name="finish",
     )(
         right,
-        [beside, across, diagonal],
+        [across, beside, diagonal],
         swapped,
         swapped_late,
         both,

time: 17.5 us -> 17.5 us (level)
  starting transfers between devices: 8.81 us -> 8.35 us
  waiting for transfers between devices: 3.53 us -> 3.99 us
    ppermute x4, waiting for transfers between devices: 2.36 us -> 2.82 us  [swap_over(): lax.ppermute(value, 'res', [(source, source ^ mask) for source in range(r...]
    ppermute x4, starting transfers between devices: 8.22 us -> 7.76 us  [swap_over(): lax.ppermute(value, 'res', [(source, source ^ mask) for source in range(r...]
  transfers between devices with their start and end apart: 7 -> 7, of which waited for: 5 -> 5; matrix products, arithmetic and copies ran while one was open for 0% -> 0% of each run, Pallas kernels for 14% -> 17%
where the time goes in v27:
time: 17.5 us; the launch traced here: 17.4 us
  starting transfers between devices  8.35 us (48%)
  Pallas kernels  4.24 us (24%)
  waiting for transfers between devices  3.99 us (23%)
  between operations  0.72 us (4%)
    ppermute x4, starting transfers between devices, swap_over(): lax.ppermute(value, 'res', [(source, source ^ mask) for source in range(r...  7.76 us
    ppermute x4, waiting for transfers between devices, swap_over(): lax.ppermute(value, 'res', [(source, source ^ mask) for source in range(r...  2.82 us
    pallas_call x1, Pallas kernels, small_slice(): pl.pallas_call(functools.partial(small_finish_kernel, scale), in_specs=[v...  1.33 us
    pallas_call x1, Pallas kernels, small_slice(): pl.pallas_call(small_project_kernel, in_specs=[hbm] * 9, out_specs=[vmem]...  1.3 us
    ppermute x1, waiting for transfers between devices, small_slice(): lax.ppermute(jnp.where(own_is_near, diagonal[1], diagonal[0]), 'seq', swap)  1.17 us
    pallas_call x1, Pallas kernels, small_slice(): pl.pallas_call(functools.partial(small_own_kernel, scale), in_specs=[vmem...  1.16 us
    ppermute x1, starting transfers between devices, small_slice(): other_cot = lax.ppermute(coupling_cotangent, 'seq', swap)  0.52 us
    pallas_call x1, Pallas kernels, small_slice(): pl.pallas_call(functools.partial(small_partner_kernel, residues), in_spec...  0.45 us
  transfers between devices with their start and end apart: 7, of which 5 were waited for; matrix products, arithmetic and copies ran while one was open for 0% of the time, Pallas kernels for 17%

profile of v27, /device:TPU:0, one launch (start us, length us, event | category | flops | bytes accessed | tf_op | source)
XLA Modules:
  0.0 17.4 jit_solution(11764647860486127186)
XLA Ops:
  0.6 0.0 copy-start
  0.6 0.5 %collective-permute-start = (bf16[4,16,128]{2,1,0:T(8,128)(2,1)}, bf16[4,16,128]{2,1,0:T(8,128)(2,1)S(1)}, u32[]{:S(2)}, u32[]{:S(2)}) collective-permute-start(bf16[4,16,128]{2,1,0:T(8,128)(2,1)} %cot_hbm.1), channel_id=1, source_target_pairs={{0,1},{1,0},{2,3},{3,2},{4,5},{5,4},{6,7},{7,6},{8,9},{9,8},{10,11... | collective-permute-start | bytes 49160 | tf_op jit(solution)/shard_map/ppermute | solution.py:671
  1.2 1.3 %project.1 = (bf16[2,32,128]{2,1,0:T(8,128)(2,1)S(1)}, f32[128,256]{1,0:T(8,128)S(1)}, f32[128,128]{1,0:T(8,128)S(1)}, bf16[256,256]{1,0:T(8,128)(2,1)S(1)}, f32...) custom-call(bf16[32,4,256]{2,1,0:T(4,128)(2,1)} %x_hbm.1, f32[1,256]{1,0:T(1,128)} %bitcast.19, ...), custom_call_target="tpu_custom_call" | custom-call | tf_op jit(solution)/shard_map/project/pallas_call | solution.py:674
  2.5 0.0 collective-permute-done.other_ref
  2.5 3.7 %collective-permute-start.1 = (bf16[4,32,128]{2,1,0:T(8,128)(2,1)S(1)}, bf16[4,32,128]{2,1,0:T(8,128)(2,1)S(1)}, u32[]{:S(2)}, u32[]{:S(2)}) collective-permute-start(bf16[4,32,128]{2,1,0:T(8,128)(2,1)S(1)} %pad_maximum_fusion.2), channel_id=1, source_target_pairs={{0,8},{2,10},{4,12},{6,14},{8,0},{10,2},{12,4},{14,6},{1,9},{3,11}... | collective-permute-start | bytes 98312 | tf_op jit(solution)/shard_map/ppermute | solution.py:717
  6.2 0.0 copy-done
  6.2 1.2 %own_pieces.1 = (f32[4,32,128]{2,1,0:T(8,128)S(1)}, bf16[512,128]{1,0:T(8,128)(2,1)S(1)}, bf16[512,128]{1,0:T(8,128)(2,1)S(1)}, bf16[1024,128]{1,0:T(8,128)(2,1)...) custom-call(bf16[4,16,128]{2,1,0:T(8,128)(2,1)S(1)} %get-tuple-element.21.own_ref, ...), custom_call_target="tpu_custom_call" | custom-call | tf_op jit(solution)/shard_map/own_pieces/pallas_call | solution.py:725
  7.4 0.8 %collective-permute-done.1.got_ref = bf16[4,32,128]{2,1,0:T(8,128)(2,1)S(1)} collective-permute-done((bf16[4,32,128]{2,1,0:T(8,128)(2,1)S(1)}, bf16[4,32,128]{2,1,0:T(8,128)(2,1)S(1)}, u32[]{:S(2)}, u32[]{:S(2)}) %collective-permute-start.1) | collective-permute-done | bytes 32800 | tf_op jit(solution)/shard_map/ppermute | solution.py:717
  8.2 0.1 collective-permute-start.2
  8.3 0.5 %partner_pieces.1 = (bf16[4,3,32,128]{3,2,1,0:T(8,128)(2,1)S(1)}, f32[4,32,128]{2,1,0:T(8,128)S(1)}, bf16[2,32,128]{2,1,0:T(8,128)(2,1)S(1)}) custom-call(bf16[4,32,128]{2,1,0:T(8,128)(2,1)S(1)} %collective-permute-done.1.got_ref, bf16[128,1024]{1,0:T(8,128)(2,1)S(1)} %get-tuple-element.23.sorted_wt_ref, f32[4,32,128]{2,1,0:T(8,128)S(1)} %get-tuple-element.24.keep_ref, ...), custom_call_target="tpu_custom_call" | custom-call | tf_op jit(solution)/shard_map/partner_pieces/pallas_call | solution.py:748
  8.8 2.8 %collective-permute-start.5 = (bf16[3,32,128]{2,1,0:T(8,128)(2,1)S(1)}, bf16[3,32,128]{2,1,0:T(8,128)(2,1)S(1)}, u32[]{:S(2)}, u32[]{:S(2)}) collective-permute-start(bf16[3,32,128]{2,1,0:T(8,128)(2,1)S(1)} %get-tuple-element.38), channel_id=1, source_target_pairs={{0,6},{2,4},{4,2},{6,0},{8,14},{10,12},{12,10},{14,8},{1,7},{3,5},... | collective-permute-start | bytes 73736 | tf_op jit(solution)/shard_map/ppermute | solution.py:717
  11.6 0.0 collective-permute-done.2.swapped_ref
  11.6 0.5 %collective-permute-start.3 = (bf16[4,32,128]{2,1,0:T(8,128)(2,1)S(1)}, bf16[4,32,128]{2,1,0:T(8,128)(2,1)S(1)}, u32[]{:S(2)}, u32[]{:S(2)}) collective-permute-start(bf16[4,32,128]{2,1,0:T(8,128)(2,1)S(1)} %get-tuple-element.44), channel_id=1, source_target_pairs={{0,4},{2,6},{4,0},{6,2},{8,12},{10,14},{12,8},{14,10},{1,5},{3,7},... | collective-permute-start | bytes 98312 | tf_op jit(solution)/shard_map/ppermute | solution.py:717
  12.1 0.7 %collective-permute-start.4 = (bf16[4,32,128]{2,1,0:T(8,128)(2,1)S(1)}, bf16[4,32,128]{2,1,0:T(8,128)(2,1)S(1)}, u32[]{:S(2)}, u32[]{:S(2)}) collective-permute-start(bf16[4,32,128]{2,1,0:T(8,128)(2,1)S(1)} %get-tuple-element.43), channel_id=1, source_target_pairs={{0,2},{2,0},{4,6},{6,4},{8,10},{10,8},{12,14},{14,12},{1,3},{3,1},... | collective-permute-start | bytes 98312 | tf_op jit(solution)/shard_map/ppermute | solution.py:717
  12.9 0.7 %collective-permute-done.5.part_refs_2_ = bf16[3,32,128]{2,1,0:T(8,128)(2,1)S(1)} collective-permute-done((bf16[3,32,128]{2,1,0:T(8,128)(2,1)S(1)}, bf16[3,32,128]{2,1,0:T(8,128)(2,1)S(1)}, u32[]{:S(2)}, u32[]{:S(2)}) %collective-permute-start.5) | collective-permute-done | bytes 24608 | tf_op jit(solution)/shard_map/ppermute | solution.py:717
  13.6 0.0 collective-permute-start.6
  13.6 1.2 %collective-permute-done.6.swapped_late_ref = bf16[32,128]{1,0:T(8,128)(2,1)S(1)} collective-permute-done((bf16[32,128]{1,0:T(8,128)(2,1)S(1)}, bf16[32,128]{1,0:T(8,128)(2,1)S(1)}, u32[]{:S(2)}, u32[]{:S(2)}) %collective-permute-start.6) | collective-permute-done | bytes 8224 | tf_op jit(solution)/shard_map/ppermute | solution.py:765
  14.8 0.8 %collective-permute-done.3.part_refs_0_ = bf16[4,32,128]{2,1,0:T(8,128)(2,1)S(1)} collective-permute-done((bf16[4,32,128]{2,1,0:T(8,128)(2,1)S(1)}, bf16[4,32,128]{2,1,0:T(8,128)(2,1)S(1)}, u32[]{:S(2)}, u32[]{:S(2)}) %collective-permute-start.3) | collective-permute-done | bytes 32800 | tf_op jit(solution)/shard_map/ppermute | solution.py:717
  15.6 0.4 %collective-permute-done.4.part_refs_1_ = bf16[4,32,128]{2,1,0:T(8,128)(2,1)S(1)} collective-permute-done((bf16[4,32,128]{2,1,0:T(8,128)(2,1)S(1)}, bf16[4,32,128]{2,1,0:T(8,128)(2,1)S(1)}, u32[]{:S(2)}, u32[]{:S(2)}) %collective-permute-start.4) | collective-permute-done | bytes 32800 | tf_op jit(solution)/shard_map/ppermute | solution.py:717
  16.0 1.3 %finish.1 = (bf16[32,4,256]{2,1,0:T(4,128)(2,1)}, bf16[4,16,128]{2,1,0:T(8,128)(2,1)}) custom-call(bf16[2,32,128]{2,1,0:T(8,128)(2,1)S(1)} %get-tuple-element.25.right_ref, bf16[4,32,128]{2,1,0:T(8,128)(2,1)S(1)} %collective-permute-done.3.part_refs_0_, bf16[4,32,128]{2,1,0:T(8,128)(2,1)S(1)} %collective-permute-done.4.part_refs_1_, ...), custom_call_target="tpu_custom_call" | custom-call | tf_op jit(solution)/shard_map/finish/pallas_call | solution.py:769
  (8 shorter events, 0.0 us)
Async XLA Ops:
  0.6 5.6 %copy-start = (bf16[1024,128]{1,0:T(8,128)(2,1)S(1)}, bf16[1024,128]{1,0:T(8,128)(2,1)}, u32[]{:S(2)}) copy-start(bf16[1024,128]{1,0:T(8,128)(2,1)} %w_ref.1) | copy-start | bytes 786436
  0.6 1.8 %collective-permute-start = (bf16[4,16,128]{2,1,0:T(8,128)(2,1)}, bf16[4,16,128]{2,1,0:T(8,128)(2,1)S(1)}, u32[]{:S(2)}, u32[]{:S(2)}) collective-permute-start(bf16[4,16,128]{2,1,0:T(8,128)(2,1)} %cot_hbm.1), channel_id=1, source_target_pairs={{0,1},{1,0},{2,3},{3,2},{4,5},{5,4},{6,7},{7,6},{8,9},{9,8},{10,11... | collective-permute-start | bytes 49160 | tf_op jit(solution)/shard_map/ppermute | solution.py:671
  2.5 5.7 %collective-permute-start.1 = (bf16[4,32,128]{2,1,0:T(8,128)(2,1)S(1)}, bf16[4,32,128]{2,1,0:T(8,128)(2,1)S(1)}, u32[]{:S(2)}, u32[]{:S(2)}) collective-permute-start(bf16[4,32,128]{2,1,0:T(8,128)(2,1)S(1)} %pad_maximum_fusion.2), channel_id=1, source_target_pairs={{0,8},{2,10},{4,12},{6,14},{8,0},{10,2},{12,4},{14,6},{1,9},{3,11}... | collective-permute-start | bytes 98312 | tf_op jit(solution)/shard_map/ppermute | solution.py:717
  8.2 3.3 %collective-permute-start.2 = (bf16[2,32,128]{2,1,0:T(8,128)(2,1)S(1)}, bf16[2,32,128]{2,1,0:T(8,128)(2,1)S(1)}, u32[]{:S(2)}, u32[]{:S(2)}) collective-permute-start(bf16[2,32,128]{2,1,0:T(8,128)(2,1)S(1)} %pad_maximum_fusion.3), channel_id=1, source_target_pairs={{0,1},{1,0},{2,3},{3,2},{4,5},{5,4},{6,7},{7,6},{8,9},{9,8},{10,11... | collective-permute-start | bytes 49160 | tf_op jit(solution)/shard_map/ppermute | solution.py:746
  8.8 4.8 %collective-permute-start.5 = (bf16[3,32,128]{2,1,0:T(8,128)(2,1)S(1)}, bf16[3,32,128]{2,1,0:T(8,128)(2,1)S(1)}, u32[]{:S(2)}, u32[]{:S(2)}) collective-permute-start(bf16[3,32,128]{2,1,0:T(8,128)(2,1)S(1)} %get-tuple-element.38), channel_id=1, source_target_pairs={{0,6},{2,4},{4,2},{6,0},{8,14},{10,12},{12,10},{14,8},{1,7},{3,5},... | collective-permute-start | bytes 73736 | tf_op jit(solution)/shard_map/ppermute | solution.py:717
  11.6 4.0 %collective-permute-start.3 = (bf16[4,32,128]{2,1,0:T(8,128)(2,1)S(1)}, bf16[4,32,128]{2,1,0:T(8,128)(2,1)S(1)}, u32[]{:S(2)}, u32[]{:S(2)}) collective-permute-start(bf16[4,32,128]{2,1,0:T(8,128)(2,1)S(1)} %get-tuple-element.44), channel_id=1, source_target_pairs={{0,4},{2,6},{4,0},{6,2},{8,12},{10,14},{12,8},{14,10},{1,5},{3,7},... | collective-permute-start | bytes 98312 | tf_op jit(solution)/shard_map/ppermute | solution.py:717
  12.1 3.9 %collective-permute-start.4 = (bf16[4,32,128]{2,1,0:T(8,128)(2,1)S(1)}, bf16[4,32,128]{2,1,0:T(8,128)(2,1)S(1)}, u32[]{:S(2)}, u32[]{:S(2)}) collective-permute-start(bf16[4,32,128]{2,1,0:T(8,128)(2,1)S(1)} %get-tuple-element.43), channel_id=1, source_target_pairs={{0,2},{2,0},{4,6},{6,4},{8,10},{10,8},{12,14},{14,12},{1,3},{3,1},... | collective-permute-start | bytes 98312 | tf_op jit(solution)/shard_map/ppermute | solution.py:717
  13.6 1.2 %collective-permute-start.6 = (bf16[32,128]{1,0:T(8,128)(2,1)S(1)}, bf16[32,128]{1,0:T(8,128)(2,1)S(1)}, u32[]{:S(2)}, u32[]{:S(2)}) collective-permute-start(bf16[32,128]{1,0:T(8,128)(2,1)S(1)} %fusion), channel_id=1, source_target_pairs={{0,1},{1,0},{2,3},{3,2},{4,5},{5,4},{6,7},{7,6},{8,9},{9,8},{10,11... | collective-permute-start | bytes 24584 | tf_op jit(solution)/shard_map/ppermute | solution.py:765

commit v28 on v27

--- a/solution.py
+++ b/solution.py
@@ -543,7 +543,6 @@
     keep_ref, normed_ref, inv_std_ref, gain_ref, spread_w_ref, columns_w_ref, sorted_w_ref, offset_ref,
     grad_hbm, pair_hbm, grad_ref, pair_ref, near_ref, beyond_ref, turn_ref, lines_ref, semaphores,
 ):
-    part_refs = [part_refs[1], part_refs[0], part_refs[2]]
     seqs, residues, _ = grad_ref.shape
     columns = pair_ref.shape[1]
     depth = LANES // residues
@@ -787,7 +786,7 @@
         name="finish",
     )(
         right,
-        [across, beside, diagonal],
+        [beside, across, diagonal],
         swapped,
         swapped_late,
         both,

time: 17.5 us -> 17.6 us (level)
  no operation moved by 1% of the time
where the time goes in v28:
time: 17.6 us; the launch traced here: 17.4 us
  starting transfers between devices  8.35 us (47%)
  Pallas kernels  4.24 us (24%)
  waiting for transfers between devices  4.08 us (23%)
  between operations  0.72 us (4%)
    ppermute x4, starting transfers between devices, swap_over(): lax.ppermute(value, 'res', [(source, source ^ mask) for source in range(r...  7.76 us
    ppermute x4, waiting for transfers between devices, swap_over(): lax.ppermute(value, 'res', [(source, source ^ mask) for source in range(r...  2.9 us
    pallas_call x1, Pallas kernels, small_slice(): pl.pallas_call(functools.partial(small_finish_kernel, scale), in_specs=[v...  1.33 us
    pallas_call x1, Pallas kernels, small_slice(): pl.pallas_call(small_project_kernel, in_specs=[hbm] * 9, out_specs=[vmem]...  1.3 us
    ppermute x1, waiting for transfers between devices, small_slice(): lax.ppermute(jnp.where(own_is_near, diagonal[1], diagonal[0]), 'seq', swap)  1.17 us
    pallas_call x1, Pallas kernels, small_slice(): pl.pallas_call(functools.partial(small_own_kernel, scale), in_specs=[vmem...  1.16 us
    ppermute x1, starting transfers between devices, small_slice(): other_cot = lax.ppermute(coupling_cotangent, 'seq', swap)  0.52 us
    pallas_call x1, Pallas kernels, small_slice(): pl.pallas_call(functools.partial(small_partner_kernel, residues), in_spec...  0.45 us
  transfers between devices with their start and end apart: 7, of which 5 were waited for; matrix products, arithmetic and copies ran while one was open for 0% of the time, Pallas kernels for 17%

profile of v28, /device:TPU:0, one launch (start us, length us, event | category | flops | bytes accessed | tf_op | source)
XLA Modules:
  0.0 17.4 jit_solution(12517703206356842575)
XLA Ops:
  0.6 0.0 copy-start
  0.6 0.5 %collective-permute-start = (bf16[4,16,128]{2,1,0:T(8,128)(2,1)}, bf16[4,16,128]{2,1,0:T(8,128)(2,1)S(1)}, u32[]{:S(2)}, u32[]{:S(2)}) collective-permute-start(bf16[4,16,128]{2,1,0:T(8,128)(2,1)} %cot_hbm.1), channel_id=1, source_target_pairs={{0,1},{1,0},{2,3},{3,2},{4,5},{5,4},{6,7},{7,6},{8,9},{9,8},{10,11... | collective-permute-start | bytes 49160 | tf_op jit(solution)/shard_map/ppermute | solution.py:670
  1.2 1.3 %project.1 = (bf16[2,32,128]{2,1,0:T(8,128)(2,1)S(1)}, f32[128,256]{1,0:T(8,128)S(1)}, f32[128,128]{1,0:T(8,128)S(1)}, bf16[256,256]{1,0:T(8,128)(2,1)S(1)}, f32...) custom-call(bf16[32,4,256]{2,1,0:T(4,128)(2,1)} %x_hbm.1, f32[1,256]{1,0:T(1,128)} %bitcast.19, ...), custom_call_target="tpu_custom_call" | custom-call | tf_op jit(solution)/shard_map/project/pallas_call | solution.py:673
  2.5 0.0 collective-permute-done.other_ref
  2.5 3.7 %collective-permute-start.1 = (bf16[4,32,128]{2,1,0:T(8,128)(2,1)S(1)}, bf16[4,32,128]{2,1,0:T(8,128)(2,1)S(1)}, u32[]{:S(2)}, u32[]{:S(2)}) collective-permute-start(bf16[4,32,128]{2,1,0:T(8,128)(2,1)S(1)} %pad_maximum_fusion.2), channel_id=1, source_target_pairs={{0,8},{2,10},{4,12},{6,14},{8,0},{10,2},{12,4},{14,6},{1,9},{3,11}... | collective-permute-start | bytes 98312 | tf_op jit(solution)/shard_map/ppermute | solution.py:716
  6.2 0.0 copy-done
  6.2 1.2 %own_pieces.1 = (f32[4,32,128]{2,1,0:T(8,128)S(1)}, bf16[512,128]{1,0:T(8,128)(2,1)S(1)}, bf16[512,128]{1,0:T(8,128)(2,1)S(1)}, bf16[1024,128]{1,0:T(8,128)(2,1)...) custom-call(bf16[4,16,128]{2,1,0:T(8,128)(2,1)S(1)} %get-tuple-element.21.own_ref, ...), custom_call_target="tpu_custom_call" | custom-call | tf_op jit(solution)/shard_map/own_pieces/pallas_call | solution.py:724
  7.4 0.8 %collective-permute-done.1.got_ref = bf16[4,32,128]{2,1,0:T(8,128)(2,1)S(1)} collective-permute-done((bf16[4,32,128]{2,1,0:T(8,128)(2,1)S(1)}, bf16[4,32,128]{2,1,0:T(8,128)(2,1)S(1)}, u32[]{:S(2)}, u32[]{:S(2)}) %collective-permute-start.1) | collective-permute-done | bytes 32800 | tf_op jit(solution)/shard_map/ppermute | solution.py:716
  8.2 0.1 collective-permute-start.2
  8.3 0.5 %partner_pieces.1 = (bf16[4,3,32,128]{3,2,1,0:T(8,128)(2,1)S(1)}, f32[4,32,128]{2,1,0:T(8,128)S(1)}, bf16[2,32,128]{2,1,0:T(8,128)(2,1)S(1)}) custom-call(bf16[4,32,128]{2,1,0:T(8,128)(2,1)S(1)} %collective-permute-done.1.got_ref, bf16[128,1024]{1,0:T(8,128)(2,1)S(1)} %get-tuple-element.23.sorted_wt_ref, f32[4,32,128]{2,1,0:T(8,128)S(1)} %get-tuple-element.24.keep_ref, ...), custom_call_target="tpu_custom_call" | custom-call | tf_op jit(solution)/shard_map/partner_pieces/pallas_call | solution.py:747
  8.8 2.8 %collective-permute-start.5 = (bf16[3,32,128]{2,1,0:T(8,128)(2,1)S(1)}, bf16[3,32,128]{2,1,0:T(8,128)(2,1)S(1)}, u32[]{:S(2)}, u32[]{:S(2)}) collective-permute-start(bf16[3,32,128]{2,1,0:T(8,128)(2,1)S(1)} %get-tuple-element.38), channel_id=1, source_target_pairs={{0,6},{2,4},{4,2},{6,0},{8,14},{10,12},{12,10},{14,8},{1,7},{3,5},... | collective-permute-start | bytes 73736 | tf_op jit(solution)/shard_map/ppermute | solution.py:716
  11.6 0.0 collective-permute-done.2.swapped_ref
  11.6 0.6 %collective-permute-start.3 = (bf16[4,32,128]{2,1,0:T(8,128)(2,1)S(1)}, bf16[4,32,128]{2,1,0:T(8,128)(2,1)S(1)}, u32[]{:S(2)}, u32[]{:S(2)}) collective-permute-start(bf16[4,32,128]{2,1,0:T(8,128)(2,1)S(1)} %get-tuple-element.44), channel_id=1, source_target_pairs={{0,2},{2,0},{4,6},{6,4},{8,10},{10,8},{12,14},{14,12},{1,3},{3,1},... | collective-permute-start | bytes 98312 | tf_op jit(solution)/shard_map/ppermute | solution.py:716
  12.2 0.7 %collective-permute-start.4 = (bf16[4,32,128]{2,1,0:T(8,128)(2,1)S(1)}, bf16[4,32,128]{2,1,0:T(8,128)(2,1)S(1)}, u32[]{:S(2)}, u32[]{:S(2)}) collective-permute-start(bf16[4,32,128]{2,1,0:T(8,128)(2,1)S(1)} %get-tuple-element.43), channel_id=1, source_target_pairs={{0,4},{2,6},{4,0},{6,2},{8,12},{10,14},{12,8},{14,10},{1,5},{3,7},... | collective-permute-start | bytes 98312 | tf_op jit(solution)/shard_map/ppermute | solution.py:716
  12.9 0.7 %collective-permute-done.5.part_refs_2_ = bf16[3,32,128]{2,1,0:T(8,128)(2,1)S(1)} collective-permute-done((bf16[3,32,128]{2,1,0:T(8,128)(2,1)S(1)}, bf16[3,32,128]{2,1,0:T(8,128)(2,1)S(1)}, u32[]{:S(2)}, u32[]{:S(2)}) %collective-permute-start.5) | collective-permute-done | bytes 24608 | tf_op jit(solution)/shard_map/ppermute | solution.py:716
  13.6 0.0 collective-permute-start.6
  13.6 1.2 %collective-permute-done.6.swapped_late_ref = bf16[32,128]{1,0:T(8,128)(2,1)S(1)} collective-permute-done((bf16[32,128]{1,0:T(8,128)(2,1)S(1)}, bf16[32,128]{1,0:T(8,128)(2,1)S(1)}, u32[]{:S(2)}, u32[]{:S(2)}) %collective-permute-start.6) | collective-permute-done | bytes 8224 | tf_op jit(solution)/shard_map/ppermute | solution.py:764
  14.8 0.8 %collective-permute-done.3.part_refs_0_ = bf16[4,32,128]{2,1,0:T(8,128)(2,1)S(1)} collective-permute-done((bf16[4,32,128]{2,1,0:T(8,128)(2,1)S(1)}, bf16[4,32,128]{2,1,0:T(8,128)(2,1)S(1)}, u32[]{:S(2)}, u32[]{:S(2)}) %collective-permute-start.3) | collective-permute-done | bytes 32800 | tf_op jit(solution)/shard_map/ppermute | solution.py:716
  15.6 0.5 %collective-permute-done.4.part_refs_1_ = bf16[4,32,128]{2,1,0:T(8,128)(2,1)S(1)} collective-permute-done((bf16[4,32,128]{2,1,0:T(8,128)(2,1)S(1)}, bf16[4,32,128]{2,1,0:T(8,128)(2,1)S(1)}, u32[]{:S(2)}, u32[]{:S(2)}) %collective-permute-start.4) | collective-permute-done | bytes 32800 | tf_op jit(solution)/shard_map/ppermute | solution.py:716
  16.1 1.3 %finish.1 = (bf16[32,4,256]{2,1,0:T(4,128)(2,1)}, bf16[4,16,128]{2,1,0:T(8,128)(2,1)}) custom-call(bf16[2,32,128]{2,1,0:T(8,128)(2,1)S(1)} %get-tuple-element.25.right_ref, bf16[4,32,128]{2,1,0:T(8,128)(2,1)S(1)} %collective-permute-done.3.part_refs_0_, bf16[4,32,128]{2,1,0:T(8,128)(2,1)S(1)} %collective-permute-done.4.part_refs_1_, ...), custom_call_target="tpu_custom_call" | custom-call | tf_op jit(solution)/shard_map/finish/pallas_call | solution.py:768
  (8 shorter events, 0.0 us)
Async XLA Ops:
  0.6 5.6 %copy-start = (bf16[1024,128]{1,0:T(8,128)(2,1)S(1)}, bf16[1024,128]{1,0:T(8,128)(2,1)}, u32[]{:S(2)}) copy-start(bf16[1024,128]{1,0:T(8,128)(2,1)} %w_ref.1) | copy-start | bytes 786436
  0.6 1.8 %collective-permute-start = (bf16[4,16,128]{2,1,0:T(8,128)(2,1)}, bf16[4,16,128]{2,1,0:T(8,128)(2,1)S(1)}, u32[]{:S(2)}, u32[]{:S(2)}) collective-permute-start(bf16[4,16,128]{2,1,0:T(8,128)(2,1)} %cot_hbm.1), channel_id=1, source_target_pairs={{0,1},{1,0},{2,3},{3,2},{4,5},{5,4},{6,7},{7,6},{8,9},{9,8},{10,11... | collective-permute-start | bytes 49160 | tf_op jit(solution)/shard_map/ppermute | solution.py:670
  2.5 5.7 %collective-permute-start.1 = (bf16[4,32,128]{2,1,0:T(8,128)(2,1)S(1)}, bf16[4,32,128]{2,1,0:T(8,128)(2,1)S(1)}, u32[]{:S(2)}, u32[]{:S(2)}) collective-permute-start(bf16[4,32,128]{2,1,0:T(8,128)(2,1)S(1)} %pad_maximum_fusion.2), channel_id=1, source_target_pairs={{0,8},{2,10},{4,12},{6,14},{8,0},{10,2},{12,4},{14,6},{1,9},{3,11}... | collective-permute-start | bytes 98312 | tf_op jit(solution)/shard_map/ppermute | solution.py:716
  8.2 3.3 %collective-permute-start.2 = (bf16[2,32,128]{2,1,0:T(8,128)(2,1)S(1)}, bf16[2,32,128]{2,1,0:T(8,128)(2,1)S(1)}, u32[]{:S(2)}, u32[]{:S(2)}) collective-permute-start(bf16[2,32,128]{2,1,0:T(8,128)(2,1)S(1)} %pad_maximum_fusion.3), channel_id=1, source_target_pairs={{0,1},{1,0},{2,3},{3,2},{4,5},{5,4},{6,7},{7,6},{8,9},{9,8},{10,11... | collective-permute-start | bytes 49160 | tf_op jit(solution)/shard_map/ppermute | solution.py:745
  8.8 4.8 %collective-permute-start.5 = (bf16[3,32,128]{2,1,0:T(8,128)(2,1)S(1)}, bf16[3,32,128]{2,1,0:T(8,128)(2,1)S(1)}, u32[]{:S(2)}, u32[]{:S(2)}) collective-permute-start(bf16[3,32,128]{2,1,0:T(8,128)(2,1)S(1)} %get-tuple-element.38), channel_id=1, source_target_pairs={{0,6},{2,4},{4,2},{6,0},{8,14},{10,12},{12,10},{14,8},{1,7},{3,5},... | collective-permute-start | bytes 73736 | tf_op jit(solution)/shard_map/ppermute | solution.py:716
  11.6 4.0 %collective-permute-start.3 = (bf16[4,32,128]{2,1,0:T(8,128)(2,1)S(1)}, bf16[4,32,128]{2,1,0:T(8,128)(2,1)S(1)}, u32[]{:S(2)}, u32[]{:S(2)}) collective-permute-start(bf16[4,32,128]{2,1,0:T(8,128)(2,1)S(1)} %get-tuple-element.44), channel_id=1, source_target_pairs={{0,2},{2,0},{4,6},{6,4},{8,10},{10,8},{12,14},{14,12},{1,3},{3,1},... | collective-permute-start | bytes 98312 | tf_op jit(solution)/shard_map/ppermute | solution.py:716
  12.2 3.9 %collective-permute-start.4 = (bf16[4,32,128]{2,1,0:T(8,128)(2,1)S(1)}, bf16[4,32,128]{2,1,0:T(8,128)(2,1)S(1)}, u32[]{:S(2)}, u32[]{:S(2)}) collective-permute-start(bf16[4,32,128]{2,1,0:T(8,128)(2,1)S(1)} %get-tuple-element.43), channel_id=1, source_target_pairs={{0,4},{2,6},{4,0},{6,2},{8,12},{10,14},{12,8},{14,10},{1,5},{3,7},... | collective-permute-start | bytes 98312 | tf_op jit(solution)/shard_map/ppermute | solution.py:716
  13.6 1.2 %collective-permute-start.6 = (bf16[32,128]{1,0:T(8,128)(2,1)S(1)}, bf16[32,128]{1,0:T(8,128)(2,1)S(1)}, u32[]{:S(2)}, u32[]{:S(2)}) collective-permute-start(bf16[32,128]{1,0:T(8,128)(2,1)S(1)} %fusion), channel_id=1, source_target_pairs={{0,1},{1,0},{2,3},{3,2},{4,5},{5,4},{6,7},{7,6},{8,9},{9,8},{10,11... | collective-permute-start | bytes 24584 | tf_op jit(solution)/shard_map/ppermute | solution.py:764

commit v29 on v27

--- a/solution.py
+++ b/solution.py
@@ -553,58 +553,6 @@
     here = rank & 3
 
     blocks_of = [right_ref] + list(part_refs)
-    right_all = jnp.concatenate(
-        [ref[0] for ref in blocks_of] + [ref[1] for ref in blocks_of], axis=1
-    )
-    spots = [
-        pl.ds(pl.multiple_of(lax.bitwise_xor(here, mask) * LANES, LANES), LANES)
-        for mask in range(ranks)
-    ]
-    outer = jnp.concatenate(
-        [outer_near_ref[spot, :] for spot in spots] + [outer_far_ref[spot, :] for spot in spots],
-        axis=0,
-    )
-    left_cot = jnp.dot(right_all, outer, preferred_element_type=F32)
-    right_cot = keep_ref[0]
-    for part_ref in part_refs:
-        right_cot = right_cot + part_ref[2].astype(F32)
-    blocks = lane_block((seqs, LANES), depth)
-    column = lane_block((seqs, LANES), 1) % residues
-    spread = jnp.concatenate(
-        [
-            jnp.concatenate(
-                [
-                    jnp.where(blocks == place, left_cot, 0.0),
-                    jnp.where(column == place, right_cot, 0.0),
-                ],
-                axis=1,
-            )
-            for place in range(residues)
-        ],
-        axis=0,
-    )
-    rows = residues * seqs
-    parts = jnp.concatenate(split_two(spread), axis=0)
-    weight = jnp.concatenate([spread_w_ref[0:LANES, :], columns_w_ref[...]], axis=0)
-    ln_cot = jnp.dot(parts, weight, preferred_element_type=F32)
-    ln_cot = ln_cot[0:rows] + ln_cot[rows : 2 * rows]
-    tiles = range(lines_ref.shape[0])
-    for place in range(residues):
-        for tile in tiles:
-            lines_ref[tile, pl.ds(place, seqs, stride=residues), :] = ln_cot[
-                place * seqs : (place + 1) * seqs, tile * LANES : (tile + 1) * LANES
-            ]
-    gained = jnp.concatenate([lines_ref[tile, 0:rows, :] for tile in tiles], axis=1) * gain_ref[...]
-    normed = normed_ref[...]
-    grad = inv_std_ref[:, 0:1] * (
-        gained
-        - jnp.mean(gained, axis=-1, keepdims=True)
-        - normed * jnp.mean(gained * normed, axis=-1, keepdims=True)
-    )
-    grad_ref[...] = grad.reshape(grad_ref.shape).astype(BF16)
-    grad_copy = pltpu.make_async_copy(grad_ref, grad_hbm, semaphores.at[0])
-    grad_copy.start()
-
     half = jnp.where(mine == lax.shift_right_logical(rank, 2), 0, 1)
     for mask, ref in enumerate(blocks_of):
         near_ref[mask] = ref[half]
@@ -640,6 +588,58 @@
     pair_ref[...] = (pair + offset_ref[...]).astype(BF16).reshape(pair_ref.shape)
     pair_copy = pltpu.make_async_copy(pair_ref, pair_hbm, semaphores.at[1])
     pair_copy.start()
+
+    right_all = jnp.concatenate(
+        [ref[0] for ref in blocks_of] + [ref[1] for ref in blocks_of], axis=1
+    )
+    spots = [
+        pl.ds(pl.multiple_of(lax.bitwise_xor(here, mask) * LANES, LANES), LANES)
+        for mask in range(ranks)
+    ]
+    outer = jnp.concatenate(
+        [outer_near_ref[spot, :] for spot in spots] + [outer_far_ref[spot, :] for spot in spots],
+        axis=0,
+    )
+    left_cot = jnp.dot(right_all, outer, preferred_element_type=F32)
+    right_cot = keep_ref[0]
+    for part_ref in part_refs:
+        right_cot = right_cot + part_ref[2].astype(F32)
+    blocks = lane_block((seqs, LANES), depth)
+    column = lane_block((seqs, LANES), 1) % residues
+    spread = jnp.concatenate(
+        [
+            jnp.concatenate(
+                [
+                    jnp.where(blocks == place, left_cot, 0.0),
+                    jnp.where(column == place, right_cot, 0.0),
+                ],
+                axis=1,
+            )
+            for place in range(residues)
+        ],
+        axis=0,
+    )
+    rows = residues * seqs
+    parts = jnp.concatenate(split_two(spread), axis=0)
+    weight = jnp.concatenate([spread_w_ref[0:LANES, :], columns_w_ref[...]], axis=0)
+    ln_cot = jnp.dot(parts, weight, preferred_element_type=F32)
+    ln_cot = ln_cot[0:rows] + ln_cot[rows : 2 * rows]
+    tiles = range(lines_ref.shape[0])
+    for place in range(residues):
+        for tile in tiles:
+            lines_ref[tile, pl.ds(place, seqs, stride=residues), :] = ln_cot[
+                place * seqs : (place + 1) * seqs, tile * LANES : (tile + 1) * LANES
+            ]
+    gained = jnp.concatenate([lines_ref[tile, 0:rows, :] for tile in tiles], axis=1) * gain_ref[...]
+    normed = normed_ref[...]
+    grad = inv_std_ref[:, 0:1] * (
+        gained
+        - jnp.mean(gained, axis=-1, keepdims=True)
+        - normed * jnp.mean(gained * normed, axis=-1, keepdims=True)
+    )
+    grad_ref[...] = grad.reshape(grad_ref.shape).astype(BF16)
+    grad_copy = pltpu.make_async_copy(grad_ref, grad_hbm, semaphores.at[0])
+    grad_copy.start()
     grad_copy.wait()
     pair_copy.wait()
 

time: 17.5 us -> 17.8 us (1.017)
  Pallas kernels: 4.24 us -> 4.57 us
    pallas_call x1, Pallas kernels: 1.33 us -> 1.66 us  [small_slice(): pl.pallas_call(functools.partial(small_finish_kernel, scale), in_specs=[v...]
  transfers between devices with their start and end apart: 7 -> 7, of which waited for: 5 -> 5; matrix products, arithmetic and copies ran while one was open for 0% -> 0% of each run, Pallas kernels for 17% -> 16%
where the time goes in v29:
time: 17.8 us; the launch traced here: 17.7 us
  starting transfers between devices  8.35 us (47%)
  Pallas kernels  4.57 us (26%)
  waiting for transfers between devices  3.99 us (22%)
  between operations  0.72 us (4%)
    ppermute x4, starting transfers between devices, swap_over(): lax.ppermute(value, 'res', [(source, source ^ mask) for source in range(r...  7.76 us
    ppermute x4, waiting for transfers between devices, swap_over(): lax.ppermute(value, 'res', [(source, source ^ mask) for source in range(r...  2.82 us
    pallas_call x1, Pallas kernels, small_slice(): pl.pallas_call(functools.partial(small_finish_kernel, scale), in_specs=[v...  1.66 us
    pallas_call x1, Pallas kernels, small_slice(): pl.pallas_call(small_project_kernel, in_specs=[hbm] * 9, out_specs=[vmem]...  1.3 us
    ppermute x1, waiting for transfers between devices, small_slice(): lax.ppermute(jnp.where(own_is_near, diagonal[1], diagonal[0]), 'seq', swap)  1.17 us
    pallas_call x1, Pallas kernels, small_slice(): pl.pallas_call(functools.partial(small_own_kernel, scale), in_specs=[vmem...  1.16 us
    ppermute x1, starting transfers between devices, small_slice(): other_cot = lax.ppermute(coupling_cotangent, 'seq', swap)  0.52 us
    pallas_call x1, Pallas kernels, small_slice(): pl.pallas_call(functools.partial(small_partner_kernel, residues), in_spec...  0.45 us
  transfers between devices with their start and end apart: 7, of which 5 were waited for; matrix products, arithmetic and copies ran while one was open for 0% of the time, Pallas kernels for 16%

profile of v29, /device:TPU:0, one launch (start us, length us, event | category | flops | bytes accessed | tf_op | source)
XLA Modules:
  0.0 17.7 jit_solution(2905340254731707300)
XLA Ops:
  0.6 0.0 copy-start
  0.6 0.5 %collective-permute-start = (bf16[4,16,128]{2,1,0:T(8,128)(2,1)}, bf16[4,16,128]{2,1,0:T(8,128)(2,1)S(1)}, u32[]{:S(2)}, u32[]{:S(2)}) collective-permute-start(bf16[4,16,128]{2,1,0:T(8,128)(2,1)} %cot_hbm.1), channel_id=1, source_target_pairs={{0,1},{1,0},{2,3},{3,2},{4,5},{5,4},{6,7},{7,6},{8,9},{9,8},{10,11... | collective-permute-start | bytes 49160 | tf_op jit(solution)/shard_map/ppermute | solution.py:671
  1.2 1.3 %project.1 = (bf16[2,32,128]{2,1,0:T(8,128)(2,1)S(1)}, f32[128,256]{1,0:T(8,128)S(1)}, f32[128,128]{1,0:T(8,128)S(1)}, bf16[256,256]{1,0:T(8,128)(2,1)S(1)}, f32...) custom-call(bf16[32,4,256]{2,1,0:T(4,128)(2,1)} %x_hbm.1, f32[1,256]{1,0:T(1,128)} %bitcast.19, ...), custom_call_target="tpu_custom_call" | custom-call | tf_op jit(solution)/shard_map/project/pallas_call | solution.py:674
  2.5 0.0 collective-permute-done.other_ref
  2.5 3.7 %collective-permute-start.1 = (bf16[4,32,128]{2,1,0:T(8,128)(2,1)S(1)}, bf16[4,32,128]{2,1,0:T(8,128)(2,1)S(1)}, u32[]{:S(2)}, u32[]{:S(2)}) collective-permute-start(bf16[4,32,128]{2,1,0:T(8,128)(2,1)S(1)} %pad_maximum_fusion.2), channel_id=1, source_target_pairs={{0,8},{2,10},{4,12},{6,14},{8,0},{10,2},{12,4},{14,6},{1,9},{3,11}... | collective-permute-start | bytes 98312 | tf_op jit(solution)/shard_map/ppermute | solution.py:717
  6.2 0.0 copy-done
  6.2 1.2 %own_pieces.1 = (f32[4,32,128]{2,1,0:T(8,128)S(1)}, bf16[512,128]{1,0:T(8,128)(2,1)S(1)}, bf16[512,128]{1,0:T(8,128)(2,1)S(1)}, bf16[1024,128]{1,0:T(8,128)(2,1)...) custom-call(bf16[4,16,128]{2,1,0:T(8,128)(2,1)S(1)} %get-tuple-element.21.own_ref, ...), custom_call_target="tpu_custom_call" | custom-call | tf_op jit(solution)/shard_map/own_pieces/pallas_call | solution.py:725
  7.4 0.8 %collective-permute-done.1.got_ref = bf16[4,32,128]{2,1,0:T(8,128)(2,1)S(1)} collective-permute-done((bf16[4,32,128]{2,1,0:T(8,128)(2,1)S(1)}, bf16[4,32,128]{2,1,0:T(8,128)(2,1)S(1)}, u32[]{:S(2)}, u32[]{:S(2)}) %collective-permute-start.1) | collective-permute-done | bytes 32800 | tf_op jit(solution)/shard_map/ppermute | solution.py:717
  8.2 0.1 collective-permute-start.2
  8.3 0.5 %partner_pieces.1 = (bf16[4,3,32,128]{3,2,1,0:T(8,128)(2,1)S(1)}, f32[4,32,128]{2,1,0:T(8,128)S(1)}, bf16[2,32,128]{2,1,0:T(8,128)(2,1)S(1)}) custom-call(bf16[4,32,128]{2,1,0:T(8,128)(2,1)S(1)} %collective-permute-done.1.got_ref, bf16[128,1024]{1,0:T(8,128)(2,1)S(1)} %get-tuple-element.23.sorted_wt_ref, f32[4,32,128]{2,1,0:T(8,128)S(1)} %get-tuple-element.24.keep_ref, ...), custom_call_target="tpu_custom_call" | custom-call | tf_op jit(solution)/shard_map/partner_pieces/pallas_call | solution.py:748
  8.8 2.8 %collective-permute-start.5 = (bf16[3,32,128]{2,1,0:T(8,128)(2,1)S(1)}, bf16[3,32,128]{2,1,0:T(8,128)(2,1)S(1)}, u32[]{:S(2)}, u32[]{:S(2)}) collective-permute-start(bf16[3,32,128]{2,1,0:T(8,128)(2,1)S(1)} %get-tuple-element.38), channel_id=1, source_target_pairs={{0,6},{2,4},{4,2},{6,0},{8,14},{10,12},{12,10},{14,8},{1,7},{3,5},... | collective-permute-start | bytes 73736 | tf_op jit(solution)/shard_map/ppermute | solution.py:717
  11.6 0.0 collective-permute-done.2.swapped_ref
  11.6 0.5 %collective-permute-start.3 = (bf16[4,32,128]{2,1,0:T(8,128)(2,1)S(1)}, bf16[4,32,128]{2,1,0:T(8,128)(2,1)S(1)}, u32[]{:S(2)}, u32[]{:S(2)}) collective-permute-start(bf16[4,32,128]{2,1,0:T(8,128)(2,1)S(1)} %get-tuple-element.44), channel_id=1, source_target_pairs={{0,4},{2,6},{4,0},{6,2},{8,12},{10,14},{12,8},{14,10},{1,5},{3,7},... | collective-permute-start | bytes 98312 | tf_op jit(solution)/shard_map/ppermute | solution.py:717
  12.1 0.7 %collective-permute-start.4 = (bf16[4,32,128]{2,1,0:T(8,128)(2,1)S(1)}, bf16[4,32,128]{2,1,0:T(8,128)(2,1)S(1)}, u32[]{:S(2)}, u32[]{:S(2)}) collective-permute-start(bf16[4,32,128]{2,1,0:T(8,128)(2,1)S(1)} %get-tuple-element.43), channel_id=1, source_target_pairs={{0,2},{2,0},{4,6},{6,4},{8,10},{10,8},{12,14},{14,12},{1,3},{3,1},... | collective-permute-start | bytes 98312 | tf_op jit(solution)/shard_map/ppermute | solution.py:717
  12.9 0.7 %collective-permute-done.5.part_refs_2_ = bf16[3,32,128]{2,1,0:T(8,128)(2,1)S(1)} collective-permute-done((bf16[3,32,128]{2,1,0:T(8,128)(2,1)S(1)}, bf16[3,32,128]{2,1,0:T(8,128)(2,1)S(1)}, u32[]{:S(2)}, u32[]{:S(2)}) %collective-permute-start.5) | collective-permute-done | bytes 24608 | tf_op jit(solution)/shard_map/ppermute | solution.py:717
  13.6 0.0 collective-permute-start.6
  13.6 1.2 %collective-permute-done.6.swapped_late_ref = bf16[32,128]{1,0:T(8,128)(2,1)S(1)} collective-permute-done((bf16[32,128]{1,0:T(8,128)(2,1)S(1)}, bf16[32,128]{1,0:T(8,128)(2,1)S(1)}, u32[]{:S(2)}, u32[]{:S(2)}) %collective-permute-start.6) | collective-permute-done | bytes 8224 | tf_op jit(solution)/shard_map/ppermute | solution.py:765
  14.8 0.8 %collective-permute-done.3.part_refs_0_ = bf16[4,32,128]{2,1,0:T(8,128)(2,1)S(1)} collective-permute-done((bf16[4,32,128]{2,1,0:T(8,128)(2,1)S(1)}, bf16[4,32,128]{2,1,0:T(8,128)(2,1)S(1)}, u32[]{:S(2)}, u32[]{:S(2)}) %collective-permute-start.3) | collective-permute-done | bytes 32800 | tf_op jit(solution)/shard_map/ppermute | solution.py:717
  15.6 0.4 %collective-permute-done.4.part_refs_1_ = bf16[4,32,128]{2,1,0:T(8,128)(2,1)S(1)} collective-permute-done((bf16[4,32,128]{2,1,0:T(8,128)(2,1)S(1)}, bf16[4,32,128]{2,1,0:T(8,128)(2,1)S(1)}, u32[]{:S(2)}, u32[]{:S(2)}) %collective-permute-start.4) | collective-permute-done | bytes 32800 | tf_op jit(solution)/shard_map/ppermute | solution.py:717
  16.0 1.7 %finish.1 = (bf16[32,4,256]{2,1,0:T(4,128)(2,1)}, bf16[4,16,128]{2,1,0:T(8,128)(2,1)}) custom-call(bf16[2,32,128]{2,1,0:T(8,128)(2,1)S(1)} %get-tuple-element.25.right_ref, bf16[4,32,128]{2,1,0:T(8,128)(2,1)S(1)} %collective-permute-done.3.part_refs_0_, bf16[4,32,128]{2,1,0:T(8,128)(2,1)S(1)} %collective-permute-done.4.part_refs_1_, ...), custom_call_target="tpu_custom_call" | custom-call | tf_op jit(solution)/shard_map/finish/pallas_call | solution.py:769
  (8 shorter events, 0.0 us)
Async XLA Ops:
  0.6 5.6 %copy-start = (bf16[1024,128]{1,0:T(8,128)(2,1)S(1)}, bf16[1024,128]{1,0:T(8,128)(2,1)}, u32[]{:S(2)}) copy-start(bf16[1024,128]{1,0:T(8,128)(2,1)} %w_ref.1) | copy-start | bytes 786436
  0.6 1.8 %collective-permute-start = (bf16[4,16,128]{2,1,0:T(8,128)(2,1)}, bf16[4,16,128]{2,1,0:T(8,128)(2,1)S(1)}, u32[]{:S(2)}, u32[]{:S(2)}) collective-permute-start(bf16[4,16,128]{2,1,0:T(8,128)(2,1)} %cot_hbm.1), channel_id=1, source_target_pairs={{0,1},{1,0},{2,3},{3,2},{4,5},{5,4},{6,7},{7,6},{8,9},{9,8},{10,11... | collective-permute-start | bytes 49160 | tf_op jit(solution)/shard_map/ppermute | solution.py:671
  2.5 5.7 %collective-permute-start.1 = (bf16[4,32,128]{2,1,0:T(8,128)(2,1)S(1)}, bf16[4,32,128]{2,1,0:T(8,128)(2,1)S(1)}, u32[]{:S(2)}, u32[]{:S(2)}) collective-permute-start(bf16[4,32,128]{2,1,0:T(8,128)(2,1)S(1)} %pad_maximum_fusion.2), channel_id=1, source_target_pairs={{0,8},{2,10},{4,12},{6,14},{8,0},{10,2},{12,4},{14,6},{1,9},{3,11}... | collective-permute-start | bytes 98312 | tf_op jit(solution)/shard_map/ppermute | solution.py:717
  8.2 3.3 %collective-permute-start.2 = (bf16[2,32,128]{2,1,0:T(8,128)(2,1)S(1)}, bf16[2,32,128]{2,1,0:T(8,128)(2,1)S(1)}, u32[]{:S(2)}, u32[]{:S(2)}) collective-permute-start(bf16[2,32,128]{2,1,0:T(8,128)(2,1)S(1)} %pad_maximum_fusion.3), channel_id=1, source_target_pairs={{0,1},{1,0},{2,3},{3,2},{4,5},{5,4},{6,7},{7,6},{8,9},{9,8},{10,11... | collective-permute-start | bytes 49160 | tf_op jit(solution)/shard_map/ppermute | solution.py:746
  8.8 4.8 %collective-permute-start.5 = (bf16[3,32,128]{2,1,0:T(8,128)(2,1)S(1)}, bf16[3,32,128]{2,1,0:T(8,128)(2,1)S(1)}, u32[]{:S(2)}, u32[]{:S(2)}) collective-permute-start(bf16[3,32,128]{2,1,0:T(8,128)(2,1)S(1)} %get-tuple-element.38), channel_id=1, source_target_pairs={{0,6},{2,4},{4,2},{6,0},{8,14},{10,12},{12,10},{14,8},{1,7},{3,5},... | collective-permute-start | bytes 73736 | tf_op jit(solution)/shard_map/ppermute | solution.py:717
  11.6 4.0 %collective-permute-start.3 = (bf16[4,32,128]{2,1,0:T(8,128)(2,1)S(1)}, bf16[4,32,128]{2,1,0:T(8,128)(2,1)S(1)}, u32[]{:S(2)}, u32[]{:S(2)}) collective-permute-start(bf16[4,32,128]{2,1,0:T(8,128)(2,1)S(1)} %get-tuple-element.44), channel_id=1, source_target_pairs={{0,4},{2,6},{4,0},{6,2},{8,12},{10,14},{12,8},{14,10},{1,5},{3,7},... | collective-permute-start | bytes 98312 | tf_op jit(solution)/shard_map/ppermute | solution.py:717
  12.1 3.9 %collective-permute-start.4 = (bf16[4,32,128]{2,1,0:T(8,128)(2,1)S(1)}, bf16[4,32,128]{2,1,0:T(8,128)(2,1)S(1)}, u32[]{:S(2)}, u32[]{:S(2)}) collective-permute-start(bf16[4,32,128]{2,1,0:T(8,128)(2,1)S(1)} %get-tuple-element.43), channel_id=1, source_target_pairs={{0,2},{2,0},{4,6},{6,4},{8,10},{10,8},{12,14},{14,12},{1,3},{3,1},... | collective-permute-start | bytes 98312 | tf_op jit(solution)/shard_map/ppermute | solution.py:717
  13.6 1.2 %collective-permute-start.6 = (bf16[32,128]{1,0:T(8,128)(2,1)S(1)}, bf16[32,128]{1,0:T(8,128)(2,1)S(1)}, u32[]{:S(2)}, u32[]{:S(2)}) collective-permute-start(bf16[32,128]{1,0:T(8,128)(2,1)S(1)} %fusion), channel_id=1, source_target_pairs={{0,1},{1,0},{2,3},{3,2},{4,5},{5,4},{6,7},{7,6},{8,9},{9,8},{10,11... | collective-permute-start | bytes 24584 | tf_op jit(solution)/shard_map/ppermute | solution.py:765

commit v30 on v27

--- a/solution.py
+++ b/solution.py
@@ -596,7 +596,8 @@
             ]
     gained = jnp.concatenate([lines_ref[tile, 0:rows, :] for tile in tiles], axis=1) * gain_ref[...]
     normed = normed_ref[...]
-    grad = inv_std_ref[:, 0:1] * (
+    inv_std = jnp.concatenate([inv_std_ref[...]] * len(tiles), axis=1)
+    grad = inv_std * (
         gained
         - jnp.mean(gained, axis=-1, keepdims=True)
         - normed * jnp.mean(gained * normed, axis=-1, keepdims=True)

time: 17.5 us -> 17.5 us (level)
  no operation moved by 1% of the time
where the time goes in v30:
time: 17.5 us; the launch traced here: 17.3 us
  starting transfers between devices  8.35 us (48%)
  Pallas kernels  4.23 us (24%)
  waiting for transfers between devices  3.99 us (23%)
  between operations  0.72 us (4%)
    ppermute x4, starting transfers between devices, swap_over(): lax.ppermute(value, 'res', [(source, source ^ mask) for source in range(r...  7.76 us
    ppermute x4, waiting for transfers between devices, swap_over(): lax.ppermute(value, 'res', [(source, source ^ mask) for source in range(r...  2.82 us
    pallas_call x1, Pallas kernels, small_slice(): pl.pallas_call(functools.partial(small_finish_kernel, scale), in_specs=[v...  1.32 us
    pallas_call x1, Pallas kernels, small_slice(): pl.pallas_call(small_project_kernel, in_specs=[hbm] * 9, out_specs=[vmem]...  1.3 us
    ppermute x1, waiting for transfers between devices, small_slice(): lax.ppermute(jnp.where(own_is_near, diagonal[1], diagonal[0]), 'seq', swap)  1.17 us
    pallas_call x1, Pallas kernels, small_slice(): pl.pallas_call(functools.partial(small_own_kernel, scale), in_specs=[vmem...  1.16 us
    ppermute x1, starting transfers between devices, small_slice(): other_cot = lax.ppermute(coupling_cotangent, 'seq', swap)  0.52 us
    pallas_call x1, Pallas kernels, small_slice(): pl.pallas_call(functools.partial(small_partner_kernel, residues), in_spec...  0.45 us
  transfers between devices with their start and end apart: 7, of which 5 were waited for; matrix products, arithmetic and copies ran while one was open for 0% of the time, Pallas kernels for 17%

profile of v30, /device:TPU:0, one launch (start us, length us, event | category | flops | bytes accessed | tf_op | source)
XLA Modules:
  0.0 17.3 jit_solution(17268285981370992422)
XLA Ops:
  0.6 0.0 copy-start
  0.6 0.5 %collective-permute-start = (bf16[4,16,128]{2,1,0:T(8,128)(2,1)}, bf16[4,16,128]{2,1,0:T(8,128)(2,1)S(1)}, u32[]{:S(2)}, u32[]{:S(2)}) collective-permute-start(bf16[4,16,128]{2,1,0:T(8,128)(2,1)} %cot_hbm.1), channel_id=1, source_target_pairs={{0,1},{1,0},{2,3},{3,2},{4,5},{5,4},{6,7},{7,6},{8,9},{9,8},{10,11... | collective-permute-start | bytes 49160 | tf_op jit(solution)/shard_map/ppermute | solution.py:672
  1.2 1.3 %project.1 = (bf16[2,32,128]{2,1,0:T(8,128)(2,1)S(1)}, f32[128,256]{1,0:T(8,128)S(1)}, f32[128,128]{1,0:T(8,128)S(1)}, bf16[256,256]{1,0:T(8,128)(2,1)S(1)}, f32...) custom-call(bf16[32,4,256]{2,1,0:T(4,128)(2,1)} %x_hbm.1, f32[1,256]{1,0:T(1,128)} %bitcast.19, ...), custom_call_target="tpu_custom_call" | custom-call | tf_op jit(solution)/shard_map/project/pallas_call | solution.py:675
  2.5 0.0 collective-permute-done.other_ref
  2.5 3.7 %collective-permute-start.1 = (bf16[4,32,128]{2,1,0:T(8,128)(2,1)S(1)}, bf16[4,32,128]{2,1,0:T(8,128)(2,1)S(1)}, u32[]{:S(2)}, u32[]{:S(2)}) collective-permute-start(bf16[4,32,128]{2,1,0:T(8,128)(2,1)S(1)} %pad_maximum_fusion.2), channel_id=1, source_target_pairs={{0,8},{2,10},{4,12},{6,14},{8,0},{10,2},{12,4},{14,6},{1,9},{3,11}... | collective-permute-start | bytes 98312 | tf_op jit(solution)/shard_map/ppermute | solution.py:718
  6.2 0.0 copy-done
  6.2 1.2 %own_pieces.1 = (f32[4,32,128]{2,1,0:T(8,128)S(1)}, bf16[512,128]{1,0:T(8,128)(2,1)S(1)}, bf16[512,128]{1,0:T(8,128)(2,1)S(1)}, bf16[1024,128]{1,0:T(8,128)(2,1)...) custom-call(bf16[4,16,128]{2,1,0:T(8,128)(2,1)S(1)} %get-tuple-element.21.own_ref, ...), custom_call_target="tpu_custom_call" | custom-call | tf_op jit(solution)/shard_map/own_pieces/pallas_call | solution.py:726
  7.4 0.8 %collective-permute-done.1.got_ref = bf16[4,32,128]{2,1,0:T(8,128)(2,1)S(1)} collective-permute-done((bf16[4,32,128]{2,1,0:T(8,128)(2,1)S(1)}, bf16[4,32,128]{2,1,0:T(8,128)(2,1)S(1)}, u32[]{:S(2)}, u32[]{:S(2)}) %collective-permute-start.1) | collective-permute-done | bytes 32800 | tf_op jit(solution)/shard_map/ppermute | solution.py:718
  8.2 0.1 collective-permute-start.2
  8.3 0.5 %partner_pieces.1 = (bf16[4,3,32,128]{3,2,1,0:T(8,128)(2,1)S(1)}, f32[4,32,128]{2,1,0:T(8,128)S(1)}, bf16[2,32,128]{2,1,0:T(8,128)(2,1)S(1)}) custom-call(bf16[4,32,128]{2,1,0:T(8,128)(2,1)S(1)} %collective-permute-done.1.got_ref, bf16[128,1024]{1,0:T(8,128)(2,1)S(1)} %get-tuple-element.23.sorted_wt_ref, f32[4,32,128]{2,1,0:T(8,128)S(1)} %get-tuple-element.24.keep_ref, ...), custom_call_target="tpu_custom_call" | custom-call | tf_op jit(solution)/shard_map/partner_pieces/pallas_call | solution.py:749
  8.8 2.8 %collective-permute-start.5 = (bf16[3,32,128]{2,1,0:T(8,128)(2,1)S(1)}, bf16[3,32,128]{2,1,0:T(8,128)(2,1)S(1)}, u32[]{:S(2)}, u32[]{:S(2)}) collective-permute-start(bf16[3,32,128]{2,1,0:T(8,128)(2,1)S(1)} %get-tuple-element.38), channel_id=1, source_target_pairs={{0,6},{2,4},{4,2},{6,0},{8,14},{10,12},{12,10},{14,8},{1,7},{3,5},... | collective-permute-start | bytes 73736 | tf_op jit(solution)/shard_map/ppermute | solution.py:718
  11.6 0.0 collective-permute-done.2.swapped_ref
  11.6 0.5 %collective-permute-start.3 = (bf16[4,32,128]{2,1,0:T(8,128)(2,1)S(1)}, bf16[4,32,128]{2,1,0:T(8,128)(2,1)S(1)}, u32[]{:S(2)}, u32[]{:S(2)}) collective-permute-start(bf16[4,32,128]{2,1,0:T(8,128)(2,1)S(1)} %get-tuple-element.44), channel_id=1, source_target_pairs={{0,4},{2,6},{4,0},{6,2},{8,12},{10,14},{12,8},{14,10},{1,5},{3,7},... | collective-permute-start | bytes 98312 | tf_op jit(solution)/shard_map/ppermute | solution.py:718
  12.1 0.7 %collective-permute-start.4 = (bf16[4,32,128]{2,1,0:T(8,128)(2,1)S(1)}, bf16[4,32,128]{2,1,0:T(8,128)(2,1)S(1)}, u32[]{:S(2)}, u32[]{:S(2)}) collective-permute-start(bf16[4,32,128]{2,1,0:T(8,128)(2,1)S(1)} %get-tuple-element.43), channel_id=1, source_target_pairs={{0,2},{2,0},{4,6},{6,4},{8,10},{10,8},{12,14},{14,12},{1,3},{3,1},... | collective-permute-start | bytes 98312 | tf_op jit(solution)/shard_map/ppermute | solution.py:718
  12.9 0.7 %collective-permute-done.5.part_refs_2_ = bf16[3,32,128]{2,1,0:T(8,128)(2,1)S(1)} collective-permute-done((bf16[3,32,128]{2,1,0:T(8,128)(2,1)S(1)}, bf16[3,32,128]{2,1,0:T(8,128)(2,1)S(1)}, u32[]{:S(2)}, u32[]{:S(2)}) %collective-permute-start.5) | collective-permute-done | bytes 24608 | tf_op jit(solution)/shard_map/ppermute | solution.py:718
  13.6 0.0 collective-permute-start.6
  13.6 1.2 %collective-permute-done.6.swapped_late_ref = bf16[32,128]{1,0:T(8,128)(2,1)S(1)} collective-permute-done((bf16[32,128]{1,0:T(8,128)(2,1)S(1)}, bf16[32,128]{1,0:T(8,128)(2,1)S(1)}, u32[]{:S(2)}, u32[]{:S(2)}) %collective-permute-start.6) | collective-permute-done | bytes 8224 | tf_op jit(solution)/shard_map/ppermute | solution.py:766
  14.8 0.8 %collective-permute-done.3.part_refs_0_ = bf16[4,32,128]{2,1,0:T(8,128)(2,1)S(1)} collective-permute-done((bf16[4,32,128]{2,1,0:T(8,128)(2,1)S(1)}, bf16[4,32,128]{2,1,0:T(8,128)(2,1)S(1)}, u32[]{:S(2)}, u32[]{:S(2)}) %collective-permute-start.3) | collective-permute-done | bytes 32800 | tf_op jit(solution)/shard_map/ppermute | solution.py:718
  15.6 0.4 %collective-permute-done.4.part_refs_1_ = bf16[4,32,128]{2,1,0:T(8,128)(2,1)S(1)} collective-permute-done((bf16[4,32,128]{2,1,0:T(8,128)(2,1)S(1)}, bf16[4,32,128]{2,1,0:T(8,128)(2,1)S(1)}, u32[]{:S(2)}, u32[]{:S(2)}) %collective-permute-start.4) | collective-permute-done | bytes 32800 | tf_op jit(solution)/shard_map/ppermute | solution.py:718
  16.0 1.3 %finish.1 = (bf16[32,4,256]{2,1,0:T(4,128)(2,1)}, bf16[4,16,128]{2,1,0:T(8,128)(2,1)}) custom-call(bf16[2,32,128]{2,1,0:T(8,128)(2,1)S(1)} %get-tuple-element.25.right_ref, bf16[4,32,128]{2,1,0:T(8,128)(2,1)S(1)} %collective-permute-done.3.part_refs_0_, bf16[4,32,128]{2,1,0:T(8,128)(2,1)S(1)} %collective-permute-done.4.part_refs_1_, ...), custom_call_target="tpu_custom_call" | custom-call | tf_op jit(solution)/shard_map/finish/pallas_call | solution.py:770
  (8 shorter events, 0.0 us)
Async XLA Ops:
  0.6 5.6 %copy-start = (bf16[1024,128]{1,0:T(8,128)(2,1)S(1)}, bf16[1024,128]{1,0:T(8,128)(2,1)}, u32[]{:S(2)}) copy-start(bf16[1024,128]{1,0:T(8,128)(2,1)} %w_ref.1) | copy-start | bytes 786436
  0.6 1.8 %collective-permute-start = (bf16[4,16,128]{2,1,0:T(8,128)(2,1)}, bf16[4,16,128]{2,1,0:T(8,128)(2,1)S(1)}, u32[]{:S(2)}, u32[]{:S(2)}) collective-permute-start(bf16[4,16,128]{2,1,0:T(8,128)(2,1)} %cot_hbm.1), channel_id=1, source_target_pairs={{0,1},{1,0},{2,3},{3,2},{4,5},{5,4},{6,7},{7,6},{8,9},{9,8},{10,11... | collective-permute-start | bytes 49160 | tf_op jit(solution)/shard_map/ppermute | solution.py:672
  2.5 5.7 %collective-permute-start.1 = (bf16[4,32,128]{2,1,0:T(8,128)(2,1)S(1)}, bf16[4,32,128]{2,1,0:T(8,128)(2,1)S(1)}, u32[]{:S(2)}, u32[]{:S(2)}) collective-permute-start(bf16[4,32,128]{2,1,0:T(8,128)(2,1)S(1)} %pad_maximum_fusion.2), channel_id=1, source_target_pairs={{0,8},{2,10},{4,12},{6,14},{8,0},{10,2},{12,4},{14,6},{1,9},{3,11}... | collective-permute-start | bytes 98312 | tf_op jit(solution)/shard_map/ppermute | solution.py:718
  8.2 3.3 %collective-permute-start.2 = (bf16[2,32,128]{2,1,0:T(8,128)(2,1)S(1)}, bf16[2,32,128]{2,1,0:T(8,128)(2,1)S(1)}, u32[]{:S(2)}, u32[]{:S(2)}) collective-permute-start(bf16[2,32,128]{2,1,0:T(8,128)(2,1)S(1)} %pad_maximum_fusion.3), channel_id=1, source_target_pairs={{0,1},{1,0},{2,3},{3,2},{4,5},{5,4},{6,7},{7,6},{8,9},{9,8},{10,11... | collective-permute-start | bytes 49160 | tf_op jit(solution)/shard_map/ppermute | solution.py:747
  8.8 4.8 %collective-permute-start.5 = (bf16[3,32,128]{2,1,0:T(8,128)(2,1)S(1)}, bf16[3,32,128]{2,1,0:T(8,128)(2,1)S(1)}, u32[]{:S(2)}, u32[]{:S(2)}) collective-permute-start(bf16[3,32,128]{2,1,0:T(8,128)(2,1)S(1)} %get-tuple-element.38), channel_id=1, source_target_pairs={{0,6},{2,4},{4,2},{6,0},{8,14},{10,12},{12,10},{14,8},{1,7},{3,5},... | collective-permute-start | bytes 73736 | tf_op jit(solution)/shard_map/ppermute | solution.py:718
  11.6 4.0 %collective-permute-start.3 = (bf16[4,32,128]{2,1,0:T(8,128)(2,1)S(1)}, bf16[4,32,128]{2,1,0:T(8,128)(2,1)S(1)}, u32[]{:S(2)}, u32[]{:S(2)}) collective-permute-start(bf16[4,32,128]{2,1,0:T(8,128)(2,1)S(1)} %get-tuple-element.44), channel_id=1, source_target_pairs={{0,4},{2,6},{4,0},{6,2},{8,12},{10,14},{12,8},{14,10},{1,5},{3,7},... | collective-permute-start | bytes 98312 | tf_op jit(solution)/shard_map/ppermute | solution.py:718
  12.1 3.9 %collective-permute-start.4 = (bf16[4,32,128]{2,1,0:T(8,128)(2,1)S(1)}, bf16[4,32,128]{2,1,0:T(8,128)(2,1)S(1)}, u32[]{:S(2)}, u32[]{:S(2)}) collective-permute-start(bf16[4,32,128]{2,1,0:T(8,128)(2,1)S(1)} %get-tuple-element.43), channel_id=1, source_target_pairs={{0,2},{2,0},{4,6},{6,4},{8,10},{10,8},{12,14},{14,12},{1,3},{3,1},... | collective-permute-start | bytes 98312 | tf_op jit(solution)/shard_map/ppermute | solution.py:718
  13.6 1.2 %collective-permute-start.6 = (bf16[32,128]{1,0:T(8,128)(2,1)S(1)}, bf16[32,128]{1,0:T(8,128)(2,1)S(1)}, u32[]{:S(2)}, u32[]{:S(2)}) collective-permute-start(bf16[32,128]{1,0:T(8,128)(2,1)S(1)} %fusion), channel_id=1, source_target_pairs={{0,1},{1,0},{2,3},{3,2},{4,5},{5,4},{6,7},{7,6},{8,9},{9,8},{10,11... | collective-permute-start | bytes 24584 | tf_op jit(solution)/shard_map/ppermute | solution.py:766
